TPU v7x, 32 devices: a whole 2x2x4 slice. The times are simulated.
32 devices in a mesh: groups: 2 (over x), dp: 16 (over z, y, core).
Axes of the slice: x: 2, y: 2, z: 4, core: 2. Of those that a mesh axis runs over, the one named last changes fastest.
Arguments:
- query: bfloat16 [8192, 4096], P(('groups', 'dp')), parts along dimension 0, may hold values from -400 to 400
- leaf_key_value: bfloat16 [8192, 1024], P(('groups', 'dp')), parts along dimension 0, may hold values from -6 to 6
- prefix_key_value: bfloat16 [4096, 1024], P(('groups', 'dp')), parts along dimension 0, may hold values from -6 to 6
- d_out: bfloat16 [8192, 4096], P(('groups', 'dp')), parts along dimension 0, may hold values from -6 to 6
- block_owner: int32 [32], P('groups'), parts along dimension 0, may hold values from 0 to 15, each once
- subtree_tokens: int32 [8], P('groups'), parts along dimension 0, may hold values from 256 to 1792, as said below
- leaf_id: int32 [32, 256], P(('groups', 'dp')), parts along dimension 0, may hold values from 0 to 63, never falling along the last dimension, each value on 1 to 128 neighbouring positions
- loss_mask: int32 [8192], P(('groups', 'dp')), parts along dimension 0, may hold values 0 or 1
Outputs:
- attended: bfloat16 [8192, 4096], P(('groups', 'dp')), parts along dimension 0
- d_query: bfloat16 [8192, 4096], P(('groups', 'dp')), parts along dimension 0
- d_leaf_kv: bfloat16 [8192, 1024], P(('groups', 'dp')), parts along dimension 0
- d_prefix_kv: bfloat16 [4096, 1024], P(('groups', 'dp')), parts along dimension 0
There are 2 independent parts, one for each index of `groups`. A program takes and returns all parts, laid end to end along the dimension named above; each array names one. Nothing has to cross between parts.
Inputs may be any that keep to these rules, and one draw needn't show every extreme that they name: `subtree_tokens`: sums to 4096; the smallest is 256 and the largest 7 * 256.
All inputs are finite; a program needn't handle non-finite values. No bound on the sum of `loss_mask` on one device may be relied on, other than what follows from the above.
Results may differ from a plain program's by a relative error of at most 0.029.
Values may be sent and summed in bfloat16 or wider, within the bound.
No kernel may reach another device: no remote copies, remote signals or barrier semaphores. Data moves between devices by JAX's collectives and lax.ppermute only.
A program may use at most 192 MiB of HBM per device.

v0:
```python
import functools

import jax
import jax.numpy as jnp
from jax import lax
from jax.experimental import pallas as pl
from jax.experimental.pallas import tpu as pltpu
from jax.sharding import PartitionSpec as P

HEAD_SIZE = 128
KEY_VALUE_HEADS = 4
GQ = 8
SCALE = HEAD_SIZE ** (-0.5)
LOG2E = 1.4426950408889634


def dot(a, b, contract):
    return lax.dot_general(a, b, (contract, ((), ())), preferred_element_type=jnp.float32)


def attention_kernel(
    owner_ref, tokens_ref, device_ref,
    q_ref, g_ref, leaf_kv_ref, leaf_ref, mask_ref, whole_ref,
    out_ref, dq_ref, dleaf_ref, dpre_ref,
    kv, kcat, vcat, kcat_t, vcat_t, bias, q_pick, g_pick, dk_sum, dv_sum, sems,
    *, prompts, per_prefix, block_len,
):
    head = pl.program_id(0)
    group = head // GQ
    within = lax.rem(head, GQ)
    count = q_ref.shape[0]
    span = per_prefix * block_len
    width = KEY_VALUE_HEADS * HEAD_SIZE

    first = device_ref[0] * count
    last = first + (count - 1)
    end = jnp.int32(0)
    pair_first = jnp.int32(0)
    pair_last = jnp.int32(0)
    border = jnp.int32(2**30)
    for p in range(prompts):
        end = end + tokens_ref[p]
        pair_first = pair_first + (end <= first).astype(jnp.int32)
        pair_last = pair_last + (end <= last).astype(jnp.int32)
        border = jnp.where(end > first, jnp.minimum(border, end), border)
    border = border - first

    def block_row(side, j):
        prefix = pair_first if side == 0 else pair_last
        return owner_ref[prefix * per_prefix + j]

    @pl.when(head == 0)
    def _():
        copies = []
        for side in range(2):
            for j in range(per_prefix):
                n = side * per_prefix + j
                rows = pl.ds(pl.multiple_of(block_row(side, j) * block_len, block_len), block_len)
                copy = pltpu.make_async_copy(
                    whole_ref.at[rows, :], kv.at[pl.ds(n * block_len, block_len), :], sems.at[n]
                )
                copy.start()
                copies.append(copy)
        leaf_row = jnp.broadcast_to(leaf_ref[...], (count, count))
        leaf_col = leaf_row.T
        key_at = lax.broadcasted_iota(jnp.int32, (count, count), 0)
        token_at = lax.broadcasted_iota(jnp.int32, (count, count), 1)
        same = (leaf_row == leaf_col) & (key_at <= token_at)
        same = same & ((key_at < border) == (token_at < border))
        bias[...] = jnp.where(same, 0.0, -1e30).astype(jnp.float32)
        mask_col = jnp.broadcast_to(mask_ref[...], (count, count)).T.astype(jnp.float32)
        in_first = key_at < border
        left = token_at < HEAD_SIZE
        pick = (in_first == left).astype(jnp.float32)
        q_pick[...] = pick.astype(jnp.bfloat16)
        g_pick[...] = (pick * mask_col).astype(jnp.bfloat16)
        dpre_ref[...] = jnp.zeros_like(dpre_ref)
        for copy in copies:
            copy.wait()

    key_cols = pl.ds(pl.multiple_of(group * HEAD_SIZE, HEAD_SIZE), HEAD_SIZE)
    value_cols = pl.ds(pl.multiple_of(width + group * HEAD_SIZE, HEAD_SIZE), HEAD_SIZE)

    @pl.when(within == 0)
    def _():
        for cat, cat_t, cols in ((kcat, kcat_t, key_cols), (vcat, vcat_t, value_cols)):
            for side in range(2):
                lanes = slice(side * HEAD_SIZE, (side + 1) * HEAD_SIZE)
                cat[0:span, lanes] = kv[side * span:(side + 1) * span, cols]
                cat[span:, lanes] = leaf_kv_ref[:, cols]
            cat_t[...] = cat[...].T
        dk_sum[...] = jnp.zeros_like(dk_sum)
        dv_sum[...] = jnp.zeros_like(dv_sum)

    q = q_ref[...]
    g = g_ref[...]
    q2 = jnp.concatenate([q, q], axis=1) * q_pick[...]
    g2 = jnp.concatenate([g, g], axis=1) * g_pick[...]
    first_side = lax.broadcasted_iota(jnp.int32, (HEAD_SIZE, count), 1) < border

    scores = dot(kcat[...], q2, ((1,), (1,))) * (SCALE * LOG2E)
    dprob = dot(vcat[...], g2, ((1,), (1,)))
    s_pre = scores[:span]
    s_leaf = scores[span:] + bias[...]
    top = jnp.maximum(
        jnp.max(s_pre, axis=0, keepdims=True), jnp.max(s_leaf, axis=0, keepdims=True)
    )
    weights = jnp.concatenate([jnp.exp2(s_pre - top), jnp.exp2(s_leaf - top)], axis=0)
    total = jnp.sum(weights, axis=0, keepdims=True)
    probs = weights * (1.0 / total)
    probs_b = probs.astype(jnp.bfloat16)
    delta = jnp.sum(probs * dprob, axis=0, keepdims=True)
    dscore = (probs * (dprob - delta)).astype(jnp.bfloat16)

    out_t = dot(vcat_t[...], probs_b, ((1,), (0,)))
    out_t = jnp.where(first_side, out_t[:HEAD_SIZE], out_t[HEAD_SIZE:])
    out_ref[...] = out_t.T.astype(jnp.bfloat16)
    dq_t = dot(kcat_t[...], dscore, ((1,), (0,)))
    dq_t = jnp.where(first_side, dq_t[:HEAD_SIZE], dq_t[HEAD_SIZE:]) * SCALE
    dq_ref[...] = dq_t.T.astype(jnp.bfloat16)
    dk_sum[...] += dot(dscore, q2, ((1,), (0,)))
    dv_sum[...] += dot(probs_b, g2, ((1,), (0,)))

    @pl.when(within == GQ - 1)
    def _():
        for total_ref, cols, factor in ((dk_sum, key_cols, SCALE), (dv_sum, value_cols, 1.0)):
            leaf = (total_ref[span:, :HEAD_SIZE] + total_ref[span:, HEAD_SIZE:]) * factor
            dleaf_ref[:, cols] = leaf.astype(jnp.bfloat16)
            for side in range(2):
                lanes = slice(side * HEAD_SIZE, (side + 1) * HEAD_SIZE)
                for j in range(per_prefix):
                    value = total_ref[j * block_len:(j + 1) * block_len, lanes] * factor
                    value = value.astype(dpre_ref.dtype)
                    where = block_row(side, j)
                    if side == 1:
                        value = value + dpre_ref[where, :, cols]
                    dpre_ref[where, :, cols] = value


def attention(owner, tokens, device, q, g, leaf_kv, leaf, mask, whole, devices):
    count = q.shape[0]
    block_len = whole.shape[0] // devices
    prompts = tokens.shape[0]
    per_prefix = owner.shape[0] // prompts
    span = per_prefix * block_len
    keys = span + count
    heads = KEY_VALUE_HEADS * GQ
    bf16, f32 = jnp.bfloat16, jnp.float32
    slab = pl.BlockSpec((count, HEAD_SIZE), lambda h, *_: (0, h))

    def full(shape):
        return pl.BlockSpec(shape, lambda h, *_: (0,) * len(shape))

    dpre_shape = (devices, block_len, whole.shape[1])
    return pl.pallas_call(
        functools.partial(
            attention_kernel, prompts=prompts, per_prefix=per_prefix, block_len=block_len
        ),
        grid_spec=pltpu.PrefetchScalarGridSpec(
            num_scalar_prefetch=3,
            grid=(heads,),
            in_specs=[
                slab, slab, full(leaf_kv.shape), full(leaf.shape), full(mask.shape),
                pl.BlockSpec(memory_space=pl.ANY),
            ],
            out_specs=[slab, slab, full(leaf_kv.shape), full(dpre_shape)],
            scratch_shapes=[
                pltpu.VMEM((2 * span, whole.shape[1]), bf16),
                pltpu.VMEM((keys, 2 * HEAD_SIZE), bf16),
                pltpu.VMEM((keys, 2 * HEAD_SIZE), bf16),
                pltpu.VMEM((2 * HEAD_SIZE, keys), bf16),
                pltpu.VMEM((2 * HEAD_SIZE, keys), bf16),
                pltpu.VMEM((count, count), f32),
                pltpu.VMEM((count, 2 * HEAD_SIZE), bf16),
                pltpu.VMEM((count, 2 * HEAD_SIZE), bf16),
                pltpu.VMEM((keys, 2 * HEAD_SIZE), f32),
                pltpu.VMEM((keys, 2 * HEAD_SIZE), f32),
                pltpu.SemaphoreType.DMA((2 * per_prefix,)),
            ],
        ),
        out_shape=[
            jax.ShapeDtypeStruct(q.shape, bf16),
            jax.ShapeDtypeStruct(q.shape, bf16),
            jax.ShapeDtypeStruct(leaf_kv.shape, bf16),
            jax.ShapeDtypeStruct(dpre_shape, bf16),
        ],
        compiler_params=pltpu.CompilerParams(
            vmem_limit_bytes=48 * 2**20, dimension_semantics=("arbitrary",)
        ),
        cost_estimate=pl.CostEstimate(
            flops=heads * 6 * 2 * keys * 256 * 256, bytes_accessed=16 * 2**20,
            transcendentals=heads * keys * count,
        ),
    )(owner, tokens, device, q, g, leaf_kv, leaf, mask, whole)


def shards(
    query, leaf_key_value, prefix_key_value, d_out, block_owner, subtree_tokens, leaf_id, loss_mask
):
    devices = lax.axis_size("dp")
    device = lax.axis_index("dp").astype(jnp.int32).reshape(1)
    whole = lax.all_gather(prefix_key_value, "dp", axis=0, tiled=True)
    attended, d_query, d_leaf, partial = attention(
        block_owner, subtree_tokens, device, query, d_out, leaf_key_value,
        leaf_id, loss_mask.reshape(1, -1), whole, devices,
    )
    mine = lax.psum_scatter(partial, "dp", scatter_dimension=0, tiled=True)
    return attended, d_query, d_leaf, mine.reshape(prefix_key_value.shape)


def solution(mesh):
    rows = P(("groups", "dp"), None)
    in_specs = (rows, rows, rows, rows, P("groups"), P("groups"), rows, P(("groups", "dp")))
    return jax.shard_map(
        shards, mesh=mesh, in_specs=in_specs, out_specs=(rows,) * 4, check_vma=False
    )
```

profile of v0, /device:TPU:0, one launch (start us, length us, event | category | flops | bytes accessed | tf_op | source)
XLA Modules:
  0.0 200.7 jit_solution(16369405273176787483)
XLA Ops:
  7.2 0.0 all-gather.2.cloned.1.call-start
  7.2 0.7 all-gather.2.cloned.1.call-update
  7.9 0.0 reduce-scatter.2.cloned.1.call-start
  7.9 55.5 %all-gather.2.cloned.1.call-done.whole_ref = bf16[2048,1024]{1,0:T(8,128)(2,1)} async-done(((bf16[128,1024]{1,0:T(8,128)(2,1)}), bf16[2048,1024]{1,0:T(8,128)(2,1)}) %all-gather.2.cloned.1.call-update) | async-done | bytes 4194320 | tf_op jit(solution)/shard_map/all_gather | solution.py:202
  63.5 0.0 copy-start
  63.5 1.6 copy-done
  65.0 0.0 copy-start.1
  65.0 1.6 copy-done.1
  66.6 0.0 copy-start.2
  66.6 1.0 copy-done.2
  67.7 0.0 copy-start.3
  67.7 0.7 copy-done.3
  68.4 0.0 copy-start.4
  68.4 0.7 copy-done.4
  69.0 0.0 copy-start.5
  69.0 0.7 copy-done.5
  69.7 0.0 copy-start.6
  69.7 0.7 copy-done.6
  70.3 52.5 %shard_map.111 = (bf16[256,4096]{1,0:T(8,128)(2,1)}, bf16[256,4096]{1,0:T(8,128)(2,1)}, bf16[256,1024]{1,0:T(8,128)(2,1)}, bf16[16,128,1024]{2,1,0:T(8,128)(2,1)}) custom-call(s32[16]{0:T(128)S(1)} %copy-done.5, s32[4]{0:T(128)S(1)} %copy-done.6, s32[1]{0:T(128)} %bitcast.device_ref, bf16[256,4096]{1,0:T(8,128)(2,1)S(1)} %copy-done, ...), custom_call_target="tpu_custom_call" | custom-call | flops 19327352832 | bytes 16777216 | tf_op jit(solution)/shard_map/pallas_call | solution.py:155
  122.8 0.0 reduce-scatter.2.cloned.1.call-update
  122.8 71.0 %reduce-scatter.2.cloned.1.call-done = bf16[1,128,1024]{2,1,0:T(8,128)(2,1)} async-done(((bf16[16,128,1024]{2,1,0:T(8,128)(2,1)}), bf16[1,128,1024]{2,1,0:T(8,128)(2,1)}) %reduce-scatter.2.cloned.1.call-update) | async-done | bytes 262160 | tf_op jit(solution)/shard_map/reduce_scatter | solution.py:207
Async XLA Ops:
  7.2 56.3 %all-gather.2.cloned.1.call-start = ((), (), s32[]{:S(2)}) async-start(), calls=%async_computation.1 | async-start | bytes 4456448 | tf_op jit(solution)/shard_map/all_gather | solution.py:202
  7.9 186.0 %reduce-scatter.2.cloned.1.call-start = ((), (), s32[]{:S(2)}) async-start(), calls=%async_computation.2 | async-start | bytes 4456448 | tf_op jit(solution)/shard_map/reduce_scatter | solution.py:207
  63.5 1.6 copy-start
  65.0 1.6 copy-start.1
  66.6 1.0 copy-start.2
  67.7 0.7 copy-start.3
  68.4 0.7 copy-start.4
  69.0 0.7 copy-start.5
  69.7 0.7 copy-start.6
Sparse Core Ops, SparseCore 0:
  10.2 53.2 all-gather.1
  123.0 70.8 reduce-scatter.1
where the time goes:
time: 201 us
  waiting for transfers between devices  127 us (63%)
  Pallas kernels  52.5 us (26%)
  between operations  14.1 us (7%)
  local copies, waits for them, and re-layouts  6.89 us (3%)
    reduce_scatter x1, waiting for transfers between devices, shards(): mine = lax.psum_scatter(partial, 'dp', scatter_dimension=0, tiled=True)  71 us
    all_gather x1, waiting for transfers between devices, shards(): whole = lax.all_gather(prefix_key_value, 'dp', axis=0, tiled=True)  55.5 us
    pallas_call x1, Pallas kernels, attention(): pl.pallas_call(functools.partial(attention_kernel, prompts=prompts, per_p...  52.5 us
    unnamed x14, local copies, waits for them, and re-layouts  6.89 us
  transfers between devices with their start and end apart: 2, of which 2 were waited for; matrix products, arithmetic and copies ran while one was open for 0% of the time, Pallas kernels for 0%

commit v1 on v0

--- a/solution.py
+++ b/solution.py
@@ -17,22 +17,25 @@
 def dot(a, b, contract):
     return lax.dot_general(a, b, (contract, ((), ())), preferred_element_type=jnp.float32)
 
+CHUNKS = 1
+
 
 def attention_kernel(
-    owner_ref, tokens_ref, device_ref,
-    q_ref, g_ref, leaf_kv_ref, leaf_ref, mask_ref, whole_ref,
-    out_ref, dq_ref, dleaf_ref, dpre_ref,
-    kv, kcat, vcat, kcat_t, vcat_t, bias, q_pick, g_pick, dk_sum, dv_sum, sems,
-    *, prompts, per_prefix, block_len,
+    owner_ref, tokens_ref, place_ref,
+    q_ref, g_ref, leaf_k_ref, leaf_v_ref, leaf_ref, mask_ref, own_ref, far_ref, *rest,
+    prompts, per_prefix, block_len, planes, ranks, chained,
 ):
+    (out_ref, dq_ref, dleaf_ref, own_sum_ref, far_sum_ref,
+     kv, kcat, vcat, kcat_t, vcat_t, bias, q_pick, g_pick, dk_sum, dv_sum, sems) = rest[2 * chained:]
     head = pl.program_id(0)
     group = head // GQ
     within = lax.rem(head, GQ)
     count = q_ref.shape[0]
     span = per_prefix * block_len
-    width = KEY_VALUE_HEADS * HEAD_SIZE
-
-    first = device_ref[0] * count
+    half = own_ref.shape[1] // 2
+
+    place = place_ref[0]
+    first = place * count
     last = first + (count - 1)
     end = jnp.int32(0)
     pair_first = jnp.int32(0)
@@ -45,22 +48,32 @@
         border = jnp.where(end > first, jnp.minimum(border, end), border)
     border = border - first
 
-    def block_row(side, j):
+    def block_place(side, j):
         prefix = pair_first if side == 0 else pair_last
-        return owner_ref[prefix * per_prefix + j]
+        owner = owner_ref[prefix * per_prefix + j]
+        same_core = lax.rem(owner, 2) == lax.rem(place, 2)
+        row = lax.rem(owner // 2 + place // 2, ranks)
+        ahead = lax.rem(owner // (2 * ranks) + planes - place // (2 * ranks), planes)
+        return same_core, row, ahead
 
     @pl.when(head == 0)
     def _():
-        copies = []
         for side in range(2):
             for j in range(per_prefix):
                 n = side * per_prefix + j
-                rows = pl.ds(pl.multiple_of(block_row(side, j) * block_len, block_len), block_len)
-                copy = pltpu.make_async_copy(
-                    whole_ref.at[rows, :], kv.at[pl.ds(n * block_len, block_len), :], sems.at[n]
-                )
-                copy.start()
-                copies.append(copy)
+                same_core, row, ahead = block_place(side, j)
+                slot = row * planes + lax.rem(planes - ahead, planes)
+                rows = pl.ds(pl.multiple_of(slot * block_len, block_len), block_len)
+                target = kv.at[pl.ds(n * block_len, block_len), :]
+
+                @pl.when(same_core)
+                def _():
+                    pltpu.make_async_copy(own_ref.at[rows, :], target, sems.at[n]).start()
+
+                @pl.when(jnp.logical_not(same_core))
+                def _():
+                    pltpu.make_async_copy(far_ref.at[rows, :], target, sems.at[n]).start()
+
         leaf_row = jnp.broadcast_to(leaf_ref[...], (count, count))
         leaf_col = leaf_row.T
         key_at = lax.broadcasted_iota(jnp.int32, (count, count), 0)
@@ -74,20 +87,24 @@
         pick = (in_first == left).astype(jnp.float32)
         q_pick[...] = pick.astype(jnp.bfloat16)
         g_pick[...] = (pick * mask_col).astype(jnp.bfloat16)
-        dpre_ref[...] = jnp.zeros_like(dpre_ref)
-        for copy in copies:
-            copy.wait()
+        own_sum_ref[...] = jnp.zeros_like(own_sum_ref)
+        far_sum_ref[...] = jnp.zeros_like(far_sum_ref)
+        for n in range(2 * per_prefix):
+            target = kv.at[pl.ds(n * block_len, block_len), :]
+            pltpu.make_async_copy(own_ref.at[pl.ds(0, block_len), :], target, sems.at[n]).wait()
 
     key_cols = pl.ds(pl.multiple_of(group * HEAD_SIZE, HEAD_SIZE), HEAD_SIZE)
-    value_cols = pl.ds(pl.multiple_of(width + group * HEAD_SIZE, HEAD_SIZE), HEAD_SIZE)
+    value_cols = pl.ds(pl.multiple_of(half + group * HEAD_SIZE, HEAD_SIZE), HEAD_SIZE)
 
     @pl.when(within == 0)
     def _():
-        for cat, cat_t, cols in ((kcat, kcat_t, key_cols), (vcat, vcat_t, value_cols)):
+        for cat, cat_t, cols, leaf in (
+            (kcat, kcat_t, key_cols, leaf_k_ref), (vcat, vcat_t, value_cols, leaf_v_ref)
+        ):
             for side in range(2):
                 lanes = slice(side * HEAD_SIZE, (side + 1) * HEAD_SIZE)
                 cat[0:span, lanes] = kv[side * span:(side + 1) * span, cols]
-                cat[span:, lanes] = leaf_kv_ref[:, cols]
+                cat[span:, lanes] = leaf[...]
             cat_t[...] = cat[...].T
         dk_sum[...] = jnp.zeros_like(dk_sum)
         dv_sum[...] = jnp.zeros_like(dv_sum)
@@ -130,42 +147,59 @@
                 lanes = slice(side * HEAD_SIZE, (side + 1) * HEAD_SIZE)
                 for j in range(per_prefix):
                     value = total_ref[j * block_len:(j + 1) * block_len, lanes] * factor
-                    value = value.astype(dpre_ref.dtype)
-                    where = block_row(side, j)
-                    if side == 1:
-                        value = value + dpre_ref[where, :, cols]
-                    dpre_ref[where, :, cols] = value
-
-
-def attention(owner, tokens, device, q, g, leaf_kv, leaf, mask, whole, devices):
+                    value = value.astype(jnp.bfloat16)
+                    same_core, row, ahead = block_place(side, j)
+                    slot = row * planes + ahead
+
+                    @pl.when(same_core)
+                    def _():
+                        own_sum_ref[slot, :, cols] += value
+
+                    @pl.when(jnp.logical_not(same_core))
+                    def _():
+                        far_sum_ref[slot, :, cols] += value
+
+
+def attention(
+    chunk, owner, tokens, place, q, g, leaf_kv, leaf, mask, own, far, earlier, planes, ranks
+):
     count = q.shape[0]
-    block_len = whole.shape[0] // devices
+    slots = planes * ranks
+    block_len = own.shape[0] // slots
     prompts = tokens.shape[0]
     per_prefix = owner.shape[0] // prompts
     span = per_prefix * block_len
     keys = span + count
-    heads = KEY_VALUE_HEADS * GQ
+    width = own.shape[1]
+    groups = width // (2 * HEAD_SIZE)
+    heads = groups * GQ
     bf16, f32 = jnp.bfloat16, jnp.float32
-    slab = pl.BlockSpec((count, HEAD_SIZE), lambda h, *_: (0, h))
+    slab = pl.BlockSpec((count, HEAD_SIZE), lambda h, *_: (0, chunk * heads + h))
+    leaf_k = pl.BlockSpec((count, HEAD_SIZE), lambda h, *_: (0, chunk * groups + h // GQ))
+    leaf_v = pl.BlockSpec(
+        (count, HEAD_SIZE), lambda h, *_: (0, KEY_VALUE_HEADS + chunk * groups + h // GQ)
+    )
+    anywhere = pl.BlockSpec(memory_space=pl.ANY)
 
     def full(shape):
         return pl.BlockSpec(shape, lambda h, *_: (0,) * len(shape))
 
-    dpre_shape = (devices, block_len, whole.shape[1])
+    sum_shape = (slots, block_len, width)
+    chained = len(earlier) > 0
     return pl.pallas_call(
         functools.partial(
-            attention_kernel, prompts=prompts, per_prefix=per_prefix, block_len=block_len
+            attention_kernel, prompts=prompts, per_prefix=per_prefix, block_len=block_len,
+            planes=planes, ranks=ranks, chained=chained,
         ),
         grid_spec=pltpu.PrefetchScalarGridSpec(
             num_scalar_prefetch=3,
             grid=(heads,),
             in_specs=[
-                slab, slab, full(leaf_kv.shape), full(leaf.shape), full(mask.shape),
-                pl.BlockSpec(memory_space=pl.ANY),
-            ],
-            out_specs=[slab, slab, full(leaf_kv.shape), full(dpre_shape)],
+                slab, slab, leaf_k, leaf_v, full(leaf.shape), full(mask.shape), anywhere, anywhere,
+            ] + [anywhere] * len(earlier),
+            out_specs=[slab, slab, full((count, width)), full(sum_shape), full(sum_shape)],
             scratch_shapes=[
-                pltpu.VMEM((2 * span, whole.shape[1]), bf16),
+                pltpu.VMEM((2 * span, width), bf16),
                 pltpu.VMEM((keys, 2 * HEAD_SIZE), bf16),
                 pltpu.VMEM((keys, 2 * HEAD_SIZE), bf16),
                 pltpu.VMEM((2 * HEAD_SIZE, keys), bf16),
@@ -181,31 +215,84 @@
         out_shape=[
             jax.ShapeDtypeStruct(q.shape, bf16),
             jax.ShapeDtypeStruct(q.shape, bf16),
-            jax.ShapeDtypeStruct(leaf_kv.shape, bf16),
-            jax.ShapeDtypeStruct(dpre_shape, bf16),
+            jax.ShapeDtypeStruct((count, width), bf16),
+            jax.ShapeDtypeStruct(sum_shape, bf16),
+            jax.ShapeDtypeStruct(sum_shape, bf16),
         ],
+        input_output_aliases={11: 0, 12: 1} if chained else {},
         compiler_params=pltpu.CompilerParams(
-            vmem_limit_bytes=48 * 2**20, dimension_semantics=("arbitrary",)
+            vmem_limit_bytes=60 * 2**20, dimension_semantics=("arbitrary",)
         ),
         cost_estimate=pl.CostEstimate(
-            flops=heads * 6 * 2 * keys * 256 * 256, bytes_accessed=16 * 2**20,
+            flops=heads * 6 * 2 * keys * 256 * 256, bytes_accessed=16 * 2**20 // CHUNKS,
             transcendentals=heads * keys * count,
         ),
-    )(owner, tokens, device, q, g, leaf_kv, leaf, mask, whole)
+    )(owner, tokens, place, q, g, leaf_kv, leaf_kv, leaf, mask, own, far, *earlier)
 
 
 def shards(
     query, leaf_key_value, prefix_key_value, d_out, block_owner, subtree_tokens, leaf_id, loss_mask
 ):
     devices = lax.axis_size("dp")
-    device = lax.axis_index("dp").astype(jnp.int32).reshape(1)
-    whole = lax.all_gather(prefix_key_value, "dp", axis=0, tiled=True)
-    attended, d_query, d_leaf, partial = attention(
-        block_owner, subtree_tokens, device, query, d_out, leaf_key_value,
-        leaf_id, loss_mask.reshape(1, -1), whole, devices,
-    )
-    mine = lax.psum_scatter(partial, "dp", scatter_dimension=0, tiled=True)
-    return attended, d_query, d_leaf, mine.reshape(prefix_key_value.shape)
+    ranks = 2 if devices == 16 else 1
+    planes = devices // (2 * ranks)
+    place = lax.axis_index("dp").astype(jnp.int32).reshape(1)
+    mask = loss_mask.reshape(1, -1)
+    f32 = jnp.float32
+
+    def index(plane, rank, core):
+        return (plane % planes * ranks + rank % ranks) * 2 + core % 2
+
+    def send(array, plane_step, rank_step, core_step):
+        pairs = [
+            (index(p, r, c), index(p + plane_step, r + rank_step, c + core_step))
+            for p in range(planes) for r in range(ranks) for c in range(2)
+        ]
+        return lax.ppermute(array, "dp", pairs)
+
+    groups = KEY_VALUE_HEADS // CHUNKS
+    step = groups * HEAD_SIZE
+    middle = KEY_VALUE_HEADS * HEAD_SIZE
+
+    def gather(chunk):
+        mine = jnp.concatenate(
+            [prefix_key_value[:, chunk * step:(chunk + 1) * step],
+             prefix_key_value[:, middle + chunk * step:middle + (chunk + 1) * step]], axis=1
+        ) if CHUNKS > 1 else prefix_key_value
+        near = [mine] + [send(mine, k, 0, 0) for k in range(1, planes)]
+        near = jnp.concatenate(near, axis=0)
+        if ranks == 2:
+            near = jnp.concatenate([near, send(near, 0, 1, 0)], axis=0)
+        return near, send(near, 0, 0, 1)
+
+    def reduce(own, far):
+        total = own.astype(f32) + send(far, 0, 0, 1).astype(f32)
+        if ranks == 2:
+            away = send(total[planes:].astype(jnp.bfloat16), 0, 1, 0)
+            total = total[:planes] + away.astype(f32)
+        mine = total[0]
+        for k in range(1, planes):
+            mine = mine + send(total[k].astype(jnp.bfloat16), k, 0, 0).astype(f32)
+        return mine.astype(jnp.bfloat16)
+
+    blocks = [gather(chunk) for chunk in range(CHUNKS)]
+    d_leaf, d_prefix, earlier = [], [], ()
+    for chunk in range(CHUNKS):
+        own, far = blocks[chunk]
+        attended, d_query, leaf_part, own_sum, far_sum = attention(
+            chunk, block_owner, subtree_tokens, place, query, d_out, leaf_key_value, leaf_id, mask,
+            own, far, earlier, planes, ranks,
+        )
+        earlier = (attended, d_query)
+        d_leaf.append(leaf_part)
+        d_prefix.append(reduce(own_sum, far_sum))
+
+    def join(parts):
+        if CHUNKS == 1:
+            return parts[0]
+        return jnp.concatenate([p[:, :step] for p in parts] + [p[:, step:] for p in parts], axis=1)
+
+    return attended, d_query, join(d_leaf), join(d_prefix)
 
 
 def solution(mesh):

time: 201 us -> 173 us (0.86)
  waiting for transfers between devices: 127 us -> 97.1 us
  starting transfers between devices: 0.08 us -> 14.8 us
  between operations: 14.1 us -> 0.74 us
  local copies, waits for them, and re-layouts: 6.89 us -> 0.36 us
  other arithmetic: 0 us -> 4.81 us
  Pallas kernels: 52.5 us -> 55.2 us
    ppermute x0 -> x10, waiting for transfers between devices: none -> 97.1 us  [send(): return lax.ppermute(array, 'dp', pairs)]
    reduce_scatter x1 -> x0, waiting for transfers between devices: 71 us -> none  [shards(): mine = lax.psum_scatter(partial, 'dp', scatter_dimension=0, tiled=True)]
    all_gather x1 -> x0, waiting for transfers between devices: 55.5 us -> none  [shards(): whole = lax.all_gather(prefix_key_value, 'dp', axis=0, tiled=True)]
    ppermute x0 -> x10, starting transfers between devices: none -> 14.8 us  [send(): return lax.ppermute(array, 'dp', pairs)]
    unnamed x14 -> x8, local copies, waits for them, and re-layouts: 6.89 us -> 0.08 us
    pallas_call x1, Pallas kernels: 52.5 us -> 55.2 us  [attention(): pl.pallas_call(functools.partial(attention_kernel, prompts=prompts, per_p...]
    add x0 -> x1, other arithmetic: none -> 2.48 us  [reduce(): total = own.astype(f32) + send(far, 0, 0, 1).astype(f32)]
  transfers between devices with their start and end apart: 2 -> 10, of which waited for: 2 -> 9; matrix products, arithmetic and copies ran while one was open for 0% -> 0% of each run, Pallas kernels for 0% -> 0%
where the time goes in v1:
time: 173 us
  waiting for transfers between devices  97.1 us (56%)
  Pallas kernels  55.2 us (32%)
  starting transfers between devices  14.8 us (9%)
  other arithmetic  4.81 us (3%)
    ppermute x10, waiting for transfers between devices, send(): return lax.ppermute(array, 'dp', pairs)  97.1 us
    pallas_call x1, Pallas kernels, attention(): pl.pallas_call(functools.partial(attention_kernel, prompts=prompts, per_p...  55.2 us
    ppermute x10, starting transfers between devices, send(): return lax.ppermute(array, 'dp', pairs)  14.8 us
  transfers between devices with their start and end apart: 10, of which 9 were waited for; matrix products, arithmetic and copies ran while one was open for 0% of the time, Pallas kernels for 0%

profile of v1, /device:TPU:0, one launch (start us, length us, event | category | flops | bytes accessed | tf_op | source)
XLA Modules:
  0.0 173.1 jit_solution(9774126979658763044)
XLA Ops:
  0.6 5.1 %collective-permute-start.2 = (bf16[128,1024]{1,0:T(8,128)(2,1)}, bf16[128,1024]{1,0:T(8,128)(2,1)S(1)}, u32[]{:S(2)}, u32[]{:S(2)}) collective-permute-start(bf16[128,1024]{1,0:T(8,128)(2,1)} %param.10), channel_id=1, source_target_pairs={{0,12},{1,13},{2,14},{3,15},{4,0},{5,1},{6,2},{7,3},{8,4},{9,5},{1... | collective-permute-start | bytes 786440 | tf_op jit(solution)/shard_map/ppermute | solution.py:251
  5.7 1.0 collective-permute-start
  6.8 6.1 %collective-permute-done.2 = bf16[128,1024]{1,0:T(8,128)(2,1)S(1)} collective-permute-done((bf16[128,1024]{1,0:T(8,128)(2,1)}, bf16[128,1024]{1,0:T(8,128)(2,1)S(1)}, u32[]{:S(2)}, u32[]{:S(2)}) %collective-permute-start.2) | collective-permute-done | bytes 262176 | tf_op jit(solution)/shard_map/ppermute | solution.py:251
  12.8 15.4 %collective-permute-done.1 = bf16[128,1024]{1,0:T(8,128)(2,1)S(1)} collective-permute-done((bf16[128,1024]{1,0:T(8,128)(2,1)}, bf16[128,1024]{1,0:T(8,128)(2,1)S(1)}, u32[]{:S(2)}, u32[]{:S(2)}) %collective-permute-start.1) | collective-permute-done | bytes 262176 | tf_op jit(solution)/shard_map/ppermute | solution.py:251
  28.3 1.0 pad_maximum_fusion
  29.3 1.6 collective-permute-start.3
  31.0 22.4 %collective-permute-done.3 = bf16[512,1024]{1,0:T(8,128)(2,1)S(1)} collective-permute-done((bf16[512,1024]{1,0:T(8,128)(2,1)S(1)}, bf16[512,1024]{1,0:T(8,128)(2,1)S(1)}, u32[]{:S(2)}, u32[]{:S(2)}) %collective-permute-start.3) | collective-permute-done | bytes 1048608 | tf_op jit(solution)/shard_map/ppermute | solution.py:251
  53.5 0.1 collective-permute-start.4
  53.5 4.3 %collective-permute-done.4.far_ref = bf16[1024,1024]{1,0:T(8,128)(2,1)} collective-permute-done((bf16[1024,1024]{1,0:T(8,128)(2,1)S(1)}, bf16[1024,1024]{1,0:T(8,128)(2,1)}, u32[]{:S(2)}, u32[]{:S(2)}) %collective-permute-start.4) | collective-permute-done | bytes 2097184 | tf_op jit(solution)/shard_map/ppermute | solution.py:251
  57.8 55.2 %shard_map.111 = (bf16[256,4096]{1,0:T(8,128)(2,1)}, bf16[256,4096]{1,0:T(8,128)(2,1)}, bf16[256,1024]{1,0:T(8,128)(2,1)}, bf16[8,128,1024]{2,1,0:T(8,128)(2,1)}, bf16[8,128,1024]{2,1,0:T(8,128)(2,1)}) custom-call(s32[16]{0:T(128)} %owner_ref.1, s32[4]{0:T(128)} %tokens_ref.1, s32[1]{0:T(128)} %bitcast.place_ref, bf16[256,4096]{1,0:T(8,128)(2,1)} %q_ref.1, ...), custom_call_target="tpu_custom_call" | custom-call | flops 19327352832 | bytes 16777216 | tf_op jit(solution)/shard_map/pallas_call | solution.py:189
  113.1 0.1 collective-permute-start.5
  113.2 4.3 %collective-permute-done.5 = bf16[8,128,1024]{2,1,0:T(8,128)(2,1)S(1)} collective-permute-done((bf16[8,128,1024]{2,1,0:T(8,128)(2,1)}, bf16[8,128,1024]{2,1,0:T(8,128)(2,1)S(1)}, u32[]{:S(2)}, u32[]{:S(2)}) %collective-permute-start.5) | collective-permute-done | bytes 2097184 | tf_op jit(solution)/shard_map/ppermute | solution.py:251
  117.5 2.5 %convert_add_fusion = f32[8,128,1024]{2,1,0:T(8,128)S(1)} fusion(bf16[8,128,1024]{2,1,0:T(8,128)(2,1)S(1)} %collective-permute-done.5, bf16[8,128,1024]{2,1,0:T(8,128)(2,1)} %get-tuple-element.12), kind=kLoop, calls=%fused_computation | loop fusion | flops 3145728 | bytes 8388608 | tf_op jit(solution)/shard_map/add | solution.py:269
  120.0 0.2 slice.48
  120.2 1.7 collective-permute-start.6
  121.8 23.6 %collective-permute-done.6 = bf16[4,128,1024]{2,1,0:T(8,128)(2,1)S(1)} collective-permute-done((bf16[4,128,1024]{2,1,0:T(8,128)(2,1)S(1)}, bf16[4,128,1024]{2,1,0:T(8,128)(2,1)S(1)}, u32[]{:S(2)}, u32[]{:S(2)}) %collective-permute-start.6) | collective-permute-done | bytes 1048608 | tf_op jit(solution)/shard_map/ppermute | solution.py:251
  145.4 0.4 fusion.4
  145.9 1.4 collective-permute-start.7
  147.3 2.5 %collective-permute-start.9 = (bf16[128,1024]{1,0:T(8,128)(2,1)S(1)}, bf16[128,1024]{1,0:T(8,128)(2,1)S(1)}, u32[]{:S(2)}, u32[]{:S(2)}) collective-permute-start(bf16[128,1024]{1,0:T(8,128)(2,1)S(1)} %get-tuple-element.17), channel_id=1, source_target_pairs={{0,12},{1,13},{2,14},{3,15},{4,0},{5,1},{6,2},{7,3},{8,4},{9,5},{1... | collective-permute-start | bytes 786440 | tf_op jit(solution)/shard_map/ppermute | solution.py:251
  149.8 1.4 collective-permute-start.8
  151.2 5.9 %collective-permute-done.7 = bf16[128,1024]{1,0:T(8,128)(2,1)S(1)} collective-permute-done((bf16[128,1024]{1,0:T(8,128)(2,1)S(1)}, bf16[128,1024]{1,0:T(8,128)(2,1)S(1)}, u32[]{:S(2)}, u32[]{:S(2)}) %collective-permute-start.7) | collective-permute-done | bytes 262176 | tf_op jit(solution)/shard_map/ppermute | solution.py:251
  157.1 3.7 %collective-permute-done.9 = bf16[128,1024]{1,0:T(8,128)(2,1)S(1)} collective-permute-done((bf16[128,1024]{1,0:T(8,128)(2,1)S(1)}, bf16[128,1024]{1,0:T(8,128)(2,1)S(1)}, u32[]{:S(2)}, u32[]{:S(2)}) %collective-permute-start.9) | collective-permute-done | bytes 262176 | tf_op jit(solution)/shard_map/ppermute | solution.py:251
  160.9 11.3 %collective-permute-done.8 = bf16[128,1024]{1,0:T(8,128)(2,1)S(1)} collective-permute-done((bf16[128,1024]{1,0:T(8,128)(2,1)S(1)}, bf16[128,1024]{1,0:T(8,128)(2,1)S(1)}, u32[]{:S(2)}, u32[]{:S(2)}) %collective-permute-start.8) | collective-permute-done | bytes 262176 | tf_op jit(solution)/shard_map/ppermute | solution.py:251
  172.2 0.9 fusion.3
  (12 shorter events, 0.2 us)
Async XLA Ops:
  0.6 30.2 %copy-start = (bf16[128,1024]{1,0:T(8,128)(2,1)S(1)}, bf16[128,1024]{1,0:T(8,128)(2,1)}, u32[]{:S(2)}) copy-start(bf16[128,1024]{1,0:T(8,128)(2,1)} %param.10) | copy-start | bytes 786436
  0.6 12.2 %collective-permute-start.2 = (bf16[128,1024]{1,0:T(8,128)(2,1)}, bf16[128,1024]{1,0:T(8,128)(2,1)S(1)}, u32[]{:S(2)}, u32[]{:S(2)}) collective-permute-start(bf16[128,1024]{1,0:T(8,128)(2,1)} %param.10), channel_id=1, source_target_pairs={{0,12},{1,13},{2,14},{3,15},{4,0},{5,1},{6,2},{7,3},{8,4},{9,5},{1... | collective-permute-start | bytes 786440 | tf_op jit(solution)/shard_map/ppermute | solution.py:251
  5.7 22.5 %collective-permute-start.1 = (bf16[128,1024]{1,0:T(8,128)(2,1)}, bf16[128,1024]{1,0:T(8,128)(2,1)S(1)}, u32[]{:S(2)}, u32[]{:S(2)}) collective-permute-start(bf16[128,1024]{1,0:T(8,128)(2,1)} %param.10), channel_id=1, source_target_pairs={{0,8},{1,9},{2,10},{3,11},{4,12},{5,13},{6,14},{7,15},{8,0},{9,1},... | collective-permute-start | bytes 786440 | tf_op jit(solution)/shard_map/ppermute | solution.py:251
  5.7 22.5 %collective-permute-start = (bf16[128,1024]{1,0:T(8,128)(2,1)}, bf16[128,1024]{1,0:T(8,128)(2,1)S(1)}, u32[]{:S(2)}, u32[]{:S(2)}) collective-permute-start(bf16[128,1024]{1,0:T(8,128)(2,1)} %param.10), channel_id=1, source_target_pairs={{0,4},{1,5},{2,6},{3,7},{4,8},{5,9},{6,10},{7,11},{8,12},{9,13},{1... | collective-permute-start | bytes 786440 | tf_op jit(solution)/shard_map/ppermute | solution.py:251
  29.3 24.1 %collective-permute-start.3 = (bf16[512,1024]{1,0:T(8,128)(2,1)S(1)}, bf16[512,1024]{1,0:T(8,128)(2,1)S(1)}, u32[]{:S(2)}, u32[]{:S(2)}) collective-permute-start(bf16[512,1024]{1,0:T(8,128)(2,1)S(1)} %pad_maximum_fusion), channel_id=1, source_target_pairs={{0,2},{1,3},{2,0},{3,1},{4,6},{5,7},{6,4},{7,5},{8,10},{9,11},{10,... | collective-permute-start | bytes 3145736 | tf_op jit(solution)/shard_map/ppermute | solution.py:251
  53.5 4.4 %copy-start.1 = (bf16[1024,1024]{1,0:T(8,128)(2,1)}, bf16[1024,1024]{1,0:T(8,128)(2,1)S(1)}, u32[]{:S(2)}) copy-start(bf16[1024,1024]{1,0:T(8,128)(2,1)S(1)} %constant_dynamic-update-slice_fusion.own_ref) | copy-start | bytes 6291460
  53.5 4.4 %collective-permute-start.4 = (bf16[1024,1024]{1,0:T(8,128)(2,1)S(1)}, bf16[1024,1024]{1,0:T(8,128)(2,1)}, u32[]{:S(2)}, u32[]{:S(2)}) collective-permute-start(bf16[1024,1024]{1,0:T(8,128)(2,1)S(1)} %constant_dynamic-update-slice_fusion.own_ref), channel_id=1, source_target_pairs={{0,1},{1,0},{2,3},{3,2},{4,5},{5,4},{6,7},{7,6},{8,9},{9,8},{10,11... | collective-permute-start | bytes 6291464 | tf_op jit(solution)/shard_map/ppermute | solution.py:251
  113.1 4.4 %collective-permute-start.5 = (bf16[8,128,1024]{2,1,0:T(8,128)(2,1)}, bf16[8,128,1024]{2,1,0:T(8,128)(2,1)S(1)}, u32[]{:S(2)}, u32[]{:S(2)}) collective-permute-start(bf16[8,128,1024]{2,1,0:T(8,128)(2,1)} %get-tuple-element.13), channel_id=1, source_target_pairs={{0,1},{1,0},{2,3},{3,2},{4,5},{5,4},{6,7},{7,6},{8,9},{9,8},{10,11... | collective-permute-start | bytes 6291464 | tf_op jit(solution)/shard_map/ppermute | solution.py:251
  120.2 25.3 %collective-permute-start.6 = (bf16[4,128,1024]{2,1,0:T(8,128)(2,1)S(1)}, bf16[4,128,1024]{2,1,0:T(8,128)(2,1)S(1)}, u32[]{:S(2)}, u32[]{:S(2)}) collective-permute-start(bf16[4,128,1024]{2,1,0:T(8,128)(2,1)S(1)} %slice.48), channel_id=1, source_target_pairs={{0,2},{1,3},{2,0},{3,1},{4,6},{5,7},{6,4},{7,5},{8,10},{9,11},{10,... | collective-permute-start | bytes 3145736 | tf_op jit(solution)/shard_map/ppermute | solution.py:251
  145.9 11.2 %collective-permute-start.7 = (bf16[128,1024]{1,0:T(8,128)(2,1)S(1)}, bf16[128,1024]{1,0:T(8,128)(2,1)S(1)}, u32[]{:S(2)}, u32[]{:S(2)}) collective-permute-start(bf16[128,1024]{1,0:T(8,128)(2,1)S(1)} %get-tuple-element.16), channel_id=1, source_target_pairs={{0,4},{1,5},{2,6},{3,7},{4,8},{5,9},{6,10},{7,11},{8,12},{9,13},{1... | collective-permute-start | bytes 786440 | tf_op jit(solution)/shard_map/ppermute | solution.py:251
  147.3 13.6 %collective-permute-start.9 = (bf16[128,1024]{1,0:T(8,128)(2,1)S(1)}, bf16[128,1024]{1,0:T(8,128)(2,1)S(1)}, u32[]{:S(2)}, u32[]{:S(2)}) collective-permute-start(bf16[128,1024]{1,0:T(8,128)(2,1)S(1)} %get-tuple-element.17), channel_id=1, source_target_pairs={{0,12},{1,13},{2,14},{3,15},{4,0},{5,1},{6,2},{7,3},{8,4},{9,5},{1... | collective-permute-start | bytes 786440 | tf_op jit(solution)/shard_map/ppermute | solution.py:251
  149.8 22.4 %collective-permute-start.8 = (bf16[128,1024]{1,0:T(8,128)(2,1)S(1)}, bf16[128,1024]{1,0:T(8,128)(2,1)S(1)}, u32[]{:S(2)}, u32[]{:S(2)}) collective-permute-start(bf16[128,1024]{1,0:T(8,128)(2,1)S(1)} %get-tuple-element.18), channel_id=1, source_target_pairs={{0,8},{1,9},{2,10},{3,11},{4,12},{5,13},{6,14},{7,15},{8,0},{9,1},... | collective-permute-start | bytes 786440 | tf_op jit(solution)/shard_map/ppermute | solution.py:251

commit v2 on v1

--- a/solution.py
+++ b/solution.py
@@ -17,21 +17,25 @@
 def dot(a, b, contract):
     return lax.dot_general(a, b, (contract, ((), ())), preferred_element_type=jnp.float32)
 
-CHUNKS = 1
+CHUNKS = 2
+PAIR = 2
+PIECE = 32
 
 
 def attention_kernel(
     owner_ref, tokens_ref, place_ref,
     q_ref, g_ref, leaf_k_ref, leaf_v_ref, leaf_ref, mask_ref, own_ref, far_ref, *rest,
-    prompts, per_prefix, block_len, planes, ranks, chained,
+    prompts, per_prefix, block_len, planes, ranks, chained, steps,
 ):
     (out_ref, dq_ref, dleaf_ref, own_sum_ref, far_sum_ref,
-     kv, kcat, vcat, kcat_t, vcat_t, bias, q_pick, g_pick, dk_sum, dv_sum, sems) = rest[2 * chained:]
-    head = pl.program_id(0)
-    group = head // GQ
-    within = lax.rem(head, GQ)
+     kv, kcat, vcat, kcat_t, vcat_t, bias, q_pick, g_pick, q2, g2, scores, dprob, probs_b, dscore,
+     dk_sum, dv_sum, sems) = rest[2 * chained:]
+    step = pl.program_id(0)
+    per_group = GQ // PAIR
     count = q_ref.shape[0]
+    columns = PAIR * count
     span = per_prefix * block_len
+    keys = span + count
     half = own_ref.shape[1] // 2
 
     place = place_ref[0]
@@ -56,7 +60,13 @@
         ahead = lax.rem(owner // (2 * ranks) + planes - place // (2 * ranks), planes)
         return same_core, row, ahead
 
-    @pl.when(head == 0)
+    def key_columns(group):
+        return pl.ds(pl.multiple_of(group * HEAD_SIZE, HEAD_SIZE), HEAD_SIZE)
+
+    def value_columns(group):
+        return pl.ds(pl.multiple_of(half + group * HEAD_SIZE, HEAD_SIZE), HEAD_SIZE)
+
+    @pl.when(step == 0)
     def _():
         for side in range(2):
             for j in range(per_prefix):
@@ -80,67 +90,120 @@
         token_at = lax.broadcasted_iota(jnp.int32, (count, count), 1)
         same = (leaf_row == leaf_col) & (key_at <= token_at)
         same = same & ((key_at < border) == (token_at < border))
-        bias[...] = jnp.where(same, 0.0, -1e30).astype(jnp.float32)
+        allowed_bias = jnp.where(same, 0.0, -1e30).astype(jnp.float32)
         mask_col = jnp.broadcast_to(mask_ref[...], (count, count)).T.astype(jnp.float32)
         in_first = key_at < border
         left = token_at < HEAD_SIZE
         pick = (in_first == left).astype(jnp.float32)
         q_pick[...] = pick.astype(jnp.bfloat16)
         g_pick[...] = (pick * mask_col).astype(jnp.bfloat16)
+        for n in range(PAIR):
+            bias[:, n * count:(n + 1) * count] = allowed_bias
         own_sum_ref[...] = jnp.zeros_like(own_sum_ref)
         far_sum_ref[...] = jnp.zeros_like(far_sum_ref)
+        dk_sum[...] = jnp.zeros_like(dk_sum)
+        dv_sum[...] = jnp.zeros_like(dv_sum)
         for n in range(2 * per_prefix):
             target = kv.at[pl.ds(n * block_len, block_len), :]
             pltpu.make_async_copy(own_ref.at[pl.ds(0, block_len), :], target, sems.at[n]).wait()
 
-    key_cols = pl.ds(pl.multiple_of(group * HEAD_SIZE, HEAD_SIZE), HEAD_SIZE)
-    value_cols = pl.ds(pl.multiple_of(half + group * HEAD_SIZE, HEAD_SIZE), HEAD_SIZE)
-
-    @pl.when(within == 0)
-    def _():
-        for cat, cat_t, cols, leaf in (
-            (kcat, kcat_t, key_cols, leaf_k_ref), (vcat, vcat_t, value_cols, leaf_v_ref)
+    new_group = lax.rem(step, per_group) == 0
+
+    @pl.when(new_group & (step < steps))
+    def _():
+        group = step // per_group
+        for cat, cols, leaf in (
+            (kcat, key_columns(group), leaf_k_ref), (vcat, value_columns(group), leaf_v_ref)
         ):
             for side in range(2):
                 lanes = slice(side * HEAD_SIZE, (side + 1) * HEAD_SIZE)
                 cat[0:span, lanes] = kv[side * span:(side + 1) * span, cols]
                 cat[span:, lanes] = leaf[...]
-            cat_t[...] = cat[...].T
-        dk_sum[...] = jnp.zeros_like(dk_sum)
-        dv_sum[...] = jnp.zeros_like(dv_sum)
-
-    q = q_ref[...]
-    g = g_ref[...]
-    q2 = jnp.concatenate([q, q], axis=1) * q_pick[...]
-    g2 = jnp.concatenate([g, g], axis=1) * g_pick[...]
-    first_side = lax.broadcasted_iota(jnp.int32, (HEAD_SIZE, count), 1) < border
-
-    scores = dot(kcat[...], q2, ((1,), (1,))) * (SCALE * LOG2E)
-    dprob = dot(vcat[...], g2, ((1,), (1,)))
-    s_pre = scores[:span]
-    s_leaf = scores[span:] + bias[...]
-    top = jnp.maximum(
-        jnp.max(s_pre, axis=0, keepdims=True), jnp.max(s_leaf, axis=0, keepdims=True)
-    )
-    weights = jnp.concatenate([jnp.exp2(s_pre - top), jnp.exp2(s_leaf - top)], axis=0)
-    total = jnp.sum(weights, axis=0, keepdims=True)
-    probs = weights * (1.0 / total)
-    probs_b = probs.astype(jnp.bfloat16)
-    delta = jnp.sum(probs * dprob, axis=0, keepdims=True)
-    dscore = (probs * (dprob - delta)).astype(jnp.bfloat16)
-
-    out_t = dot(vcat_t[...], probs_b, ((1,), (0,)))
-    out_t = jnp.where(first_side, out_t[:HEAD_SIZE], out_t[HEAD_SIZE:])
-    out_ref[...] = out_t.T.astype(jnp.bfloat16)
-    dq_t = dot(kcat_t[...], dscore, ((1,), (0,)))
-    dq_t = jnp.where(first_side, dq_t[:HEAD_SIZE], dq_t[HEAD_SIZE:]) * SCALE
-    dq_ref[...] = dq_t.T.astype(jnp.bfloat16)
-    dk_sum[...] += dot(dscore, q2, ((1,), (0,)))
-    dv_sum[...] += dot(probs_b, g2, ((1,), (0,)))
-
-    @pl.when(within == GQ - 1)
-    def _():
-        for total_ref, cols, factor in ((dk_sum, key_cols, SCALE), (dv_sum, value_cols, 1.0)):
+
+    def later_products():
+        token_at = lax.rem(lax.broadcasted_iota(jnp.int32, (HEAD_SIZE, columns), 1), count)
+        first_side = token_at < border
+        for source, cat_t, factor, target in (
+            (probs_b, vcat_t, 1.0, out_ref), (dscore, kcat_t, SCALE, dq_ref)
+        ):
+            both = dot(cat_t[...], source[...], ((1,), (0,)))
+            mine = jnp.where(first_side, both[:HEAD_SIZE], both[HEAD_SIZE:])
+            if factor != 1.0:
+                mine = mine * factor
+            for n in range(PAIR):
+                lanes = slice(n * HEAD_SIZE, (n + 1) * HEAD_SIZE)
+                target[:, lanes] = mine[:, n * count:(n + 1) * count].T.astype(jnp.bfloat16)
+        dk_sum[...] += dot(dscore[...], q2[...], ((1,), (0,)))
+        dv_sum[...] += dot(probs_b[...], g2[...], ((1,), (0,)))
+
+    def first_products():
+        new_q, new_g = [], []
+        for n in range(PAIR):
+            q = q_ref[:, n * HEAD_SIZE:(n + 1) * HEAD_SIZE]
+            g = g_ref[:, n * HEAD_SIZE:(n + 1) * HEAD_SIZE]
+            new_q.append(jnp.concatenate([q, q], axis=1) * q_pick[...])
+            new_g.append(jnp.concatenate([g, g], axis=1) * g_pick[...])
+        new_q = jnp.concatenate(new_q, axis=0)
+        new_g = jnp.concatenate(new_g, axis=0)
+        scores[...] = dot(kcat[...], new_q, ((1,), (1,)))
+        dprob[...] = dot(vcat[...], new_g, ((1,), (1,)))
+        return new_q, new_g
+
+    def softmax(new_q, new_g):
+        def fold(value, op):
+            value = value.reshape(PIECE // 8, 8, columns)
+            total = value[0]
+            for n in range(1, PIECE // 8):
+                total = op(total, value[n])
+            return total
+
+        def score_piece(at):
+            value = scores[at:at + PIECE, :]
+            if at >= span:
+                value = value + bias[at - span:at - span + PIECE, :]
+            return value
+
+        top = None
+        for at in range(0, keys, PIECE):
+            piece = fold(score_piece(at), jnp.maximum)
+            top = piece if top is None else jnp.maximum(top, piece)
+        top = jnp.max(top, axis=0, keepdims=True)
+        total = jnp.zeros((8, columns), jnp.float32)
+        delta = jnp.zeros((8, columns), jnp.float32)
+        for at in range(0, keys, PIECE):
+            weight = jnp.exp2((score_piece(at) - top) * (SCALE * LOG2E))
+            scores[at:at + PIECE, :] = weight
+            total = total + fold(weight, jnp.add)
+            delta = delta + fold(weight * dprob[at:at + PIECE, :], jnp.add)
+        inverse = 1.0 / jnp.sum(total, axis=0, keepdims=True)
+        delta = jnp.sum(delta, axis=0, keepdims=True) * inverse
+        for at in range(0, keys, PIECE):
+            probs = scores[at:at + PIECE, :] * inverse
+            probs_b[at:at + PIECE, :] = probs.astype(jnp.bfloat16)
+            dscore[at:at + PIECE, :] = (probs * (dprob[at:at + PIECE, :] - delta)).astype(jnp.bfloat16)
+        q2[...] = new_q
+        g2[...] = new_g
+
+    @pl.when(step == 0)
+    def _():
+        softmax(*first_products())
+
+    @pl.when((step > 0) & (step < steps))
+    def _():
+        new = first_products()
+        later_products()
+        softmax(*new)
+
+    @pl.when(step == steps)
+    def _():
+        later_products()
+
+    @pl.when(new_group & (step > 0))
+    def _():
+        group = step // per_group - 1
+        for total_ref, cols, factor in (
+            (dk_sum, key_columns(group), SCALE), (dv_sum, value_columns(group), 1.0)
+        ):
             leaf = (total_ref[span:, :HEAD_SIZE] + total_ref[span:, HEAD_SIZE:]) * factor
             dleaf_ref[:, cols] = leaf.astype(jnp.bfloat16)
             for side in range(2):
@@ -158,6 +221,13 @@
                     @pl.when(jnp.logical_not(same_core))
                     def _():
                         far_sum_ref[slot, :, cols] += value
+        dk_sum[...] = jnp.zeros_like(dk_sum)
+        dv_sum[...] = jnp.zeros_like(dv_sum)
+
+    @pl.when(new_group & (step < steps))
+    def _():
+        kcat_t[...] = kcat[...].T
+        vcat_t[...] = vcat[...].T
 
 
 def attention(
@@ -173,11 +243,23 @@
     width = own.shape[1]
     groups = width // (2 * HEAD_SIZE)
     heads = groups * GQ
+    steps = heads // PAIR
+    per_group = GQ // PAIR
     bf16, f32 = jnp.bfloat16, jnp.float32
-    slab = pl.BlockSpec((count, HEAD_SIZE), lambda h, *_: (0, chunk * heads + h))
-    leaf_k = pl.BlockSpec((count, HEAD_SIZE), lambda h, *_: (0, chunk * groups + h // GQ))
+
+    def now(i):
+        return jnp.minimum(i, steps - 1)
+
+    ahead = pl.BlockSpec((count, PAIR * HEAD_SIZE), lambda i, *_: (0, chunk * steps + now(i)))
+    behind = pl.BlockSpec(
+        (count, PAIR * HEAD_SIZE), lambda i, *_: (0, chunk * steps + jnp.maximum(i - 1, 0))
+    )
+    leaf_k = pl.BlockSpec(
+        (count, HEAD_SIZE), lambda i, *_: (0, chunk * groups + now(i) // per_group)
+    )
     leaf_v = pl.BlockSpec(
-        (count, HEAD_SIZE), lambda h, *_: (0, KEY_VALUE_HEADS + chunk * groups + h // GQ)
+        (count, HEAD_SIZE),
+        lambda i, *_: (0, KEY_VALUE_HEADS + chunk * groups + now(i) // per_group),
     )
     anywhere = pl.BlockSpec(memory_space=pl.ANY)
 
@@ -189,24 +271,30 @@
     return pl.pallas_call(
         functools.partial(
             attention_kernel, prompts=prompts, per_prefix=per_prefix, block_len=block_len,
-            planes=planes, ranks=ranks, chained=chained,
+            planes=planes, ranks=ranks, chained=chained, steps=steps,
         ),
         grid_spec=pltpu.PrefetchScalarGridSpec(
             num_scalar_prefetch=3,
-            grid=(heads,),
+            grid=(steps + 1,),
             in_specs=[
-                slab, slab, leaf_k, leaf_v, full(leaf.shape), full(mask.shape), anywhere, anywhere,
+                ahead, ahead, leaf_k, leaf_v, full(leaf.shape), full(mask.shape), anywhere, anywhere,
             ] + [anywhere] * len(earlier),
-            out_specs=[slab, slab, full((count, width)), full(sum_shape), full(sum_shape)],
+            out_specs=[behind, behind, full((count, width)), full(sum_shape), full(sum_shape)],
             scratch_shapes=[
                 pltpu.VMEM((2 * span, width), bf16),
                 pltpu.VMEM((keys, 2 * HEAD_SIZE), bf16),
                 pltpu.VMEM((keys, 2 * HEAD_SIZE), bf16),
                 pltpu.VMEM((2 * HEAD_SIZE, keys), bf16),
                 pltpu.VMEM((2 * HEAD_SIZE, keys), bf16),
-                pltpu.VMEM((count, count), f32),
+                pltpu.VMEM((count, PAIR * count), f32),
                 pltpu.VMEM((count, 2 * HEAD_SIZE), bf16),
                 pltpu.VMEM((count, 2 * HEAD_SIZE), bf16),
+                pltpu.VMEM((PAIR * count, 2 * HEAD_SIZE), bf16),
+                pltpu.VMEM((PAIR * count, 2 * HEAD_SIZE), bf16),
+                pltpu.VMEM((keys, PAIR * count), f32),
+                pltpu.VMEM((keys, PAIR * count), f32),
+                pltpu.VMEM((keys, PAIR * count), bf16),
+                pltpu.VMEM((keys, PAIR * count), bf16),
                 pltpu.VMEM((keys, 2 * HEAD_SIZE), f32),
                 pltpu.VMEM((keys, 2 * HEAD_SIZE), f32),
                 pltpu.SemaphoreType.DMA((2 * per_prefix,)),
@@ -254,38 +342,47 @@
     step = groups * HEAD_SIZE
     middle = KEY_VALUE_HEADS * HEAD_SIZE
 
-    def gather(chunk):
+    def tie(value, *others):
+        return lax.optimization_barrier((value, *others))[0]
+
+    def by_planes(chunk):
         mine = jnp.concatenate(
             [prefix_key_value[:, chunk * step:(chunk + 1) * step],
              prefix_key_value[:, middle + chunk * step:middle + (chunk + 1) * step]], axis=1
         ) if CHUNKS > 1 else prefix_key_value
         near = [mine] + [send(mine, k, 0, 0) for k in range(1, planes)]
-        near = jnp.concatenate(near, axis=0)
+        return jnp.concatenate(near, axis=0)
+
+    def by_ranks(near):
+        return jnp.concatenate([near, send(near, 0, 1, 0)], axis=0) if ranks == 2 else near
+
+    def reduce_cores(own, far):
+        return own.astype(f32) + send(far, 0, 0, 1).astype(f32)
+
+    def reduce_planes(total, away):
         if ranks == 2:
-            near = jnp.concatenate([near, send(near, 0, 1, 0)], axis=0)
-        return near, send(near, 0, 0, 1)
-
-    def reduce(own, far):
-        total = own.astype(f32) + send(far, 0, 0, 1).astype(f32)
-        if ranks == 2:
-            away = send(total[planes:].astype(jnp.bfloat16), 0, 1, 0)
-            total = total[:planes] + away.astype(f32)
+            total = total[:planes] + send(away, 0, 1, 0).astype(f32)
         mine = total[0]
         for k in range(1, planes):
             mine = mine + send(total[k].astype(jnp.bfloat16), k, 0, 0).astype(f32)
         return mine.astype(jnp.bfloat16)
 
-    blocks = [gather(chunk) for chunk in range(CHUNKS)]
-    d_leaf, d_prefix, earlier = [], [], ()
+    near = [by_planes(chunk) for chunk in range(CHUNKS)]
+    own = [by_ranks(n) for n in near]
+    d_leaf, d_prefix, earlier, done = [], [], (), []
     for chunk in range(CHUNKS):
-        own, far = blocks[chunk]
+        mine = tie(own[chunk], d_leaf[-1] if chunk else near[-1])
+        far = send(mine, 0, 0, 1)
         attended, d_query, leaf_part, own_sum, far_sum = attention(
-            chunk, block_owner, subtree_tokens, place, query, d_out, leaf_key_value, leaf_id, mask,
-            own, far, earlier, planes, ranks,
+            chunk, block_owner, subtree_tokens, tie(place, *done), query, d_out, leaf_key_value,
+            leaf_id, mask, mine, far, earlier, planes, ranks,
         )
         earlier = (attended, d_query)
         d_leaf.append(leaf_part)
-        d_prefix.append(reduce(own_sum, far_sum))
+        total = reduce_cores(own_sum, far_sum)
+        away = total[planes:].astype(jnp.bfloat16)
+        done = [away]
+        d_prefix.append(reduce_planes(total, away))
 
     def join(parts):
         if CHUNKS == 1:

time: 173 us -> 125 us (0.72)
  waiting for transfers between devices: 97.1 us -> 37.5 us
  starting transfers between devices: 14.8 us -> 26.6 us
  local copies, waits for them, and re-layouts: 0.36 us -> 6.08 us
  Pallas kernels: 55.2 us -> 50 us
    ppermute x10 -> x20, waiting for transfers between devices: 97.1 us -> 37.5 us  [send(): return lax.ppermute(array, 'dp', pairs)]
    ppermute x10 -> x20, starting transfers between devices: 14.8 us -> 26.6 us  [send(): return lax.ppermute(array, 'dp', pairs)]
    pallas_call x1 -> x2, Pallas kernels: 55.2 us -> 50 us  [attention(): pl.pallas_call(functools.partial(attention_kernel, prompts=prompts, per_p...]
    unnamed x8 -> x20, local copies, waits for them, and re-layouts: 0.08 us -> 4.01 us
    add x1 -> x2, other arithmetic: 2.48 us -> 0.64 us  [reduce_cores(): return own.astype(f32) + send(far, 0, 0, 1).astype(f32)]
  transfers between devices with their start and end apart: 10 -> 20, of which waited for: 9 -> 12; matrix products, arithmetic and copies ran while one was open for 0% -> 4% of each run, Pallas kernels for 0% -> 40%
where the time goes in v2:
time: 125 us
  Pallas kernels  50 us (40%)
  waiting for transfers between devices  37.5 us (30%)
  starting transfers between devices  26.6 us (21%)
  local copies, waits for them, and re-layouts  6.08 us (5%)
  other arithmetic  3.53 us (3%)
    pallas_call x2, Pallas kernels, attention(): pl.pallas_call(functools.partial(attention_kernel, prompts=prompts, per_p...  50 us
    ppermute x20, waiting for transfers between devices, send(): return lax.ppermute(array, 'dp', pairs)  37.5 us
    ppermute x20, starting transfers between devices, send(): return lax.ppermute(array, 'dp', pairs)  26.6 us
    unnamed x20, local copies, waits for them, and re-layouts  4.01 us
  transfers between devices with their start and end apart: 20, of which 12 were waited for; matrix products, arithmetic and copies ran while one was open for 4% of the time, Pallas kernels for 40%

profile of v2, /device:TPU:0, one launch (start us, length us, event | category | flops | bytes accessed | tf_op | source)
XLA Modules:
  0.0 124.6 jit_solution(7519240708627732213)
XLA Ops:
  1.6 3.1 %collective-permute-start = (bf16[128,512]{1,0:T(8,128)(2,1)S(1)}, bf16[128,512]{1,0:T(8,128)(2,1)S(1)}, u32[]{:S(2)}, u32[]{:S(2)}) collective-permute-start(bf16[128,512]{1,0:T(8,128)(2,1)S(1)} %get-tuple-element.54), channel_id=1, source_target_pairs={{0,4},{1,5},{2,6},{3,7},{4,8},{5,9},{6,10},{7,11},{8,12},{9,13},{1... | collective-permute-start | bytes 393224 | tf_op jit(solution)/shard_map/ppermute | solution.py:339
  4.7 2.6 %collective-permute-start.1 = (bf16[128,512]{1,0:T(8,128)(2,1)S(1)}, bf16[128,512]{1,0:T(8,128)(2,1)S(1)}, u32[]{:S(2)}, u32[]{:S(2)}) collective-permute-start(bf16[128,512]{1,0:T(8,128)(2,1)S(1)} %get-tuple-element.54), channel_id=1, source_target_pairs={{0,8},{1,9},{2,10},{3,11},{4,12},{5,13},{6,14},{7,15},{8,0},{9,1},... | collective-permute-start | bytes 393224 | tf_op jit(solution)/shard_map/ppermute | solution.py:339
  7.3 1.3 %collective-permute-start.2 = (bf16[128,512]{1,0:T(8,128)(2,1)S(1)}, bf16[128,512]{1,0:T(8,128)(2,1)S(1)}, u32[]{:S(2)}, u32[]{:S(2)}) collective-permute-start(bf16[128,512]{1,0:T(8,128)(2,1)S(1)} %get-tuple-element.54), channel_id=1, source_target_pairs={{0,12},{1,13},{2,14},{3,15},{4,0},{5,1},{6,2},{7,3},{8,4},{9,5},{1... | collective-permute-start | bytes 393224 | tf_op jit(solution)/shard_map/ppermute | solution.py:339
  8.6 2.5 %collective-permute-done = bf16[128,512]{1,0:T(8,128)(2,1)S(1)} collective-permute-done((bf16[128,512]{1,0:T(8,128)(2,1)S(1)}, bf16[128,512]{1,0:T(8,128)(2,1)S(1)}, u32[]{:S(2)}, u32[]{:S(2)}) %collective-permute-start) | collective-permute-done | bytes 131104 | tf_op jit(solution)/shard_map/ppermute | solution.py:339
  11.1 4.8 %collective-permute-done.1 = bf16[128,512]{1,0:T(8,128)(2,1)S(1)} collective-permute-done((bf16[128,512]{1,0:T(8,128)(2,1)S(1)}, bf16[128,512]{1,0:T(8,128)(2,1)S(1)}, u32[]{:S(2)}, u32[]{:S(2)}) %collective-permute-start.1) | collective-permute-done | bytes 131104 | tf_op jit(solution)/shard_map/ppermute | solution.py:339
  16.0 1.6 %collective-permute-start.3 = (bf16[512,512]{1,0:T(8,128)(2,1)S(1)}, bf16[512,512]{1,0:T(8,128)(2,1)S(1)}, u32[]{:S(2)}, u32[]{:S(2)}) collective-permute-start(bf16[512,512]{1,0:T(8,128)(2,1)S(1)} %pad_maximum_fusion), channel_id=1, source_target_pairs={{0,2},{1,3},{2,0},{3,1},{4,6},{5,7},{6,4},{7,5},{8,10},{9,11},{10,... | collective-permute-start | bytes 1572872 | tf_op jit(solution)/shard_map/ppermute | solution.py:339
  18.2 3.3 %collective-permute-start.4 = (bf16[128,512]{1,0:T(8,128)(2,1)S(1)}, bf16[128,512]{1,0:T(8,128)(2,1)S(1)}, u32[]{:S(2)}, u32[]{:S(2)}) collective-permute-start(bf16[128,512]{1,0:T(8,128)(2,1)S(1)} %get-tuple-element.53), channel_id=1, source_target_pairs={{0,4},{1,5},{2,6},{3,7},{4,8},{5,9},{6,10},{7,11},{8,12},{9,13},{1... | collective-permute-start | bytes 393224 | tf_op jit(solution)/shard_map/ppermute | solution.py:339
  21.5 1.6 %collective-permute-start.5 = (bf16[128,512]{1,0:T(8,128)(2,1)S(1)}, bf16[128,512]{1,0:T(8,128)(2,1)S(1)}, u32[]{:S(2)}, u32[]{:S(2)}) collective-permute-start(bf16[128,512]{1,0:T(8,128)(2,1)S(1)} %get-tuple-element.53), channel_id=1, source_target_pairs={{0,8},{1,9},{2,10},{3,11},{4,12},{5,13},{6,14},{7,15},{8,0},{9,1},... | collective-permute-start | bytes 393224 | tf_op jit(solution)/shard_map/ppermute | solution.py:339
  23.9 3.0 %collective-permute-done.4 = bf16[128,512]{1,0:T(8,128)(2,1)S(1)} collective-permute-done((bf16[128,512]{1,0:T(8,128)(2,1)S(1)}, bf16[128,512]{1,0:T(8,128)(2,1)S(1)}, u32[]{:S(2)}, u32[]{:S(2)}) %collective-permute-start.4) | collective-permute-done | bytes 131104 | tf_op jit(solution)/shard_map/ppermute | solution.py:339
  26.9 4.3 %collective-permute-done.5 = bf16[128,512]{1,0:T(8,128)(2,1)S(1)} collective-permute-done((bf16[128,512]{1,0:T(8,128)(2,1)S(1)}, bf16[128,512]{1,0:T(8,128)(2,1)S(1)}, u32[]{:S(2)}, u32[]{:S(2)}) %collective-permute-start.5) | collective-permute-done | bytes 131104 | tf_op jit(solution)/shard_map/ppermute | solution.py:339
  32.6 1.4 %collective-permute-done.7.far_ref = bf16[1024,512]{1,0:T(8,128)(2,1)S(1)} collective-permute-done((bf16[1024,512]{1,0:T(8,128)(2,1)S(1)}, bf16[1024,512]{1,0:T(8,128)(2,1)S(1)}, u32[]{:S(2)}, u32[]{:S(2)}) %collective-permute-start.7) | collective-permute-done | bytes 1048608 | tf_op jit(solution)/shard_map/ppermute | solution.py:339
  35.1 24.9 %shard_map.111 = (bf16[256,4096]{1,0:T(8,128)(2,1)}, bf16[256,4096]{1,0:T(8,128)(2,1)}, bf16[256,512]{1,0:T(8,128)(2,1)}, bf16[8,128,512]{2,1,0:T(8,128)(2,1)}, bf16[8,128,512]{2,1,0:T(8,128)(2,1)}) custom-call(s32[16]{0:T(128)} %owner_ref.3, s32[4]{0:T(128)} %tokens_ref.3, s32[1]{0:T(128)} %bitcast.place_ref, bf16[256,4096]{1,0:T(8,128)(2,1)} %q_ref.3, ...), custom_call_target="tpu_custom_call" | custom-call | flops 9663676416 | bytes 8388608 | tf_op jit(solution)/shard_map/pallas_call | solution.py:271
  63.9 1.3 %collective-permute-done.10.far_ref = bf16[1024,512]{1,0:T(8,128)(2,1)S(1)} collective-permute-done((bf16[1024,512]{1,0:T(8,128)(2,1)}, bf16[1024,512]{1,0:T(8,128)(2,1)S(1)}, u32[]{:S(2)}, u32[]{:S(2)}) %collective-permute-start.10) | collective-permute-done | bytes 1048608 | tf_op jit(solution)/shard_map/ppermute | solution.py:339
  66.2 25.1 %shard_map.112 = (bf16[256,4096]{1,0:T(8,128)(2,1)}, bf16[256,4096]{1,0:T(8,128)(2,1)}, bf16[256,512]{1,0:T(8,128)(2,1)}, bf16[8,128,512]{2,1,0:T(8,128)(2,1)}, bf16[8,128,512]{2,1,0:T(8,128)(2,1)}) custom-call(s32[16]{0:T(128)} %owner_ref.3, s32[4]{0:T(128)} %tokens_ref.3, s32[1]{0:T(128)} %bitcast.place_ref, ...), custom_call_target="tpu_custom_call", output_to_operand_aliasing={{0}: (11, {}), {1}: (12, {})} | custom-call | flops 9663676416 | bytes 8388608 | tf_op jit(solution)/shard_map/pallas_call | solution.py:271
  92.0 3.3 %collective-permute-start.12 = (bf16[128,512]{1,0:T(8,128)(2,1)S(1)}, bf16[128,512]{1,0:T(8,128)(2,1)S(1)}, u32[]{:S(2)}, u32[]{:S(2)}) collective-permute-start(bf16[128,512]{1,0:T(8,128)(2,1)S(1)} %get-tuple-element.34), channel_id=1, source_target_pairs={{0,4},{1,5},{2,6},{3,7},{4,8},{5,9},{6,10},{7,11},{8,12},{9,13},{1... | collective-permute-start | bytes 393224 | tf_op jit(solution)/shard_map/ppermute | solution.py:339
  95.4 1.7 %collective-permute-start.13 = (bf16[128,512]{1,0:T(8,128)(2,1)S(1)}, bf16[128,512]{1,0:T(8,128)(2,1)S(1)}, u32[]{:S(2)}, u32[]{:S(2)}) collective-permute-start(bf16[128,512]{1,0:T(8,128)(2,1)S(1)} %get-tuple-element.36), channel_id=1, source_target_pairs={{0,8},{1,9},{2,10},{3,11},{4,12},{5,13},{6,14},{7,15},{8,0},{9,1},... | collective-permute-start | bytes 393224 | tf_op jit(solution)/shard_map/ppermute | solution.py:339
  99.7 1.3 %collective-permute-done.12 = bf16[128,512]{1,0:T(8,128)(2,1)S(1)} collective-permute-done((bf16[128,512]{1,0:T(8,128)(2,1)S(1)}, bf16[128,512]{1,0:T(8,128)(2,1)S(1)}, u32[]{:S(2)}, u32[]{:S(2)}) %collective-permute-start.12) | collective-permute-done | bytes 131104 | tf_op jit(solution)/shard_map/ppermute | solution.py:339
  100.9 5.1 %collective-permute-done.13 = bf16[128,512]{1,0:T(8,128)(2,1)S(1)} collective-permute-done((bf16[128,512]{1,0:T(8,128)(2,1)S(1)}, bf16[128,512]{1,0:T(8,128)(2,1)S(1)}, u32[]{:S(2)}, u32[]{:S(2)}) %collective-permute-start.13) | collective-permute-done | bytes 131104 | tf_op jit(solution)/shard_map/ppermute | solution.py:339
  106.1 5.6 %collective-permute-done.16 = bf16[4,128,512]{2,1,0:T(8,128)(2,1)S(1)} collective-permute-done((bf16[4,128,512]{2,1,0:T(8,128)(2,1)S(1)}, bf16[4,128,512]{2,1,0:T(8,128)(2,1)S(1)}, u32[]{:S(2)}, u32[]{:S(2)}) %collective-permute-start.16) | collective-permute-done | bytes 524320 | tf_op jit(solution)/shard_map/ppermute | solution.py:339
  112.0 1.1 collective-permute-start.17
  113.0 1.2 collective-permute-start.18
  114.3 1.6 %collective-permute-start.19 = (bf16[128,512]{1,0:T(8,128)(2,1)S(1)}, bf16[128,512]{1,0:T(8,128)(2,1)S(1)}, u32[]{:S(2)}, u32[]{:S(2)}) collective-permute-start(bf16[128,512]{1,0:T(8,128)(2,1)S(1)} %get-tuple-element.38), channel_id=1, source_target_pairs={{0,12},{1,13},{2,14},{3,15},{4,0},{5,1},{6,2},{7,3},{8,4},{9,5},{1... | collective-permute-start | bytes 393224 | tf_op jit(solution)/shard_map/ppermute | solution.py:339
  115.9 4.4 %collective-permute-done.17 = bf16[128,512]{1,0:T(8,128)(2,1)S(1)} collective-permute-done((bf16[128,512]{1,0:T(8,128)(2,1)S(1)}, bf16[128,512]{1,0:T(8,128)(2,1)S(1)}, u32[]{:S(2)}, u32[]{:S(2)}) %collective-permute-start.17) | collective-permute-done | bytes 131104 | tf_op jit(solution)/shard_map/ppermute | solution.py:339
  120.3 3.4 %collective-permute-done.18 = bf16[128,512]{1,0:T(8,128)(2,1)S(1)} collective-permute-done((bf16[128,512]{1,0:T(8,128)(2,1)S(1)}, bf16[128,512]{1,0:T(8,128)(2,1)S(1)}, u32[]{:S(2)}, u32[]{:S(2)}) %collective-permute-start.18) | collective-permute-done | bytes 131104 | tf_op jit(solution)/shard_map/ppermute | solution.py:339
  (61 shorter events, 14.0 us)
Async XLA Ops:
  1.6 9.5 %collective-permute-start = (bf16[128,512]{1,0:T(8,128)(2,1)S(1)}, bf16[128,512]{1,0:T(8,128)(2,1)S(1)}, u32[]{:S(2)}, u32[]{:S(2)}) collective-permute-start(bf16[128,512]{1,0:T(8,128)(2,1)S(1)} %get-tuple-element.54), channel_id=1, source_target_pairs={{0,4},{1,5},{2,6},{3,7},{4,8},{5,9},{6,10},{7,11},{8,12},{9,13},{1... | collective-permute-start | bytes 393224 | tf_op jit(solution)/shard_map/ppermute | solution.py:339
  4.7 11.2 %collective-permute-start.1 = (bf16[128,512]{1,0:T(8,128)(2,1)S(1)}, bf16[128,512]{1,0:T(8,128)(2,1)S(1)}, u32[]{:S(2)}, u32[]{:S(2)}) collective-permute-start(bf16[128,512]{1,0:T(8,128)(2,1)S(1)} %get-tuple-element.54), channel_id=1, source_target_pairs={{0,8},{1,9},{2,10},{3,11},{4,12},{5,13},{6,14},{7,15},{8,0},{9,1},... | collective-permute-start | bytes 393224 | tf_op jit(solution)/shard_map/ppermute | solution.py:339
  7.3 8.6 %collective-permute-start.2 = (bf16[128,512]{1,0:T(8,128)(2,1)S(1)}, bf16[128,512]{1,0:T(8,128)(2,1)S(1)}, u32[]{:S(2)}, u32[]{:S(2)}) collective-permute-start(bf16[128,512]{1,0:T(8,128)(2,1)S(1)} %get-tuple-element.54), channel_id=1, source_target_pairs={{0,12},{1,13},{2,14},{3,15},{4,0},{5,1},{6,2},{7,3},{8,4},{9,5},{1... | collective-permute-start | bytes 393224 | tf_op jit(solution)/shard_map/ppermute | solution.py:339
  16.0 15.3 %collective-permute-start.3 = (bf16[512,512]{1,0:T(8,128)(2,1)S(1)}, bf16[512,512]{1,0:T(8,128)(2,1)S(1)}, u32[]{:S(2)}, u32[]{:S(2)}) collective-permute-start(bf16[512,512]{1,0:T(8,128)(2,1)S(1)} %pad_maximum_fusion), channel_id=1, source_target_pairs={{0,2},{1,3},{2,0},{3,1},{4,6},{5,7},{6,4},{7,5},{8,10},{9,11},{10,... | collective-permute-start | bytes 1572872 | tf_op jit(solution)/shard_map/ppermute | solution.py:339
  18.2 8.7 %collective-permute-start.4 = (bf16[128,512]{1,0:T(8,128)(2,1)S(1)}, bf16[128,512]{1,0:T(8,128)(2,1)S(1)}, u32[]{:S(2)}, u32[]{:S(2)}) collective-permute-start(bf16[128,512]{1,0:T(8,128)(2,1)S(1)} %get-tuple-element.53), channel_id=1, source_target_pairs={{0,4},{1,5},{2,6},{3,7},{4,8},{5,9},{6,10},{7,11},{8,12},{9,13},{1... | collective-permute-start | bytes 393224 | tf_op jit(solution)/shard_map/ppermute | solution.py:339
  21.5 9.7 %collective-permute-start.5 = (bf16[128,512]{1,0:T(8,128)(2,1)S(1)}, bf16[128,512]{1,0:T(8,128)(2,1)S(1)}, u32[]{:S(2)}, u32[]{:S(2)}) collective-permute-start(bf16[128,512]{1,0:T(8,128)(2,1)S(1)} %get-tuple-element.53), channel_id=1, source_target_pairs={{0,8},{1,9},{2,10},{3,11},{4,12},{5,13},{6,14},{7,15},{8,0},{9,1},... | collective-permute-start | bytes 393224 | tf_op jit(solution)/shard_map/ppermute | solution.py:339
  23.1 8.1 %collective-permute-start.6 = (bf16[128,512]{1,0:T(8,128)(2,1)S(1)}, bf16[128,512]{1,0:T(8,128)(2,1)S(1)}, u32[]{:S(2)}, u32[]{:S(2)}) collective-permute-start(bf16[128,512]{1,0:T(8,128)(2,1)S(1)} %get-tuple-element.53), channel_id=1, source_target_pairs={{0,12},{1,13},{2,14},{3,15},{4,0},{5,1},{6,2},{7,3},{8,4},{9,5},{1... | collective-permute-start | bytes 393224 | tf_op jit(solution)/shard_map/ppermute | solution.py:339
  31.3 2.7 %copy-start.4 = (bf16[1024,512]{1,0:T(8,128)(2,1)}, bf16[1024,512]{1,0:T(8,128)(2,1)S(1)}, u32[]{:S(2)}) copy-start(bf16[1024,512]{1,0:T(8,128)(2,1)S(1)} %constant_dynamic-update-slice_fusion.own_ref) | copy-start | bytes 3145732
  31.3 2.7 %collective-permute-start.7 = (bf16[1024,512]{1,0:T(8,128)(2,1)S(1)}, bf16[1024,512]{1,0:T(8,128)(2,1)S(1)}, u32[]{:S(2)}, u32[]{:S(2)}) collective-permute-start(bf16[1024,512]{1,0:T(8,128)(2,1)S(1)} %constant_dynamic-update-slice_fusion.own_ref), channel_id=1, source_target_pairs={{0,1},{1,0},{2,3},{3,2},{4,5},{5,4},{6,7},{7,6},{8,9},{9,8},{10,11... | collective-permute-start | bytes 3145736 | tf_op jit(solution)/shard_map/ppermute | solution.py:339
  31.4 30.1 %collective-permute-start.9 = (bf16[512,512]{1,0:T(8,128)(2,1)S(1)}, bf16[512,512]{1,0:T(8,128)(2,1)S(1)}, u32[]{:S(2)}, u32[]{:S(2)}) collective-permute-start(bf16[512,512]{1,0:T(8,128)(2,1)S(1)} %pad_maximum_fusion.1), channel_id=1, source_target_pairs={{0,2},{1,3},{2,0},{3,1},{4,6},{5,7},{6,4},{7,5},{8,10},{9,11},{10,... | collective-permute-start | bytes 1572872 | tf_op jit(solution)/shard_map/ppermute | solution.py:339
  60.0 2.9 %copy-start.1 = (bf16[8,128,512]{2,1,0:T(8,128)(2,1)S(1)}, bf16[8,128,512]{2,1,0:T(8,128)(2,1)}, u32[]{:S(2)}) copy-start(bf16[8,128,512]{2,1,0:T(8,128)(2,1)} %get-tuple-element.18) | copy-start | bytes 3145732
  60.0 2.9 %collective-permute-start.8 = (bf16[8,128,512]{2,1,0:T(8,128)(2,1)}, bf16[8,128,512]{2,1,0:T(8,128)(2,1)S(1)}, u32[]{:S(2)}, u32[]{:S(2)}) collective-permute-start(bf16[8,128,512]{2,1,0:T(8,128)(2,1)} %get-tuple-element.19), channel_id=1, source_target_pairs={{0,1},{1,0},{2,3},{3,2},{4,5},{5,4},{6,7},{7,6},{8,9},{9,8},{10,11... | collective-permute-start | bytes 3145736 | tf_op jit(solution)/shard_map/ppermute | solution.py:339
  62.4 2.9 %collective-permute-start.10 = (bf16[1024,512]{1,0:T(8,128)(2,1)}, bf16[1024,512]{1,0:T(8,128)(2,1)S(1)}, u32[]{:S(2)}, u32[]{:S(2)}) collective-permute-start(bf16[1024,512]{1,0:T(8,128)(2,1)} %constant_dynamic-update-slice_fusion.5.own_ref), channel_id=1, source_target_pairs={{0,1},{1,0},{2,3},{3,2},{4,5},{5,4},{6,7},{7,6},{8,9},{9,8},{10,11... | collective-permute-start | bytes 3145736 | tf_op jit(solution)/shard_map/ppermute | solution.py:339
  63.4 28.4 %collective-permute-start.11 = (bf16[4,128,512]{2,1,0:T(8,128)(2,1)S(1)}, bf16[4,128,512]{2,1,0:T(8,128)(2,1)S(1)}, u32[]{:S(2)}, u32[]{:S(2)}) collective-permute-start(bf16[4,128,512]{2,1,0:T(8,128)(2,1)S(1)} %slice.149), channel_id=1, source_target_pairs={{0,2},{1,3},{2,0},{3,1},{4,6},{5,7},{6,4},{7,5},{8,10},{9,11},{10,... | collective-permute-start | bytes 1572872 | tf_op jit(solution)/shard_map/ppermute | solution.py:339
  66.2 25.5 %copy-start.3 = (bf16[256,512]{1,0:T(8,128)(2,1)S(1)}, bf16[256,512]{1,0:T(8,128)(2,1)}, u32[]{:S(2)}) copy-start(bf16[256,512]{1,0:T(8,128)(2,1)} %get-tuple-element.21) | copy-start | bytes 786436
  91.3 6.5 %collective-permute-start.15 = (bf16[8,128,512]{2,1,0:T(8,128)(2,1)}, bf16[8,128,512]{2,1,0:T(8,128)(2,1)S(1)}, u32[]{:S(2)}, u32[]{:S(2)}) collective-permute-start(bf16[8,128,512]{2,1,0:T(8,128)(2,1)} %get-tuple-element.29), channel_id=1, source_target_pairs={{0,1},{1,0},{2,3},{3,2},{4,5},{5,4},{6,7},{7,6},{8,9},{9,8},{10,11... | collective-permute-start | bytes 3145736 | tf_op jit(solution)/shard_map/ppermute | solution.py:339
  91.8 6.0 %copy-start = (bf16[8,128,512]{2,1,0:T(8,128)(2,1)S(1)}, bf16[8,128,512]{2,1,0:T(8,128)(2,1)}, u32[]{:S(2)}) copy-start(bf16[8,128,512]{2,1,0:T(8,128)(2,1)} %get-tuple-element.28) | copy-start | bytes 3145732
  92.0 8.9 %collective-permute-start.12 = (bf16[128,512]{1,0:T(8,128)(2,1)S(1)}, bf16[128,512]{1,0:T(8,128)(2,1)S(1)}, u32[]{:S(2)}, u32[]{:S(2)}) collective-permute-start(bf16[128,512]{1,0:T(8,128)(2,1)S(1)} %get-tuple-element.34), channel_id=1, source_target_pairs={{0,4},{1,5},{2,6},{3,7},{4,8},{5,9},{6,10},{7,11},{8,12},{9,13},{1... | collective-permute-start | bytes 393224 | tf_op jit(solution)/shard_map/ppermute | solution.py:339
  95.4 10.7 %collective-permute-start.13 = (bf16[128,512]{1,0:T(8,128)(2,1)S(1)}, bf16[128,512]{1,0:T(8,128)(2,1)S(1)}, u32[]{:S(2)}, u32[]{:S(2)}) collective-permute-start(bf16[128,512]{1,0:T(8,128)(2,1)S(1)} %get-tuple-element.36), channel_id=1, source_target_pairs={{0,8},{1,9},{2,10},{3,11},{4,12},{5,13},{6,14},{7,15},{8,0},{9,1},... | collective-permute-start | bytes 393224 | tf_op jit(solution)/shard_map/ppermute | solution.py:339
  97.1 9.0 %collective-permute-start.14 = (bf16[128,512]{1,0:T(8,128)(2,1)S(1)}, bf16[128,512]{1,0:T(8,128)(2,1)S(1)}, u32[]{:S(2)}, u32[]{:S(2)}) collective-permute-start(bf16[128,512]{1,0:T(8,128)(2,1)S(1)} %get-tuple-element.35), channel_id=1, source_target_pairs={{0,12},{1,13},{2,14},{3,15},{4,0},{5,1},{6,2},{7,3},{8,4},{9,5},{1... | collective-permute-start | bytes 393224 | tf_op jit(solution)/shard_map/ppermute | solution.py:339
  98.2 13.5 %collective-permute-start.16 = (bf16[4,128,512]{2,1,0:T(8,128)(2,1)S(1)}, bf16[4,128,512]{2,1,0:T(8,128)(2,1)S(1)}, u32[]{:S(2)}, u32[]{:S(2)}) collective-permute-start(bf16[4,128,512]{2,1,0:T(8,128)(2,1)S(1)} %slice.148), channel_id=1, source_target_pairs={{0,2},{1,3},{2,0},{3,1},{4,6},{5,7},{6,4},{7,5},{8,10},{9,11},{10,... | collective-permute-start | bytes 1572872 | tf_op jit(solution)/shard_map/ppermute | solution.py:339
  112.0 8.3 %collective-permute-start.17 = (bf16[128,512]{1,0:T(8,128)(2,1)S(1)}, bf16[128,512]{1,0:T(8,128)(2,1)S(1)}, u32[]{:S(2)}, u32[]{:S(2)}) collective-permute-start(bf16[128,512]{1,0:T(8,128)(2,1)S(1)} %get-tuple-element.37), channel_id=1, source_target_pairs={{0,4},{1,5},{2,6},{3,7},{4,8},{5,9},{6,10},{7,11},{8,12},{9,13},{1... | collective-permute-start | bytes 393224 | tf_op jit(solution)/shard_map/ppermute | solution.py:339
  113.0 10.7 %collective-permute-start.18 = (bf16[128,512]{1,0:T(8,128)(2,1)S(1)}, bf16[128,512]{1,0:T(8,128)(2,1)S(1)}, u32[]{:S(2)}, u32[]{:S(2)}) collective-permute-start(bf16[128,512]{1,0:T(8,128)(2,1)S(1)} %get-tuple-element.39), channel_id=1, source_target_pairs={{0,8},{1,9},{2,10},{3,11},{4,12},{5,13},{6,14},{7,15},{8,0},{9,1},... | collective-permute-start | bytes 393224 | tf_op jit(solution)/shard_map/ppermute | solution.py:339
  114.3 9.5 %collective-permute-start.19 = (bf16[128,512]{1,0:T(8,128)(2,1)S(1)}, bf16[128,512]{1,0:T(8,128)(2,1)S(1)}, u32[]{:S(2)}, u32[]{:S(2)}) collective-permute-start(bf16[128,512]{1,0:T(8,128)(2,1)S(1)} %get-tuple-element.38), channel_id=1, source_target_pairs={{0,12},{1,13},{2,14},{3,15},{4,0},{5,1},{6,2},{7,3},{8,4},{9,5},{1... | collective-permute-start | bytes 393224 | tf_op jit(solution)/shard_map/ppermute | solution.py:339
  (3 other events, 3.0 us)

commit v3 on v2

--- a/solution.py
+++ b/solution.py
@@ -17,26 +17,27 @@
 def dot(a, b, contract):
     return lax.dot_general(a, b, (contract, ((), ())), preferred_element_type=jnp.float32)
 
-CHUNKS = 2
+CHUNKS = (1, 2, 1)
 PAIR = 2
 PIECE = 32
 
 
 def attention_kernel(
     owner_ref, tokens_ref, place_ref,
-    q_ref, g_ref, leaf_k_ref, leaf_v_ref, leaf_ref, mask_ref, own_ref, far_ref, *rest,
+    q_ref, g_ref, leaf_k_ref, leaf_v_ref, leaf_ref, mask_ref, *rest,
     prompts, per_prefix, block_len, planes, ranks, chained, steps,
 ):
+    sources = rest[:2 * ranks]
     (out_ref, dq_ref, dleaf_ref, own_sum_ref, far_sum_ref,
      kv, kcat, vcat, kcat_t, vcat_t, bias, q_pick, g_pick, q2, g2, scores, dprob, probs_b, dscore,
-     dk_sum, dv_sum, sems) = rest[2 * chained:]
+     dk_sum, dv_sum, sems) = rest[2 * ranks + 2 * chained:]
     step = pl.program_id(0)
     per_group = GQ // PAIR
     count = q_ref.shape[0]
     columns = PAIR * count
     span = per_prefix * block_len
     keys = span + count
-    half = own_ref.shape[1] // 2
+    half = sources[0].shape[1] // 2
 
     place = place_ref[0]
     first = place * count
@@ -72,17 +73,13 @@
             for j in range(per_prefix):
                 n = side * per_prefix + j
                 same_core, row, ahead = block_place(side, j)
-                slot = row * planes + lax.rem(planes - ahead, planes)
+                slot = lax.rem(planes - ahead, planes)
                 rows = pl.ds(pl.multiple_of(slot * block_len, block_len), block_len)
                 target = kv.at[pl.ds(n * block_len, block_len), :]
-
-                @pl.when(same_core)
-                def _():
-                    pltpu.make_async_copy(own_ref.at[rows, :], target, sems.at[n]).start()
-
-                @pl.when(jnp.logical_not(same_core))
-                def _():
-                    pltpu.make_async_copy(far_ref.at[rows, :], target, sems.at[n]).start()
+                for at, source in enumerate(sources):
+                    @pl.when((same_core == (at % 2 == 0)) & (row == at // 2))
+                    def _():
+                        pltpu.make_async_copy(source.at[rows, :], target, sems.at[n]).start()
 
         leaf_row = jnp.broadcast_to(leaf_ref[...], (count, count))
         leaf_col = leaf_row.T
@@ -105,7 +102,9 @@
         dv_sum[...] = jnp.zeros_like(dv_sum)
         for n in range(2 * per_prefix):
             target = kv.at[pl.ds(n * block_len, block_len), :]
-            pltpu.make_async_copy(own_ref.at[pl.ds(0, block_len), :], target, sems.at[n]).wait()
+            pltpu.make_async_copy(
+                sources[0].at[pl.ds(0, block_len), :], target, sems.at[n]
+            ).wait()
 
     new_group = lax.rem(step, per_group) == 0
 
@@ -145,33 +144,31 @@
             new_g.append(jnp.concatenate([g, g], axis=1) * g_pick[...])
         new_q = jnp.concatenate(new_q, axis=0)
         new_g = jnp.concatenate(new_g, axis=0)
-        scores[...] = dot(kcat[...], new_q, ((1,), (1,)))
-        dprob[...] = dot(vcat[...], new_g, ((1,), (1,)))
-        return new_q, new_g
-
-    def softmax(new_q, new_g):
-        def fold(value, op):
-            value = value.reshape(PIECE // 8, 8, columns)
-            total = value[0]
-            for n in range(1, PIECE // 8):
-                total = op(total, value[n])
-            return total
-
-        def score_piece(at):
-            value = scores[at:at + PIECE, :]
-            if at >= span:
-                value = value + bias[at - span:at - span + PIECE, :]
-            return value
-
+        product = dot(kcat[...], new_q, ((1,), (1,)))
         top = None
         for at in range(0, keys, PIECE):
-            piece = fold(score_piece(at), jnp.maximum)
+            piece = product[at:at + PIECE]
+            if at >= span:
+                piece = piece + bias[at - span:at - span + PIECE, :]
+            scores[at:at + PIECE, :] = piece
+            piece = fold(piece, jnp.maximum)
             top = piece if top is None else jnp.maximum(top, piece)
+        dprob[...] = dot(vcat[...], new_g, ((1,), (1,)))
+        return new_q, new_g, top
+
+    def fold(value, op):
+        value = value.reshape(PIECE // 8, 8, columns)
+        total = value[0]
+        for n in range(1, PIECE // 8):
+            total = op(total, value[n])
+        return total
+
+    def softmax(new_q, new_g, top):
         top = jnp.max(top, axis=0, keepdims=True)
         total = jnp.zeros((8, columns), jnp.float32)
         delta = jnp.zeros((8, columns), jnp.float32)
         for at in range(0, keys, PIECE):
-            weight = jnp.exp2((score_piece(at) - top) * (SCALE * LOG2E))
+            weight = jnp.exp2((scores[at:at + PIECE, :] - top) * (SCALE * LOG2E))
             scores[at:at + PIECE, :] = weight
             total = total + fold(weight, jnp.add)
             delta = delta + fold(weight * dprob[at:at + PIECE, :], jnp.add)
@@ -231,35 +228,37 @@
 
 
 def attention(
-    chunk, owner, tokens, place, q, g, leaf_kv, leaf, mask, own, far, earlier, planes, ranks
+    chunk, owner, tokens, place, q, g, leaf_kv, leaf, mask, sources, earlier, planes, ranks
 ):
     count = q.shape[0]
     slots = planes * ranks
-    block_len = own.shape[0] // slots
+    block_len = sources[0].shape[0] // planes
     prompts = tokens.shape[0]
     per_prefix = owner.shape[0] // prompts
     span = per_prefix * block_len
     keys = span + count
-    width = own.shape[1]
-    groups = width // (2 * HEAD_SIZE)
+    width = sources[0].shape[1]
+    groups = CHUNKS[chunk]
+    skipped = sum(CHUNKS[:chunk])
     heads = groups * GQ
     steps = heads // PAIR
     per_group = GQ // PAIR
+    skipped_steps = skipped * per_group
     bf16, f32 = jnp.bfloat16, jnp.float32
 
     def now(i):
         return jnp.minimum(i, steps - 1)
 
-    ahead = pl.BlockSpec((count, PAIR * HEAD_SIZE), lambda i, *_: (0, chunk * steps + now(i)))
+    ahead = pl.BlockSpec((count, PAIR * HEAD_SIZE), lambda i, *_: (0, skipped_steps + now(i)))
     behind = pl.BlockSpec(
-        (count, PAIR * HEAD_SIZE), lambda i, *_: (0, chunk * steps + jnp.maximum(i - 1, 0))
+        (count, PAIR * HEAD_SIZE), lambda i, *_: (0, skipped_steps + jnp.maximum(i - 1, 0))
     )
     leaf_k = pl.BlockSpec(
-        (count, HEAD_SIZE), lambda i, *_: (0, chunk * groups + now(i) // per_group)
+        (count, HEAD_SIZE), lambda i, *_: (0, skipped + now(i) // per_group)
     )
     leaf_v = pl.BlockSpec(
         (count, HEAD_SIZE),
-        lambda i, *_: (0, KEY_VALUE_HEADS + chunk * groups + now(i) // per_group),
+        lambda i, *_: (0, KEY_VALUE_HEADS + skipped + now(i) // per_group),
     )
     anywhere = pl.BlockSpec(memory_space=pl.ANY)
 
@@ -277,8 +276,8 @@
             num_scalar_prefetch=3,
             grid=(steps + 1,),
             in_specs=[
-                ahead, ahead, leaf_k, leaf_v, full(leaf.shape), full(mask.shape), anywhere, anywhere,
-            ] + [anywhere] * len(earlier),
+                ahead, ahead, leaf_k, leaf_v, full(leaf.shape), full(mask.shape),
+            ] + [anywhere] * (2 * ranks + len(earlier)),
             out_specs=[behind, behind, full((count, width)), full(sum_shape), full(sum_shape)],
             scratch_shapes=[
                 pltpu.VMEM((2 * span, width), bf16),
@@ -307,15 +306,15 @@
             jax.ShapeDtypeStruct(sum_shape, bf16),
             jax.ShapeDtypeStruct(sum_shape, bf16),
         ],
-        input_output_aliases={11: 0, 12: 1} if chained else {},
+        input_output_aliases={9 + 2 * ranks: 0, 10 + 2 * ranks: 1} if chained else {},
         compiler_params=pltpu.CompilerParams(
-            vmem_limit_bytes=60 * 2**20, dimension_semantics=("arbitrary",)
+            vmem_limit_bytes=32 * 2**20, dimension_semantics=("arbitrary",)
         ),
         cost_estimate=pl.CostEstimate(
-            flops=heads * 6 * 2 * keys * 256 * 256, bytes_accessed=16 * 2**20 // CHUNKS,
+            flops=heads * 6 * 2 * keys * 256 * 256, bytes_accessed=groups * 4 * 2**20,
             transcendentals=heads * keys * count,
         ),
-    )(owner, tokens, place, q, g, leaf_kv, leaf_kv, leaf, mask, own, far, *earlier)
+    )(owner, tokens, place, q, g, leaf_kv, leaf_kv, leaf, mask, *sources, *earlier)
 
 
 def shards(
@@ -338,56 +337,67 @@
         ]
         return lax.ppermute(array, "dp", pairs)
 
-    groups = KEY_VALUE_HEADS // CHUNKS
-    step = groups * HEAD_SIZE
     middle = KEY_VALUE_HEADS * HEAD_SIZE
 
     def tie(value, *others):
         return lax.optimization_barrier((value, *others))[0]
 
     def by_planes(chunk):
+        low = sum(CHUNKS[:chunk]) * HEAD_SIZE
+        high = low + CHUNKS[chunk] * HEAD_SIZE
         mine = jnp.concatenate(
-            [prefix_key_value[:, chunk * step:(chunk + 1) * step],
-             prefix_key_value[:, middle + chunk * step:middle + (chunk + 1) * step]], axis=1
-        ) if CHUNKS > 1 else prefix_key_value
-        near = [mine] + [send(mine, k, 0, 0) for k in range(1, planes)]
-        return jnp.concatenate(near, axis=0)
-
-    def by_ranks(near):
-        return jnp.concatenate([near, send(near, 0, 1, 0)], axis=0) if ranks == 2 else near
+            [prefix_key_value[:, low:high], prefix_key_value[:, middle + low:middle + high]], axis=1
+        )
+        return jnp.concatenate([mine] + [send(mine, k, 0, 0) for k in range(1, planes)], axis=0)
 
     def reduce_cores(own, far):
         return own.astype(f32) + send(far, 0, 0, 1).astype(f32)
 
+    def reduce_ranks(total, away):
+        return total[:planes] + send(away, 0, 1, 0).astype(f32) if ranks == 2 else total
+
     def reduce_planes(total, away):
-        if ranks == 2:
-            total = total[:planes] + send(away, 0, 1, 0).astype(f32)
         mine = total[0]
         for k in range(1, planes):
-            mine = mine + send(total[k].astype(jnp.bfloat16), k, 0, 0).astype(f32)
+            mine = mine + send(away[k - 1], k, 0, 0).astype(f32)
         return mine.astype(jnp.bfloat16)
 
-    near = [by_planes(chunk) for chunk in range(CHUNKS)]
-    own = [by_ranks(n) for n in near]
-    d_leaf, d_prefix, earlier, done = [], [], (), []
-    for chunk in range(CHUNKS):
-        mine = tie(own[chunk], d_leaf[-1] if chunk else near[-1])
-        far = send(mine, 0, 0, 1)
+    chunks = len(CHUNKS)
+    near = [by_planes(chunk) for chunk in range(chunks)]
+    other = [send(n, 0, 1, 0) for n in near] if ranks == 2 else []
+    d_leaf, d_prefix, earlier = [], [], ()
+    by_cores, by_ranks = [], []
+    for chunk in range(chunks):
+        first = [place] + near[chunk + 1:chunk + 2]
+        if chunk >= 1:
+            first.append(by_cores[chunk - 1][1])
+        if chunk >= 2:
+            total, away = by_cores[chunk - 2]
+            total = reduce_ranks(total, away)
+            away = [total[k].astype(jnp.bfloat16) for k in range(1, planes)]
+            by_ranks.append((total, away))
+            first.extend(away)
+        sources = [near[chunk], send(near[chunk], 0, 0, 1)]
+        if ranks == 2:
+            row = tie(other[chunk], d_leaf[-1] if chunk else near[1])
+            sources += [row, send(row, 0, 0, 1)]
         attended, d_query, leaf_part, own_sum, far_sum = attention(
-            chunk, block_owner, subtree_tokens, tie(place, *done), query, d_out, leaf_key_value,
-            leaf_id, mask, mine, far, earlier, planes, ranks,
+            chunk, block_owner, subtree_tokens, tie(*first), query, d_out, leaf_key_value,
+            leaf_id, mask, sources, earlier, planes, ranks,
         )
         earlier = (attended, d_query)
         d_leaf.append(leaf_part)
         total = reduce_cores(own_sum, far_sum)
-        away = total[planes:].astype(jnp.bfloat16)
-        done = [away]
-        d_prefix.append(reduce_planes(total, away))
+        by_cores.append((total, total[planes:].astype(jnp.bfloat16)))
+    for chunk in range(chunks):
+        if chunk >= len(by_ranks):
+            total = reduce_ranks(*by_cores[chunk])
+            by_ranks.append((total, [total[k].astype(jnp.bfloat16) for k in range(1, planes)]))
+        d_prefix.append(reduce_planes(*by_ranks[chunk]))
 
     def join(parts):
-        if CHUNKS == 1:
-            return parts[0]
-        return jnp.concatenate([p[:, :step] for p in parts] + [p[:, step:] for p in parts], axis=1)
+        halves = [jnp.split(p, 2, axis=1) for p in parts]
+        return jnp.concatenate([h[0] for h in halves] + [h[1] for h in halves], axis=1)
 
     return attended, d_query, join(d_leaf), join(d_prefix)
 

time: 125 us -> 129 us (1.032)
  starting transfers between devices: 26.6 us -> 39 us
  waiting for transfers between devices: 37.5 us -> 33.4 us
  other arithmetic: 3.53 us -> 1.17 us
    ppermute x20 -> x33, starting transfers between devices: 26.6 us -> 39 us  [send(): return lax.ppermute(array, 'dp', pairs)]
    ppermute x20 -> x33, waiting for transfers between devices: 37.5 us -> 33.4 us  [send(): return lax.ppermute(array, 'dp', pairs)]
    concatenate x5 -> x6, other arithmetic: 1.68 us -> 0.11 us  [the longest x3 0.08 us: by_planes(): jnp.concatenate([mine] + [send(mine, k, 0, 0) for k in range(1, planes)],...]
    pallas_call x2 -> x3, Pallas kernels: 50 us -> 48.8 us  [attention(): pl.pallas_call(functools.partial(attention_kernel, prompts=prompts, per_p...]
    unnamed x20 -> x28, local copies, waits for them, and re-layouts: 4.01 us -> 3.46 us
  transfers between devices with their start and end apart: 20 -> 33, of which waited for: 12 -> 15; matrix products, arithmetic and copies ran while one was open for 4% -> 2% of each run, Pallas kernels for 40% -> 38%
where the time goes in v3:
time: 129 us
  Pallas kernels  48.8 us (38%)
  starting transfers between devices  39 us (30%)
  waiting for transfers between devices  33.4 us (26%)
  local copies, waits for them, and re-layouts  5.53 us (4%)
    pallas_call x3, Pallas kernels, attention(): pl.pallas_call(functools.partial(attention_kernel, prompts=prompts, per_p...  48.8 us
    ppermute x33, starting transfers between devices, send(): return lax.ppermute(array, 'dp', pairs)  39 us
    ppermute x33, waiting for transfers between devices, send(): return lax.ppermute(array, 'dp', pairs)  33.4 us
    unnamed x28, local copies, waits for them, and re-layouts  3.46 us
  transfers between devices with their start and end apart: 33, of which 15 were waited for; matrix products, arithmetic and copies ran while one was open for 2% of the time, Pallas kernels for 38%

profile of v3, /device:TPU:0, one launch (start us, length us, event | category | flops | bytes accessed | tf_op | source)
XLA Modules:
  0.0 128.9 jit_solution(12107274571474573159)
XLA Ops:
  1.7 3.1 %collective-permute-start.6 = (bf16[128,256]{1,0:T(8,128)(2,1)S(1)}, bf16[128,256]{1,0:T(8,128)(2,1)S(1)}, u32[]{:S(2)}, u32[]{:S(2)}) collective-permute-start(bf16[128,256]{1,0:T(8,128)(2,1)S(1)} %pad_maximum_fusion.5), channel_id=1, source_target_pairs={{0,4},{1,5},{2,6},{3,7},{4,8},{5,9},{6,10},{7,11},{8,12},{9,13},{1... | collective-permute-start | bytes 196616 | tf_op jit(solution)/shard_map/ppermute | solution.py:338
  4.8 2.6 %collective-permute-start.7 = (bf16[128,256]{1,0:T(8,128)(2,1)S(1)}, bf16[128,256]{1,0:T(8,128)(2,1)S(1)}, u32[]{:S(2)}, u32[]{:S(2)}) collective-permute-start(bf16[128,256]{1,0:T(8,128)(2,1)S(1)} %pad_maximum_fusion.5), channel_id=1, source_target_pairs={{0,8},{1,9},{2,10},{3,11},{4,12},{5,13},{6,14},{7,15},{8,0},{9,1},... | collective-permute-start | bytes 196616 | tf_op jit(solution)/shard_map/ppermute | solution.py:338
  9.6 2.2 %collective-permute-done.7 = bf16[128,256]{1,0:T(8,128)(2,1)S(1)} collective-permute-done((bf16[128,256]{1,0:T(8,128)(2,1)S(1)}, bf16[128,256]{1,0:T(8,128)(2,1)S(1)}, u32[]{:S(2)}, u32[]{:S(2)}) %collective-permute-start.7) | collective-permute-done | bytes 65568 | tf_op jit(solution)/shard_map/ppermute | solution.py:338
  12.1 1.6 %collective-permute-start.10 = (bf16[512,256]{1,0:T(8,128)(2,1)S(1)}, bf16[512,256]{1,0:T(8,128)(2,1)S(1)}, u32[]{:S(2)}, u32[]{:S(2)}) collective-permute-start(bf16[512,256]{1,0:T(8,128)(2,1)S(1)} %pad_maximum_fusion.2.rest_0_), channel_id=1, source_target_pairs={{0,2},{1,3},{2,0},{3,1},{4,6},{5,7},{6,4},{7,5},{8,10},{9,11},{10,... | collective-permute-start | bytes 786440 | tf_op jit(solution)/shard_map/ppermute | solution.py:338
  13.7 1.6 %collective-permute-start.3 = (bf16[128,512]{1,0:T(8,128)(2,1)S(1)}, bf16[128,512]{1,0:T(8,128)(2,1)S(1)}, u32[]{:S(2)}, u32[]{:S(2)}) collective-permute-start(bf16[128,512]{1,0:T(8,128)(2,1)S(1)} %pad_maximum_fusion.3), channel_id=1, source_target_pairs={{0,4},{1,5},{2,6},{3,7},{4,8},{5,9},{6,10},{7,11},{8,12},{9,13},{1... | collective-permute-start | bytes 393224 | tf_op jit(solution)/shard_map/ppermute | solution.py:338
  15.3 2.0 %collective-permute-start.4 = (bf16[128,512]{1,0:T(8,128)(2,1)S(1)}, bf16[128,512]{1,0:T(8,128)(2,1)S(1)}, u32[]{:S(2)}, u32[]{:S(2)}) collective-permute-start(bf16[128,512]{1,0:T(8,128)(2,1)S(1)} %pad_maximum_fusion.3), channel_id=1, source_target_pairs={{0,8},{1,9},{2,10},{3,11},{4,12},{5,13},{6,14},{7,15},{8,0},{9,1},... | collective-permute-start | bytes 393224 | tf_op jit(solution)/shard_map/ppermute | solution.py:338
  17.8 4.3 %collective-permute-done.3 = bf16[128,512]{1,0:T(8,128)(2,1)S(1)} collective-permute-done((bf16[128,512]{1,0:T(8,128)(2,1)S(1)}, bf16[128,512]{1,0:T(8,128)(2,1)S(1)}, u32[]{:S(2)}, u32[]{:S(2)}) %collective-permute-start.3) | collective-permute-done | bytes 131104 | tf_op jit(solution)/shard_map/ppermute | solution.py:338
  22.1 3.1 %collective-permute-done.4 = bf16[128,512]{1,0:T(8,128)(2,1)S(1)} collective-permute-done((bf16[128,512]{1,0:T(8,128)(2,1)S(1)}, bf16[128,512]{1,0:T(8,128)(2,1)S(1)}, u32[]{:S(2)}, u32[]{:S(2)}) %collective-permute-start.4) | collective-permute-done | bytes 131104 | tf_op jit(solution)/shard_map/ppermute | solution.py:338
  29.7 12.7 %shard_map.111 = (bf16[256,4096]{1,0:T(8,128)(2,1)}, bf16[256,4096]{1,0:T(8,128)(2,1)}, bf16[256,256]{1,0:T(8,128)(2,1)S(1)}, bf16[8,128,256]{2,1,0:T(8,128)(2,1)S(1)}, bf16[8,128,256]{2,1,0:T(8,128)(2,1)S(1)}) custom-call(s32[16]{0:T(128)S(1)} %copy-done.5, s32[4]{0:T(128)S(1)} %copy-done.6, s32[1]{0:T(128)} %bitcast.place_ref, ...), custom_call_target="tpu_custom_call" | custom-call | flops 4831838208 | bytes 4194304 | tf_op jit(solution)/shard_map/pallas_call | solution.py:270
  43.0 3.2 %collective-permute-start = (bf16[128,256]{1,0:T(8,128)(2,1)S(1)}, bf16[128,256]{1,0:T(8,128)(2,1)S(1)}, u32[]{:S(2)}, u32[]{:S(2)}) collective-permute-start(bf16[128,256]{1,0:T(8,128)(2,1)S(1)} %pad_maximum_fusion.4), channel_id=1, source_target_pairs={{0,4},{1,5},{2,6},{3,7},{4,8},{5,9},{6,10},{7,11},{8,12},{9,13},{1... | collective-permute-start | bytes 196616 | tf_op jit(solution)/shard_map/ppermute | solution.py:338
  49.3 3.1 %collective-permute-done.1 = bf16[128,256]{1,0:T(8,128)(2,1)S(1)} collective-permute-done((bf16[128,256]{1,0:T(8,128)(2,1)S(1)}, bf16[128,256]{1,0:T(8,128)(2,1)S(1)}, u32[]{:S(2)}, u32[]{:S(2)}) %collective-permute-start.1) | collective-permute-done | bytes 65568 | tf_op jit(solution)/shard_map/ppermute | solution.py:338
  55.1 23.2 %shard_map.112 = (bf16[256,4096]{1,0:T(8,128)(2,1)}, bf16[256,4096]{1,0:T(8,128)(2,1)}, bf16[256,512]{1,0:T(8,128)(2,1)S(1)}, bf16[8,128,512]{2,1,0:T(8,128)(2,1)S(1)}, bf16[8,128,512]{2,1,0:T(8,128)(2,1)S(1)}) custom-call(s32[16]{0:T(128)S(1)} %copy-done.5, s32[4]{0:T(128)S(1)} %copy-done.6, ...), custom_call_target="tpu_custom_call", output_to_operand_aliasing={{0}: (13, {}), {1}: (14, {})} | custom-call | flops 9663676416 | bytes 8388608 | tf_op jit(solution)/shard_map/pallas_call | solution.py:270
  78.6 1.6 %collective-permute-start.21 = (bf16[128,256]{1,0:T(8,128)(2,1)S(1)}, bf16[128,256]{1,0:T(8,128)(2,1)S(1)}, u32[]{:S(2)}, u32[]{:S(2)}) collective-permute-start(bf16[128,256]{1,0:T(8,128)(2,1)S(1)} %get-tuple-element.60), channel_id=1, source_target_pairs={{0,4},{1,5},{2,6},{3,7},{4,8},{5,9},{6,10},{7,11},{8,12},{9,13},{1... | collective-permute-start | bytes 196616 | tf_op jit(solution)/shard_map/ppermute | solution.py:338
  80.2 1.6 %collective-permute-start.22 = (bf16[128,256]{1,0:T(8,128)(2,1)S(1)}, bf16[128,256]{1,0:T(8,128)(2,1)S(1)}, u32[]{:S(2)}, u32[]{:S(2)}) collective-permute-start(bf16[128,256]{1,0:T(8,128)(2,1)S(1)} %get-tuple-element.59), channel_id=1, source_target_pairs={{0,8},{1,9},{2,10},{3,11},{4,12},{5,13},{6,14},{7,15},{8,0},{9,1},... | collective-permute-start | bytes 196616 | tf_op jit(solution)/shard_map/ppermute | solution.py:338
  82.7 2.7 %collective-permute-done.21 = bf16[128,256]{1,0:T(8,128)(2,1)S(1)} collective-permute-done((bf16[128,256]{1,0:T(8,128)(2,1)S(1)}, bf16[128,256]{1,0:T(8,128)(2,1)S(1)}, u32[]{:S(2)}, u32[]{:S(2)}) %collective-permute-start.21) | collective-permute-done | bytes 65568 | tf_op jit(solution)/shard_map/ppermute | solution.py:338
  85.4 2.4 %collective-permute-done.22 = bf16[128,256]{1,0:T(8,128)(2,1)S(1)} collective-permute-done((bf16[128,256]{1,0:T(8,128)(2,1)S(1)}, bf16[128,256]{1,0:T(8,128)(2,1)S(1)}, u32[]{:S(2)}, u32[]{:S(2)}) %collective-permute-start.22) | collective-permute-done | bytes 65568 | tf_op jit(solution)/shard_map/ppermute | solution.py:338
  89.4 12.8 %shard_map.113 = (bf16[256,4096]{1,0:T(8,128)(2,1)}, bf16[256,4096]{1,0:T(8,128)(2,1)}, bf16[256,256]{1,0:T(8,128)(2,1)S(1)}, bf16[8,128,256]{2,1,0:T(8,128)(2,1)S(1)}, bf16[8,128,256]{2,1,0:T(8,128)(2,1)S(1)}) custom-call(s32[16]{0:T(128)S(1)} %copy-done.5, s32[4]{0:T(128)S(1)} %copy-done.6, ...), custom_call_target="tpu_custom_call", output_to_operand_aliasing={{0}: (13, {}), {1}: (14, {})} | custom-call | flops 4831838208 | bytes 4194304 | tf_op jit(solution)/shard_map/pallas_call | solution.py:270
  102.3 1.8 %collective-permute-done.28 = bf16[8,128,256]{2,1,0:T(8,128)(2,1)S(1)} collective-permute-done((bf16[8,128,256]{2,1,0:T(8,128)(2,1)S(1)}, bf16[8,128,256]{2,1,0:T(8,128)(2,1)S(1)}, u32[]{:S(2)}, u32[]{:S(2)}) %collective-permute-start.28) | collective-permute-done | bytes 524320 | tf_op jit(solution)/shard_map/ppermute | solution.py:338
  105.6 2.0 %collective-permute-start.25 = (bf16[128,512]{1,0:T(8,128)(2,1)S(1)}, bf16[128,512]{1,0:T(8,128)(2,1)S(1)}, u32[]{:S(2)}, u32[]{:S(2)}) collective-permute-start(bf16[128,512]{1,0:T(8,128)(2,1)S(1)} %get-tuple-element.52), channel_id=1, source_target_pairs={{0,4},{1,5},{2,6},{3,7},{4,8},{5,9},{6,10},{7,11},{8,12},{9,13},{1... | collective-permute-start | bytes 393224 | tf_op jit(solution)/shard_map/ppermute | solution.py:338
  110.0 3.9 %collective-permute-done.25 = bf16[128,512]{1,0:T(8,128)(2,1)S(1)} collective-permute-done((bf16[128,512]{1,0:T(8,128)(2,1)S(1)}, bf16[128,512]{1,0:T(8,128)(2,1)S(1)}, u32[]{:S(2)}, u32[]{:S(2)}) %collective-permute-start.25) | collective-permute-done | bytes 131104 | tf_op jit(solution)/shard_map/ppermute | solution.py:338
  113.9 4.5 %collective-permute-done.26 = bf16[128,512]{1,0:T(8,128)(2,1)S(1)} collective-permute-done((bf16[128,512]{1,0:T(8,128)(2,1)S(1)}, bf16[128,512]{1,0:T(8,128)(2,1)S(1)}, u32[]{:S(2)}, u32[]{:S(2)}) %collective-permute-start.26) | collective-permute-done | bytes 131104 | tf_op jit(solution)/shard_map/ppermute | solution.py:338
  118.6 3.3 %collective-permute-start.30 = (bf16[128,256]{1,0:T(8,128)(2,1)S(1)}, bf16[128,256]{1,0:T(8,128)(2,1)S(1)}, u32[]{:S(2)}, u32[]{:S(2)}) collective-permute-start(bf16[128,256]{1,0:T(8,128)(2,1)S(1)} %get-tuple-element.55), channel_id=1, source_target_pairs={{0,4},{1,5},{2,6},{3,7},{4,8},{5,9},{6,10},{7,11},{8,12},{9,13},{1... | collective-permute-start | bytes 196616 | tf_op jit(solution)/shard_map/ppermute | solution.py:338
  122.7 1.7 %collective-permute-start.32 = (bf16[128,256]{1,0:T(8,128)(2,1)S(1)}, bf16[128,256]{1,0:T(8,128)(2,1)S(1)}, u32[]{:S(2)}, u32[]{:S(2)}) collective-permute-start(bf16[128,256]{1,0:T(8,128)(2,1)S(1)} %get-tuple-element.56), channel_id=1, source_target_pairs={{0,12},{1,13},{2,14},{3,15},{4,0},{5,1},{6,2},{7,3},{8,4},{9,5},{1... | collective-permute-start | bytes 196616 | tf_op jit(solution)/shard_map/ppermute | solution.py:338
  124.8 3.3 %collective-permute-done.31 = bf16[128,256]{1,0:T(8,128)(2,1)S(1)} collective-permute-done((bf16[128,256]{1,0:T(8,128)(2,1)S(1)}, bf16[128,256]{1,0:T(8,128)(2,1)S(1)}, u32[]{:S(2)}, u32[]{:S(2)}) %collective-permute-start.31) | collective-permute-done | bytes 65568 | tf_op jit(solution)/shard_map/ppermute | solution.py:338
  (98 shorter events, 23.4 us)
Async XLA Ops:
  1.7 7.9 %collective-permute-start.6 = (bf16[128,256]{1,0:T(8,128)(2,1)S(1)}, bf16[128,256]{1,0:T(8,128)(2,1)S(1)}, u32[]{:S(2)}, u32[]{:S(2)}) collective-permute-start(bf16[128,256]{1,0:T(8,128)(2,1)S(1)} %pad_maximum_fusion.5), channel_id=1, source_target_pairs={{0,4},{1,5},{2,6},{3,7},{4,8},{5,9},{6,10},{7,11},{8,12},{9,13},{1... | collective-permute-start | bytes 196616 | tf_op jit(solution)/shard_map/ppermute | solution.py:338
  4.8 7.1 %collective-permute-start.7 = (bf16[128,256]{1,0:T(8,128)(2,1)S(1)}, bf16[128,256]{1,0:T(8,128)(2,1)S(1)}, u32[]{:S(2)}, u32[]{:S(2)}) collective-permute-start(bf16[128,256]{1,0:T(8,128)(2,1)S(1)} %pad_maximum_fusion.5), channel_id=1, source_target_pairs={{0,8},{1,9},{2,10},{3,11},{4,12},{5,13},{6,14},{7,15},{8,0},{9,1},... | collective-permute-start | bytes 196616 | tf_op jit(solution)/shard_map/ppermute | solution.py:338
  12.1 13.2 %collective-permute-start.10 = (bf16[512,256]{1,0:T(8,128)(2,1)S(1)}, bf16[512,256]{1,0:T(8,128)(2,1)S(1)}, u32[]{:S(2)}, u32[]{:S(2)}) collective-permute-start(bf16[512,256]{1,0:T(8,128)(2,1)S(1)} %pad_maximum_fusion.2.rest_0_), channel_id=1, source_target_pairs={{0,2},{1,3},{2,0},{3,1},{4,6},{5,7},{6,4},{7,5},{8,10},{9,11},{10,... | collective-permute-start | bytes 786440 | tf_op jit(solution)/shard_map/ppermute | solution.py:338
  13.7 8.4 %collective-permute-start.3 = (bf16[128,512]{1,0:T(8,128)(2,1)S(1)}, bf16[128,512]{1,0:T(8,128)(2,1)S(1)}, u32[]{:S(2)}, u32[]{:S(2)}) collective-permute-start(bf16[128,512]{1,0:T(8,128)(2,1)S(1)} %pad_maximum_fusion.3), channel_id=1, source_target_pairs={{0,4},{1,5},{2,6},{3,7},{4,8},{5,9},{6,10},{7,11},{8,12},{9,13},{1... | collective-permute-start | bytes 393224 | tf_op jit(solution)/shard_map/ppermute | solution.py:338
  15.3 9.9 %collective-permute-start.4 = (bf16[128,512]{1,0:T(8,128)(2,1)S(1)}, bf16[128,512]{1,0:T(8,128)(2,1)S(1)}, u32[]{:S(2)}, u32[]{:S(2)}) collective-permute-start(bf16[128,512]{1,0:T(8,128)(2,1)S(1)} %pad_maximum_fusion.3), channel_id=1, source_target_pairs={{0,8},{1,9},{2,10},{3,11},{4,12},{5,13},{6,14},{7,15},{8,0},{9,1},... | collective-permute-start | bytes 393224 | tf_op jit(solution)/shard_map/ppermute | solution.py:338
  17.3 7.9 %collective-permute-start.5 = (bf16[128,512]{1,0:T(8,128)(2,1)S(1)}, bf16[128,512]{1,0:T(8,128)(2,1)S(1)}, u32[]{:S(2)}, u32[]{:S(2)}) collective-permute-start(bf16[128,512]{1,0:T(8,128)(2,1)S(1)} %pad_maximum_fusion.3), channel_id=1, source_target_pairs={{0,12},{1,13},{2,14},{3,15},{4,0},{5,1},{6,2},{7,3},{8,4},{9,5},{1... | collective-permute-start | bytes 393224 | tf_op jit(solution)/shard_map/ppermute | solution.py:338
  17.8 8.9 %collective-permute-start.9 = (bf16[512,256]{1,0:T(8,128)(2,1)S(1)}, bf16[512,256]{1,0:T(8,128)(2,1)S(1)}, u32[]{:S(2)}, u32[]{:S(2)}) collective-permute-start(bf16[512,256]{1,0:T(8,128)(2,1)S(1)} %pad_maximum_fusion.2.rest_0_), channel_id=1, source_target_pairs={{0,1},{1,0},{2,3},{3,2},{4,5},{5,4},{6,7},{7,6},{8,9},{9,8},{10,11... | collective-permute-start | bytes 786440 | tf_op jit(solution)/shard_map/ppermute | solution.py:338
  25.4 23.2 %collective-permute-start.14 = (bf16[512,512]{1,0:T(8,128)(2,1)S(1)}, bf16[512,512]{1,0:T(8,128)(2,1)S(1)}, u32[]{:S(2)}, u32[]{:S(2)}) collective-permute-start(bf16[512,512]{1,0:T(8,128)(2,1)S(1)} %pad_maximum_fusion.rest_0_), channel_id=1, source_target_pairs={{0,2},{1,3},{2,0},{3,1},{4,6},{5,7},{6,4},{7,5},{8,10},{9,11},{10,... | collective-permute-start | bytes 1572872 | tf_op jit(solution)/shard_map/ppermute | solution.py:338
  42.4 11.4 %collective-permute-start.12 = (bf16[8,128,256]{2,1,0:T(8,128)(2,1)S(1)}, bf16[8,128,256]{2,1,0:T(8,128)(2,1)S(1)}, u32[]{:S(2)}, u32[]{:S(2)}) collective-permute-start(bf16[8,128,256]{2,1,0:T(8,128)(2,1)S(1)} %get-tuple-element.28), channel_id=1, source_target_pairs={{0,1},{1,0},{2,3},{3,2},{4,5},{5,4},{6,7},{7,6},{8,9},{9,8},{10,11... | collective-permute-start | bytes 1572872 | tf_op jit(solution)/shard_map/ppermute | solution.py:338
  43.0 6.3 %collective-permute-start = (bf16[128,256]{1,0:T(8,128)(2,1)S(1)}, bf16[128,256]{1,0:T(8,128)(2,1)S(1)}, u32[]{:S(2)}, u32[]{:S(2)}) collective-permute-start(bf16[128,256]{1,0:T(8,128)(2,1)S(1)} %pad_maximum_fusion.4), channel_id=1, source_target_pairs={{0,4},{1,5},{2,6},{3,7},{4,8},{5,9},{6,10},{7,11},{8,12},{9,13},{1... | collective-permute-start | bytes 196616 | tf_op jit(solution)/shard_map/ppermute | solution.py:338
  46.2 6.2 %collective-permute-start.1 = (bf16[128,256]{1,0:T(8,128)(2,1)S(1)}, bf16[128,256]{1,0:T(8,128)(2,1)S(1)}, u32[]{:S(2)}, u32[]{:S(2)}) collective-permute-start(bf16[128,256]{1,0:T(8,128)(2,1)S(1)} %pad_maximum_fusion.4), channel_id=1, source_target_pairs={{0,8},{1,9},{2,10},{3,11},{4,12},{5,13},{6,14},{7,15},{8,0},{9,1},... | collective-permute-start | bytes 196616 | tf_op jit(solution)/shard_map/ppermute | solution.py:338
  48.6 6.5 %collective-permute-start.13 = (bf16[512,512]{1,0:T(8,128)(2,1)S(1)}, bf16[512,512]{1,0:T(8,128)(2,1)S(1)}, u32[]{:S(2)}, u32[]{:S(2)}) collective-permute-start(bf16[512,512]{1,0:T(8,128)(2,1)S(1)} %pad_maximum_fusion.rest_0_), channel_id=1, source_target_pairs={{0,1},{1,0},{2,3},{3,2},{4,5},{5,4},{6,7},{7,6},{8,9},{9,8},{10,11... | collective-permute-start | bytes 1572872 | tf_op jit(solution)/shard_map/ppermute | solution.py:338
  52.8 29.9 %collective-permute-start.19 = (bf16[512,256]{1,0:T(8,128)(2,1)S(1)}, bf16[512,256]{1,0:T(8,128)(2,1)S(1)}, u32[]{:S(2)}, u32[]{:S(2)}) collective-permute-start(bf16[512,256]{1,0:T(8,128)(2,1)S(1)} %pad_maximum_fusion.1.rest_0_), channel_id=1, source_target_pairs={{0,2},{1,3},{2,0},{3,1},{4,6},{5,7},{6,4},{7,5},{8,10},{9,11},{10,... | collective-permute-start | bytes 786440 | tf_op jit(solution)/shard_map/ppermute | solution.py:338
  54.0 24.4 %collective-permute-start.17 = (bf16[4,128,256]{2,1,0:T(8,128)(2,1)S(1)}, bf16[4,128,256]{2,1,0:T(8,128)(2,1)S(1)}, u32[]{:S(2)}, u32[]{:S(2)}) collective-permute-start(bf16[4,128,256]{2,1,0:T(8,128)(2,1)S(1)} %slice.170), channel_id=1, source_target_pairs={{0,2},{1,3},{2,0},{3,1},{4,6},{5,7},{6,4},{7,5},{8,10},{9,11},{10,... | collective-permute-start | bytes 786440 | tf_op jit(solution)/shard_map/ppermute | solution.py:338
  78.4 9.5 %collective-permute-start.16 = (bf16[8,128,512]{2,1,0:T(8,128)(2,1)S(1)}, bf16[8,128,512]{2,1,0:T(8,128)(2,1)S(1)}, u32[]{:S(2)}, u32[]{:S(2)}) collective-permute-start(bf16[8,128,512]{2,1,0:T(8,128)(2,1)S(1)} %get-tuple-element.35), channel_id=1, source_target_pairs={{0,1},{1,0},{2,3},{3,2},{4,5},{5,4},{6,7},{7,6},{8,9},{9,8},{10,11... | collective-permute-start | bytes 3145736 | tf_op jit(solution)/shard_map/ppermute | solution.py:338
  78.6 6.8 %collective-permute-start.21 = (bf16[128,256]{1,0:T(8,128)(2,1)S(1)}, bf16[128,256]{1,0:T(8,128)(2,1)S(1)}, u32[]{:S(2)}, u32[]{:S(2)}) collective-permute-start(bf16[128,256]{1,0:T(8,128)(2,1)S(1)} %get-tuple-element.60), channel_id=1, source_target_pairs={{0,4},{1,5},{2,6},{3,7},{4,8},{5,9},{6,10},{7,11},{8,12},{9,13},{1... | collective-permute-start | bytes 196616 | tf_op jit(solution)/shard_map/ppermute | solution.py:338
  80.2 7.6 %collective-permute-start.22 = (bf16[128,256]{1,0:T(8,128)(2,1)S(1)}, bf16[128,256]{1,0:T(8,128)(2,1)S(1)}, u32[]{:S(2)}, u32[]{:S(2)}) collective-permute-start(bf16[128,256]{1,0:T(8,128)(2,1)S(1)} %get-tuple-element.59), channel_id=1, source_target_pairs={{0,8},{1,9},{2,10},{3,11},{4,12},{5,13},{6,14},{7,15},{8,0},{9,1},... | collective-permute-start | bytes 196616 | tf_op jit(solution)/shard_map/ppermute | solution.py:338
  82.6 6.7 %collective-permute-start.18 = (bf16[512,256]{1,0:T(8,128)(2,1)S(1)}, bf16[512,256]{1,0:T(8,128)(2,1)S(1)}, u32[]{:S(2)}, u32[]{:S(2)}) collective-permute-start(bf16[512,256]{1,0:T(8,128)(2,1)S(1)} %pad_maximum_fusion.1.rest_0_), channel_id=1, source_target_pairs={{0,1},{1,0},{2,3},{3,2},{4,5},{5,4},{6,7},{7,6},{8,9},{9,8},{10,11... | collective-permute-start | bytes 786440 | tf_op jit(solution)/shard_map/ppermute | solution.py:338
  88.2 17.1 %collective-permute-start.24 = (bf16[4,128,512]{2,1,0:T(8,128)(2,1)S(1)}, bf16[4,128,512]{2,1,0:T(8,128)(2,1)S(1)}, u32[]{:S(2)}, u32[]{:S(2)}) collective-permute-start(bf16[4,128,512]{2,1,0:T(8,128)(2,1)S(1)} %slice.168), channel_id=1, source_target_pairs={{0,2},{1,3},{2,0},{3,1},{4,6},{5,7},{6,4},{7,5},{8,10},{9,11},{10,... | collective-permute-start | bytes 1572872 | tf_op jit(solution)/shard_map/ppermute | solution.py:338
  104.3 14.2 %collective-permute-start.29 = (bf16[4,128,256]{2,1,0:T(8,128)(2,1)S(1)}, bf16[4,128,256]{2,1,0:T(8,128)(2,1)S(1)}, u32[]{:S(2)}, u32[]{:S(2)}) collective-permute-start(bf16[4,128,256]{2,1,0:T(8,128)(2,1)S(1)} %slice.169), channel_id=1, source_target_pairs={{0,2},{1,3},{2,0},{3,1},{4,6},{5,7},{6,4},{7,5},{8,10},{9,11},{10,... | collective-permute-start | bytes 786440 | tf_op jit(solution)/shard_map/ppermute | solution.py:338
  105.6 8.3 %collective-permute-start.25 = (bf16[128,512]{1,0:T(8,128)(2,1)S(1)}, bf16[128,512]{1,0:T(8,128)(2,1)S(1)}, u32[]{:S(2)}, u32[]{:S(2)}) collective-permute-start(bf16[128,512]{1,0:T(8,128)(2,1)S(1)} %get-tuple-element.52), channel_id=1, source_target_pairs={{0,4},{1,5},{2,6},{3,7},{4,8},{5,9},{6,10},{7,11},{8,12},{9,13},{1... | collective-permute-start | bytes 393224 | tf_op jit(solution)/shard_map/ppermute | solution.py:338
  107.5 10.9 %collective-permute-start.26 = (bf16[128,512]{1,0:T(8,128)(2,1)S(1)}, bf16[128,512]{1,0:T(8,128)(2,1)S(1)}, u32[]{:S(2)}, u32[]{:S(2)}) collective-permute-start(bf16[128,512]{1,0:T(8,128)(2,1)S(1)} %get-tuple-element.54), channel_id=1, source_target_pairs={{0,8},{1,9},{2,10},{3,11},{4,12},{5,13},{6,14},{7,15},{8,0},{9,1},... | collective-permute-start | bytes 393224 | tf_op jit(solution)/shard_map/ppermute | solution.py:338
  108.8 9.6 %collective-permute-start.27 = (bf16[128,512]{1,0:T(8,128)(2,1)S(1)}, bf16[128,512]{1,0:T(8,128)(2,1)S(1)}, u32[]{:S(2)}, u32[]{:S(2)}) collective-permute-start(bf16[128,512]{1,0:T(8,128)(2,1)S(1)} %get-tuple-element.53), channel_id=1, source_target_pairs={{0,12},{1,13},{2,14},{3,15},{4,0},{5,1},{6,2},{7,3},{8,4},{9,5},{1... | collective-permute-start | bytes 393224 | tf_op jit(solution)/shard_map/ppermute | solution.py:338
  118.6 6.2 %collective-permute-start.30 = (bf16[128,256]{1,0:T(8,128)(2,1)S(1)}, bf16[128,256]{1,0:T(8,128)(2,1)S(1)}, u32[]{:S(2)}, u32[]{:S(2)}) collective-permute-start(bf16[128,256]{1,0:T(8,128)(2,1)S(1)} %get-tuple-element.55), channel_id=1, source_target_pairs={{0,4},{1,5},{2,6},{3,7},{4,8},{5,9},{6,10},{7,11},{8,12},{9,13},{1... | collective-permute-start | bytes 196616 | tf_op jit(solution)/shard_map/ppermute | solution.py:338
  (18 other events, 194.8 us)

commit v4 on v3

--- a/solution.py
+++ b/solution.py
@@ -17,24 +17,26 @@
 def dot(a, b, contract):
     return lax.dot_general(a, b, (contract, ((), ())), preferred_element_type=jnp.float32)
 
-CHUNKS = (1, 2, 1)
-PAIR = 2
+CHUNKS = (2, 2)
+STEP_HEADS = (4, 2)
 PIECE = 32
 
 
 def attention_kernel(
     owner_ref, tokens_ref, place_ref,
     q_ref, g_ref, leaf_k_ref, leaf_v_ref, leaf_ref, mask_ref, *rest,
-    prompts, per_prefix, block_len, planes, ranks, chained, steps,
+    prompts, per_prefix, block_len, planes, ranks, chained, steps, step_heads,
 ):
     sources = rest[:2 * ranks]
-    (out_ref, dq_ref, dleaf_ref, own_sum_ref, far_sum_ref,
-     kv, kcat, vcat, kcat_t, vcat_t, bias, q_pick, g_pick, q2, g2, scores, dprob, probs_b, dscore,
-     dk_sum, dv_sum, sems) = rest[2 * ranks + 2 * chained:]
+    rest = rest[2 * ranks + 2 * chained:]
+    out_ref, dq_ref, dleaf_ref = rest[:3]
+    totals = rest[3:3 + 2 * ranks]
+    (kv, kcat, vcat, kcat_t, vcat_t, bias, q_pick, g_pick, q2, g2, scores, dprob, probs_b, dscore,
+     dk_sum, dv_sum, sems) = rest[3 + 2 * ranks:]
     step = pl.program_id(0)
-    per_group = GQ // PAIR
+    per_group = GQ // step_heads
     count = q_ref.shape[0]
-    columns = PAIR * count
+    columns = step_heads * count
     span = per_prefix * block_len
     keys = span + count
     half = sources[0].shape[1] // 2
@@ -94,10 +96,10 @@
         pick = (in_first == left).astype(jnp.float32)
         q_pick[...] = pick.astype(jnp.bfloat16)
         g_pick[...] = (pick * mask_col).astype(jnp.bfloat16)
-        for n in range(PAIR):
+        for n in range(step_heads):
             bias[:, n * count:(n + 1) * count] = allowed_bias
-        own_sum_ref[...] = jnp.zeros_like(own_sum_ref)
-        far_sum_ref[...] = jnp.zeros_like(far_sum_ref)
+        for ref in totals:
+            ref[...] = jnp.zeros_like(ref)
         dk_sum[...] = jnp.zeros_like(dk_sum)
         dv_sum[...] = jnp.zeros_like(dv_sum)
         for n in range(2 * per_prefix):
@@ -119,7 +121,12 @@
                 cat[0:span, lanes] = kv[side * span:(side + 1) * span, cols]
                 cat[span:, lanes] = leaf[...]
 
-    def later_products():
+
+    def later_rows():
+        dk_sum[...] += dot(dscore[...], q2[...], ((1,), (0,)))
+        dv_sum[...] += dot(probs_b[...], g2[...], ((1,), (0,)))
+
+    def later_columns():
         token_at = lax.rem(lax.broadcasted_iota(jnp.int32, (HEAD_SIZE, columns), 1), count)
         first_side = token_at < border
         for source, cat_t, factor, target in (
@@ -129,21 +136,26 @@
             mine = jnp.where(first_side, both[:HEAD_SIZE], both[HEAD_SIZE:])
             if factor != 1.0:
                 mine = mine * factor
-            for n in range(PAIR):
+            for n in range(step_heads):
                 lanes = slice(n * HEAD_SIZE, (n + 1) * HEAD_SIZE)
                 target[:, lanes] = mine[:, n * count:(n + 1) * count].T.astype(jnp.bfloat16)
-        dk_sum[...] += dot(dscore[...], q2[...], ((1,), (0,)))
-        dv_sum[...] += dot(probs_b[...], g2[...], ((1,), (0,)))
-
-    def first_products():
-        new_q, new_g = [], []
-        for n in range(PAIR):
-            q = q_ref[:, n * HEAD_SIZE:(n + 1) * HEAD_SIZE]
-            g = g_ref[:, n * HEAD_SIZE:(n + 1) * HEAD_SIZE]
-            new_q.append(jnp.concatenate([q, q], axis=1) * q_pick[...])
-            new_g.append(jnp.concatenate([g, g], axis=1) * g_pick[...])
-        new_q = jnp.concatenate(new_q, axis=0)
-        new_g = jnp.concatenate(new_g, axis=0)
+
+
+    def pick(source, chosen):
+        parts = []
+        for n in range(step_heads):
+            part = source[:, n * HEAD_SIZE:(n + 1) * HEAD_SIZE]
+            parts.append(jnp.concatenate([part, part], axis=1) * chosen[...])
+        return jnp.concatenate(parts, axis=0)
+
+    def fold(value, op):
+        value = value.reshape(PIECE // 8, 8, columns)
+        total = value[0]
+        for n in range(1, PIECE // 8):
+            total = op(total, value[n])
+        return total
+
+    def score(new_q):
         product = dot(kcat[...], new_q, ((1,), (1,)))
         top = None
         for at in range(0, keys, PIECE):
@@ -153,47 +165,52 @@
             scores[at:at + PIECE, :] = piece
             piece = fold(piece, jnp.maximum)
             top = piece if top is None else jnp.maximum(top, piece)
-        dprob[...] = dot(vcat[...], new_g, ((1,), (1,)))
-        return new_q, new_g, top
-
-    def fold(value, op):
-        value = value.reshape(PIECE // 8, 8, columns)
-        total = value[0]
-        for n in range(1, PIECE // 8):
-            total = op(total, value[n])
-        return total
-
-    def softmax(new_q, new_g, top):
-        top = jnp.max(top, axis=0, keepdims=True)
+        return jnp.max(top, axis=0, keepdims=True)
+
+    def sums(top):
         total = jnp.zeros((8, columns), jnp.float32)
         delta = jnp.zeros((8, columns), jnp.float32)
         for at in range(0, keys, PIECE):
             weight = jnp.exp2((scores[at:at + PIECE, :] - top) * (SCALE * LOG2E))
-            scores[at:at + PIECE, :] = weight
             total = total + fold(weight, jnp.add)
             delta = delta + fold(weight * dprob[at:at + PIECE, :], jnp.add)
-        inverse = 1.0 / jnp.sum(total, axis=0, keepdims=True)
-        delta = jnp.sum(delta, axis=0, keepdims=True) * inverse
+        total = jnp.sum(total, axis=0, keepdims=True)
+        return total, jnp.sum(delta, axis=0, keepdims=True) / total
+
+    def finish(top, total, delta):
+        shift = jnp.log2(total)
         for at in range(0, keys, PIECE):
-            probs = scores[at:at + PIECE, :] * inverse
+            power = (scores[at:at + PIECE, :] - top) * (SCALE * LOG2E)
+            probs = jnp.exp2(power - shift)
             probs_b[at:at + PIECE, :] = probs.astype(jnp.bfloat16)
             dscore[at:at + PIECE, :] = (probs * (dprob[at:at + PIECE, :] - delta)).astype(jnp.bfloat16)
+
+    def work(later):
+        new_q = pick(q_ref, q_pick)
+        new_g = pick(g_ref, g_pick)
+        top = score(new_q)
+        if later:
+            later_rows()
+        dprob[...] = dot(vcat[...], new_g, ((1,), (1,)))
+        total, delta = sums(top)
+        if later:
+            later_columns()
+        finish(top, total, delta)
         q2[...] = new_q
         g2[...] = new_g
 
     @pl.when(step == 0)
     def _():
-        softmax(*first_products())
+        work(False)
 
     @pl.when((step > 0) & (step < steps))
     def _():
-        new = first_products()
-        later_products()
-        softmax(*new)
+        work(True)
 
     @pl.when(step == steps)
     def _():
-        later_products()
+        later_rows()
+        later_columns()
 
     @pl.when(new_group & (step > 0))
     def _():
@@ -209,15 +226,11 @@
                     value = total_ref[j * block_len:(j + 1) * block_len, lanes] * factor
                     value = value.astype(jnp.bfloat16)
                     same_core, row, ahead = block_place(side, j)
-                    slot = row * planes + ahead
-
-                    @pl.when(same_core)
-                    def _():
-                        own_sum_ref[slot, :, cols] += value
-
-                    @pl.when(jnp.logical_not(same_core))
-                    def _():
-                        far_sum_ref[slot, :, cols] += value
+                    for at, ref in enumerate(totals):
+                        @pl.when((same_core == (at % 2 == 0)) & (row == at // 2))
+                        def _():
+                            ref[ahead, :, cols] += value
+
         dk_sum[...] = jnp.zeros_like(dk_sum)
         dv_sum[...] = jnp.zeros_like(dv_sum)
 
@@ -231,7 +244,6 @@
     chunk, owner, tokens, place, q, g, leaf_kv, leaf, mask, sources, earlier, planes, ranks
 ):
     count = q.shape[0]
-    slots = planes * ranks
     block_len = sources[0].shape[0] // planes
     prompts = tokens.shape[0]
     per_prefix = owner.shape[0] // prompts
@@ -239,19 +251,20 @@
     keys = span + count
     width = sources[0].shape[1]
     groups = CHUNKS[chunk]
+    step_heads = STEP_HEADS[chunk]
     skipped = sum(CHUNKS[:chunk])
     heads = groups * GQ
-    steps = heads // PAIR
-    per_group = GQ // PAIR
+    steps = heads // step_heads
+    per_group = GQ // step_heads
     skipped_steps = skipped * per_group
     bf16, f32 = jnp.bfloat16, jnp.float32
 
     def now(i):
         return jnp.minimum(i, steps - 1)
 
-    ahead = pl.BlockSpec((count, PAIR * HEAD_SIZE), lambda i, *_: (0, skipped_steps + now(i)))
+    ahead = pl.BlockSpec((count, step_heads * HEAD_SIZE), lambda i, *_: (0, skipped_steps + now(i)))
     behind = pl.BlockSpec(
-        (count, PAIR * HEAD_SIZE), lambda i, *_: (0, skipped_steps + jnp.maximum(i - 1, 0))
+        (count, step_heads * HEAD_SIZE), lambda i, *_: (0, skipped_steps + jnp.maximum(i - 1, 0))
     )
     leaf_k = pl.BlockSpec(
         (count, HEAD_SIZE), lambda i, *_: (0, skipped + now(i) // per_group)
@@ -265,12 +278,12 @@
     def full(shape):
         return pl.BlockSpec(shape, lambda h, *_: (0,) * len(shape))
 
-    sum_shape = (slots, block_len, width)
+    sum_shape = (planes, block_len, width)
     chained = len(earlier) > 0
     return pl.pallas_call(
         functools.partial(
             attention_kernel, prompts=prompts, per_prefix=per_prefix, block_len=block_len,
-            planes=planes, ranks=ranks, chained=chained, steps=steps,
+            planes=planes, ranks=ranks, chained=chained, steps=steps, step_heads=step_heads,
         ),
         grid_spec=pltpu.PrefetchScalarGridSpec(
             num_scalar_prefetch=3,
@@ -278,22 +291,22 @@
             in_specs=[
                 ahead, ahead, leaf_k, leaf_v, full(leaf.shape), full(mask.shape),
             ] + [anywhere] * (2 * ranks + len(earlier)),
-            out_specs=[behind, behind, full((count, width)), full(sum_shape), full(sum_shape)],
+            out_specs=[behind, behind, full((count, width))] + [full(sum_shape)] * (2 * ranks),
             scratch_shapes=[
                 pltpu.VMEM((2 * span, width), bf16),
                 pltpu.VMEM((keys, 2 * HEAD_SIZE), bf16),
                 pltpu.VMEM((keys, 2 * HEAD_SIZE), bf16),
                 pltpu.VMEM((2 * HEAD_SIZE, keys), bf16),
                 pltpu.VMEM((2 * HEAD_SIZE, keys), bf16),
-                pltpu.VMEM((count, PAIR * count), f32),
+                pltpu.VMEM((count, step_heads * count), f32),
                 pltpu.VMEM((count, 2 * HEAD_SIZE), bf16),
                 pltpu.VMEM((count, 2 * HEAD_SIZE), bf16),
-                pltpu.VMEM((PAIR * count, 2 * HEAD_SIZE), bf16),
-                pltpu.VMEM((PAIR * count, 2 * HEAD_SIZE), bf16),
-                pltpu.VMEM((keys, PAIR * count), f32),
-                pltpu.VMEM((keys, PAIR * count), f32),
-                pltpu.VMEM((keys, PAIR * count), bf16),
-                pltpu.VMEM((keys, PAIR * count), bf16),
+                pltpu.VMEM((step_heads * count, 2 * HEAD_SIZE), bf16),
+                pltpu.VMEM((step_heads * count, 2 * HEAD_SIZE), bf16),
+                pltpu.VMEM((keys, step_heads * count), f32),
+                pltpu.VMEM((keys, step_heads * count), f32),
+                pltpu.VMEM((keys, step_heads * count), bf16),
+                pltpu.VMEM((keys, step_heads * count), bf16),
                 pltpu.VMEM((keys, 2 * HEAD_SIZE), f32),
                 pltpu.VMEM((keys, 2 * HEAD_SIZE), f32),
                 pltpu.SemaphoreType.DMA((2 * per_prefix,)),
@@ -303,12 +316,10 @@
             jax.ShapeDtypeStruct(q.shape, bf16),
             jax.ShapeDtypeStruct(q.shape, bf16),
             jax.ShapeDtypeStruct((count, width), bf16),
-            jax.ShapeDtypeStruct(sum_shape, bf16),
-            jax.ShapeDtypeStruct(sum_shape, bf16),
-        ],
+        ] + [jax.ShapeDtypeStruct(sum_shape, bf16)] * (2 * ranks),
         input_output_aliases={9 + 2 * ranks: 0, 10 + 2 * ranks: 1} if chained else {},
         compiler_params=pltpu.CompilerParams(
-            vmem_limit_bytes=32 * 2**20, dimension_semantics=("arbitrary",)
+            vmem_limit_bytes=54 * 2**20, dimension_semantics=("arbitrary",)
         ),
         cost_estimate=pl.CostEstimate(
             flops=heads * 6 * 2 * keys * 256 * 256, bytes_accessed=groups * 4 * 2**20,
@@ -350,50 +361,42 @@
         )
         return jnp.concatenate([mine] + [send(mine, k, 0, 0) for k in range(1, planes)], axis=0)
 
-    def reduce_cores(own, far):
-        return own.astype(f32) + send(far, 0, 0, 1).astype(f32)
-
-    def reduce_ranks(total, away):
-        return total[:planes] + send(away, 0, 1, 0).astype(f32) if ranks == 2 else total
-
-    def reduce_planes(total, away):
+    def add(own, received):
+        return own.astype(f32) + received.astype(f32)
+
+    def reduce_ranks(totals, away):
+        total = add(totals[0], send(totals[1], 0, 0, 1))
+        return add(total, send(away, 0, 1, 0)) if ranks == 2 else total
+
+    def reduce_planes(total):
         mine = total[0]
         for k in range(1, planes):
-            mine = mine + send(away[k - 1], k, 0, 0).astype(f32)
+            mine = add(mine, send(total[k].astype(jnp.bfloat16), k, 0, 0))
         return mine.astype(jnp.bfloat16)
 
     chunks = len(CHUNKS)
     near = [by_planes(chunk) for chunk in range(chunks)]
+    near_far = [send(n, 0, 0, 1) for n in near]
     other = [send(n, 0, 1, 0) for n in near] if ranks == 2 else []
     d_leaf, d_prefix, earlier = [], [], ()
-    by_cores, by_ranks = [], []
+    parts = []
     for chunk in range(chunks):
-        first = [place] + near[chunk + 1:chunk + 2]
-        if chunk >= 1:
-            first.append(by_cores[chunk - 1][1])
-        if chunk >= 2:
-            total, away = by_cores[chunk - 2]
-            total = reduce_ranks(total, away)
-            away = [total[k].astype(jnp.bfloat16) for k in range(1, planes)]
-            by_ranks.append((total, away))
-            first.extend(away)
-        sources = [near[chunk], send(near[chunk], 0, 0, 1)]
+        first = [place] + near[chunk + 1:chunk + 2] + near_far[chunk + 1:chunk + 2]
+        if chunk and ranks == 2:
+            first.append(parts[-1][1])
+        sources = [near[chunk], near_far[chunk]]
         if ranks == 2:
             row = tie(other[chunk], d_leaf[-1] if chunk else near[1])
             sources += [row, send(row, 0, 0, 1)]
-        attended, d_query, leaf_part, own_sum, far_sum = attention(
+        attended, d_query, leaf_part, *totals = attention(
             chunk, block_owner, subtree_tokens, tie(*first), query, d_out, leaf_key_value,
             leaf_id, mask, sources, earlier, planes, ranks,
         )
         earlier = (attended, d_query)
         d_leaf.append(leaf_part)
-        total = reduce_cores(own_sum, far_sum)
-        by_cores.append((total, total[planes:].astype(jnp.bfloat16)))
-    for chunk in range(chunks):
-        if chunk >= len(by_ranks):
-            total = reduce_ranks(*by_cores[chunk])
-            by_ranks.append((total, [total[k].astype(jnp.bfloat16) for k in range(1, planes)]))
-        d_prefix.append(reduce_planes(*by_ranks[chunk]))
+        away = add(totals[2], send(totals[3], 0, 0, 1)).astype(jnp.bfloat16) if ranks == 2 else None
+        parts.append((totals, away))
+    d_prefix = [reduce_planes(reduce_ranks(*part)) for part in parts]
 
     def join(parts):
         halves = [jnp.split(p, 2, axis=1) for p in parts]

time: 129 us -> 117 us (0.907)
  starting transfers between devices: 39 us -> 28.5 us
  Pallas kernels: 48.8 us -> 44.6 us
  other arithmetic: 1.17 us -> 3.61 us
  waiting for transfers between devices: 33.4 us -> 35.5 us
  local copies, waits for them, and re-layouts: 5.53 us -> 3.66 us
    ppermute x33 -> x24, starting transfers between devices: 39 us -> 28.5 us  [send(): return lax.ppermute(array, 'dp', pairs)]
    pallas_call x3 -> x2, Pallas kernels: 48.8 us -> 44.6 us  [attention(): pl.pallas_call(functools.partial(attention_kernel, prompts=prompts, per_p...]
    ppermute x33 -> x24, waiting for transfers between devices: 33.4 us -> 35.5 us  [send(): return lax.ppermute(array, 'dp', pairs)]
    unnamed x28 -> x24, local copies, waits for them, and re-layouts: 3.46 us -> 1.63 us
    concatenate x0 -> x2, other arithmetic: none -> 1.59 us  [join(): jnp.concatenate([h[0] for h in halves] + [h[1] for h in halves], axis=1)]
    convert_element_type x0 -> x2, other arithmetic: none -> 1.31 us  [shards(): add(totals[2], send(totals[3], 0, 0, 1)).astype(jnp.bfloat16)]
  transfers between devices with their start and end apart: 33 -> 24, of which waited for: 15 -> 12; matrix products, arithmetic and copies ran while one was open for 2% -> 3% of each run, Pallas kernels for 38% -> 38%
where the time goes in v4:
time: 117 us
  Pallas kernels  44.6 us (38%)
  waiting for transfers between devices  35.5 us (30%)
  starting transfers between devices  28.5 us (24%)
  local copies, waits for them, and re-layouts  3.66 us (3%)
  other arithmetic  3.61 us (3%)
    pallas_call x2, Pallas kernels, attention(): pl.pallas_call(functools.partial(attention_kernel, prompts=prompts, per_p...  44.6 us
    ppermute x24, waiting for transfers between devices, send(): return lax.ppermute(array, 'dp', pairs)  35.5 us
    ppermute x24, starting transfers between devices, send(): return lax.ppermute(array, 'dp', pairs)  28.5 us
  transfers between devices with their start and end apart: 24, of which 12 were waited for; matrix products, arithmetic and copies ran while one was open for 3% of the time, Pallas kernels for 38%

profile of v4, /device:TPU:0, one launch (start us, length us, event | category | flops | bytes accessed | tf_op | source)
XLA Modules:
  0.0 116.7 jit_solution(9848870112270969537)
XLA Ops:
  1.6 3.1 %collective-permute-start.4 = (bf16[128,512]{1,0:T(8,128)(2,1)S(1)}, bf16[128,512]{1,0:T(8,128)(2,1)S(1)}, u32[]{:S(2)}, u32[]{:S(2)}) collective-permute-start(bf16[128,512]{1,0:T(8,128)(2,1)S(1)} %pad_maximum_fusion.5), channel_id=1, source_target_pairs={{0,4},{1,5},{2,6},{3,7},{4,8},{5,9},{6,10},{7,11},{8,12},{9,13},{1... | collective-permute-start | bytes 393224 | tf_op jit(solution)/shard_map/ppermute | solution.py:349
  4.7 2.6 %collective-permute-start.5 = (bf16[128,512]{1,0:T(8,128)(2,1)S(1)}, bf16[128,512]{1,0:T(8,128)(2,1)S(1)}, u32[]{:S(2)}, u32[]{:S(2)}) collective-permute-start(bf16[128,512]{1,0:T(8,128)(2,1)S(1)} %pad_maximum_fusion.5), channel_id=1, source_target_pairs={{0,8},{1,9},{2,10},{3,11},{4,12},{5,13},{6,14},{7,15},{8,0},{9,1},... | collective-permute-start | bytes 393224 | tf_op jit(solution)/shard_map/ppermute | solution.py:349
  7.3 1.3 %collective-permute-start.6 = (bf16[128,512]{1,0:T(8,128)(2,1)S(1)}, bf16[128,512]{1,0:T(8,128)(2,1)S(1)}, u32[]{:S(2)}, u32[]{:S(2)}) collective-permute-start(bf16[128,512]{1,0:T(8,128)(2,1)S(1)} %pad_maximum_fusion.5), channel_id=1, source_target_pairs={{0,12},{1,13},{2,14},{3,15},{4,0},{5,1},{6,2},{7,3},{8,4},{9,5},{1... | collective-permute-start | bytes 393224 | tf_op jit(solution)/shard_map/ppermute | solution.py:349
  8.6 2.5 %collective-permute-done.4 = bf16[128,512]{1,0:T(8,128)(2,1)S(1)} collective-permute-done((bf16[128,512]{1,0:T(8,128)(2,1)S(1)}, bf16[128,512]{1,0:T(8,128)(2,1)S(1)}, u32[]{:S(2)}, u32[]{:S(2)}) %collective-permute-start.4) | collective-permute-done | bytes 131104 | tf_op jit(solution)/shard_map/ppermute | solution.py:349
  11.1 4.8 %collective-permute-done.5 = bf16[128,512]{1,0:T(8,128)(2,1)S(1)} collective-permute-done((bf16[128,512]{1,0:T(8,128)(2,1)S(1)}, bf16[128,512]{1,0:T(8,128)(2,1)S(1)}, u32[]{:S(2)}, u32[]{:S(2)}) %collective-permute-start.5) | collective-permute-done | bytes 131104 | tf_op jit(solution)/shard_map/ppermute | solution.py:349
  16.0 1.6 %collective-permute-start.8 = (bf16[512,512]{1,0:T(8,128)(2,1)S(1)}, bf16[512,512]{1,0:T(8,128)(2,1)S(1)}, u32[]{:S(2)}, u32[]{:S(2)}) collective-permute-start(bf16[512,512]{1,0:T(8,128)(2,1)S(1)} %pad_maximum_fusion.1.rest_0_), channel_id=1, source_target_pairs={{0,2},{1,3},{2,0},{3,1},{4,6},{5,7},{6,4},{7,5},{8,10},{9,11},{10,... | collective-permute-start | bytes 1572872 | tf_op jit(solution)/shard_map/ppermute | solution.py:349
  17.6 3.3 %collective-permute-start = (bf16[128,512]{1,0:T(8,128)(2,1)S(1)}, bf16[128,512]{1,0:T(8,128)(2,1)S(1)}, u32[]{:S(2)}, u32[]{:S(2)}) collective-permute-start(bf16[128,512]{1,0:T(8,128)(2,1)S(1)} %pad_maximum_fusion.4), channel_id=1, source_target_pairs={{0,4},{1,5},{2,6},{3,7},{4,8},{5,9},{6,10},{7,11},{8,12},{9,13},{1... | collective-permute-start | bytes 393224 | tf_op jit(solution)/shard_map/ppermute | solution.py:349
  20.9 1.6 %collective-permute-start.1 = (bf16[128,512]{1,0:T(8,128)(2,1)S(1)}, bf16[128,512]{1,0:T(8,128)(2,1)S(1)}, u32[]{:S(2)}, u32[]{:S(2)}) collective-permute-start(bf16[128,512]{1,0:T(8,128)(2,1)S(1)} %pad_maximum_fusion.4), channel_id=1, source_target_pairs={{0,8},{1,9},{2,10},{3,11},{4,12},{5,13},{6,14},{7,15},{8,0},{9,1},... | collective-permute-start | bytes 393224 | tf_op jit(solution)/shard_map/ppermute | solution.py:349
  23.3 2.9 %collective-permute-done = bf16[128,512]{1,0:T(8,128)(2,1)S(1)} collective-permute-done((bf16[128,512]{1,0:T(8,128)(2,1)S(1)}, bf16[128,512]{1,0:T(8,128)(2,1)S(1)}, u32[]{:S(2)}, u32[]{:S(2)}) %collective-permute-start) | collective-permute-done | bytes 131104 | tf_op jit(solution)/shard_map/ppermute | solution.py:349
  26.3 4.3 %collective-permute-done.1 = bf16[128,512]{1,0:T(8,128)(2,1)S(1)} collective-permute-done((bf16[128,512]{1,0:T(8,128)(2,1)S(1)}, bf16[128,512]{1,0:T(8,128)(2,1)S(1)}, u32[]{:S(2)}, u32[]{:S(2)}) %collective-permute-start.1) | collective-permute-done | bytes 131104 | tf_op jit(solution)/shard_map/ppermute | solution.py:349
  34.2 22.0 %shard_map.111 = (bf16[256,4096]{1,0:T(8,128)(2,1)}, bf16[256,4096]{1,0:T(8,128)(2,1)}, bf16[256,512]{1,0:T(8,128)(2,1)}, bf16[4,128,512]{2,1,0:T(8,128)(2,1)}, ...) custom-call(s32[16]{0:T(128)} %owner_ref.3, s32[4]{0:T(128)} %tokens_ref.3, ...), custom_call_target="tpu_custom_call" | custom-call | flops 9663676416 | bytes 8388608 | tf_op jit(solution)/shard_map/pallas_call | solution.py:283
  56.9 1.0 fusion.10
  58.4 1.2 %add_convert_fusion.1 = bf16[4,128,512]{2,1,0:T(8,128)(2,1)S(1)} fusion(bf16[4,128,512]{2,1,0:T(8,128)(2,1)S(1)} %collective-permute-done.10, bf16[4,128,512]{2,1,0:T(8,128)(2,1)} %get-tuple-element.24), kind=kLoop, calls=%fused_computation.3 | loop fusion | flops 1048576 | bytes 1572864 | tf_op jit(solution)/shard_map/convert_element_type | solution.py:397
  60.9 22.6 %shard_map.112 = (bf16[256,4096]{1,0:T(8,128)(2,1)}, bf16[256,4096]{1,0:T(8,128)(2,1)}, bf16[256,512]{1,0:T(8,128)(2,1)}, bf16[4,128,512]{2,1,0:T(8,128)(2,1)}, ...) custom-call(s32[16]{0:T(128)} %owner_ref.3, ...), custom_call_target="tpu_custom_call", output_to_operand_aliasing={{0}: (13, {}), {1}: (14, {})} | custom-call | flops 9663676416 | bytes 8388608 | tf_op jit(solution)/shard_map/pallas_call | solution.py:283
  84.5 3.4 %collective-permute-start.15 = (bf16[128,512]{1,0:T(8,128)(2,1)S(1)}, bf16[128,512]{1,0:T(8,128)(2,1)S(1)}, u32[]{:S(2)}, u32[]{:S(2)}) collective-permute-start(bf16[128,512]{1,0:T(8,128)(2,1)S(1)} %get-tuple-element.44), channel_id=1, source_target_pairs={{0,4},{1,5},{2,6},{3,7},{4,8},{5,9},{6,10},{7,11},{8,12},{9,13},{1... | collective-permute-start | bytes 393224 | tf_op jit(solution)/shard_map/ppermute | solution.py:349
  87.9 1.6 %collective-permute-start.16 = (bf16[128,512]{1,0:T(8,128)(2,1)S(1)}, bf16[128,512]{1,0:T(8,128)(2,1)S(1)}, u32[]{:S(2)}, u32[]{:S(2)}) collective-permute-start(bf16[128,512]{1,0:T(8,128)(2,1)S(1)} %get-tuple-element.46), channel_id=1, source_target_pairs={{0,8},{1,9},{2,10},{3,11},{4,12},{5,13},{6,14},{7,15},{8,0},{9,1},... | collective-permute-start | bytes 393224 | tf_op jit(solution)/shard_map/ppermute | solution.py:349
  90.5 1.5 %collective-permute-start.20 = (bf16[4,128,512]{2,1,0:T(8,128)(2,1)S(1)}, bf16[4,128,512]{2,1,0:T(8,128)(2,1)S(1)}, u32[]{:S(2)}, u32[]{:S(2)}) collective-permute-start(bf16[4,128,512]{2,1,0:T(8,128)(2,1)S(1)} %add_convert_fusion), channel_id=1, source_target_pairs={{0,2},{1,3},{2,0},{3,1},{4,6},{5,7},{6,4},{7,5},{8,10},{9,11},{10,... | collective-permute-start | bytes 1572872 | tf_op jit(solution)/shard_map/ppermute | solution.py:349
  93.4 5.1 %collective-permute-done.16 = bf16[128,512]{1,0:T(8,128)(2,1)S(1)} collective-permute-done((bf16[128,512]{1,0:T(8,128)(2,1)S(1)}, bf16[128,512]{1,0:T(8,128)(2,1)S(1)}, u32[]{:S(2)}, u32[]{:S(2)}) %collective-permute-start.16) | collective-permute-done | bytes 131104 | tf_op jit(solution)/shard_map/ppermute | solution.py:349
  98.5 5.4 %collective-permute-done.20 = bf16[4,128,512]{2,1,0:T(8,128)(2,1)S(1)} collective-permute-done((bf16[4,128,512]{2,1,0:T(8,128)(2,1)S(1)}, bf16[4,128,512]{2,1,0:T(8,128)(2,1)S(1)}, u32[]{:S(2)}, u32[]{:S(2)}) %collective-permute-start.20) | collective-permute-done | bytes 524320 | tf_op jit(solution)/shard_map/ppermute | solution.py:349
  104.2 1.0 collective-permute-start.21
  105.2 1.3 %collective-permute-start.22 = (bf16[128,512]{1,0:T(8,128)(2,1)S(1)}, bf16[128,512]{1,0:T(8,128)(2,1)S(1)}, u32[]{:S(2)}, u32[]{:S(2)}) collective-permute-start(bf16[128,512]{1,0:T(8,128)(2,1)S(1)} %get-tuple-element.49), channel_id=1, source_target_pairs={{0,8},{1,9},{2,10},{3,11},{4,12},{5,13},{6,14},{7,15},{8,0},{9,1},... | collective-permute-start | bytes 393224 | tf_op jit(solution)/shard_map/ppermute | solution.py:349
  106.5 1.6 %collective-permute-start.23 = (bf16[128,512]{1,0:T(8,128)(2,1)S(1)}, bf16[128,512]{1,0:T(8,128)(2,1)S(1)}, u32[]{:S(2)}, u32[]{:S(2)}) collective-permute-start(bf16[128,512]{1,0:T(8,128)(2,1)S(1)} %get-tuple-element.48), channel_id=1, source_target_pairs={{0,12},{1,13},{2,14},{3,15},{4,0},{5,1},{6,2},{7,3},{8,4},{9,5},{1... | collective-permute-start | bytes 393224 | tf_op jit(solution)/shard_map/ppermute | solution.py:349
  108.1 4.4 %collective-permute-done.21 = bf16[128,512]{1,0:T(8,128)(2,1)S(1)} collective-permute-done((bf16[128,512]{1,0:T(8,128)(2,1)S(1)}, bf16[128,512]{1,0:T(8,128)(2,1)S(1)}, u32[]{:S(2)}, u32[]{:S(2)}) %collective-permute-start.21) | collective-permute-done | bytes 131104 | tf_op jit(solution)/shard_map/ppermute | solution.py:349
  112.5 3.3 %collective-permute-done.22 = bf16[128,512]{1,0:T(8,128)(2,1)S(1)} collective-permute-done((bf16[128,512]{1,0:T(8,128)(2,1)S(1)}, bf16[128,512]{1,0:T(8,128)(2,1)S(1)}, u32[]{:S(2)}, u32[]{:S(2)}) %collective-permute-start.22) | collective-permute-done | bytes 131104 | tf_op jit(solution)/shard_map/ppermute | solution.py:349
  (69 shorter events, 12.3 us)
Async XLA Ops:
  1.6 9.5 %collective-permute-start.4 = (bf16[128,512]{1,0:T(8,128)(2,1)S(1)}, bf16[128,512]{1,0:T(8,128)(2,1)S(1)}, u32[]{:S(2)}, u32[]{:S(2)}) collective-permute-start(bf16[128,512]{1,0:T(8,128)(2,1)S(1)} %pad_maximum_fusion.5), channel_id=1, source_target_pairs={{0,4},{1,5},{2,6},{3,7},{4,8},{5,9},{6,10},{7,11},{8,12},{9,13},{1... | collective-permute-start | bytes 393224 | tf_op jit(solution)/shard_map/ppermute | solution.py:349
  4.7 11.2 %collective-permute-start.5 = (bf16[128,512]{1,0:T(8,128)(2,1)S(1)}, bf16[128,512]{1,0:T(8,128)(2,1)S(1)}, u32[]{:S(2)}, u32[]{:S(2)}) collective-permute-start(bf16[128,512]{1,0:T(8,128)(2,1)S(1)} %pad_maximum_fusion.5), channel_id=1, source_target_pairs={{0,8},{1,9},{2,10},{3,11},{4,12},{5,13},{6,14},{7,15},{8,0},{9,1},... | collective-permute-start | bytes 393224 | tf_op jit(solution)/shard_map/ppermute | solution.py:349
  7.3 8.6 %collective-permute-start.6 = (bf16[128,512]{1,0:T(8,128)(2,1)S(1)}, bf16[128,512]{1,0:T(8,128)(2,1)S(1)}, u32[]{:S(2)}, u32[]{:S(2)}) collective-permute-start(bf16[128,512]{1,0:T(8,128)(2,1)S(1)} %pad_maximum_fusion.5), channel_id=1, source_target_pairs={{0,12},{1,13},{2,14},{3,15},{4,0},{5,1},{6,2},{7,3},{8,4},{9,5},{1... | collective-permute-start | bytes 393224 | tf_op jit(solution)/shard_map/ppermute | solution.py:349
  16.0 14.8 %collective-permute-start.8 = (bf16[512,512]{1,0:T(8,128)(2,1)S(1)}, bf16[512,512]{1,0:T(8,128)(2,1)S(1)}, u32[]{:S(2)}, u32[]{:S(2)}) collective-permute-start(bf16[512,512]{1,0:T(8,128)(2,1)S(1)} %pad_maximum_fusion.1.rest_0_), channel_id=1, source_target_pairs={{0,2},{1,3},{2,0},{3,1},{4,6},{5,7},{6,4},{7,5},{8,10},{9,11},{10,... | collective-permute-start | bytes 1572872 | tf_op jit(solution)/shard_map/ppermute | solution.py:349
  17.6 8.7 %collective-permute-start = (bf16[128,512]{1,0:T(8,128)(2,1)S(1)}, bf16[128,512]{1,0:T(8,128)(2,1)S(1)}, u32[]{:S(2)}, u32[]{:S(2)}) collective-permute-start(bf16[128,512]{1,0:T(8,128)(2,1)S(1)} %pad_maximum_fusion.4), channel_id=1, source_target_pairs={{0,4},{1,5},{2,6},{3,7},{4,8},{5,9},{6,10},{7,11},{8,12},{9,13},{1... | collective-permute-start | bytes 393224 | tf_op jit(solution)/shard_map/ppermute | solution.py:349
  20.9 9.7 %collective-permute-start.1 = (bf16[128,512]{1,0:T(8,128)(2,1)S(1)}, bf16[128,512]{1,0:T(8,128)(2,1)S(1)}, u32[]{:S(2)}, u32[]{:S(2)}) collective-permute-start(bf16[128,512]{1,0:T(8,128)(2,1)S(1)} %pad_maximum_fusion.4), channel_id=1, source_target_pairs={{0,8},{1,9},{2,10},{3,11},{4,12},{5,13},{6,14},{7,15},{8,0},{9,1},... | collective-permute-start | bytes 393224 | tf_op jit(solution)/shard_map/ppermute | solution.py:349
  22.5 8.1 %collective-permute-start.2 = (bf16[128,512]{1,0:T(8,128)(2,1)S(1)}, bf16[128,512]{1,0:T(8,128)(2,1)S(1)}, u32[]{:S(2)}, u32[]{:S(2)}) collective-permute-start(bf16[128,512]{1,0:T(8,128)(2,1)S(1)} %pad_maximum_fusion.4), channel_id=1, source_target_pairs={{0,12},{1,13},{2,14},{3,15},{4,0},{5,1},{6,2},{7,3},{8,4},{9,5},{1... | collective-permute-start | bytes 393224 | tf_op jit(solution)/shard_map/ppermute | solution.py:349
  23.3 9.3 %collective-permute-start.7 = (bf16[512,512]{1,0:T(8,128)(2,1)S(1)}, bf16[512,512]{1,0:T(8,128)(2,1)S(1)}, u32[]{:S(2)}, u32[]{:S(2)}) collective-permute-start(bf16[512,512]{1,0:T(8,128)(2,1)S(1)} %pad_maximum_fusion.1.rest_0_), channel_id=1, source_target_pairs={{0,1},{1,0},{2,3},{3,2},{4,5},{5,4},{6,7},{7,6},{8,9},{9,8},{10,11... | collective-permute-start | bytes 1572872 | tf_op jit(solution)/shard_map/ppermute | solution.py:349
  30.7 2.0 %collective-permute-start.3 = (bf16[512,512]{1,0:T(8,128)(2,1)S(1)}, bf16[512,512]{1,0:T(8,128)(2,1)S(1)}, u32[]{:S(2)}, u32[]{:S(2)}) collective-permute-start(bf16[512,512]{1,0:T(8,128)(2,1)S(1)} %pad_maximum_fusion.rest_0_), channel_id=1, source_target_pairs={{0,1},{1,0},{2,3},{3,2},{4,5},{5,4},{6,7},{7,6},{8,9},{9,8},{10,11... | collective-permute-start | bytes 1572872 | tf_op jit(solution)/shard_map/ppermute | solution.py:349
  30.8 2.6 %collective-permute-start.9 = (bf16[512,512]{1,0:T(8,128)(2,1)S(1)}, bf16[512,512]{1,0:T(8,128)(2,1)S(1)}, u32[]{:S(2)}, u32[]{:S(2)}) collective-permute-start(bf16[512,512]{1,0:T(8,128)(2,1)S(1)} %collective-permute-done.8.rest_2_), channel_id=1, source_target_pairs={{0,1},{1,0},{2,3},{3,2},{4,5},{5,4},{6,7},{7,6},{8,9},{9,8},{10,11... | collective-permute-start | bytes 1572872 | tf_op jit(solution)/shard_map/ppermute | solution.py:349
  31.3 25.1 %collective-permute-start.11 = (bf16[512,512]{1,0:T(8,128)(2,1)S(1)}, bf16[512,512]{1,0:T(8,128)(2,1)S(1)}, u32[]{:S(2)}, u32[]{:S(2)}) collective-permute-start(bf16[512,512]{1,0:T(8,128)(2,1)S(1)} %pad_maximum_fusion.rest_0_), channel_id=1, source_target_pairs={{0,2},{1,3},{2,0},{3,1},{4,6},{5,7},{6,4},{7,5},{8,10},{9,11},{10,... | collective-permute-start | bytes 1572872 | tf_op jit(solution)/shard_map/ppermute | solution.py:349
  56.2 2.2 %collective-permute-start.10 = (bf16[4,128,512]{2,1,0:T(8,128)(2,1)}, bf16[4,128,512]{2,1,0:T(8,128)(2,1)S(1)}, u32[]{:S(2)}, u32[]{:S(2)}) collective-permute-start(bf16[4,128,512]{2,1,0:T(8,128)(2,1)} %get-tuple-element.25), channel_id=1, source_target_pairs={{0,1},{1,0},{2,3},{3,2},{4,5},{5,4},{6,7},{7,6},{8,9},{9,8},{10,11... | collective-permute-start | bytes 1572872 | tf_op jit(solution)/shard_map/ppermute | solution.py:349
  56.4 3.7 %collective-permute-start.12 = (bf16[512,512]{1,0:T(8,128)(2,1)S(1)}, bf16[512,512]{1,0:T(8,128)(2,1)S(1)}, u32[]{:S(2)}, u32[]{:S(2)}) collective-permute-start(bf16[512,512]{1,0:T(8,128)(2,1)S(1)} %collective-permute-done.11.rest_2_), channel_id=1, source_target_pairs={{0,1},{1,0},{2,3},{3,2},{4,5},{5,4},{6,7},{7,6},{8,9},{9,8},{10,11... | collective-permute-start | bytes 1572872 | tf_op jit(solution)/shard_map/ppermute | solution.py:349
  56.8 27.4 %collective-permute-start.13 = (bf16[4,128,512]{2,1,0:T(8,128)(2,1)}, bf16[4,128,512]{2,1,0:T(8,128)(2,1)S(1)}, u32[]{:S(2)}, u32[]{:S(2)}) collective-permute-start(bf16[4,128,512]{2,1,0:T(8,128)(2,1)} %get-tuple-element.35), channel_id=1, source_target_pairs={{0,1},{1,0},{2,3},{3,2},{4,5},{5,4},{6,7},{7,6},{8,9},{9,8},{10,11... | collective-permute-start | bytes 1572872 | tf_op jit(solution)/shard_map/ppermute | solution.py:349
  59.6 24.6 %collective-permute-start.14 = (bf16[4,128,512]{2,1,0:T(8,128)(2,1)S(1)}, bf16[4,128,512]{2,1,0:T(8,128)(2,1)S(1)}, u32[]{:S(2)}, u32[]{:S(2)}) collective-permute-start(bf16[4,128,512]{2,1,0:T(8,128)(2,1)S(1)} %add_convert_fusion.1), channel_id=1, source_target_pairs={{0,2},{1,3},{2,0},{3,1},{4,6},{5,7},{6,4},{7,5},{8,10},{9,11},{10,... | collective-permute-start | bytes 1572872 | tf_op jit(solution)/shard_map/ppermute | solution.py:349
  83.6 6.8 %collective-permute-start.19 = (bf16[4,128,512]{2,1,0:T(8,128)(2,1)}, bf16[4,128,512]{2,1,0:T(8,128)(2,1)S(1)}, u32[]{:S(2)}, u32[]{:S(2)}) collective-permute-start(bf16[4,128,512]{2,1,0:T(8,128)(2,1)} %get-tuple-element.39), channel_id=1, source_target_pairs={{0,1},{1,0},{2,3},{3,2},{4,5},{5,4},{6,7},{7,6},{8,9},{9,8},{10,11... | collective-permute-start | bytes 1572872 | tf_op jit(solution)/shard_map/ppermute | solution.py:349
  83.6 14.9 %collective-permute-start.18 = (bf16[4,128,512]{2,1,0:T(8,128)(2,1)}, bf16[4,128,512]{2,1,0:T(8,128)(2,1)S(1)}, u32[]{:S(2)}, u32[]{:S(2)}) collective-permute-start(bf16[4,128,512]{2,1,0:T(8,128)(2,1)} %get-tuple-element.37), channel_id=1, source_target_pairs={{0,1},{1,0},{2,3},{3,2},{4,5},{5,4},{6,7},{7,6},{8,9},{9,8},{10,11... | collective-permute-start | bytes 1572872 | tf_op jit(solution)/shard_map/ppermute | solution.py:349
  84.5 8.9 %collective-permute-start.15 = (bf16[128,512]{1,0:T(8,128)(2,1)S(1)}, bf16[128,512]{1,0:T(8,128)(2,1)S(1)}, u32[]{:S(2)}, u32[]{:S(2)}) collective-permute-start(bf16[128,512]{1,0:T(8,128)(2,1)S(1)} %get-tuple-element.44), channel_id=1, source_target_pairs={{0,4},{1,5},{2,6},{3,7},{4,8},{5,9},{6,10},{7,11},{8,12},{9,13},{1... | collective-permute-start | bytes 393224 | tf_op jit(solution)/shard_map/ppermute | solution.py:349
  87.9 10.5 %collective-permute-start.16 = (bf16[128,512]{1,0:T(8,128)(2,1)S(1)}, bf16[128,512]{1,0:T(8,128)(2,1)S(1)}, u32[]{:S(2)}, u32[]{:S(2)}) collective-permute-start(bf16[128,512]{1,0:T(8,128)(2,1)S(1)} %get-tuple-element.46), channel_id=1, source_target_pairs={{0,8},{1,9},{2,10},{3,11},{4,12},{5,13},{6,14},{7,15},{8,0},{9,1},... | collective-permute-start | bytes 393224 | tf_op jit(solution)/shard_map/ppermute | solution.py:349
  89.5 8.9 %collective-permute-start.17 = (bf16[128,512]{1,0:T(8,128)(2,1)S(1)}, bf16[128,512]{1,0:T(8,128)(2,1)S(1)}, u32[]{:S(2)}, u32[]{:S(2)}) collective-permute-start(bf16[128,512]{1,0:T(8,128)(2,1)S(1)} %get-tuple-element.45), channel_id=1, source_target_pairs={{0,12},{1,13},{2,14},{3,15},{4,0},{5,1},{6,2},{7,3},{8,4},{9,5},{1... | collective-permute-start | bytes 393224 | tf_op jit(solution)/shard_map/ppermute | solution.py:349
  90.5 13.4 %collective-permute-start.20 = (bf16[4,128,512]{2,1,0:T(8,128)(2,1)S(1)}, bf16[4,128,512]{2,1,0:T(8,128)(2,1)S(1)}, u32[]{:S(2)}, u32[]{:S(2)}) collective-permute-start(bf16[4,128,512]{2,1,0:T(8,128)(2,1)S(1)} %add_convert_fusion), channel_id=1, source_target_pairs={{0,2},{1,3},{2,0},{3,1},{4,6},{5,7},{6,4},{7,5},{8,10},{9,11},{10,... | collective-permute-start | bytes 1572872 | tf_op jit(solution)/shard_map/ppermute | solution.py:349
  104.2 8.3 %collective-permute-start.21 = (bf16[128,512]{1,0:T(8,128)(2,1)S(1)}, bf16[128,512]{1,0:T(8,128)(2,1)S(1)}, u32[]{:S(2)}, u32[]{:S(2)}) collective-permute-start(bf16[128,512]{1,0:T(8,128)(2,1)S(1)} %get-tuple-element.47), channel_id=1, source_target_pairs={{0,4},{1,5},{2,6},{3,7},{4,8},{5,9},{6,10},{7,11},{8,12},{9,13},{1... | collective-permute-start | bytes 393224 | tf_op jit(solution)/shard_map/ppermute | solution.py:349
  105.2 10.7 %collective-permute-start.22 = (bf16[128,512]{1,0:T(8,128)(2,1)S(1)}, bf16[128,512]{1,0:T(8,128)(2,1)S(1)}, u32[]{:S(2)}, u32[]{:S(2)}) collective-permute-start(bf16[128,512]{1,0:T(8,128)(2,1)S(1)} %get-tuple-element.49), channel_id=1, source_target_pairs={{0,8},{1,9},{2,10},{3,11},{4,12},{5,13},{6,14},{7,15},{8,0},{9,1},... | collective-permute-start | bytes 393224 | tf_op jit(solution)/shard_map/ppermute | solution.py:349
  106.5 9.4 %collective-permute-start.23 = (bf16[128,512]{1,0:T(8,128)(2,1)S(1)}, bf16[128,512]{1,0:T(8,128)(2,1)S(1)}, u32[]{:S(2)}, u32[]{:S(2)}) collective-permute-start(bf16[128,512]{1,0:T(8,128)(2,1)S(1)} %get-tuple-element.48), channel_id=1, source_target_pairs={{0,12},{1,13},{2,14},{3,15},{4,0},{5,1},{6,2},{7,3},{8,4},{9,5},{1... | collective-permute-start | bytes 393224 | tf_op jit(solution)/shard_map/ppermute | solution.py:349
  (12 other events, 132.6 us)

commit v5 on v4

--- a/solution.py
+++ b/solution.py
@@ -22,26 +22,7 @@
 PIECE = 32
 
 
-def attention_kernel(
-    owner_ref, tokens_ref, place_ref,
-    q_ref, g_ref, leaf_k_ref, leaf_v_ref, leaf_ref, mask_ref, *rest,
-    prompts, per_prefix, block_len, planes, ranks, chained, steps, step_heads,
-):
-    sources = rest[:2 * ranks]
-    rest = rest[2 * ranks + 2 * chained:]
-    out_ref, dq_ref, dleaf_ref = rest[:3]
-    totals = rest[3:3 + 2 * ranks]
-    (kv, kcat, vcat, kcat_t, vcat_t, bias, q_pick, g_pick, q2, g2, scores, dprob, probs_b, dscore,
-     dk_sum, dv_sum, sems) = rest[3 + 2 * ranks:]
-    step = pl.program_id(0)
-    per_group = GQ // step_heads
-    count = q_ref.shape[0]
-    columns = step_heads * count
-    span = per_prefix * block_len
-    keys = span + count
-    half = sources[0].shape[1] // 2
-
-    place = place_ref[0]
+def prefixes_here(tokens_ref, place, count, prompts):
     first = place * count
     last = first + (count - 1)
     end = jnp.int32(0)
@@ -53,7 +34,29 @@
         pair_first = pair_first + (end <= first).astype(jnp.int32)
         pair_last = pair_last + (end <= last).astype(jnp.int32)
         border = jnp.where(end > first, jnp.minimum(border, end), border)
-    border = border - first
+    return pair_first, pair_last, border - first
+
+
+def gradient_kernel(
+    owner_ref, tokens_ref, place_ref,
+    q_ref, g_ref, leaf_k_ref, leaf_v_ref, leaf_ref, mask_ref, *rest,
+    prompts, per_prefix, block_len, planes, ranks, steps, step_heads,
+):
+    sources = rest[:2 * ranks]
+    dleaf_ref, probs_out, dscore_out, kcat_t, vcat_t = rest[2 * ranks:2 * ranks + 5]
+    totals = rest[2 * ranks + 5:4 * ranks + 5]
+    (kv, kcat, vcat, bias, q_pick, g_pick, q2, g2, scores, dprob, probs_b, dscore,
+     dk_sum, dv_sum, sems, out_sems) = rest[4 * ranks + 5:]
+    step = pl.program_id(0)
+    per_group = GQ // step_heads
+    count = q_ref.shape[0]
+    columns = step_heads * count
+    span = per_prefix * block_len
+    keys = span + count
+    half = sources[0].shape[1] // 2
+
+    place = place_ref[0]
+    pair_first, pair_last, border = prefixes_here(tokens_ref, place, count, prompts)
 
     def block_place(side, j):
         prefix = pair_first if side == 0 else pair_last
@@ -113,32 +116,28 @@
     @pl.when(new_group & (step < steps))
     def _():
         group = step // per_group
-        for cat, cols, leaf in (
-            (kcat, key_columns(group), leaf_k_ref), (vcat, value_columns(group), leaf_v_ref)
+        for cat, cat_t, cols, leaf in (
+            (kcat, kcat_t, key_columns(group), leaf_k_ref),
+            (vcat, vcat_t, value_columns(group), leaf_v_ref),
         ):
             for side in range(2):
                 lanes = slice(side * HEAD_SIZE, (side + 1) * HEAD_SIZE)
                 cat[0:span, lanes] = kv[side * span:(side + 1) * span, cols]
                 cat[span:, lanes] = leaf[...]
-
+            cat_t[0] = cat[...].T
+
+    slot = lax.rem(step, 2)
+    before = 1 - slot
+
+    def copies_out(at, slot):
+        return [
+            pltpu.make_async_copy(probs_b.at[slot], probs_out.at[at], out_sems.at[0, slot]),
+            pltpu.make_async_copy(dscore.at[slot], dscore_out.at[at], out_sems.at[1, slot]),
+        ]
 
     def later_rows():
-        dk_sum[...] += dot(dscore[...], q2[...], ((1,), (0,)))
-        dv_sum[...] += dot(probs_b[...], g2[...], ((1,), (0,)))
-
-    def later_columns():
-        token_at = lax.rem(lax.broadcasted_iota(jnp.int32, (HEAD_SIZE, columns), 1), count)
-        first_side = token_at < border
-        for source, cat_t, factor, target in (
-            (probs_b, vcat_t, 1.0, out_ref), (dscore, kcat_t, SCALE, dq_ref)
-        ):
-            both = dot(cat_t[...], source[...], ((1,), (0,)))
-            mine = jnp.where(first_side, both[:HEAD_SIZE], both[HEAD_SIZE:])
-            if factor != 1.0:
-                mine = mine * factor
-            for n in range(step_heads):
-                lanes = slice(n * HEAD_SIZE, (n + 1) * HEAD_SIZE)
-                target[:, lanes] = mine[:, n * count:(n + 1) * count].T.astype(jnp.bfloat16)
+        dk_sum[...] += dot(dscore[before], q2[...], ((1,), (0,)))
+        dv_sum[...] += dot(probs_b[before], g2[...], ((1,), (0,)))
 
 
     def pick(source, chosen):
@@ -182,8 +181,8 @@
         for at in range(0, keys, PIECE):
             power = (scores[at:at + PIECE, :] - top) * (SCALE * LOG2E)
             probs = jnp.exp2(power - shift)
-            probs_b[at:at + PIECE, :] = probs.astype(jnp.bfloat16)
-            dscore[at:at + PIECE, :] = (probs * (dprob[at:at + PIECE, :] - delta)).astype(jnp.bfloat16)
+            probs_b[slot, at:at + PIECE, :] = probs.astype(jnp.bfloat16)
+            dscore[slot, at:at + PIECE, :] = (probs * (dprob[at:at + PIECE, :] - delta)).astype(jnp.bfloat16)
 
     def work(later):
         new_q = pick(q_ref, q_pick)
@@ -193,12 +192,15 @@
             later_rows()
         dprob[...] = dot(vcat[...], new_g, ((1,), (1,)))
         total, delta = sums(top)
-        if later:
-            later_columns()
         finish(top, total, delta)
         q2[...] = new_q
         g2[...] = new_g
 
+    @pl.when((step >= 2) & (step < steps))
+    def _():
+        for copy in copies_out(step - 2, slot):
+            copy.wait()
+
     @pl.when(step == 0)
     def _():
         work(False)
@@ -207,10 +209,17 @@
     def _():
         work(True)
 
+    @pl.when(step < steps)
+    def _():
+        for copy in copies_out(step, slot):
+            copy.start()
+
     @pl.when(step == steps)
     def _():
         later_rows()
-        later_columns()
+        for at in range(max(steps - 2, 0), steps):
+            for copy in copies_out(at, at % 2):
+                copy.wait()
 
     @pl.when(new_group & (step > 0))
     def _():
@@ -234,15 +243,33 @@
         dk_sum[...] = jnp.zeros_like(dk_sum)
         dv_sum[...] = jnp.zeros_like(dv_sum)
 
-    @pl.when(new_group & (step < steps))
-    def _():
-        kcat_t[...] = kcat[...].T
-        vcat_t[...] = vcat[...].T
-
-
-def attention(
-    chunk, owner, tokens, place, q, g, leaf_kv, leaf, mask, sources, earlier, planes, ranks
+
+def query_kernel(
+    tokens_ref, place_ref, probs_ref, dscore_ref, vcat_t, kcat_t, *rest, prompts, step_heads, chained
 ):
+    out_ref, dq_ref = rest[2 * chained:]
+    count = out_ref.shape[0]
+    border = prefixes_here(tokens_ref, place_ref[0], count, prompts)[2]
+    columns = step_heads * count
+    token_at = lax.rem(lax.broadcasted_iota(jnp.int32, (HEAD_SIZE, columns), 1), count)
+    first_side = token_at < border
+    for source, cat_t, factor, target in (
+        (probs_ref, vcat_t, 1.0, out_ref), (dscore_ref, kcat_t, SCALE, dq_ref)
+    ):
+        both = dot(cat_t[0], source[0], ((1,), (0,)))
+        mine = jnp.where(first_side, both[:HEAD_SIZE], both[HEAD_SIZE:])
+        if factor != 1.0:
+            mine = mine * factor
+        for n in range(step_heads):
+            lanes = slice(n * HEAD_SIZE, (n + 1) * HEAD_SIZE)
+            target[:, lanes] = mine[:, n * count:(n + 1) * count].T.astype(jnp.bfloat16)
+
+
+def full(shape):
+    return pl.BlockSpec(shape, lambda i, *_: (0,) * len(shape))
+
+
+def gradients(chunk, owner, tokens, place, q, g, leaf_kv, leaf, mask, sources, planes, ranks):
     count = q.shape[0]
     block_len = sources[0].shape[0] // planes
     prompts = tokens.shape[0]
@@ -257,14 +284,14 @@
     steps = heads // step_heads
     per_group = GQ // step_heads
     skipped_steps = skipped * per_group
+    columns = step_heads * count
     bf16, f32 = jnp.bfloat16, jnp.float32
 
     def now(i):
         return jnp.minimum(i, steps - 1)
 
-    ahead = pl.BlockSpec((count, step_heads * HEAD_SIZE), lambda i, *_: (0, skipped_steps + now(i)))
-    behind = pl.BlockSpec(
-        (count, step_heads * HEAD_SIZE), lambda i, *_: (0, skipped_steps + jnp.maximum(i - 1, 0))
+    slab = pl.BlockSpec(
+        (count, step_heads * HEAD_SIZE), lambda i, *_: (0, skipped_steps + now(i))
     )
     leaf_k = pl.BlockSpec(
         (count, HEAD_SIZE), lambda i, *_: (0, skipped + now(i) // per_group)
@@ -273,59 +300,88 @@
         (count, HEAD_SIZE),
         lambda i, *_: (0, KEY_VALUE_HEADS + skipped + now(i) // per_group),
     )
+    cat_t = pl.BlockSpec((1, 2 * HEAD_SIZE, keys), lambda i, *_: (now(i) // per_group, 0, 0))
     anywhere = pl.BlockSpec(memory_space=pl.ANY)
-
-    def full(shape):
-        return pl.BlockSpec(shape, lambda h, *_: (0,) * len(shape))
-
     sum_shape = (planes, block_len, width)
-    chained = len(earlier) > 0
+    probs_shape = jax.ShapeDtypeStruct((steps, keys, columns), bf16)
+    cat_t_shape = jax.ShapeDtypeStruct((groups, 2 * HEAD_SIZE, keys), bf16)
     return pl.pallas_call(
         functools.partial(
-            attention_kernel, prompts=prompts, per_prefix=per_prefix, block_len=block_len,
-            planes=planes, ranks=ranks, chained=chained, steps=steps, step_heads=step_heads,
+            gradient_kernel, prompts=prompts, per_prefix=per_prefix, block_len=block_len,
+            planes=planes, ranks=ranks, steps=steps, step_heads=step_heads,
         ),
         grid_spec=pltpu.PrefetchScalarGridSpec(
             num_scalar_prefetch=3,
             grid=(steps + 1,),
             in_specs=[
-                ahead, ahead, leaf_k, leaf_v, full(leaf.shape), full(mask.shape),
-            ] + [anywhere] * (2 * ranks + len(earlier)),
-            out_specs=[behind, behind, full((count, width))] + [full(sum_shape)] * (2 * ranks),
+                slab, slab, leaf_k, leaf_v, full(leaf.shape), full(mask.shape),
+            ] + [anywhere] * (2 * ranks),
+            out_specs=[full((count, width)), anywhere, anywhere, cat_t, cat_t]
+            + [full(sum_shape)] * (2 * ranks),
             scratch_shapes=[
                 pltpu.VMEM((2 * span, width), bf16),
                 pltpu.VMEM((keys, 2 * HEAD_SIZE), bf16),
                 pltpu.VMEM((keys, 2 * HEAD_SIZE), bf16),
-                pltpu.VMEM((2 * HEAD_SIZE, keys), bf16),
-                pltpu.VMEM((2 * HEAD_SIZE, keys), bf16),
-                pltpu.VMEM((count, step_heads * count), f32),
+                pltpu.VMEM((count, columns), f32),
                 pltpu.VMEM((count, 2 * HEAD_SIZE), bf16),
                 pltpu.VMEM((count, 2 * HEAD_SIZE), bf16),
-                pltpu.VMEM((step_heads * count, 2 * HEAD_SIZE), bf16),
-                pltpu.VMEM((step_heads * count, 2 * HEAD_SIZE), bf16),
-                pltpu.VMEM((keys, step_heads * count), f32),
-                pltpu.VMEM((keys, step_heads * count), f32),
-                pltpu.VMEM((keys, step_heads * count), bf16),
-                pltpu.VMEM((keys, step_heads * count), bf16),
+                pltpu.VMEM((columns, 2 * HEAD_SIZE), bf16),
+                pltpu.VMEM((columns, 2 * HEAD_SIZE), bf16),
+                pltpu.VMEM((keys, columns), f32),
+                pltpu.VMEM((keys, columns), f32),
+                pltpu.VMEM((2, keys, columns), bf16),
+                pltpu.VMEM((2, keys, columns), bf16),
                 pltpu.VMEM((keys, 2 * HEAD_SIZE), f32),
                 pltpu.VMEM((keys, 2 * HEAD_SIZE), f32),
                 pltpu.SemaphoreType.DMA((2 * per_prefix,)),
+                pltpu.SemaphoreType.DMA((2, 2)),
             ],
         ),
         out_shape=[
-            jax.ShapeDtypeStruct(q.shape, bf16),
-            jax.ShapeDtypeStruct(q.shape, bf16),
-            jax.ShapeDtypeStruct((count, width), bf16),
+            jax.ShapeDtypeStruct((count, width), bf16), probs_shape, probs_shape, cat_t_shape,
+            cat_t_shape,
         ] + [jax.ShapeDtypeStruct(sum_shape, bf16)] * (2 * ranks),
-        input_output_aliases={9 + 2 * ranks: 0, 10 + 2 * ranks: 1} if chained else {},
         compiler_params=pltpu.CompilerParams(
             vmem_limit_bytes=54 * 2**20, dimension_semantics=("arbitrary",)
         ),
         cost_estimate=pl.CostEstimate(
-            flops=heads * 6 * 2 * keys * 256 * 256, bytes_accessed=groups * 4 * 2**20,
-            transcendentals=heads * keys * count,
-        ),
-    )(owner, tokens, place, q, g, leaf_kv, leaf_kv, leaf, mask, *sources, *earlier)
+            flops=heads * 4 * 2 * keys * 256 * 256, bytes_accessed=groups * 8 * 2**20,
+            transcendentals=2 * heads * keys * count,
+        ),
+    )(owner, tokens, place, q, g, leaf_kv, leaf_kv, leaf, mask, *sources)
+
+
+def queries(chunk, part, tokens, place, probs, dscore, kcat_t, vcat_t, like, earlier):
+    step_heads = STEP_HEADS[chunk]
+    per_group = GQ // step_heads
+    count, keys = like.shape[0], probs.shape[1]
+    first = (sum(CHUNKS[:chunk]) + part) * per_group
+    chained = len(earlier) > 0
+    block = pl.BlockSpec(
+        (1, keys, step_heads * count), lambda i, *_: (part * per_group + i, 0, 0)
+    )
+    cat_t = pl.BlockSpec((1, 2 * HEAD_SIZE, keys), lambda i, *_: (part, 0, 0))
+    slab = pl.BlockSpec((count, step_heads * HEAD_SIZE), lambda i, *_: (0, first + i))
+    anywhere = pl.BlockSpec(memory_space=pl.ANY)
+    return pl.pallas_call(
+        functools.partial(
+            query_kernel, prompts=tokens.shape[0], step_heads=step_heads, chained=chained
+        ),
+        grid_spec=pltpu.PrefetchScalarGridSpec(
+            num_scalar_prefetch=2,
+            grid=(per_group,),
+            in_specs=[block, block, cat_t, cat_t] + [anywhere] * len(earlier),
+            out_specs=[slab, slab],
+        ),
+        out_shape=[jax.ShapeDtypeStruct(like.shape, jnp.bfloat16)] * 2,
+        input_output_aliases={6: 0, 7: 1} if chained else {},
+        compiler_params=pltpu.CompilerParams(
+            vmem_limit_bytes=54 * 2**20, dimension_semantics=("arbitrary",)
+        ),
+        cost_estimate=pl.CostEstimate(
+            flops=GQ * 2 * 2 * keys * 256 * 256, bytes_accessed=8 * 2**20, transcendentals=0,
+        ),
+    )(tokens, place, probs, dscore, vcat_t, kcat_t, *earlier)
 
 
 def shards(
@@ -368,18 +424,19 @@
         total = add(totals[0], send(totals[1], 0, 0, 1))
         return add(total, send(away, 0, 1, 0)) if ranks == 2 else total
 
-    def reduce_planes(total):
-        mine = total[0]
+    def for_planes(total):
+        return total[0], [total[k].astype(jnp.bfloat16) for k in range(1, planes)]
+
+    def reduce_planes(mine, away):
         for k in range(1, planes):
-            mine = add(mine, send(total[k].astype(jnp.bfloat16), k, 0, 0))
+            mine = add(mine, send(away[k - 1], k, 0, 0))
         return mine.astype(jnp.bfloat16)
 
     chunks = len(CHUNKS)
     near = [by_planes(chunk) for chunk in range(chunks)]
     near_far = [send(n, 0, 0, 1) for n in near]
     other = [send(n, 0, 1, 0) for n in near] if ranks == 2 else []
-    d_leaf, d_prefix, earlier = [], [], ()
-    parts = []
+    d_leaf, parts, left = [], [], []
     for chunk in range(chunks):
         first = [place] + near[chunk + 1:chunk + 2] + near_far[chunk + 1:chunk + 2]
         if chunk and ranks == 2:
@@ -388,15 +445,27 @@
         if ranks == 2:
             row = tie(other[chunk], d_leaf[-1] if chunk else near[1])
             sources += [row, send(row, 0, 0, 1)]
-        attended, d_query, leaf_part, *totals = attention(
+        leaf_part, probs, dscore, kcat_t, vcat_t, *totals = gradients(
             chunk, block_owner, subtree_tokens, tie(*first), query, d_out, leaf_key_value,
-            leaf_id, mask, sources, earlier, planes, ranks,
+            leaf_id, mask, sources, planes, ranks,
         )
-        earlier = (attended, d_query)
+        left.append((probs, dscore, kcat_t, vcat_t))
         d_leaf.append(leaf_part)
         away = add(totals[2], send(totals[3], 0, 0, 1)).astype(jnp.bfloat16) if ranks == 2 else None
         parts.append((totals, away))
-    d_prefix = [reduce_planes(reduce_ranks(*part)) for part in parts]
+    totals = [for_planes(reduce_ranks(*part)) for part in parts]
+    d_prefix = [reduce_planes(*total) for total in totals]
+    earlier = ()
+    work = [(chunk, part) for chunk in range(chunks) for part in range(CHUNKS[chunk])]
+    for at, (chunk, part) in enumerate(work):
+        if at < len(work) - 1:
+            begun = [away for total in totals[:-1] for away in total[1]]
+            begun += [parts[-1][1]] if ranks == 2 else []
+        else:
+            begun = totals[-1][1]
+        after = tie(place, d_leaf[-1], *begun)
+        earlier = queries(chunk, part, subtree_tokens, after, *left[chunk], query, earlier)
+    attended, d_query = earlier
 
     def join(parts):
         halves = [jnp.split(p, 2, axis=1) for p in parts]

time: 117 us -> 126 us (1.077)
  Pallas kernels: 44.6 us -> 68 us
  waiting for transfers between devices: 35.5 us -> 24.4 us
  starting transfers between devices: 28.5 us -> 23.9 us
    pallas_call x2 -> x6, Pallas kernels: 44.6 us -> 68 us  [the longest x2 43.8 us: gradients(): pl.pallas_call(functools.partial(gradient_kernel, prompts=prompts, per_pr...]
    ppermute x24, waiting for transfers between devices: 35.5 us -> 24.4 us  [send(): return lax.ppermute(array, 'dp', pairs)]
    ppermute x24, starting transfers between devices: 28.5 us -> 23.9 us  [send(): return lax.ppermute(array, 'dp', pairs)]
  transfers between devices with their start and end apart: 24 -> 24, of which waited for: 12 -> 8; matrix products, arithmetic and copies ran while one was open for 3% -> 4% of each run, Pallas kernels for 38% -> 54%
where the time goes in v5:
time: 126 us; the launch traced here: 125 us
  Pallas kernels  68 us (54%)
  waiting for transfers between devices  24.4 us (19%)
  starting transfers between devices  23.9 us (19%)
  local copies, waits for them, and re-layouts  4.68 us (4%)
  other arithmetic  3.6 us (3%)
    pallas_call x2, Pallas kernels, gradients(): pl.pallas_call(functools.partial(gradient_kernel, prompts=prompts, per_pr...  43.8 us
    ppermute x24, waiting for transfers between devices, send(): return lax.ppermute(array, 'dp', pairs)  24.4 us
    pallas_call x4, Pallas kernels, queries(): pl.pallas_call(functools.partial(query_kernel, prompts=tokens.shape[0], s...  24.2 us
    ppermute x24, starting transfers between devices, send(): return lax.ppermute(array, 'dp', pairs)  23.9 us
  transfers between devices with their start and end apart: 24, of which 8 were waited for; matrix products, arithmetic and copies ran while one was open for 4% of the time, Pallas kernels for 54%

profile of v5, /device:TPU:0, one launch (start us, length us, event | category | flops | bytes accessed | tf_op | source)
XLA Modules:
  0.0 125.5 jit_solution(16770896963858882065)
XLA Ops:
  1.6 5.1 %collective-permute-start.6 = (bf16[128,512]{1,0:T(8,128)(2,1)S(1)}, bf16[128,512]{1,0:T(8,128)(2,1)S(1)}, u32[]{:S(2)}, u32[]{:S(2)}) collective-permute-start(bf16[128,512]{1,0:T(8,128)(2,1)S(1)} %pad_maximum_fusion.5), channel_id=1, source_target_pairs={{0,12},{1,13},{2,14},{3,15},{4,0},{5,1},{6,2},{7,3},{8,4},{9,5},{1... | collective-permute-start | bytes 393224 | tf_op jit(solution)/shard_map/ppermute | solution.py:405
  6.7 1.0 collective-permute-start.4
  7.7 2.9 %collective-permute-done.6 = bf16[128,512]{1,0:T(8,128)(2,1)S(1)} collective-permute-done((bf16[128,512]{1,0:T(8,128)(2,1)S(1)}, bf16[128,512]{1,0:T(8,128)(2,1)S(1)}, u32[]{:S(2)}, u32[]{:S(2)}) %collective-permute-start.6) | collective-permute-done | bytes 131104 | tf_op jit(solution)/shard_map/ppermute | solution.py:405
  10.6 7.3 %collective-permute-done.5 = bf16[128,512]{1,0:T(8,128)(2,1)S(1)} collective-permute-done((bf16[128,512]{1,0:T(8,128)(2,1)S(1)}, bf16[128,512]{1,0:T(8,128)(2,1)S(1)}, u32[]{:S(2)}, u32[]{:S(2)}) %collective-permute-start.5) | collective-permute-done | bytes 131104 | tf_op jit(solution)/shard_map/ppermute | solution.py:405
  18.0 1.6 %collective-permute-start.8 = (bf16[512,512]{1,0:T(8,128)(2,1)S(1)}, bf16[512,512]{1,0:T(8,128)(2,1)S(1)}, u32[]{:S(2)}, u32[]{:S(2)}) collective-permute-start(bf16[512,512]{1,0:T(8,128)(2,1)S(1)} %pad_maximum_fusion.1.rest_0_), channel_id=1, source_target_pairs={{0,2},{1,3},{2,0},{3,1},{4,6},{5,7},{6,4},{7,5},{8,10},{9,11},{10,... | collective-permute-start | bytes 1572872 | tf_op jit(solution)/shard_map/ppermute | solution.py:405
  19.6 1.7 %collective-permute-start.2 = (bf16[128,512]{1,0:T(8,128)(2,1)S(1)}, bf16[128,512]{1,0:T(8,128)(2,1)S(1)}, u32[]{:S(2)}, u32[]{:S(2)}) collective-permute-start(bf16[128,512]{1,0:T(8,128)(2,1)S(1)} %pad_maximum_fusion.4), channel_id=1, source_target_pairs={{0,12},{1,13},{2,14},{3,15},{4,0},{5,1},{6,2},{7,3},{8,4},{9,5},{1... | collective-permute-start | bytes 393224 | tf_op jit(solution)/shard_map/ppermute | solution.py:405
  21.2 1.1 collective-permute-start.1
  22.3 1.9 %collective-permute-start = (bf16[128,512]{1,0:T(8,128)(2,1)S(1)}, bf16[128,512]{1,0:T(8,128)(2,1)S(1)}, u32[]{:S(2)}, u32[]{:S(2)}) collective-permute-start(bf16[128,512]{1,0:T(8,128)(2,1)S(1)} %pad_maximum_fusion.4), channel_id=1, source_target_pairs={{0,4},{1,5},{2,6},{3,7},{4,8},{5,9},{6,10},{7,11},{8,12},{9,13},{1... | collective-permute-start | bytes 393224 | tf_op jit(solution)/shard_map/ppermute | solution.py:405
  24.3 1.1 collective-permute-done.2
  25.4 7.9 %collective-permute-done.1 = bf16[128,512]{1,0:T(8,128)(2,1)S(1)} collective-permute-done((bf16[128,512]{1,0:T(8,128)(2,1)S(1)}, bf16[128,512]{1,0:T(8,128)(2,1)S(1)}, u32[]{:S(2)}, u32[]{:S(2)}) %collective-permute-start.1) | collective-permute-done | bytes 131104 | tf_op jit(solution)/shard_map/ppermute | solution.py:405
  36.9 21.6 %shard_map.111 = (bf16[256,512]{1,0:T(8,128)(2,1)}, bf16[4,768,1024]{2,1,0:T(8,128)(2,1)}, bf16[4,768,1024]{2,1,0:T(8,128)(2,1)}, bf16[2,256,768]{2,1,0:T(8,128)...) custom-call(s32[16]{0:T(128)} %owner_ref.3, ...), custom_call_target="tpu_custom_call" | custom-call | flops 6442450944 | bytes 16777216 | tf_op jit(solution)/shard_map/pallas_call | solution.py:308
  60.7 1.2 add_convert_fusion.1
  63.2 22.2 %shard_map.112 = (bf16[256,512]{1,0:T(8,128)(2,1)}, bf16[8,768,512]{2,1,0:T(8,128)(2,1)}, bf16[8,768,512]{2,1,0:T(8,128)(2,1)}, bf16[2,256,768]{2,1,0:T(8,128)(2...) custom-call(s32[16]{0:T(128)} %owner_ref.3, ...), custom_call_target="tpu_custom_call" | custom-call | flops 6442450944 | bytes 16777216 | tf_op jit(solution)/shard_map/pallas_call | solution.py:308
  86.0 1.0 fusion.11
  88.2 1.4 %collective-permute-start.19 = (bf16[128,512]{1,0:T(8,128)(2,1)S(1)}, bf16[128,512]{1,0:T(8,128)(2,1)S(1)}, u32[]{:S(2)}, u32[]{:S(2)}) collective-permute-start(bf16[128,512]{1,0:T(8,128)(2,1)S(1)} %get-tuple-element.73), channel_id=1, source_target_pairs={{0,8},{1,9},{2,10},{3,11},{4,12},{5,13},{6,14},{7,15},{8,0},{9,1},... | collective-permute-start | bytes 393224 | tf_op jit(solution)/shard_map/ppermute | solution.py:405
  89.6 1.9 %collective-permute-start.18 = (bf16[128,512]{1,0:T(8,128)(2,1)S(1)}, bf16[128,512]{1,0:T(8,128)(2,1)S(1)}, u32[]{:S(2)}, u32[]{:S(2)}) collective-permute-start(bf16[128,512]{1,0:T(8,128)(2,1)S(1)} %get-tuple-element.74), channel_id=1, source_target_pairs={{0,4},{1,5},{2,6},{3,7},{4,8},{5,9},{6,10},{7,11},{8,12},{9,13},{1... | collective-permute-start | bytes 393224 | tf_op jit(solution)/shard_map/ppermute | solution.py:405
  91.7 1.6 %collective-permute-start.15 = (bf16[4,128,512]{2,1,0:T(8,128)(2,1)S(1)}, bf16[4,128,512]{2,1,0:T(8,128)(2,1)S(1)}, u32[]{:S(2)}, u32[]{:S(2)}) collective-permute-start(bf16[4,128,512]{2,1,0:T(8,128)(2,1)S(1)} %add_convert_fusion), channel_id=1, source_target_pairs={{0,2},{1,3},{2,0},{3,1},{4,6},{5,7},{6,4},{7,5},{8,10},{9,11},{10,... | collective-permute-start | bytes 1572872 | tf_op jit(solution)/shard_map/ppermute | solution.py:405
  93.3 5.6 %shard_map.113 = (bf16[256,4096]{1,0:T(8,128)(2,1)}, bf16[256,4096]{1,0:T(8,128)(2,1)}) custom-call(s32[4]{0:T(128)} %tokens_ref.11, s32[1]{0:T(128)} %bitcast.place_ref, bf16[4,768,1024]{2,1,0:T(8,128)(2,1)} %get-tuple-element.56.probs_ref, bf16[4,768,1024]{2,1,0:T(8,128)(2,1)} %get-tuple-element.57.dscore_ref, ...), custom_call_target="tpu_custom_call" | custom-call | flops 1610612736 | bytes 8388608 | tf_op jit(solution)/shard_map/pallas_call | solution.py:366
  98.9 5.6 %shard_map.114 = (bf16[256,4096]{1,0:T(8,128)(2,1)}, bf16[256,4096]{1,0:T(8,128)(2,1)}) custom-call(s32[4]{0:T(128)} %tokens_ref.11, s32[1]{0:T(128)} %bitcast.place_ref, bf16[4,768,1024]{2,1,0:T(8,128)(2,1)} %get-tuple-element.56.probs_ref, bf16[4,768,1024]{2,1,0:T(8,128)(2,1)} %get-tuple-element.57.dscore_ref, ...), custom_call_target="tpu_custom_call", output_to_operand_aliasing={{0}: (6, {}), {1}: (7, {})} | custom-call | flops 1610612736 | bytes 8388608 | tf_op jit(solution)/shard_map/pallas_call | solution.py:366
  104.5 6.6 %shard_map.115 = (bf16[256,4096]{1,0:T(8,128)(2,1)}, bf16[256,4096]{1,0:T(8,128)(2,1)}) custom-call(s32[4]{0:T(128)} %tokens_ref.11, s32[1]{0:T(128)} %bitcast.place_ref, bf16[8,768,512]{2,1,0:T(8,128)(2,1)} %get-tuple-element.49.probs_ref, bf16[8,768,512]{2,1,0:T(8,128)(2,1)} %get-tuple-element.50.dscore_ref, ...), custom_call_target="tpu_custom_call", output_to_operand_aliasing={{0}: (6, {}), {1}: (7, {})} | custom-call | flops 1610612736 | bytes 8388608 | tf_op jit(solution)/shard_map/pallas_call | solution.py:366
  111.5 1.9 %collective-permute-start.23 = (bf16[128,512]{1,0:T(8,128)(2,1)S(1)}, bf16[128,512]{1,0:T(8,128)(2,1)S(1)}, u32[]{:S(2)}, u32[]{:S(2)}) collective-permute-start(bf16[128,512]{1,0:T(8,128)(2,1)S(1)} %get-tuple-element.75), channel_id=1, source_target_pairs={{0,12},{1,13},{2,14},{3,15},{4,0},{5,1},{6,2},{7,3},{8,4},{9,5},{1... | collective-permute-start | bytes 393224 | tf_op jit(solution)/shard_map/ppermute | solution.py:405
  113.4 1.8 %collective-permute-start.21 = (bf16[128,512]{1,0:T(8,128)(2,1)S(1)}, bf16[128,512]{1,0:T(8,128)(2,1)S(1)}, u32[]{:S(2)}, u32[]{:S(2)}) collective-permute-start(bf16[128,512]{1,0:T(8,128)(2,1)S(1)} %get-tuple-element.77), channel_id=1, source_target_pairs={{0,4},{1,5},{2,6},{3,7},{4,8},{5,9},{6,10},{7,11},{8,12},{9,13},{1... | collective-permute-start | bytes 393224 | tf_op jit(solution)/shard_map/ppermute | solution.py:405
  115.2 6.5 %shard_map.116 = (bf16[256,4096]{1,0:T(8,128)(2,1)}, bf16[256,4096]{1,0:T(8,128)(2,1)}) custom-call(s32[4]{0:T(128)} %tokens_ref.11, s32[1]{0:T(128)} %bitcast.place_ref, bf16[8,768,512]{2,1,0:T(8,128)(2,1)} %get-tuple-element.49.probs_ref, bf16[8,768,512]{2,1,0:T(8,128)(2,1)} %get-tuple-element.50.dscore_ref, ...), custom_call_target="tpu_custom_call", output_to_operand_aliasing={{0}: (6, {}), {1}: (7, {})} | custom-call | flops 1610612736 | bytes 8388608 | tf_op jit(solution)/shard_map/pallas_call | solution.py:366
  121.7 3.0 %collective-permute-done.22 = bf16[128,512]{1,0:T(8,128)(2,1)S(1)} collective-permute-done((bf16[128,512]{1,0:T(8,128)(2,1)S(1)}, bf16[128,512]{1,0:T(8,128)(2,1)S(1)}, u32[]{:S(2)}, u32[]{:S(2)}) %collective-permute-start.22) | collective-permute-done | bytes 131104 | tf_op jit(solution)/shard_map/ppermute | solution.py:405
  (71 shorter events, 11.2 us)
Async XLA Ops:
  1.6 9.0 %collective-permute-start.6 = (bf16[128,512]{1,0:T(8,128)(2,1)S(1)}, bf16[128,512]{1,0:T(8,128)(2,1)S(1)}, u32[]{:S(2)}, u32[]{:S(2)}) collective-permute-start(bf16[128,512]{1,0:T(8,128)(2,1)S(1)} %pad_maximum_fusion.5), channel_id=1, source_target_pairs={{0,12},{1,13},{2,14},{3,15},{4,0},{5,1},{6,2},{7,3},{8,4},{9,5},{1... | collective-permute-start | bytes 393224 | tf_op jit(solution)/shard_map/ppermute | solution.py:405
  6.7 11.2 %collective-permute-start.5 = (bf16[128,512]{1,0:T(8,128)(2,1)S(1)}, bf16[128,512]{1,0:T(8,128)(2,1)S(1)}, u32[]{:S(2)}, u32[]{:S(2)}) collective-permute-start(bf16[128,512]{1,0:T(8,128)(2,1)S(1)} %pad_maximum_fusion.5), channel_id=1, source_target_pairs={{0,8},{1,9},{2,10},{3,11},{4,12},{5,13},{6,14},{7,15},{8,0},{9,1},... | collective-permute-start | bytes 393224 | tf_op jit(solution)/shard_map/ppermute | solution.py:405
  6.7 11.2 %collective-permute-start.4 = (bf16[128,512]{1,0:T(8,128)(2,1)S(1)}, bf16[128,512]{1,0:T(8,128)(2,1)S(1)}, u32[]{:S(2)}, u32[]{:S(2)}) collective-permute-start(bf16[128,512]{1,0:T(8,128)(2,1)S(1)} %pad_maximum_fusion.5), channel_id=1, source_target_pairs={{0,4},{1,5},{2,6},{3,7},{4,8},{5,9},{6,10},{7,11},{8,12},{9,13},{1... | collective-permute-start | bytes 393224 | tf_op jit(solution)/shard_map/ppermute | solution.py:405
  18.0 15.5 %collective-permute-start.8 = (bf16[512,512]{1,0:T(8,128)(2,1)S(1)}, bf16[512,512]{1,0:T(8,128)(2,1)S(1)}, u32[]{:S(2)}, u32[]{:S(2)}) collective-permute-start(bf16[512,512]{1,0:T(8,128)(2,1)S(1)} %pad_maximum_fusion.1.rest_0_), channel_id=1, source_target_pairs={{0,2},{1,3},{2,0},{3,1},{4,6},{5,7},{6,4},{7,5},{8,10},{9,11},{10,... | collective-permute-start | bytes 1572872 | tf_op jit(solution)/shard_map/ppermute | solution.py:405
  19.6 5.9 %collective-permute-start.2 = (bf16[128,512]{1,0:T(8,128)(2,1)S(1)}, bf16[128,512]{1,0:T(8,128)(2,1)S(1)}, u32[]{:S(2)}, u32[]{:S(2)}) collective-permute-start(bf16[128,512]{1,0:T(8,128)(2,1)S(1)} %pad_maximum_fusion.4), channel_id=1, source_target_pairs={{0,12},{1,13},{2,14},{3,15},{4,0},{5,1},{6,2},{7,3},{8,4},{9,5},{1... | collective-permute-start | bytes 393224 | tf_op jit(solution)/shard_map/ppermute | solution.py:405
  21.2 12.1 %collective-permute-start.1 = (bf16[128,512]{1,0:T(8,128)(2,1)S(1)}, bf16[128,512]{1,0:T(8,128)(2,1)S(1)}, u32[]{:S(2)}, u32[]{:S(2)}) collective-permute-start(bf16[128,512]{1,0:T(8,128)(2,1)S(1)} %pad_maximum_fusion.4), channel_id=1, source_target_pairs={{0,8},{1,9},{2,10},{3,11},{4,12},{5,13},{6,14},{7,15},{8,0},{9,1},... | collective-permute-start | bytes 393224 | tf_op jit(solution)/shard_map/ppermute | solution.py:405
  22.3 11.0 %collective-permute-start = (bf16[128,512]{1,0:T(8,128)(2,1)S(1)}, bf16[128,512]{1,0:T(8,128)(2,1)S(1)}, u32[]{:S(2)}, u32[]{:S(2)}) collective-permute-start(bf16[128,512]{1,0:T(8,128)(2,1)S(1)} %pad_maximum_fusion.4), channel_id=1, source_target_pairs={{0,4},{1,5},{2,6},{3,7},{4,8},{5,9},{6,10},{7,11},{8,12},{9,13},{1... | collective-permute-start | bytes 393224 | tf_op jit(solution)/shard_map/ppermute | solution.py:405
  24.3 11.1 %collective-permute-start.7 = (bf16[512,512]{1,0:T(8,128)(2,1)S(1)}, bf16[512,512]{1,0:T(8,128)(2,1)S(1)}, u32[]{:S(2)}, u32[]{:S(2)}) collective-permute-start(bf16[512,512]{1,0:T(8,128)(2,1)S(1)} %pad_maximum_fusion.1.rest_0_), channel_id=1, source_target_pairs={{0,1},{1,0},{2,3},{3,2},{4,5},{5,4},{6,7},{7,6},{8,9},{9,8},{10,11... | collective-permute-start | bytes 1572872 | tf_op jit(solution)/shard_map/ppermute | solution.py:405
  33.3 2.0 %collective-permute-start.3 = (bf16[512,512]{1,0:T(8,128)(2,1)S(1)}, bf16[512,512]{1,0:T(8,128)(2,1)S(1)}, u32[]{:S(2)}, u32[]{:S(2)}) collective-permute-start(bf16[512,512]{1,0:T(8,128)(2,1)S(1)} %pad_maximum_fusion.rest_0_), channel_id=1, source_target_pairs={{0,1},{1,0},{2,3},{3,2},{4,5},{5,4},{6,7},{7,6},{8,9},{9,8},{10,11... | collective-permute-start | bytes 1572872 | tf_op jit(solution)/shard_map/ppermute | solution.py:405
  33.4 2.6 %collective-permute-start.9 = (bf16[512,512]{1,0:T(8,128)(2,1)S(1)}, bf16[512,512]{1,0:T(8,128)(2,1)S(1)}, u32[]{:S(2)}, u32[]{:S(2)}) collective-permute-start(bf16[512,512]{1,0:T(8,128)(2,1)S(1)} %collective-permute-done.8.rest_2_), channel_id=1, source_target_pairs={{0,1},{1,0},{2,3},{3,2},{4,5},{5,4},{6,7},{7,6},{8,9},{9,8},{10,11... | collective-permute-start | bytes 1572872 | tf_op jit(solution)/shard_map/ppermute | solution.py:405
  33.9 24.7 %collective-permute-start.11 = (bf16[512,512]{1,0:T(8,128)(2,1)S(1)}, bf16[512,512]{1,0:T(8,128)(2,1)S(1)}, u32[]{:S(2)}, u32[]{:S(2)}) collective-permute-start(bf16[512,512]{1,0:T(8,128)(2,1)S(1)} %pad_maximum_fusion.rest_0_), channel_id=1, source_target_pairs={{0,2},{1,3},{2,0},{3,1},{4,6},{5,7},{6,4},{7,5},{8,10},{9,11},{10,... | collective-permute-start | bytes 1572872 | tf_op jit(solution)/shard_map/ppermute | solution.py:405
  58.5 2.2 %collective-permute-start.10 = (bf16[4,128,512]{2,1,0:T(8,128)(2,1)}, bf16[4,128,512]{2,1,0:T(8,128)(2,1)S(1)}, u32[]{:S(2)}, u32[]{:S(2)}) collective-permute-start(bf16[4,128,512]{2,1,0:T(8,128)(2,1)} %get-tuple-element.39), channel_id=1, source_target_pairs={{0,1},{1,0},{2,3},{3,2},{4,5},{5,4},{6,7},{7,6},{8,9},{9,8},{10,11... | collective-permute-start | bytes 1572872 | tf_op jit(solution)/shard_map/ppermute | solution.py:405
  58.6 3.8 %collective-permute-start.12 = (bf16[512,512]{1,0:T(8,128)(2,1)S(1)}, bf16[512,512]{1,0:T(8,128)(2,1)S(1)}, u32[]{:S(2)}, u32[]{:S(2)}) collective-permute-start(bf16[512,512]{1,0:T(8,128)(2,1)S(1)} %collective-permute-done.11.rest_2_), channel_id=1, source_target_pairs={{0,1},{1,0},{2,3},{3,2},{4,5},{5,4},{6,7},{7,6},{8,9},{9,8},{10,11... | collective-permute-start | bytes 1572872 | tf_op jit(solution)/shard_map/ppermute | solution.py:405
  59.1 28.8 %collective-permute-start.16 = (bf16[4,128,512]{2,1,0:T(8,128)(2,1)}, bf16[4,128,512]{2,1,0:T(8,128)(2,1)S(1)}, u32[]{:S(2)}, u32[]{:S(2)}) collective-permute-start(bf16[4,128,512]{2,1,0:T(8,128)(2,1)} %get-tuple-element.54), channel_id=1, source_target_pairs={{0,1},{1,0},{2,3},{3,2},{4,5},{5,4},{6,7},{7,6},{8,9},{9,8},{10,11... | collective-permute-start | bytes 1572872 | tf_op jit(solution)/shard_map/ppermute | solution.py:405
  61.9 26.0 %collective-permute-start.17 = (bf16[4,128,512]{2,1,0:T(8,128)(2,1)S(1)}, bf16[4,128,512]{2,1,0:T(8,128)(2,1)S(1)}, u32[]{:S(2)}, u32[]{:S(2)}) collective-permute-start(bf16[4,128,512]{2,1,0:T(8,128)(2,1)S(1)} %add_convert_fusion.1), channel_id=1, source_target_pairs={{0,2},{1,3},{2,0},{3,1},{4,6},{5,7},{6,4},{7,5},{8,10},{9,11},{10,... | collective-permute-start | bytes 1572872 | tf_op jit(solution)/shard_map/ppermute | solution.py:405
  85.4 25.7 %collective-permute-start.13 = (bf16[4,128,512]{2,1,0:T(8,128)(2,1)}, bf16[4,128,512]{2,1,0:T(8,128)(2,1)S(1)}, u32[]{:S(2)}, u32[]{:S(2)}) collective-permute-start(bf16[4,128,512]{2,1,0:T(8,128)(2,1)} %get-tuple-element.45), channel_id=1, source_target_pairs={{0,1},{1,0},{2,3},{3,2},{4,5},{5,4},{6,7},{7,6},{8,9},{9,8},{10,11... | collective-permute-start | bytes 1572872 | tf_op jit(solution)/shard_map/ppermute | solution.py:405
  85.5 6.1 %collective-permute-start.14 = (bf16[4,128,512]{2,1,0:T(8,128)(2,1)}, bf16[4,128,512]{2,1,0:T(8,128)(2,1)S(1)}, u32[]{:S(2)}, u32[]{:S(2)}) collective-permute-start(bf16[4,128,512]{2,1,0:T(8,128)(2,1)} %get-tuple-element.47), channel_id=1, source_target_pairs={{0,1},{1,0},{2,3},{3,2},{4,5},{5,4},{6,7},{7,6},{8,9},{9,8},{10,11... | collective-permute-start | bytes 1572872 | tf_op jit(solution)/shard_map/ppermute | solution.py:405
  88.2 22.9 %collective-permute-start.20 = (bf16[128,512]{1,0:T(8,128)(2,1)S(1)}, bf16[128,512]{1,0:T(8,128)(2,1)S(1)}, u32[]{:S(2)}, u32[]{:S(2)}) collective-permute-start(bf16[128,512]{1,0:T(8,128)(2,1)S(1)} %get-tuple-element.72), channel_id=1, source_target_pairs={{0,12},{1,13},{2,14},{3,15},{4,0},{5,1},{6,2},{7,3},{8,4},{9,5},{1... | collective-permute-start | bytes 393224 | tf_op jit(solution)/shard_map/ppermute | solution.py:405
  88.2 22.8 %collective-permute-start.19 = (bf16[128,512]{1,0:T(8,128)(2,1)S(1)}, bf16[128,512]{1,0:T(8,128)(2,1)S(1)}, u32[]{:S(2)}, u32[]{:S(2)}) collective-permute-start(bf16[128,512]{1,0:T(8,128)(2,1)S(1)} %get-tuple-element.73), channel_id=1, source_target_pairs={{0,8},{1,9},{2,10},{3,11},{4,12},{5,13},{6,14},{7,15},{8,0},{9,1},... | collective-permute-start | bytes 393224 | tf_op jit(solution)/shard_map/ppermute | solution.py:405
  89.6 21.4 %collective-permute-start.18 = (bf16[128,512]{1,0:T(8,128)(2,1)S(1)}, bf16[128,512]{1,0:T(8,128)(2,1)S(1)}, u32[]{:S(2)}, u32[]{:S(2)}) collective-permute-start(bf16[128,512]{1,0:T(8,128)(2,1)S(1)} %get-tuple-element.74), channel_id=1, source_target_pairs={{0,4},{1,5},{2,6},{3,7},{4,8},{5,9},{6,10},{7,11},{8,12},{9,13},{1... | collective-permute-start | bytes 393224 | tf_op jit(solution)/shard_map/ppermute | solution.py:405
  91.7 19.4 %collective-permute-start.15 = (bf16[4,128,512]{2,1,0:T(8,128)(2,1)S(1)}, bf16[4,128,512]{2,1,0:T(8,128)(2,1)S(1)}, u32[]{:S(2)}, u32[]{:S(2)}) collective-permute-start(bf16[4,128,512]{2,1,0:T(8,128)(2,1)S(1)} %add_convert_fusion), channel_id=1, source_target_pairs={{0,2},{1,3},{2,0},{3,1},{4,6},{5,7},{6,4},{7,5},{8,10},{9,11},{10,... | collective-permute-start | bytes 1572872 | tf_op jit(solution)/shard_map/ppermute | solution.py:405
  111.5 10.2 %collective-permute-start.23 = (bf16[128,512]{1,0:T(8,128)(2,1)S(1)}, bf16[128,512]{1,0:T(8,128)(2,1)S(1)}, u32[]{:S(2)}, u32[]{:S(2)}) collective-permute-start(bf16[128,512]{1,0:T(8,128)(2,1)S(1)} %get-tuple-element.75), channel_id=1, source_target_pairs={{0,12},{1,13},{2,14},{3,15},{4,0},{5,1},{6,2},{7,3},{8,4},{9,5},{1... | collective-permute-start | bytes 393224 | tf_op jit(solution)/shard_map/ppermute | solution.py:405
  113.4 11.2 %collective-permute-start.22 = (bf16[128,512]{1,0:T(8,128)(2,1)S(1)}, bf16[128,512]{1,0:T(8,128)(2,1)S(1)}, u32[]{:S(2)}, u32[]{:S(2)}) collective-permute-start(bf16[128,512]{1,0:T(8,128)(2,1)S(1)} %get-tuple-element.76), channel_id=1, source_target_pairs={{0,8},{1,9},{2,10},{3,11},{4,12},{5,13},{6,14},{7,15},{8,0},{9,1},... | collective-permute-start | bytes 393224 | tf_op jit(solution)/shard_map/ppermute | solution.py:405
  113.4 11.2 %collective-permute-start.21 = (bf16[128,512]{1,0:T(8,128)(2,1)S(1)}, bf16[128,512]{1,0:T(8,128)(2,1)S(1)}, u32[]{:S(2)}, u32[]{:S(2)}) collective-permute-start(bf16[128,512]{1,0:T(8,128)(2,1)S(1)} %get-tuple-element.77), channel_id=1, source_target_pairs={{0,4},{1,5},{2,6},{3,7},{4,8},{5,9},{6,10},{7,11},{8,12},{9,13},{1... | collective-permute-start | bytes 393224 | tf_op jit(solution)/shard_map/ppermute | solution.py:405
  (11 other events, 111.7 us)

commit v6 on v5

--- a/solution.py
+++ b/solution.py
@@ -18,7 +18,7 @@
     return lax.dot_general(a, b, (contract, ((), ())), preferred_element_type=jnp.float32)
 
 CHUNKS = (2, 2)
-STEP_HEADS = (4, 2)
+PAIR = 2
 PIECE = 32
 
 
@@ -39,18 +39,18 @@
 
 def gradient_kernel(
     owner_ref, tokens_ref, place_ref,
-    q_ref, g_ref, leaf_k_ref, leaf_v_ref, leaf_ref, mask_ref, *rest,
-    prompts, per_prefix, block_len, planes, ranks, steps, step_heads,
+    q_next, g_next, q_here, g_here, leaf_k_ref, leaf_v_ref, leaf_ref, mask_ref, *rest,
+    prompts, per_prefix, block_len, planes, ranks, steps,
 ):
     sources = rest[:2 * ranks]
     dleaf_ref, probs_out, dscore_out, kcat_t, vcat_t = rest[2 * ranks:2 * ranks + 5]
     totals = rest[2 * ranks + 5:4 * ranks + 5]
-    (kv, kcat, vcat, bias, q_pick, g_pick, q2, g2, scores, dprob, probs_b, dscore,
+    (kv, kcat, vcat, bias, q_pick, g_pick, q2, g2, tops, scores, dprob, probs_b, dscore,
      dk_sum, dv_sum, sems, out_sems) = rest[4 * ranks + 5:]
     step = pl.program_id(0)
-    per_group = GQ // step_heads
-    count = q_ref.shape[0]
-    columns = step_heads * count
+    per_group = GQ // PAIR
+    count = q_next.shape[0]
+    columns = PAIR * count
     span = per_prefix * block_len
     keys = span + count
     half = sources[0].shape[1] // 2
@@ -99,53 +99,50 @@
         pick = (in_first == left).astype(jnp.float32)
         q_pick[...] = pick.astype(jnp.bfloat16)
         g_pick[...] = (pick * mask_col).astype(jnp.bfloat16)
-        for n in range(step_heads):
+        for n in range(PAIR):
             bias[:, n * count:(n + 1) * count] = allowed_bias
         for ref in totals:
             ref[...] = jnp.zeros_like(ref)
-        dk_sum[...] = jnp.zeros_like(dk_sum)
-        dv_sum[...] = jnp.zeros_like(dv_sum)
+        for ref in (dk_sum, dv_sum, q2, g2):
+            ref[...] = jnp.zeros_like(ref)
+        probs_b[0, 1] = jnp.zeros((keys, columns), jnp.bfloat16)
+        dscore[0, 1] = jnp.zeros((keys, columns), jnp.bfloat16)
         for n in range(2 * per_prefix):
             target = kv.at[pl.ds(n * block_len, block_len), :]
             pltpu.make_async_copy(
                 sources[0].at[pl.ds(0, block_len), :], target, sems.at[n]
             ).wait()
 
-    new_group = lax.rem(step, per_group) == 0
-
-    @pl.when(new_group & (step < steps))
-    def _():
-        group = step // per_group
+    @pl.when((lax.rem(2 * step, per_group) == 0) & (step < steps))
+    def _():
+        group = 2 * step // per_group
         for cat, cat_t, cols, leaf in (
             (kcat, kcat_t, key_columns(group), leaf_k_ref),
             (vcat, vcat_t, value_columns(group), leaf_v_ref),
         ):
             for side in range(2):
                 lanes = slice(side * HEAD_SIZE, (side + 1) * HEAD_SIZE)
-                cat[0:span, lanes] = kv[side * span:(side + 1) * span, cols]
-                cat[span:, lanes] = leaf[...]
-            cat_t[0] = cat[...].T
+                cat[lax.rem(group, 2), 0:span, lanes] = kv[side * span:(side + 1) * span, cols]
+                cat[lax.rem(group, 2), span:, lanes] = leaf[...]
+            cat_t[0] = cat[lax.rem(group, 2)].T
 
     slot = lax.rem(step, 2)
     before = 1 - slot
 
-    def copies_out(at, slot):
+    def copies_out(step):
+        slot = lax.rem(step, 2)
         return [
-            pltpu.make_async_copy(probs_b.at[slot], probs_out.at[at], out_sems.at[0, slot]),
-            pltpu.make_async_copy(dscore.at[slot], dscore_out.at[at], out_sems.at[1, slot]),
+            pltpu.make_async_copy(held.at[slot], out.at[pl.ds(2 * (step - 1), 2)], out_sems.at[n, slot])
+            for n, (held, out) in enumerate(((probs_b, probs_out), (dscore, dscore_out)))
         ]
 
-    def later_rows():
-        dk_sum[...] += dot(dscore[before], q2[...], ((1,), (0,)))
-        dv_sum[...] += dot(probs_b[before], g2[...], ((1,), (0,)))
-
-
-    def pick(source, chosen):
-        parts = []
-        for n in range(step_heads):
-            part = source[:, n * HEAD_SIZE:(n + 1) * HEAD_SIZE]
-            parts.append(jnp.concatenate([part, part], axis=1) * chosen[...])
-        return jnp.concatenate(parts, axis=0)
+    def group_slot(pair):
+        return lax.rem(pair // per_group, 2)
+
+    def rows(slot, side, pair):
+        into = group_slot(pair)
+        dk_sum[into] += dot(dscore[slot, side], q2[side], ((1,), (0,)))
+        dv_sum[into] += dot(probs_b[slot, side], g2[side], ((1,), (0,)))
 
     def fold(value, op):
         value = value.reshape(PIECE // 8, 8, columns)
@@ -154,115 +151,135 @@
             total = op(total, value[n])
         return total
 
-    def score(new_q):
-        product = dot(kcat[...], new_q, ((1,), (1,)))
+    def pick_side(source, chosen):
+        parts = []
+        for n in range(PAIR):
+            part = source[:, n * HEAD_SIZE:(n + 1) * HEAD_SIZE]
+            parts.append(jnp.concatenate([part, part], axis=1) * chosen[...])
+        return jnp.concatenate(parts, axis=0)
+
+    def first(side, pair, q_ref, g_ref):
+        new_q = pick_side(q_ref, q_pick)
+        new_g = pick_side(g_ref, g_pick)
+        q2[side] = new_q
+        g2[side] = new_g
+        product = dot(kcat[group_slot(pair)], new_q, ((1,), (1,)))
         top = None
         for at in range(0, keys, PIECE):
             piece = product[at:at + PIECE]
             if at >= span:
                 piece = piece + bias[at - span:at - span + PIECE, :]
-            scores[at:at + PIECE, :] = piece
+            scores[side, at:at + PIECE, :] = piece
             piece = fold(piece, jnp.maximum)
             top = piece if top is None else jnp.maximum(top, piece)
-        return jnp.max(top, axis=0, keepdims=True)
-
-    def sums(top):
+        tops[side] = jnp.broadcast_to(jnp.max(top, axis=0, keepdims=True), (8, columns))
+        dprob[side] = dot(vcat[group_slot(pair)], new_g, ((1,), (1,)))
+
+    def sums(side):
+        top = tops[side, 0:1, :]
         total = jnp.zeros((8, columns), jnp.float32)
         delta = jnp.zeros((8, columns), jnp.float32)
         for at in range(0, keys, PIECE):
-            weight = jnp.exp2((scores[at:at + PIECE, :] - top) * (SCALE * LOG2E))
+            weight = jnp.exp2((scores[side, at:at + PIECE, :] - top) * (SCALE * LOG2E))
             total = total + fold(weight, jnp.add)
-            delta = delta + fold(weight * dprob[at:at + PIECE, :], jnp.add)
+            delta = delta + fold(weight * dprob[side, at:at + PIECE, :], jnp.add)
         total = jnp.sum(total, axis=0, keepdims=True)
-        return total, jnp.sum(delta, axis=0, keepdims=True) / total
-
-    def finish(top, total, delta):
+        return top, total, jnp.sum(delta, axis=0, keepdims=True) / total
+
+    def finish(side, top, total, delta):
         shift = jnp.log2(total)
         for at in range(0, keys, PIECE):
-            power = (scores[at:at + PIECE, :] - top) * (SCALE * LOG2E)
+            power = (scores[side, at:at + PIECE, :] - top) * (SCALE * LOG2E)
             probs = jnp.exp2(power - shift)
-            probs_b[slot, at:at + PIECE, :] = probs.astype(jnp.bfloat16)
-            dscore[slot, at:at + PIECE, :] = (probs * (dprob[at:at + PIECE, :] - delta)).astype(jnp.bfloat16)
-
-    def work(later):
-        new_q = pick(q_ref, q_pick)
-        new_g = pick(g_ref, g_pick)
-        top = score(new_q)
-        if later:
-            later_rows()
-        dprob[...] = dot(vcat[...], new_g, ((1,), (1,)))
-        total, delta = sums(top)
-        finish(top, total, delta)
-        q2[...] = new_q
-        g2[...] = new_g
-
-    @pl.when((step >= 2) & (step < steps))
-    def _():
-        for copy in copies_out(step - 2, slot):
+            probs_b[slot, side, at:at + PIECE, :] = probs.astype(jnp.bfloat16)
+            dscore[slot, side, at:at + PIECE, :] = (
+                probs * (dprob[side, at:at + PIECE, :] - delta)
+            ).astype(jnp.bfloat16)
+
+    def work(more):
+        rows(before, 1, jnp.maximum(2 * step - 3, 0))
+        found = sums(0)
+        first(1, 2 * step - 1, q_here, g_here)
+        finish(0, *found)
+        found = sums(1)
+        rows(slot, 0, 2 * step - 2)
+        if more:
+            first(0, 2 * step, q_next, g_next)
+        finish(1, *found)
+
+    @pl.when((step >= 3) & (step <= steps))
+    def _():
+        for copy in copies_out(step - 2):
             copy.wait()
 
     @pl.when(step == 0)
     def _():
+        first(0, 0, q_next, g_next)
+
+    @pl.when((step > 0) & (step < steps))
+    def _():
+        work(True)
+
+    @pl.when(step == steps)
+    def _():
         work(False)
 
-    @pl.when((step > 0) & (step < steps))
-    def _():
-        work(True)
-
-    @pl.when(step < steps)
-    def _():
-        for copy in copies_out(step, slot):
+    @pl.when((step > 0) & (step <= steps))
+    def _():
+        for copy in copies_out(step):
             copy.start()
 
-    @pl.when(step == steps)
-    def _():
-        later_rows()
-        for at in range(max(steps - 2, 0), steps):
-            for copy in copies_out(at, at % 2):
+    @pl.when(step == steps + 1)
+    def _():
+        rows(before, 1, 2 * step - 3)
+        for at in range(max(steps - 1, 1), steps + 1):
+            for copy in copies_out(at):
                 copy.wait()
 
-    @pl.when(new_group & (step > 0))
-    def _():
-        group = step // per_group - 1
+    @pl.when((lax.rem(2 * step - 2, per_group) == 0) & (step > 1))
+    def _():
+        group = (2 * step - 2) // per_group - 1
+        at = lax.rem(group, 2)
         for total_ref, cols, factor in (
             (dk_sum, key_columns(group), SCALE), (dv_sum, value_columns(group), 1.0)
         ):
-            leaf = (total_ref[span:, :HEAD_SIZE] + total_ref[span:, HEAD_SIZE:]) * factor
+            leaf = (total_ref[at, span:, :HEAD_SIZE] + total_ref[at, span:, HEAD_SIZE:]) * factor
             dleaf_ref[:, cols] = leaf.astype(jnp.bfloat16)
             for side in range(2):
                 lanes = slice(side * HEAD_SIZE, (side + 1) * HEAD_SIZE)
                 for j in range(per_prefix):
-                    value = total_ref[j * block_len:(j + 1) * block_len, lanes] * factor
+                    value = total_ref[at, j * block_len:(j + 1) * block_len, lanes] * factor
                     value = value.astype(jnp.bfloat16)
                     same_core, row, ahead = block_place(side, j)
-                    for at, ref in enumerate(totals):
-                        @pl.when((same_core == (at % 2 == 0)) & (row == at // 2))
+                    for holder, ref in enumerate(totals):
+                        @pl.when((same_core == (holder % 2 == 0)) & (row == holder // 2))
                         def _():
                             ref[ahead, :, cols] += value
 
-        dk_sum[...] = jnp.zeros_like(dk_sum)
-        dv_sum[...] = jnp.zeros_like(dv_sum)
+            total_ref[at] = jnp.zeros((keys, 2 * HEAD_SIZE), jnp.float32)
 
 
 def query_kernel(
-    tokens_ref, place_ref, probs_ref, dscore_ref, vcat_t, kcat_t, *rest, prompts, step_heads, chained
+    tokens_ref, place_ref, probs_ref, dscore_ref, vcat_t, kcat_t, *rest, prompts, chained
 ):
     out_ref, dq_ref = rest[2 * chained:]
     count = out_ref.shape[0]
     border = prefixes_here(tokens_ref, place_ref[0], count, prompts)[2]
-    columns = step_heads * count
+    columns = PAIR * count
     token_at = lax.rem(lax.broadcasted_iota(jnp.int32, (HEAD_SIZE, columns), 1), count)
     first_side = token_at < border
     for source, cat_t, factor, target in (
         (probs_ref, vcat_t, 1.0, out_ref), (dscore_ref, kcat_t, SCALE, dq_ref)
     ):
-        both = dot(cat_t[0], source[0], ((1,), (0,)))
-        mine = jnp.where(first_side, both[:HEAD_SIZE], both[HEAD_SIZE:])
-        if factor != 1.0:
-            mine = mine * factor
-        for n in range(step_heads):
-            lanes = slice(n * HEAD_SIZE, (n + 1) * HEAD_SIZE)
-            target[:, lanes] = mine[:, n * count:(n + 1) * count].T.astype(jnp.bfloat16)
+        for pair in range(source.shape[0]):
+            both = dot(cat_t[0], source[pair], ((1,), (0,)))
+            mine = jnp.where(first_side, both[:HEAD_SIZE], both[HEAD_SIZE:])
+            if factor != 1.0:
+                mine = mine * factor
+            for n in range(PAIR):
+                at = (pair * PAIR + n) * HEAD_SIZE
+                turned = mine[:, n * count:(n + 1) * count].T
+                target[:, at:at + HEAD_SIZE] = turned.astype(jnp.bfloat16)
 
 
 def full(shape):
@@ -278,61 +295,65 @@
     keys = span + count
     width = sources[0].shape[1]
     groups = CHUNKS[chunk]
-    step_heads = STEP_HEADS[chunk]
     skipped = sum(CHUNKS[:chunk])
     heads = groups * GQ
-    steps = heads // step_heads
-    per_group = GQ // step_heads
-    skipped_steps = skipped * per_group
-    columns = step_heads * count
+    pairs = heads // PAIR
+    steps = pairs // 2
+    per_group = GQ // PAIR
+    skipped_pairs = skipped * per_group
+    columns = PAIR * count
     bf16, f32 = jnp.bfloat16, jnp.float32
 
-    def now(i):
-        return jnp.minimum(i, steps - 1)
-
-    slab = pl.BlockSpec(
-        (count, step_heads * HEAD_SIZE), lambda i, *_: (0, skipped_steps + now(i))
+    def following(i):
+        return jnp.minimum(2 * i, pairs - 1)
+
+    def group_of(i):
+        return following(i) // per_group
+
+    def here(i):
+        return jnp.clip(2 * i - 1, 0, pairs - 1)
+
+    slab = (count, PAIR * HEAD_SIZE)
+    ahead = pl.BlockSpec(slab, lambda i, *_: (0, skipped_pairs + following(i)))
+    present = pl.BlockSpec(slab, lambda i, *_: (0, skipped_pairs + here(i)))
+    leaf_k = pl.BlockSpec((count, HEAD_SIZE), lambda i, *_: (0, skipped + group_of(i)))
+    leaf_v = pl.BlockSpec(
+        (count, HEAD_SIZE), lambda i, *_: (0, KEY_VALUE_HEADS + skipped + group_of(i))
     )
-    leaf_k = pl.BlockSpec(
-        (count, HEAD_SIZE), lambda i, *_: (0, skipped + now(i) // per_group)
-    )
-    leaf_v = pl.BlockSpec(
-        (count, HEAD_SIZE),
-        lambda i, *_: (0, KEY_VALUE_HEADS + skipped + now(i) // per_group),
-    )
-    cat_t = pl.BlockSpec((1, 2 * HEAD_SIZE, keys), lambda i, *_: (now(i) // per_group, 0, 0))
+    cat_t = pl.BlockSpec((1, 2 * HEAD_SIZE, keys), lambda i, *_: (group_of(i), 0, 0))
     anywhere = pl.BlockSpec(memory_space=pl.ANY)
     sum_shape = (planes, block_len, width)
-    probs_shape = jax.ShapeDtypeStruct((steps, keys, columns), bf16)
+    probs_shape = jax.ShapeDtypeStruct((pairs, keys, columns), bf16)
     cat_t_shape = jax.ShapeDtypeStruct((groups, 2 * HEAD_SIZE, keys), bf16)
     return pl.pallas_call(
         functools.partial(
             gradient_kernel, prompts=prompts, per_prefix=per_prefix, block_len=block_len,
-            planes=planes, ranks=ranks, steps=steps, step_heads=step_heads,
+            planes=planes, ranks=ranks, steps=steps,
         ),
         grid_spec=pltpu.PrefetchScalarGridSpec(
             num_scalar_prefetch=3,
-            grid=(steps + 1,),
+            grid=(steps + 2,),
             in_specs=[
-                slab, slab, leaf_k, leaf_v, full(leaf.shape), full(mask.shape),
+                ahead, ahead, present, present, leaf_k, leaf_v, full(leaf.shape), full(mask.shape),
             ] + [anywhere] * (2 * ranks),
             out_specs=[full((count, width)), anywhere, anywhere, cat_t, cat_t]
             + [full(sum_shape)] * (2 * ranks),
             scratch_shapes=[
                 pltpu.VMEM((2 * span, width), bf16),
-                pltpu.VMEM((keys, 2 * HEAD_SIZE), bf16),
-                pltpu.VMEM((keys, 2 * HEAD_SIZE), bf16),
+                pltpu.VMEM((2, keys, 2 * HEAD_SIZE), bf16),
+                pltpu.VMEM((2, keys, 2 * HEAD_SIZE), bf16),
                 pltpu.VMEM((count, columns), f32),
                 pltpu.VMEM((count, 2 * HEAD_SIZE), bf16),
                 pltpu.VMEM((count, 2 * HEAD_SIZE), bf16),
-                pltpu.VMEM((columns, 2 * HEAD_SIZE), bf16),
-                pltpu.VMEM((columns, 2 * HEAD_SIZE), bf16),
-                pltpu.VMEM((keys, columns), f32),
-                pltpu.VMEM((keys, columns), f32),
-                pltpu.VMEM((2, keys, columns), bf16),
-                pltpu.VMEM((2, keys, columns), bf16),
-                pltpu.VMEM((keys, 2 * HEAD_SIZE), f32),
-                pltpu.VMEM((keys, 2 * HEAD_SIZE), f32),
+                pltpu.VMEM((2, columns, 2 * HEAD_SIZE), bf16),
+                pltpu.VMEM((2, columns, 2 * HEAD_SIZE), bf16),
+                pltpu.VMEM((2, 8, columns), f32),
+                pltpu.VMEM((2, keys, columns), f32),
+                pltpu.VMEM((2, keys, columns), f32),
+                pltpu.VMEM((2, 2, keys, columns), bf16),
+                pltpu.VMEM((2, 2, keys, columns), bf16),
+                pltpu.VMEM((2, keys, 2 * HEAD_SIZE), f32),
+                pltpu.VMEM((2, keys, 2 * HEAD_SIZE), f32),
                 pltpu.SemaphoreType.DMA((2 * per_prefix,)),
                 pltpu.SemaphoreType.DMA((2, 2)),
             ],
@@ -348,28 +369,30 @@
             flops=heads * 4 * 2 * keys * 256 * 256, bytes_accessed=groups * 8 * 2**20,
             transcendentals=2 * heads * keys * count,
         ),
-    )(owner, tokens, place, q, g, leaf_kv, leaf_kv, leaf, mask, *sources)
+    )(owner, tokens, place, q, g, q, g, leaf_kv, leaf_kv, leaf, mask, *sources)
 
 
 def queries(chunk, part, tokens, place, probs, dscore, kcat_t, vcat_t, like, earlier):
-    step_heads = STEP_HEADS[chunk]
-    per_group = GQ // step_heads
     count, keys = like.shape[0], probs.shape[1]
-    first = (sum(CHUNKS[:chunk]) + part) * per_group
+    together = 2
+    steps = GQ // (PAIR * together)
+    first = (sum(CHUNKS[:chunk]) + part) * steps
     chained = len(earlier) > 0
     block = pl.BlockSpec(
-        (1, keys, step_heads * count), lambda i, *_: (part * per_group + i, 0, 0)
+        (together, keys, PAIR * count), lambda i, *_: (part * steps + i, 0, 0)
     )
     cat_t = pl.BlockSpec((1, 2 * HEAD_SIZE, keys), lambda i, *_: (part, 0, 0))
-    slab = pl.BlockSpec((count, step_heads * HEAD_SIZE), lambda i, *_: (0, first + i))
+    slab = pl.BlockSpec(
+        (count, together * PAIR * HEAD_SIZE), lambda i, *_: (0, first + i)
+    )
     anywhere = pl.BlockSpec(memory_space=pl.ANY)
     return pl.pallas_call(
         functools.partial(
-            query_kernel, prompts=tokens.shape[0], step_heads=step_heads, chained=chained
+            query_kernel, prompts=tokens.shape[0], chained=chained
         ),
         grid_spec=pltpu.PrefetchScalarGridSpec(
             num_scalar_prefetch=2,
-            grid=(per_group,),
+            grid=(steps,),
             in_specs=[block, block, cat_t, cat_t] + [anywhere] * len(earlier),
             out_specs=[slab, slab],
         ),
@@ -458,7 +481,7 @@
     earlier = ()
     work = [(chunk, part) for chunk in range(chunks) for part in range(CHUNKS[chunk])]
     for at, (chunk, part) in enumerate(work):
-        if at < len(work) - 1:
+        if at < len(work) - 2:
             begun = [away for total in totals[:-1] for away in total[1]]
             begun += [parts[-1][1]] if ranks == 2 else []
         else:

time: 126 us -> 121 us (0.960)
  waiting for transfers between devices: 24.4 us -> 21.5 us
  Pallas kernels: 68 us -> 66.1 us
    ppermute x24, waiting for transfers between devices: 24.4 us -> 21.5 us  [send(): return lax.ppermute(array, 'dp', pairs)]
    pallas_call x4, Pallas kernels: 24.2 us -> 22.5 us  [queries(): pl.pallas_call(functools.partial(query_kernel, prompts=tokens.shape[0], c...]
  transfers between devices with their start and end apart: 24 -> 24, of which waited for: 8 -> 8; matrix products, arithmetic and copies ran while one was open for 4% -> 4% of each run, Pallas kernels for 54% -> 55%
where the time goes in v6:
time: 121 us
  Pallas kernels  66.1 us (55%)
  starting transfers between devices  24 us (20%)
  waiting for transfers between devices  21.5 us (18%)
  local copies, waits for them, and re-layouts  4.68 us (4%)
  other arithmetic  3.6 us (3%)
    pallas_call x2, Pallas kernels, gradients(): pl.pallas_call(functools.partial(gradient_kernel, prompts=prompts, per_pr...  43.6 us
    ppermute x24, starting transfers between devices, send(): return lax.ppermute(array, 'dp', pairs)  24 us
    pallas_call x4, Pallas kernels, queries(): pl.pallas_call(functools.partial(query_kernel, prompts=tokens.shape[0], c...  22.5 us
    ppermute x24, waiting for transfers between devices, send(): return lax.ppermute(array, 'dp', pairs)  21.5 us
  transfers between devices with their start and end apart: 24, of which 8 were waited for; matrix products, arithmetic and copies ran while one was open for 4% of the time, Pallas kernels for 55%

profile of v6, /device:TPU:0, one launch (start us, length us, event | category | flops | bytes accessed | tf_op | source)
XLA Modules:
  0.0 120.8 jit_solution(18288298457280168974)
XLA Ops:
  1.6 5.1 %collective-permute-start.6 = (bf16[128,512]{1,0:T(8,128)(2,1)S(1)}, bf16[128,512]{1,0:T(8,128)(2,1)S(1)}, u32[]{:S(2)}, u32[]{:S(2)}) collective-permute-start(bf16[128,512]{1,0:T(8,128)(2,1)S(1)} %pad_maximum_fusion.5), channel_id=1, source_target_pairs={{0,12},{1,13},{2,14},{3,15},{4,0},{5,1},{6,2},{7,3},{8,4},{9,5},{1... | collective-permute-start | bytes 393224 | tf_op jit(solution)/shard_map/ppermute | solution.py:428
  6.7 1.0 collective-permute-start.4
  7.7 2.9 %collective-permute-done.6 = bf16[128,512]{1,0:T(8,128)(2,1)S(1)} collective-permute-done((bf16[128,512]{1,0:T(8,128)(2,1)S(1)}, bf16[128,512]{1,0:T(8,128)(2,1)S(1)}, u32[]{:S(2)}, u32[]{:S(2)}) %collective-permute-start.6) | collective-permute-done | bytes 131104 | tf_op jit(solution)/shard_map/ppermute | solution.py:428
  10.6 7.3 %collective-permute-done.5 = bf16[128,512]{1,0:T(8,128)(2,1)S(1)} collective-permute-done((bf16[128,512]{1,0:T(8,128)(2,1)S(1)}, bf16[128,512]{1,0:T(8,128)(2,1)S(1)}, u32[]{:S(2)}, u32[]{:S(2)}) %collective-permute-start.5) | collective-permute-done | bytes 131104 | tf_op jit(solution)/shard_map/ppermute | solution.py:428
  18.0 1.6 %collective-permute-start.8 = (bf16[512,512]{1,0:T(8,128)(2,1)S(1)}, bf16[512,512]{1,0:T(8,128)(2,1)S(1)}, u32[]{:S(2)}, u32[]{:S(2)}) collective-permute-start(bf16[512,512]{1,0:T(8,128)(2,1)S(1)} %pad_maximum_fusion.1.rest_0_), channel_id=1, source_target_pairs={{0,2},{1,3},{2,0},{3,1},{4,6},{5,7},{6,4},{7,5},{8,10},{9,11},{10,... | collective-permute-start | bytes 1572872 | tf_op jit(solution)/shard_map/ppermute | solution.py:428
  19.6 1.7 %collective-permute-start.2 = (bf16[128,512]{1,0:T(8,128)(2,1)S(1)}, bf16[128,512]{1,0:T(8,128)(2,1)S(1)}, u32[]{:S(2)}, u32[]{:S(2)}) collective-permute-start(bf16[128,512]{1,0:T(8,128)(2,1)S(1)} %pad_maximum_fusion.4), channel_id=1, source_target_pairs={{0,12},{1,13},{2,14},{3,15},{4,0},{5,1},{6,2},{7,3},{8,4},{9,5},{1... | collective-permute-start | bytes 393224 | tf_op jit(solution)/shard_map/ppermute | solution.py:428
  21.2 1.1 collective-permute-start.1
  22.3 1.9 %collective-permute-start = (bf16[128,512]{1,0:T(8,128)(2,1)S(1)}, bf16[128,512]{1,0:T(8,128)(2,1)S(1)}, u32[]{:S(2)}, u32[]{:S(2)}) collective-permute-start(bf16[128,512]{1,0:T(8,128)(2,1)S(1)} %pad_maximum_fusion.4), channel_id=1, source_target_pairs={{0,4},{1,5},{2,6},{3,7},{4,8},{5,9},{6,10},{7,11},{8,12},{9,13},{1... | collective-permute-start | bytes 393224 | tf_op jit(solution)/shard_map/ppermute | solution.py:428
  24.3 1.1 collective-permute-done.2
  25.4 7.9 %collective-permute-done.1 = bf16[128,512]{1,0:T(8,128)(2,1)S(1)} collective-permute-done((bf16[128,512]{1,0:T(8,128)(2,1)S(1)}, bf16[128,512]{1,0:T(8,128)(2,1)S(1)}, u32[]{:S(2)}, u32[]{:S(2)}) %collective-permute-start.1) | collective-permute-done | bytes 131104 | tf_op jit(solution)/shard_map/ppermute | solution.py:428
  36.9 21.7 %shard_map.111 = (bf16[256,512]{1,0:T(8,128)(2,1)}, bf16[8,768,512]{2,1,0:T(8,128)(2,1)}, bf16[8,768,512]{2,1,0:T(8,128)(2,1)}, bf16[2,256,768]{2,1,0:T(8,128)(2...) custom-call(s32[16]{0:T(128)} %owner_ref.3, ...), custom_call_target="tpu_custom_call" | custom-call | flops 6442450944 | bytes 16777216 | tf_op jit(solution)/shard_map/pallas_call | solution.py:328
  59.3 1.0 fusion.10
  60.8 1.2 add_convert_fusion.1
  63.4 21.9 %shard_map.112 = (bf16[256,512]{1,0:T(8,128)(2,1)}, bf16[8,768,512]{2,1,0:T(8,128)(2,1)}, bf16[8,768,512]{2,1,0:T(8,128)(2,1)}, bf16[2,256,768]{2,1,0:T(8,128)(2...) custom-call(s32[16]{0:T(128)} %owner_ref.3, ...), custom_call_target="tpu_custom_call" | custom-call | flops 6442450944 | bytes 16777216 | tf_op jit(solution)/shard_map/pallas_call | solution.py:328
  85.9 1.0 fusion.11
  88.1 1.4 %collective-permute-start.19 = (bf16[128,512]{1,0:T(8,128)(2,1)S(1)}, bf16[128,512]{1,0:T(8,128)(2,1)S(1)}, u32[]{:S(2)}, u32[]{:S(2)}) collective-permute-start(bf16[128,512]{1,0:T(8,128)(2,1)S(1)} %get-tuple-element.73), channel_id=1, source_target_pairs={{0,8},{1,9},{2,10},{3,11},{4,12},{5,13},{6,14},{7,15},{8,0},{9,1},... | collective-permute-start | bytes 393224 | tf_op jit(solution)/shard_map/ppermute | solution.py:428
  89.5 1.9 %collective-permute-start.18 = (bf16[128,512]{1,0:T(8,128)(2,1)S(1)}, bf16[128,512]{1,0:T(8,128)(2,1)S(1)}, u32[]{:S(2)}, u32[]{:S(2)}) collective-permute-start(bf16[128,512]{1,0:T(8,128)(2,1)S(1)} %get-tuple-element.74), channel_id=1, source_target_pairs={{0,4},{1,5},{2,6},{3,7},{4,8},{5,9},{6,10},{7,11},{8,12},{9,13},{1... | collective-permute-start | bytes 393224 | tf_op jit(solution)/shard_map/ppermute | solution.py:428
  91.6 1.6 %collective-permute-start.15 = (bf16[4,128,512]{2,1,0:T(8,128)(2,1)S(1)}, bf16[4,128,512]{2,1,0:T(8,128)(2,1)S(1)}, u32[]{:S(2)}, u32[]{:S(2)}) collective-permute-start(bf16[4,128,512]{2,1,0:T(8,128)(2,1)S(1)} %add_convert_fusion), channel_id=1, source_target_pairs={{0,2},{1,3},{2,0},{3,1},{4,6},{5,7},{6,4},{7,5},{8,10},{9,11},{10,... | collective-permute-start | bytes 1572872 | tf_op jit(solution)/shard_map/ppermute | solution.py:428
  93.2 5.6 %shard_map.113 = (bf16[256,4096]{1,0:T(8,128)(2,1)}, bf16[256,4096]{1,0:T(8,128)(2,1)}) custom-call(s32[4]{0:T(128)} %tokens_ref.11, s32[1]{0:T(128)} %bitcast.place_ref, bf16[8,768,512]{2,1,0:T(8,128)(2,1)} %get-tuple-element.56.probs_ref, bf16[8,768,512]{2,1,0:T(8,128)(2,1)} %get-tuple-element.57.dscore_ref, ...), custom_call_target="tpu_custom_call" | custom-call | flops 1610612736 | bytes 8388608 | tf_op jit(solution)/shard_map/pallas_call | solution.py:389
  98.8 5.7 %shard_map.114 = (bf16[256,4096]{1,0:T(8,128)(2,1)}, bf16[256,4096]{1,0:T(8,128)(2,1)}) custom-call(s32[4]{0:T(128)} %tokens_ref.11, s32[1]{0:T(128)} %bitcast.place_ref, bf16[8,768,512]{2,1,0:T(8,128)(2,1)} %get-tuple-element.56.probs_ref, bf16[8,768,512]{2,1,0:T(8,128)(2,1)} %get-tuple-element.57.dscore_ref, ...), custom_call_target="tpu_custom_call", output_to_operand_aliasing={{0}: (6, {}), {1}: (7, {})} | custom-call | flops 1610612736 | bytes 8388608 | tf_op jit(solution)/shard_map/pallas_call | solution.py:389
  105.0 2.2 %collective-permute-start.23 = (bf16[128,512]{1,0:T(8,128)(2,1)S(1)}, bf16[128,512]{1,0:T(8,128)(2,1)S(1)}, u32[]{:S(2)}, u32[]{:S(2)}) collective-permute-start(bf16[128,512]{1,0:T(8,128)(2,1)S(1)} %get-tuple-element.75), channel_id=1, source_target_pairs={{0,12},{1,13},{2,14},{3,15},{4,0},{5,1},{6,2},{7,3},{8,4},{9,5},{1... | collective-permute-start | bytes 393224 | tf_op jit(solution)/shard_map/ppermute | solution.py:428
  107.2 1.5 %collective-permute-start.21 = (bf16[128,512]{1,0:T(8,128)(2,1)S(1)}, bf16[128,512]{1,0:T(8,128)(2,1)S(1)}, u32[]{:S(2)}, u32[]{:S(2)}) collective-permute-start(bf16[128,512]{1,0:T(8,128)(2,1)S(1)} %get-tuple-element.77), channel_id=1, source_target_pairs={{0,4},{1,5},{2,6},{3,7},{4,8},{5,9},{6,10},{7,11},{8,12},{9,13},{1... | collective-permute-start | bytes 393224 | tf_op jit(solution)/shard_map/ppermute | solution.py:428
  108.7 5.6 %shard_map.115 = (bf16[256,4096]{1,0:T(8,128)(2,1)}, bf16[256,4096]{1,0:T(8,128)(2,1)}) custom-call(s32[4]{0:T(128)} %tokens_ref.11, s32[1]{0:T(128)} %bitcast.place_ref, bf16[8,768,512]{2,1,0:T(8,128)(2,1)} %get-tuple-element.49.probs_ref, bf16[8,768,512]{2,1,0:T(8,128)(2,1)} %get-tuple-element.50.dscore_ref, ...), custom_call_target="tpu_custom_call", output_to_operand_aliasing={{0}: (6, {}), {1}: (7, {})} | custom-call | flops 1610612736 | bytes 8388608 | tf_op jit(solution)/shard_map/pallas_call | solution.py:389
  114.3 5.6 %shard_map.116 = (bf16[256,4096]{1,0:T(8,128)(2,1)}, bf16[256,4096]{1,0:T(8,128)(2,1)}) custom-call(s32[4]{0:T(128)} %tokens_ref.11, s32[1]{0:T(128)} %bitcast.place_ref, bf16[8,768,512]{2,1,0:T(8,128)(2,1)} %get-tuple-element.49.probs_ref, bf16[8,768,512]{2,1,0:T(8,128)(2,1)} %get-tuple-element.50.dscore_ref, ...), custom_call_target="tpu_custom_call", output_to_operand_aliasing={{0}: (6, {}), {1}: (7, {})} | custom-call | flops 1610612736 | bytes 8388608 | tf_op jit(solution)/shard_map/pallas_call | solution.py:389
  (71 shorter events, 10.4 us)
Async XLA Ops:
  1.6 9.0 %collective-permute-start.6 = (bf16[128,512]{1,0:T(8,128)(2,1)S(1)}, bf16[128,512]{1,0:T(8,128)(2,1)S(1)}, u32[]{:S(2)}, u32[]{:S(2)}) collective-permute-start(bf16[128,512]{1,0:T(8,128)(2,1)S(1)} %pad_maximum_fusion.5), channel_id=1, source_target_pairs={{0,12},{1,13},{2,14},{3,15},{4,0},{5,1},{6,2},{7,3},{8,4},{9,5},{1... | collective-permute-start | bytes 393224 | tf_op jit(solution)/shard_map/ppermute | solution.py:428
  6.7 11.2 %collective-permute-start.5 = (bf16[128,512]{1,0:T(8,128)(2,1)S(1)}, bf16[128,512]{1,0:T(8,128)(2,1)S(1)}, u32[]{:S(2)}, u32[]{:S(2)}) collective-permute-start(bf16[128,512]{1,0:T(8,128)(2,1)S(1)} %pad_maximum_fusion.5), channel_id=1, source_target_pairs={{0,8},{1,9},{2,10},{3,11},{4,12},{5,13},{6,14},{7,15},{8,0},{9,1},... | collective-permute-start | bytes 393224 | tf_op jit(solution)/shard_map/ppermute | solution.py:428
  6.7 11.2 %collective-permute-start.4 = (bf16[128,512]{1,0:T(8,128)(2,1)S(1)}, bf16[128,512]{1,0:T(8,128)(2,1)S(1)}, u32[]{:S(2)}, u32[]{:S(2)}) collective-permute-start(bf16[128,512]{1,0:T(8,128)(2,1)S(1)} %pad_maximum_fusion.5), channel_id=1, source_target_pairs={{0,4},{1,5},{2,6},{3,7},{4,8},{5,9},{6,10},{7,11},{8,12},{9,13},{1... | collective-permute-start | bytes 393224 | tf_op jit(solution)/shard_map/ppermute | solution.py:428
  18.0 15.5 %collective-permute-start.8 = (bf16[512,512]{1,0:T(8,128)(2,1)S(1)}, bf16[512,512]{1,0:T(8,128)(2,1)S(1)}, u32[]{:S(2)}, u32[]{:S(2)}) collective-permute-start(bf16[512,512]{1,0:T(8,128)(2,1)S(1)} %pad_maximum_fusion.1.rest_0_), channel_id=1, source_target_pairs={{0,2},{1,3},{2,0},{3,1},{4,6},{5,7},{6,4},{7,5},{8,10},{9,11},{10,... | collective-permute-start | bytes 1572872 | tf_op jit(solution)/shard_map/ppermute | solution.py:428
  19.6 5.9 %collective-permute-start.2 = (bf16[128,512]{1,0:T(8,128)(2,1)S(1)}, bf16[128,512]{1,0:T(8,128)(2,1)S(1)}, u32[]{:S(2)}, u32[]{:S(2)}) collective-permute-start(bf16[128,512]{1,0:T(8,128)(2,1)S(1)} %pad_maximum_fusion.4), channel_id=1, source_target_pairs={{0,12},{1,13},{2,14},{3,15},{4,0},{5,1},{6,2},{7,3},{8,4},{9,5},{1... | collective-permute-start | bytes 393224 | tf_op jit(solution)/shard_map/ppermute | solution.py:428
  21.2 12.1 %collective-permute-start.1 = (bf16[128,512]{1,0:T(8,128)(2,1)S(1)}, bf16[128,512]{1,0:T(8,128)(2,1)S(1)}, u32[]{:S(2)}, u32[]{:S(2)}) collective-permute-start(bf16[128,512]{1,0:T(8,128)(2,1)S(1)} %pad_maximum_fusion.4), channel_id=1, source_target_pairs={{0,8},{1,9},{2,10},{3,11},{4,12},{5,13},{6,14},{7,15},{8,0},{9,1},... | collective-permute-start | bytes 393224 | tf_op jit(solution)/shard_map/ppermute | solution.py:428
  22.3 11.0 %collective-permute-start = (bf16[128,512]{1,0:T(8,128)(2,1)S(1)}, bf16[128,512]{1,0:T(8,128)(2,1)S(1)}, u32[]{:S(2)}, u32[]{:S(2)}) collective-permute-start(bf16[128,512]{1,0:T(8,128)(2,1)S(1)} %pad_maximum_fusion.4), channel_id=1, source_target_pairs={{0,4},{1,5},{2,6},{3,7},{4,8},{5,9},{6,10},{7,11},{8,12},{9,13},{1... | collective-permute-start | bytes 393224 | tf_op jit(solution)/shard_map/ppermute | solution.py:428
  24.3 11.1 %collective-permute-start.7 = (bf16[512,512]{1,0:T(8,128)(2,1)S(1)}, bf16[512,512]{1,0:T(8,128)(2,1)S(1)}, u32[]{:S(2)}, u32[]{:S(2)}) collective-permute-start(bf16[512,512]{1,0:T(8,128)(2,1)S(1)} %pad_maximum_fusion.1.rest_0_), channel_id=1, source_target_pairs={{0,1},{1,0},{2,3},{3,2},{4,5},{5,4},{6,7},{7,6},{8,9},{9,8},{10,11... | collective-permute-start | bytes 1572872 | tf_op jit(solution)/shard_map/ppermute | solution.py:428
  33.3 2.0 %collective-permute-start.3 = (bf16[512,512]{1,0:T(8,128)(2,1)S(1)}, bf16[512,512]{1,0:T(8,128)(2,1)S(1)}, u32[]{:S(2)}, u32[]{:S(2)}) collective-permute-start(bf16[512,512]{1,0:T(8,128)(2,1)S(1)} %pad_maximum_fusion.rest_0_), channel_id=1, source_target_pairs={{0,1},{1,0},{2,3},{3,2},{4,5},{5,4},{6,7},{7,6},{8,9},{9,8},{10,11... | collective-permute-start | bytes 1572872 | tf_op jit(solution)/shard_map/ppermute | solution.py:428
  33.4 2.6 %collective-permute-start.9 = (bf16[512,512]{1,0:T(8,128)(2,1)S(1)}, bf16[512,512]{1,0:T(8,128)(2,1)S(1)}, u32[]{:S(2)}, u32[]{:S(2)}) collective-permute-start(bf16[512,512]{1,0:T(8,128)(2,1)S(1)} %collective-permute-done.8.rest_2_), channel_id=1, source_target_pairs={{0,1},{1,0},{2,3},{3,2},{4,5},{5,4},{6,7},{7,6},{8,9},{9,8},{10,11... | collective-permute-start | bytes 1572872 | tf_op jit(solution)/shard_map/ppermute | solution.py:428
  33.9 24.8 %collective-permute-start.11 = (bf16[512,512]{1,0:T(8,128)(2,1)S(1)}, bf16[512,512]{1,0:T(8,128)(2,1)S(1)}, u32[]{:S(2)}, u32[]{:S(2)}) collective-permute-start(bf16[512,512]{1,0:T(8,128)(2,1)S(1)} %pad_maximum_fusion.rest_0_), channel_id=1, source_target_pairs={{0,2},{1,3},{2,0},{3,1},{4,6},{5,7},{6,4},{7,5},{8,10},{9,11},{10,... | collective-permute-start | bytes 1572872 | tf_op jit(solution)/shard_map/ppermute | solution.py:428
  58.6 2.2 %collective-permute-start.10 = (bf16[4,128,512]{2,1,0:T(8,128)(2,1)}, bf16[4,128,512]{2,1,0:T(8,128)(2,1)S(1)}, u32[]{:S(2)}, u32[]{:S(2)}) collective-permute-start(bf16[4,128,512]{2,1,0:T(8,128)(2,1)} %get-tuple-element.39), channel_id=1, source_target_pairs={{0,1},{1,0},{2,3},{3,2},{4,5},{5,4},{6,7},{7,6},{8,9},{9,8},{10,11... | collective-permute-start | bytes 1572872 | tf_op jit(solution)/shard_map/ppermute | solution.py:428
  58.8 3.8 %collective-permute-start.12 = (bf16[512,512]{1,0:T(8,128)(2,1)S(1)}, bf16[512,512]{1,0:T(8,128)(2,1)S(1)}, u32[]{:S(2)}, u32[]{:S(2)}) collective-permute-start(bf16[512,512]{1,0:T(8,128)(2,1)S(1)} %collective-permute-done.11.rest_2_), channel_id=1, source_target_pairs={{0,1},{1,0},{2,3},{3,2},{4,5},{5,4},{6,7},{7,6},{8,9},{9,8},{10,11... | collective-permute-start | bytes 1572872 | tf_op jit(solution)/shard_map/ppermute | solution.py:428
  59.2 28.6 %collective-permute-start.16 = (bf16[4,128,512]{2,1,0:T(8,128)(2,1)}, bf16[4,128,512]{2,1,0:T(8,128)(2,1)S(1)}, u32[]{:S(2)}, u32[]{:S(2)}) collective-permute-start(bf16[4,128,512]{2,1,0:T(8,128)(2,1)} %get-tuple-element.54), channel_id=1, source_target_pairs={{0,1},{1,0},{2,3},{3,2},{4,5},{5,4},{6,7},{7,6},{8,9},{9,8},{10,11... | collective-permute-start | bytes 1572872 | tf_op jit(solution)/shard_map/ppermute | solution.py:428
  62.0 25.8 %collective-permute-start.17 = (bf16[4,128,512]{2,1,0:T(8,128)(2,1)S(1)}, bf16[4,128,512]{2,1,0:T(8,128)(2,1)S(1)}, u32[]{:S(2)}, u32[]{:S(2)}) collective-permute-start(bf16[4,128,512]{2,1,0:T(8,128)(2,1)S(1)} %add_convert_fusion.1), channel_id=1, source_target_pairs={{0,2},{1,3},{2,0},{3,1},{4,6},{5,7},{6,4},{7,5},{8,10},{9,11},{10,... | collective-permute-start | bytes 1572872 | tf_op jit(solution)/shard_map/ppermute | solution.py:428
  85.3 19.3 %collective-permute-start.13 = (bf16[4,128,512]{2,1,0:T(8,128)(2,1)}, bf16[4,128,512]{2,1,0:T(8,128)(2,1)S(1)}, u32[]{:S(2)}, u32[]{:S(2)}) collective-permute-start(bf16[4,128,512]{2,1,0:T(8,128)(2,1)} %get-tuple-element.45), channel_id=1, source_target_pairs={{0,1},{1,0},{2,3},{3,2},{4,5},{5,4},{6,7},{7,6},{8,9},{9,8},{10,11... | collective-permute-start | bytes 1572872 | tf_op jit(solution)/shard_map/ppermute | solution.py:428
  85.4 6.1 %collective-permute-start.14 = (bf16[4,128,512]{2,1,0:T(8,128)(2,1)}, bf16[4,128,512]{2,1,0:T(8,128)(2,1)S(1)}, u32[]{:S(2)}, u32[]{:S(2)}) collective-permute-start(bf16[4,128,512]{2,1,0:T(8,128)(2,1)} %get-tuple-element.47), channel_id=1, source_target_pairs={{0,1},{1,0},{2,3},{3,2},{4,5},{5,4},{6,7},{7,6},{8,9},{9,8},{10,11... | collective-permute-start | bytes 1572872 | tf_op jit(solution)/shard_map/ppermute | solution.py:428
  88.0 16.5 %collective-permute-start.20 = (bf16[128,512]{1,0:T(8,128)(2,1)S(1)}, bf16[128,512]{1,0:T(8,128)(2,1)S(1)}, u32[]{:S(2)}, u32[]{:S(2)}) collective-permute-start(bf16[128,512]{1,0:T(8,128)(2,1)S(1)} %get-tuple-element.72), channel_id=1, source_target_pairs={{0,12},{1,13},{2,14},{3,15},{4,0},{5,1},{6,2},{7,3},{8,4},{9,5},{1... | collective-permute-start | bytes 393224 | tf_op jit(solution)/shard_map/ppermute | solution.py:428
  88.1 16.4 %collective-permute-start.19 = (bf16[128,512]{1,0:T(8,128)(2,1)S(1)}, bf16[128,512]{1,0:T(8,128)(2,1)S(1)}, u32[]{:S(2)}, u32[]{:S(2)}) collective-permute-start(bf16[128,512]{1,0:T(8,128)(2,1)S(1)} %get-tuple-element.73), channel_id=1, source_target_pairs={{0,8},{1,9},{2,10},{3,11},{4,12},{5,13},{6,14},{7,15},{8,0},{9,1},... | collective-permute-start | bytes 393224 | tf_op jit(solution)/shard_map/ppermute | solution.py:428
  89.5 15.0 %collective-permute-start.18 = (bf16[128,512]{1,0:T(8,128)(2,1)S(1)}, bf16[128,512]{1,0:T(8,128)(2,1)S(1)}, u32[]{:S(2)}, u32[]{:S(2)}) collective-permute-start(bf16[128,512]{1,0:T(8,128)(2,1)S(1)} %get-tuple-element.74), channel_id=1, source_target_pairs={{0,4},{1,5},{2,6},{3,7},{4,8},{5,9},{6,10},{7,11},{8,12},{9,13},{1... | collective-permute-start | bytes 393224 | tf_op jit(solution)/shard_map/ppermute | solution.py:428
  91.6 13.1 %collective-permute-start.15 = (bf16[4,128,512]{2,1,0:T(8,128)(2,1)S(1)}, bf16[4,128,512]{2,1,0:T(8,128)(2,1)S(1)}, u32[]{:S(2)}, u32[]{:S(2)}) collective-permute-start(bf16[4,128,512]{2,1,0:T(8,128)(2,1)S(1)} %add_convert_fusion), channel_id=1, source_target_pairs={{0,2},{1,3},{2,0},{3,1},{4,6},{5,7},{6,4},{7,5},{8,10},{9,11},{10,... | collective-permute-start | bytes 1572872 | tf_op jit(solution)/shard_map/ppermute | solution.py:428
  105.0 14.9 %collective-permute-start.23 = (bf16[128,512]{1,0:T(8,128)(2,1)S(1)}, bf16[128,512]{1,0:T(8,128)(2,1)S(1)}, u32[]{:S(2)}, u32[]{:S(2)}) collective-permute-start(bf16[128,512]{1,0:T(8,128)(2,1)S(1)} %get-tuple-element.75), channel_id=1, source_target_pairs={{0,12},{1,13},{2,14},{3,15},{4,0},{5,1},{6,2},{7,3},{8,4},{9,5},{1... | collective-permute-start | bytes 393224 | tf_op jit(solution)/shard_map/ppermute | solution.py:428
  107.2 12.7 %collective-permute-start.22 = (bf16[128,512]{1,0:T(8,128)(2,1)S(1)}, bf16[128,512]{1,0:T(8,128)(2,1)S(1)}, u32[]{:S(2)}, u32[]{:S(2)}) collective-permute-start(bf16[128,512]{1,0:T(8,128)(2,1)S(1)} %get-tuple-element.76), channel_id=1, source_target_pairs={{0,8},{1,9},{2,10},{3,11},{4,12},{5,13},{6,14},{7,15},{8,0},{9,1},... | collective-permute-start | bytes 393224 | tf_op jit(solution)/shard_map/ppermute | solution.py:428
  107.2 12.7 %collective-permute-start.21 = (bf16[128,512]{1,0:T(8,128)(2,1)S(1)}, bf16[128,512]{1,0:T(8,128)(2,1)S(1)}, u32[]{:S(2)}, u32[]{:S(2)}) collective-permute-start(bf16[128,512]{1,0:T(8,128)(2,1)S(1)} %get-tuple-element.77), channel_id=1, source_target_pairs={{0,4},{1,5},{2,6},{3,7},{4,8},{5,9},{6,10},{7,11},{8,12},{9,13},{1... | collective-permute-start | bytes 393224 | tf_op jit(solution)/shard_map/ppermute | solution.py:428
  (11 other events, 111.0 us)

commit v7 on v4

--- a/solution.py
+++ b/solution.py
@@ -18,7 +18,7 @@
     return lax.dot_general(a, b, (contract, ((), ())), preferred_element_type=jnp.float32)
 
 CHUNKS = (2, 2)
-STEP_HEADS = (4, 2)
+CALLS = ((0, 0, 2, 4), (1, 0, 1, 2), (1, 1, 1, 2))
 PIECE = 32
 
 
@@ -26,12 +26,13 @@
     owner_ref, tokens_ref, place_ref,
     q_ref, g_ref, leaf_k_ref, leaf_v_ref, leaf_ref, mask_ref, *rest,
     prompts, per_prefix, block_len, planes, ranks, chained, steps, step_heads,
+    skipped,
 ):
     sources = rest[:2 * ranks]
     rest = rest[2 * ranks + 2 * chained:]
     out_ref, dq_ref, dleaf_ref = rest[:3]
     totals = rest[3:3 + 2 * ranks]
-    (kv, kcat, vcat, kcat_t, vcat_t, bias, q_pick, g_pick, q2, g2, scores, dprob, probs_b, dscore,
+    (kv, kcat, vcat, kcat_t, vcat_t, bias, q_pick, g_pick, q2, g2, scores, late_scores, dprob, probs_b, dscore,
      dk_sum, dv_sum, sems) = rest[3 + 2 * ranks:]
     step = pl.program_id(0)
     per_group = GQ // step_heads
@@ -40,6 +41,7 @@
     span = per_prefix * block_len
     keys = span + count
     half = sources[0].shape[1] // 2
+    half_out = dleaf_ref.shape[1] // 2
 
     place = place_ref[0]
     first = place * count
@@ -63,11 +65,8 @@
         ahead = lax.rem(owner // (2 * ranks) + planes - place // (2 * ranks), planes)
         return same_core, row, ahead
 
-    def key_columns(group):
-        return pl.ds(pl.multiple_of(group * HEAD_SIZE, HEAD_SIZE), HEAD_SIZE)
-
-    def value_columns(group):
-        return pl.ds(pl.multiple_of(half + group * HEAD_SIZE, HEAD_SIZE), HEAD_SIZE)
+    def head_columns(low, group):
+        return pl.ds(pl.multiple_of(low + group * HEAD_SIZE, HEAD_SIZE), HEAD_SIZE)
 
     @pl.when(step == 0)
     def _():
@@ -100,8 +99,8 @@
             bias[:, n * count:(n + 1) * count] = allowed_bias
         for ref in totals:
             ref[...] = jnp.zeros_like(ref)
-        dk_sum[...] = jnp.zeros_like(dk_sum)
-        dv_sum[...] = jnp.zeros_like(dv_sum)
+        for ref in (dk_sum, dv_sum, probs_b, dscore):
+            ref[...] = jnp.zeros_like(ref)
         for n in range(2 * per_prefix):
             target = kv.at[pl.ds(n * block_len, block_len), :]
             pltpu.make_async_copy(
@@ -114,7 +113,8 @@
     def _():
         group = step // per_group
         for cat, cols, leaf in (
-            (kcat, key_columns(group), leaf_k_ref), (vcat, value_columns(group), leaf_v_ref)
+            (kcat, head_columns(0, skipped + group), leaf_k_ref),
+            (vcat, head_columns(half, skipped + group), leaf_v_ref),
         ):
             for side in range(2):
                 lanes = slice(side * HEAD_SIZE, (side + 1) * HEAD_SIZE)
@@ -149,41 +149,88 @@
         return jnp.concatenate(parts, axis=0)
 
     def fold(value, op):
-        value = value.reshape(PIECE // 8, 8, columns)
+        value = value.reshape(PIECE // 8, 8, value.shape[1])
         total = value[0]
         for n in range(1, PIECE // 8):
             total = op(total, value[n])
         return total
 
+    def late(wide):
+        return jnp.concatenate(
+            [wide[:, n * count + count // 2:(n + 1) * count] for n in range(step_heads)], axis=1
+        )
+
+    def spread(value, narrow, op):
+        parts = []
+        for n in range(step_heads):
+            low, middle, high = n * count, n * count + count // 2, (n + 1) * count
+            mine = narrow[:, n * (count // 2):(n + 1) * (count // 2)]
+            parts += [value[:, low:middle], op(value[:, middle:high], mine)]
+        return jnp.concatenate(parts, axis=1)
+
+    early_keys = span + count // 2
+
     def score(new_q):
         product = dot(kcat[...], new_q, ((1,), (1,)))
-        top = None
+        top, late_top = None, None
         for at in range(0, keys, PIECE):
             piece = product[at:at + PIECE]
-            if at >= span:
-                piece = piece + bias[at - span:at - span + PIECE, :]
-            scores[at:at + PIECE, :] = piece
-            piece = fold(piece, jnp.maximum)
-            top = piece if top is None else jnp.maximum(top, piece)
+            if at < early_keys:
+                if at >= span:
+                    piece = piece + bias[at - span:at - span + PIECE, :]
+                scores[at:at + PIECE, :] = piece
+                piece = fold(piece, jnp.maximum)
+                top = piece if top is None else jnp.maximum(top, piece)
+            else:
+                piece = late(piece) + late(bias[at - span:at - span + PIECE, :])
+                late_scores[at - early_keys:at - early_keys + PIECE, :] = piece
+                piece = fold(piece, jnp.maximum)
+                late_top = piece if late_top is None else jnp.maximum(late_top, piece)
+        top = spread(top, late_top, jnp.maximum)
         return jnp.max(top, axis=0, keepdims=True)
+
+    def pieces():
+        for at in range(0, early_keys, PIECE):
+            yield scores[at:at + PIECE, :], at, False
+        for at in range(early_keys, keys, PIECE):
+            yield late_scores[at - early_keys:at - early_keys + PIECE, :], at, True
 
     def sums(top):
         total = jnp.zeros((8, columns), jnp.float32)
         delta = jnp.zeros((8, columns), jnp.float32)
-        for at in range(0, keys, PIECE):
-            weight = jnp.exp2((scores[at:at + PIECE, :] - top) * (SCALE * LOG2E))
-            total = total + fold(weight, jnp.add)
-            delta = delta + fold(weight * dprob[at:at + PIECE, :], jnp.add)
-        total = jnp.sum(total, axis=0, keepdims=True)
-        return total, jnp.sum(delta, axis=0, keepdims=True) / total
+        late_total = jnp.zeros((8, columns // 2), jnp.float32)
+        late_delta = jnp.zeros((8, columns // 2), jnp.float32)
+        late_top = late(top)
+        for value, at, is_late in pieces():
+            weight = jnp.exp2((value - (late_top if is_late else top)) * (SCALE * LOG2E))
+            if is_late:
+                late_total = late_total + fold(weight, jnp.add)
+                late_delta = late_delta + fold(weight * late(dprob[at:at + PIECE, :]), jnp.add)
+            else:
+                total = total + fold(weight, jnp.add)
+                delta = delta + fold(weight * dprob[at:at + PIECE, :], jnp.add)
+        total = jnp.sum(spread(total, late_total, jnp.add), axis=0, keepdims=True)
+        delta = jnp.sum(spread(delta, late_delta, jnp.add), axis=0, keepdims=True)
+        return total, delta / total
 
     def finish(top, total, delta):
         shift = jnp.log2(total)
-        for at in range(0, keys, PIECE):
-            power = (scores[at:at + PIECE, :] - top) * (SCALE * LOG2E)
-            probs = jnp.exp2(power - shift)
-            probs_b[at:at + PIECE, :] = probs.astype(jnp.bfloat16)
-            dscore[at:at + PIECE, :] = (probs * (dprob[at:at + PIECE, :] - delta)).astype(jnp.bfloat16)
+        late_top, late_shift, late_delta = late(top), late(shift), late(delta)
+        for value, at, is_late in pieces():
+            power = (value - (late_top if is_late else top)) * (SCALE * LOG2E)
+            probs = jnp.exp2(power - (late_shift if is_late else shift))
+            rows = slice(at, at + PIECE)
+            if not is_late:
+                probs_b[rows, :] = probs.astype(jnp.bfloat16)
+                dscore[rows, :] = (probs * (dprob[rows, :] - delta)).astype(jnp.bfloat16)
+                continue
+            change = (probs * (late(dprob[rows, :]) - late_delta)).astype(jnp.bfloat16)
+            probs = probs.astype(jnp.bfloat16)
+            for n in range(step_heads):
+                mine = slice(n * (count // 2), (n + 1) * (count // 2))
+                lanes = slice(n * count + count // 2, (n + 1) * count)
+                probs_b[rows, lanes] = probs[:, mine]
+                dscore[rows, lanes] = change[:, mine]
 
     def work(later):
         new_q = pick(q_ref, q_pick)
@@ -216,7 +263,7 @@
     def _():
         group = step // per_group - 1
         for total_ref, cols, factor in (
-            (dk_sum, key_columns(group), SCALE), (dv_sum, value_columns(group), 1.0)
+            (dk_sum, head_columns(0, group), SCALE), (dv_sum, head_columns(half_out, group), 1.0)
         ):
             leaf = (total_ref[span:, :HEAD_SIZE] + total_ref[span:, HEAD_SIZE:]) * factor
             dleaf_ref[:, cols] = leaf.astype(jnp.bfloat16)
@@ -241,18 +288,17 @@
 
 
 def attention(
-    chunk, owner, tokens, place, q, g, leaf_kv, leaf, mask, sources, earlier, planes, ranks
+    call, owner, tokens, place, q, g, leaf_kv, leaf, mask, sources, earlier, planes, ranks
 ):
+    chunk, chunk_skipped, groups, step_heads = call
     count = q.shape[0]
     block_len = sources[0].shape[0] // planes
     prompts = tokens.shape[0]
     per_prefix = owner.shape[0] // prompts
     span = per_prefix * block_len
     keys = span + count
-    width = sources[0].shape[1]
-    groups = CHUNKS[chunk]
-    step_heads = STEP_HEADS[chunk]
-    skipped = sum(CHUNKS[:chunk])
+    width = 2 * groups * HEAD_SIZE
+    skipped = sum(CHUNKS[:chunk]) + chunk_skipped
     heads = groups * GQ
     steps = heads // step_heads
     per_group = GQ // step_heads
@@ -284,6 +330,7 @@
         functools.partial(
             attention_kernel, prompts=prompts, per_prefix=per_prefix, block_len=block_len,
             planes=planes, ranks=ranks, chained=chained, steps=steps, step_heads=step_heads,
+            skipped=chunk_skipped,
         ),
         grid_spec=pltpu.PrefetchScalarGridSpec(
             num_scalar_prefetch=3,
@@ -293,7 +340,7 @@
             ] + [anywhere] * (2 * ranks + len(earlier)),
             out_specs=[behind, behind, full((count, width))] + [full(sum_shape)] * (2 * ranks),
             scratch_shapes=[
-                pltpu.VMEM((2 * span, width), bf16),
+                pltpu.VMEM((2 * span, sources[0].shape[1]), bf16),
                 pltpu.VMEM((keys, 2 * HEAD_SIZE), bf16),
                 pltpu.VMEM((keys, 2 * HEAD_SIZE), bf16),
                 pltpu.VMEM((2 * HEAD_SIZE, keys), bf16),
@@ -303,7 +350,8 @@
                 pltpu.VMEM((count, 2 * HEAD_SIZE), bf16),
                 pltpu.VMEM((step_heads * count, 2 * HEAD_SIZE), bf16),
                 pltpu.VMEM((step_heads * count, 2 * HEAD_SIZE), bf16),
-                pltpu.VMEM((keys, step_heads * count), f32),
+                pltpu.VMEM((span + count // 2, step_heads * count), f32),
+                pltpu.VMEM((count - count // 2, step_heads * count // 2), f32),
                 pltpu.VMEM((keys, step_heads * count), f32),
                 pltpu.VMEM((keys, step_heads * count), bf16),
                 pltpu.VMEM((keys, step_heads * count), bf16),
@@ -364,39 +412,52 @@
     def add(own, received):
         return own.astype(f32) + received.astype(f32)
 
-    def reduce_ranks(totals, away):
+    def reduce_ranks(totals, away, *last):
         total = add(totals[0], send(totals[1], 0, 0, 1))
-        return add(total, send(away, 0, 1, 0)) if ranks == 2 else total
-
-    def reduce_planes(total):
-        mine = total[0]
+        return add(total, tie(send(away, 0, 1, 0), *last)) if ranks == 2 else total
+
+    def for_planes(total):
+        return total[0], [total[k].astype(jnp.bfloat16) for k in range(1, planes)]
+
+    def reduce_planes(mine, away, last):
         for k in range(1, planes):
-            mine = add(mine, send(total[k].astype(jnp.bfloat16), k, 0, 0))
+            mine = add(mine, tie(send(away[k - 1], k, 0, 0), last))
         return mine.astype(jnp.bfloat16)
 
     chunks = len(CHUNKS)
     near = [by_planes(chunk) for chunk in range(chunks)]
     near_far = [send(n, 0, 0, 1) for n in near]
     other = [send(n, 0, 1, 0) for n in near] if ranks == 2 else []
-    d_leaf, d_prefix, earlier = [], [], ()
-    parts = []
-    for chunk in range(chunks):
-        first = [place] + near[chunk + 1:chunk + 2] + near_far[chunk + 1:chunk + 2]
-        if chunk and ranks == 2:
+    d_leaf, parts, by_ranks, earlier = [], [], [], ()
+    for at, call in enumerate(CALLS):
+        chunk, new_chunk = call[0], call[1] == 0
+        first = [place]
+        if new_chunk:
+            first += near[chunk + 1:chunk + 2] + near_far[chunk + 1:chunk + 2]
+            sources = [near[chunk], near_far[chunk]]
+            if ranks == 2:
+                row = tie(other[chunk], d_leaf[-1] if chunk else near[1])
+                sources += [row, send(row, 0, 0, 1)]
+        if at >= 1 and ranks == 2:
             first.append(parts[-1][1])
-        sources = [near[chunk], near_far[chunk]]
-        if ranks == 2:
-            row = tie(other[chunk], d_leaf[-1] if chunk else near[1])
-            sources += [row, send(row, 0, 0, 1)]
+        if at >= 2:
+            by_ranks.append(for_planes(reduce_ranks(*parts[at - 2])))
+            first += by_ranks[-1][1]
         attended, d_query, leaf_part, *totals = attention(
-            chunk, block_owner, subtree_tokens, tie(*first), query, d_out, leaf_key_value,
+            call, block_owner, subtree_tokens, tie(*first), query, d_out, leaf_key_value,
             leaf_id, mask, sources, earlier, planes, ranks,
         )
         earlier = (attended, d_query)
         d_leaf.append(leaf_part)
+        if at == len(CALLS) - 1:
+            d_prefix = [reduce_planes(*total, leaf_part) for total in by_ranks]
+            totals[-1] = tie(totals[-1], *d_prefix)
         away = add(totals[2], send(totals[3], 0, 0, 1)).astype(jnp.bfloat16) if ranks == 2 else None
         parts.append((totals, away))
-    d_prefix = [reduce_planes(reduce_ranks(*part)) for part in parts]
+    for part in parts[len(d_prefix):]:
+        total = for_planes(reduce_ranks(*part, d_leaf[-1]))
+        d_prefix.append(reduce_planes(*total, d_leaf[-1] if ranks == 1 else parts[-1][1]))
+    d_leaf = [tie(part, d_leaf[-1]) for part in d_leaf[:-1]] + d_leaf[-1:]
 
     def join(parts):
         halves = [jnp.split(p, 2, axis=1) for p in parts]

time: 117 us -> 125 us (1.068)
  Pallas kernels: 44.6 us -> 49.3 us
  waiting for transfers between devices: 35.5 us -> 37.4 us
    pallas_call x2 -> x3, Pallas kernels: 44.6 us -> 49.3 us  [attention(): pl.pallas_call(functools.partial(attention_kernel, prompts=prompts, per_p...]
    ppermute x24 -> x30, waiting for transfers between devices: 35.5 us -> 37.4 us  [send(): return lax.ppermute(array, 'dp', pairs)]
    concatenate x2 -> x0, other arithmetic: 1.59 us -> none  [join(): jnp.concatenate([h[0] for h in halves] + [h[1] for h in halves], axis=1)]
    unnamed x24 -> x46, local copies, waits for them, and re-layouts: 1.63 us -> 2.88 us
    ppermute x24 -> x30, starting transfers between devices: 28.5 us -> 29.6 us  [send(): return lax.ppermute(array, 'dp', pairs)]
  transfers between devices with their start and end apart: 24 -> 30, of which waited for: 12 -> 14; matrix products, arithmetic and copies ran while one was open for 3% -> 2% of each run, Pallas kernels for 38% -> 40%
where the time goes in v7:
time: 125 us; the launch traced here: 124 us
  Pallas kernels  49.3 us (39%)
  waiting for transfers between devices  37.4 us (30%)
  starting transfers between devices  29.6 us (24%)
  local copies, waits for them, and re-layouts  3.93 us (3%)
  other arithmetic  2.92 us (2%)
    pallas_call x3, Pallas kernels, attention(): pl.pallas_call(functools.partial(attention_kernel, prompts=prompts, per_p...  49.3 us
    ppermute x30, waiting for transfers between devices, send(): return lax.ppermute(array, 'dp', pairs)  37.4 us
    ppermute x30, starting transfers between devices, send(): return lax.ppermute(array, 'dp', pairs)  29.6 us
    unnamed x46, local copies, waits for them, and re-layouts  2.88 us
  transfers between devices with their start and end apart: 30, of which 14 were waited for; matrix products, arithmetic and copies ran while one was open for 2% of the time, Pallas kernels for 40%

profile of v7, /device:TPU:0, one launch (start us, length us, event | category | flops | bytes accessed | tf_op | source)
XLA Modules:
  0.0 124.2 jit_solution(6156199451580980806)
XLA Ops:
  1.6 5.1 %collective-permute-start.6 = (bf16[128,512]{1,0:T(8,128)(2,1)S(1)}, bf16[128,512]{1,0:T(8,128)(2,1)S(1)}, u32[]{:S(2)}, u32[]{:S(2)}) collective-permute-start(bf16[128,512]{1,0:T(8,128)(2,1)S(1)} %pad_maximum_fusion.3), channel_id=1, source_target_pairs={{0,12},{1,13},{2,14},{3,15},{4,0},{5,1},{6,2},{7,3},{8,4},{9,5},{1... | collective-permute-start | bytes 393224 | tf_op jit(solution)/shard_map/ppermute | solution.py:397
  7.7 2.9 %collective-permute-done.6 = bf16[128,512]{1,0:T(8,128)(2,1)S(1)} collective-permute-done((bf16[128,512]{1,0:T(8,128)(2,1)S(1)}, bf16[128,512]{1,0:T(8,128)(2,1)S(1)}, u32[]{:S(2)}, u32[]{:S(2)}) %collective-permute-start.6) | collective-permute-done | bytes 131104 | tf_op jit(solution)/shard_map/ppermute | solution.py:397
  10.6 7.3 %collective-permute-done.5 = bf16[128,512]{1,0:T(8,128)(2,1)S(1)} collective-permute-done((bf16[128,512]{1,0:T(8,128)(2,1)S(1)}, bf16[128,512]{1,0:T(8,128)(2,1)S(1)}, u32[]{:S(2)}, u32[]{:S(2)}) %collective-permute-start.5) | collective-permute-done | bytes 131104 | tf_op jit(solution)/shard_map/ppermute | solution.py:397
  18.0 1.6 %collective-permute-start.8 = (bf16[512,512]{1,0:T(8,128)(2,1)S(1)}, bf16[512,512]{1,0:T(8,128)(2,1)S(1)}, u32[]{:S(2)}, u32[]{:S(2)}) collective-permute-start(bf16[512,512]{1,0:T(8,128)(2,1)S(1)} %pad_maximum_fusion.1.rest_0_), channel_id=1, source_target_pairs={{0,2},{1,3},{2,0},{3,1},{4,6},{5,7},{6,4},{7,5},{8,10},{9,11},{10,... | collective-permute-start | bytes 1572872 | tf_op jit(solution)/shard_map/ppermute | solution.py:397
  19.6 1.7 %collective-permute-start.2 = (bf16[128,512]{1,0:T(8,128)(2,1)S(1)}, bf16[128,512]{1,0:T(8,128)(2,1)S(1)}, u32[]{:S(2)}, u32[]{:S(2)}) collective-permute-start(bf16[128,512]{1,0:T(8,128)(2,1)S(1)} %pad_maximum_fusion.2), channel_id=1, source_target_pairs={{0,12},{1,13},{2,14},{3,15},{4,0},{5,1},{6,2},{7,3},{8,4},{9,5},{1... | collective-permute-start | bytes 393224 | tf_op jit(solution)/shard_map/ppermute | solution.py:397
  22.3 1.9 %collective-permute-start = (bf16[128,512]{1,0:T(8,128)(2,1)S(1)}, bf16[128,512]{1,0:T(8,128)(2,1)S(1)}, u32[]{:S(2)}, u32[]{:S(2)}) collective-permute-start(bf16[128,512]{1,0:T(8,128)(2,1)S(1)} %pad_maximum_fusion.2), channel_id=1, source_target_pairs={{0,4},{1,5},{2,6},{3,7},{4,8},{5,9},{6,10},{7,11},{8,12},{9,13},{1... | collective-permute-start | bytes 393224 | tf_op jit(solution)/shard_map/ppermute | solution.py:397
  24.3 1.1 collective-permute-done.2
  25.4 7.9 %collective-permute-done.1 = bf16[128,512]{1,0:T(8,128)(2,1)S(1)} collective-permute-done((bf16[128,512]{1,0:T(8,128)(2,1)S(1)}, bf16[128,512]{1,0:T(8,128)(2,1)S(1)}, u32[]{:S(2)}, u32[]{:S(2)}) %collective-permute-start.1) | collective-permute-done | bytes 131104 | tf_op jit(solution)/shard_map/ppermute | solution.py:397
  36.9 21.9 %shard_map.111 = (bf16[256,4096]{1,0:T(8,128)(2,1)}, bf16[256,4096]{1,0:T(8,128)(2,1)}, bf16[256,512]{1,0:T(8,128)(2,1)}, bf16[4,128,512]{2,1,0:T(8,128)(2,1)}, ...) custom-call(s32[16]{0:T(128)} %owner_ref.5, s32[4]{0:T(128)} %tokens_ref.5, ...), custom_call_target="tpu_custom_call" | custom-call | flops 9663676416 | bytes 8388608 | tf_op jit(solution)/shard_map/pallas_call | solution.py:329
  59.6 1.5 %collective-permute-done.10 = bf16[4,128,512]{2,1,0:T(8,128)(2,1)S(1)} collective-permute-done((bf16[4,128,512]{2,1,0:T(8,128)(2,1)}, bf16[4,128,512]{2,1,0:T(8,128)(2,1)S(1)}, u32[]{:S(2)}, u32[]{:S(2)}) %collective-permute-start.10) | collective-permute-done | bytes 524320 | tf_op jit(solution)/shard_map/ppermute | solution.py:397
  61.0 1.2 add_convert_fusion
  63.6 13.8 %shard_map.112 = (bf16[256,4096]{1,0:T(8,128)(2,1)}, bf16[256,4096]{1,0:T(8,128)(2,1)}, bf16[256,256]{1,0:T(8,128)(2,1)}, bf16[4,128,256]{2,1,0:T(8,128)(2,1)}, ...) custom-call(s32[16]{0:T(128)} %owner_ref.5, ...), custom_call_target="tpu_custom_call", output_to_operand_aliasing={{0}: (13, {}), {1}: (14, {})} | custom-call | flops 4831838208 | bytes 4194304 | tf_op jit(solution)/shard_map/pallas_call | solution.py:329
  77.9 1.2 collective-permute-done.13
  80.2 1.6 %collective-permute-start.20 = (bf16[4,128,256]{2,1,0:T(8,128)(2,1)S(1)}, bf16[4,128,256]{2,1,0:T(8,128)(2,1)S(1)}, u32[]{:S(2)}, u32[]{:S(2)}) collective-permute-start(bf16[4,128,256]{2,1,0:T(8,128)(2,1)S(1)} %add_convert_fusion.2), channel_id=1, source_target_pairs={{0,2},{1,3},{2,0},{3,1},{4,6},{5,7},{6,4},{7,5},{8,10},{9,11},{10,... | collective-permute-start | bytes 786440 | tf_op jit(solution)/shard_map/ppermute | solution.py:397
  82.1 1.4 %collective-permute-start.17 = (bf16[128,512]{1,0:T(8,128)(2,1)S(1)}, bf16[128,512]{1,0:T(8,128)(2,1)S(1)}, u32[]{:S(2)}, u32[]{:S(2)}) collective-permute-start(bf16[128,512]{1,0:T(8,128)(2,1)S(1)} %get-tuple-element.91), channel_id=1, source_target_pairs={{0,8},{1,9},{2,10},{3,11},{4,12},{5,13},{6,14},{7,15},{8,0},{9,1},... | collective-permute-start | bytes 393224 | tf_op jit(solution)/shard_map/ppermute | solution.py:397
  83.5 1.9 %collective-permute-start.16 = (bf16[128,512]{1,0:T(8,128)(2,1)S(1)}, bf16[128,512]{1,0:T(8,128)(2,1)S(1)}, u32[]{:S(2)}, u32[]{:S(2)}) collective-permute-start(bf16[128,512]{1,0:T(8,128)(2,1)S(1)} %get-tuple-element.92), channel_id=1, source_target_pairs={{0,4},{1,5},{2,6},{3,7},{4,8},{5,9},{6,10},{7,11},{8,12},{9,13},{1... | collective-permute-start | bytes 393224 | tf_op jit(solution)/shard_map/ppermute | solution.py:397
  85.5 13.6 %shard_map.113 = (bf16[256,4096]{1,0:T(8,128)(2,1)}, bf16[256,4096]{1,0:T(8,128)(2,1)}, bf16[256,256]{1,0:T(8,128)(2,1)}, bf16[4,128,256]{2,1,0:T(8,128)(2,1)}, ...) custom-call(s32[16]{0:T(128)} %owner_ref.5, ...), custom_call_target="tpu_custom_call", output_to_operand_aliasing={{0}: (13, {}), {1}: (14, {})} | custom-call | flops 4831838208 | bytes 4194304 | tf_op jit(solution)/shard_map/pallas_call | solution.py:329
  100.1 3.3 %collective-permute-start.24 = (bf16[128,256]{1,0:T(8,128)(2,1)S(1)}, bf16[128,256]{1,0:T(8,128)(2,1)S(1)}, u32[]{:S(2)}, u32[]{:S(2)}) collective-permute-start(bf16[128,256]{1,0:T(8,128)(2,1)S(1)} %get-tuple-element.97), channel_id=1, source_target_pairs={{0,12},{1,13},{2,14},{3,15},{4,0},{5,1},{6,2},{7,3},{8,4},{9,5},{1... | collective-permute-start | bytes 196616 | tf_op jit(solution)/shard_map/ppermute | solution.py:397
  103.7 1.5 %collective-permute-done.22 = bf16[4,128,256]{2,1,0:T(8,128)(2,1)S(1)} collective-permute-done((bf16[4,128,256]{2,1,0:T(8,128)(2,1)S(1)}, bf16[4,128,256]{2,1,0:T(8,128)(2,1)S(1)}, u32[]{:S(2)}, u32[]{:S(2)}) %collective-permute-start.22) | collective-permute-done | bytes 262176 | tf_op jit(solution)/shard_map/ppermute | solution.py:397
  106.2 3.4 %collective-permute-done.23 = bf16[128,256]{1,0:T(8,128)(2,1)S(1)} collective-permute-done((bf16[128,256]{1,0:T(8,128)(2,1)S(1)}, bf16[128,256]{1,0:T(8,128)(2,1)S(1)}, u32[]{:S(2)}, u32[]{:S(2)}) %collective-permute-start.23) | collective-permute-done | bytes 65568 | tf_op jit(solution)/shard_map/ppermute | solution.py:397
  109.6 4.0 %collective-permute-done.26 = bf16[4,128,256]{2,1,0:T(8,128)(2,1)S(1)} collective-permute-done((bf16[4,128,256]{2,1,0:T(8,128)(2,1)S(1)}, bf16[4,128,256]{2,1,0:T(8,128)(2,1)S(1)}, u32[]{:S(2)}, u32[]{:S(2)}) %collective-permute-start.26) | collective-permute-done | bytes 262176 | tf_op jit(solution)/shard_map/ppermute | solution.py:397
  114.4 3.2 %collective-permute-start.29 = (bf16[128,256]{1,0:T(8,128)(2,1)S(1)}, bf16[128,256]{1,0:T(8,128)(2,1)S(1)}, u32[]{:S(2)}, u32[]{:S(2)}) collective-permute-start(bf16[128,256]{1,0:T(8,128)(2,1)S(1)} %get-tuple-element.94), channel_id=1, source_target_pairs={{0,12},{1,13},{2,14},{3,15},{4,0},{5,1},{6,2},{7,3},{8,4},{9,5},{1... | collective-permute-start | bytes 196616 | tf_op jit(solution)/shard_map/ppermute | solution.py:397
  118.8 1.8 %collective-permute-done.27 = bf16[128,256]{1,0:T(8,128)(2,1)S(1)} collective-permute-done((bf16[128,256]{1,0:T(8,128)(2,1)S(1)}, bf16[128,256]{1,0:T(8,128)(2,1)S(1)}, u32[]{:S(2)}, u32[]{:S(2)}) %collective-permute-start.27) | collective-permute-done | bytes 65568 | tf_op jit(solution)/shard_map/ppermute | solution.py:397
  120.6 2.8 %collective-permute-done.28 = bf16[128,256]{1,0:T(8,128)(2,1)S(1)} collective-permute-done((bf16[128,256]{1,0:T(8,128)(2,1)S(1)}, bf16[128,256]{1,0:T(8,128)(2,1)S(1)}, u32[]{:S(2)}, u32[]{:S(2)}) %collective-permute-start.28) | collective-permute-done | bytes 65568 | tf_op jit(solution)/shard_map/ppermute | solution.py:397
  (104 shorter events, 15.6 us)
Async XLA Ops:
  1.6 9.0 %collective-permute-start.6 = (bf16[128,512]{1,0:T(8,128)(2,1)S(1)}, bf16[128,512]{1,0:T(8,128)(2,1)S(1)}, u32[]{:S(2)}, u32[]{:S(2)}) collective-permute-start(bf16[128,512]{1,0:T(8,128)(2,1)S(1)} %pad_maximum_fusion.3), channel_id=1, source_target_pairs={{0,12},{1,13},{2,14},{3,15},{4,0},{5,1},{6,2},{7,3},{8,4},{9,5},{1... | collective-permute-start | bytes 393224 | tf_op jit(solution)/shard_map/ppermute | solution.py:397
  6.7 11.2 %collective-permute-start.5 = (bf16[128,512]{1,0:T(8,128)(2,1)S(1)}, bf16[128,512]{1,0:T(8,128)(2,1)S(1)}, u32[]{:S(2)}, u32[]{:S(2)}) collective-permute-start(bf16[128,512]{1,0:T(8,128)(2,1)S(1)} %pad_maximum_fusion.3), channel_id=1, source_target_pairs={{0,8},{1,9},{2,10},{3,11},{4,12},{5,13},{6,14},{7,15},{8,0},{9,1},... | collective-permute-start | bytes 393224 | tf_op jit(solution)/shard_map/ppermute | solution.py:397
  6.7 11.2 %collective-permute-start.4 = (bf16[128,512]{1,0:T(8,128)(2,1)S(1)}, bf16[128,512]{1,0:T(8,128)(2,1)S(1)}, u32[]{:S(2)}, u32[]{:S(2)}) collective-permute-start(bf16[128,512]{1,0:T(8,128)(2,1)S(1)} %pad_maximum_fusion.3), channel_id=1, source_target_pairs={{0,4},{1,5},{2,6},{3,7},{4,8},{5,9},{6,10},{7,11},{8,12},{9,13},{1... | collective-permute-start | bytes 393224 | tf_op jit(solution)/shard_map/ppermute | solution.py:397
  18.0 15.5 %collective-permute-start.8 = (bf16[512,512]{1,0:T(8,128)(2,1)S(1)}, bf16[512,512]{1,0:T(8,128)(2,1)S(1)}, u32[]{:S(2)}, u32[]{:S(2)}) collective-permute-start(bf16[512,512]{1,0:T(8,128)(2,1)S(1)} %pad_maximum_fusion.1.rest_0_), channel_id=1, source_target_pairs={{0,2},{1,3},{2,0},{3,1},{4,6},{5,7},{6,4},{7,5},{8,10},{9,11},{10,... | collective-permute-start | bytes 1572872 | tf_op jit(solution)/shard_map/ppermute | solution.py:397
  19.6 5.9 %collective-permute-start.2 = (bf16[128,512]{1,0:T(8,128)(2,1)S(1)}, bf16[128,512]{1,0:T(8,128)(2,1)S(1)}, u32[]{:S(2)}, u32[]{:S(2)}) collective-permute-start(bf16[128,512]{1,0:T(8,128)(2,1)S(1)} %pad_maximum_fusion.2), channel_id=1, source_target_pairs={{0,12},{1,13},{2,14},{3,15},{4,0},{5,1},{6,2},{7,3},{8,4},{9,5},{1... | collective-permute-start | bytes 393224 | tf_op jit(solution)/shard_map/ppermute | solution.py:397
  21.2 12.1 %collective-permute-start.1 = (bf16[128,512]{1,0:T(8,128)(2,1)S(1)}, bf16[128,512]{1,0:T(8,128)(2,1)S(1)}, u32[]{:S(2)}, u32[]{:S(2)}) collective-permute-start(bf16[128,512]{1,0:T(8,128)(2,1)S(1)} %pad_maximum_fusion.2), channel_id=1, source_target_pairs={{0,8},{1,9},{2,10},{3,11},{4,12},{5,13},{6,14},{7,15},{8,0},{9,1},... | collective-permute-start | bytes 393224 | tf_op jit(solution)/shard_map/ppermute | solution.py:397
  22.3 11.0 %collective-permute-start = (bf16[128,512]{1,0:T(8,128)(2,1)S(1)}, bf16[128,512]{1,0:T(8,128)(2,1)S(1)}, u32[]{:S(2)}, u32[]{:S(2)}) collective-permute-start(bf16[128,512]{1,0:T(8,128)(2,1)S(1)} %pad_maximum_fusion.2), channel_id=1, source_target_pairs={{0,4},{1,5},{2,6},{3,7},{4,8},{5,9},{6,10},{7,11},{8,12},{9,13},{1... | collective-permute-start | bytes 393224 | tf_op jit(solution)/shard_map/ppermute | solution.py:397
  24.3 11.1 %collective-permute-start.7 = (bf16[512,512]{1,0:T(8,128)(2,1)S(1)}, bf16[512,512]{1,0:T(8,128)(2,1)S(1)}, u32[]{:S(2)}, u32[]{:S(2)}) collective-permute-start(bf16[512,512]{1,0:T(8,128)(2,1)S(1)} %pad_maximum_fusion.1.rest_0_), channel_id=1, source_target_pairs={{0,1},{1,0},{2,3},{3,2},{4,5},{5,4},{6,7},{7,6},{8,9},{9,8},{10,11... | collective-permute-start | bytes 1572872 | tf_op jit(solution)/shard_map/ppermute | solution.py:397
  33.9 25.1 %collective-permute-start.11 = (bf16[512,512]{1,0:T(8,128)(2,1)S(1)}, bf16[512,512]{1,0:T(8,128)(2,1)S(1)}, u32[]{:S(2)}, u32[]{:S(2)}) collective-permute-start(bf16[512,512]{1,0:T(8,128)(2,1)S(1)} %pad_maximum_fusion.rest_0_), channel_id=1, source_target_pairs={{0,2},{1,3},{2,0},{3,1},{4,6},{5,7},{6,4},{7,5},{8,10},{9,11},{10,... | collective-permute-start | bytes 1572872 | tf_op jit(solution)/shard_map/ppermute | solution.py:397
  59.4 22.4 %collective-permute-start.14 = (bf16[4,128,512]{2,1,0:T(8,128)(2,1)}, bf16[4,128,512]{2,1,0:T(8,128)(2,1)S(1)}, u32[]{:S(2)}, u32[]{:S(2)}) collective-permute-start(bf16[4,128,512]{2,1,0:T(8,128)(2,1)} %get-tuple-element.56), channel_id=1, source_target_pairs={{0,1},{1,0},{2,3},{3,2},{4,5},{5,4},{6,7},{7,6},{8,9},{9,8},{10,11... | collective-permute-start | bytes 1572872 | tf_op jit(solution)/shard_map/ppermute | solution.py:397
  62.2 19.6 %collective-permute-start.15 = (bf16[4,128,512]{2,1,0:T(8,128)(2,1)S(1)}, bf16[4,128,512]{2,1,0:T(8,128)(2,1)S(1)}, u32[]{:S(2)}, u32[]{:S(2)}) collective-permute-start(bf16[4,128,512]{2,1,0:T(8,128)(2,1)S(1)} %add_convert_fusion), channel_id=1, source_target_pairs={{0,2},{1,3},{2,0},{3,1},{4,6},{5,7},{6,4},{7,5},{8,10},{9,11},{10,... | collective-permute-start | bytes 1572872 | tf_op jit(solution)/shard_map/ppermute | solution.py:397
  77.4 21.8 %collective-permute-start.19 = (bf16[4,128,256]{2,1,0:T(8,128)(2,1)}, bf16[4,128,256]{2,1,0:T(8,128)(2,1)S(1)}, u32[]{:S(2)}, u32[]{:S(2)}) collective-permute-start(bf16[4,128,256]{2,1,0:T(8,128)(2,1)} %get-tuple-element.70), channel_id=1, source_target_pairs={{0,1},{1,0},{2,3},{3,2},{4,5},{5,4},{6,7},{7,6},{8,9},{9,8},{10,11... | collective-permute-start | bytes 786440 | tf_op jit(solution)/shard_map/ppermute | solution.py:397
  80.2 19.0 %collective-permute-start.20 = (bf16[4,128,256]{2,1,0:T(8,128)(2,1)S(1)}, bf16[4,128,256]{2,1,0:T(8,128)(2,1)S(1)}, u32[]{:S(2)}, u32[]{:S(2)}) collective-permute-start(bf16[4,128,256]{2,1,0:T(8,128)(2,1)S(1)} %add_convert_fusion.2), channel_id=1, source_target_pairs={{0,2},{1,3},{2,0},{3,1},{4,6},{5,7},{6,4},{7,5},{8,10},{9,11},{10,... | collective-permute-start | bytes 786440 | tf_op jit(solution)/shard_map/ppermute | solution.py:397
  82.1 18.1 %collective-permute-start.18 = (bf16[128,512]{1,0:T(8,128)(2,1)S(1)}, bf16[128,512]{1,0:T(8,128)(2,1)S(1)}, u32[]{:S(2)}, u32[]{:S(2)}) collective-permute-start(bf16[128,512]{1,0:T(8,128)(2,1)S(1)} %get-tuple-element.90), channel_id=1, source_target_pairs={{0,12},{1,13},{2,14},{3,15},{4,0},{5,1},{6,2},{7,3},{8,4},{9,5},{1... | collective-permute-start | bytes 393224 | tf_op jit(solution)/shard_map/ppermute | solution.py:397
  82.1 21.3 %collective-permute-start.17 = (bf16[128,512]{1,0:T(8,128)(2,1)S(1)}, bf16[128,512]{1,0:T(8,128)(2,1)S(1)}, u32[]{:S(2)}, u32[]{:S(2)}) collective-permute-start(bf16[128,512]{1,0:T(8,128)(2,1)S(1)} %get-tuple-element.91), channel_id=1, source_target_pairs={{0,8},{1,9},{2,10},{3,11},{4,12},{5,13},{6,14},{7,15},{8,0},{9,1},... | collective-permute-start | bytes 393224 | tf_op jit(solution)/shard_map/ppermute | solution.py:397
  83.5 19.9 %collective-permute-start.16 = (bf16[128,512]{1,0:T(8,128)(2,1)S(1)}, bf16[128,512]{1,0:T(8,128)(2,1)S(1)}, u32[]{:S(2)}, u32[]{:S(2)}) collective-permute-start(bf16[128,512]{1,0:T(8,128)(2,1)S(1)} %get-tuple-element.92), channel_id=1, source_target_pairs={{0,4},{1,5},{2,6},{3,7},{4,8},{5,9},{6,10},{7,11},{8,12},{9,13},{1... | collective-permute-start | bytes 393224 | tf_op jit(solution)/shard_map/ppermute | solution.py:397
  99.1 14.5 %collective-permute-start.25 = (bf16[4,128,256]{2,1,0:T(8,128)(2,1)}, bf16[4,128,256]{2,1,0:T(8,128)(2,1)S(1)}, u32[]{:S(2)}, u32[]{:S(2)}) collective-permute-start(bf16[4,128,256]{2,1,0:T(8,128)(2,1)} %get-tuple-element.79), channel_id=1, source_target_pairs={{0,1},{1,0},{2,3},{3,2},{4,5},{5,4},{6,7},{7,6},{8,9},{9,8},{10,11... | collective-permute-start | bytes 786440 | tf_op jit(solution)/shard_map/ppermute | solution.py:397
  99.4 6.8 %collective-permute-start.21 = (bf16[128,256]{1,0:T(8,128)(2,1)S(1)}, bf16[128,256]{1,0:T(8,128)(2,1)S(1)}, u32[]{:S(2)}, u32[]{:S(2)}) collective-permute-start(bf16[128,256]{1,0:T(8,128)(2,1)S(1)} %get-tuple-element.96), channel_id=1, source_target_pairs={{0,4},{1,5},{2,6},{3,7},{4,8},{5,9},{6,10},{7,11},{8,12},{9,13},{1... | collective-permute-start | bytes 196616 | tf_op jit(solution)/shard_map/ppermute | solution.py:397
  100.1 6.1 %collective-permute-start.24 = (bf16[128,256]{1,0:T(8,128)(2,1)S(1)}, bf16[128,256]{1,0:T(8,128)(2,1)S(1)}, u32[]{:S(2)}, u32[]{:S(2)}) collective-permute-start(bf16[128,256]{1,0:T(8,128)(2,1)S(1)} %get-tuple-element.97), channel_id=1, source_target_pairs={{0,12},{1,13},{2,14},{3,15},{4,0},{5,1},{6,2},{7,3},{8,4},{9,5},{1... | collective-permute-start | bytes 196616 | tf_op jit(solution)/shard_map/ppermute | solution.py:397
  103.4 6.2 %collective-permute-start.23 = (bf16[128,256]{1,0:T(8,128)(2,1)S(1)}, bf16[128,256]{1,0:T(8,128)(2,1)S(1)}, u32[]{:S(2)}, u32[]{:S(2)}) collective-permute-start(bf16[128,256]{1,0:T(8,128)(2,1)S(1)} %get-tuple-element.98), channel_id=1, source_target_pairs={{0,8},{1,9},{2,10},{3,11},{4,12},{5,13},{6,14},{7,15},{8,0},{9,1},... | collective-permute-start | bytes 196616 | tf_op jit(solution)/shard_map/ppermute | solution.py:397
  105.2 8.4 %collective-permute-start.26 = (bf16[4,128,256]{2,1,0:T(8,128)(2,1)S(1)}, bf16[4,128,256]{2,1,0:T(8,128)(2,1)S(1)}, u32[]{:S(2)}, u32[]{:S(2)}) collective-permute-start(bf16[4,128,256]{2,1,0:T(8,128)(2,1)S(1)} %add_convert_fusion.1), channel_id=1, source_target_pairs={{0,2},{1,3},{2,0},{3,1},{4,6},{5,7},{6,4},{7,5},{8,10},{9,11},{10,... | collective-permute-start | bytes 786440 | tf_op jit(solution)/shard_map/ppermute | solution.py:397
  113.7 6.8 %collective-permute-start.27 = (bf16[128,256]{1,0:T(8,128)(2,1)S(1)}, bf16[128,256]{1,0:T(8,128)(2,1)S(1)}, u32[]{:S(2)}, u32[]{:S(2)}) collective-permute-start(bf16[128,256]{1,0:T(8,128)(2,1)S(1)} %get-tuple-element.93), channel_id=1, source_target_pairs={{0,4},{1,5},{2,6},{3,7},{4,8},{5,9},{6,10},{7,11},{8,12},{9,13},{1... | collective-permute-start | bytes 196616 | tf_op jit(solution)/shard_map/ppermute | solution.py:397
  114.4 6.1 %collective-permute-start.29 = (bf16[128,256]{1,0:T(8,128)(2,1)S(1)}, bf16[128,256]{1,0:T(8,128)(2,1)S(1)}, u32[]{:S(2)}, u32[]{:S(2)}) collective-permute-start(bf16[128,256]{1,0:T(8,128)(2,1)S(1)} %get-tuple-element.94), channel_id=1, source_target_pairs={{0,12},{1,13},{2,14},{3,15},{4,0},{5,1},{6,2},{7,3},{8,4},{9,5},{1... | collective-permute-start | bytes 196616 | tf_op jit(solution)/shard_map/ppermute | solution.py:397
  117.6 5.8 %collective-permute-start.28 = (bf16[128,256]{1,0:T(8,128)(2,1)S(1)}, bf16[128,256]{1,0:T(8,128)(2,1)S(1)}, u32[]{:S(2)}, u32[]{:S(2)}) collective-permute-start(bf16[128,256]{1,0:T(8,128)(2,1)S(1)} %get-tuple-element.95), channel_id=1, source_target_pairs={{0,8},{1,9},{2,10},{3,11},{4,12},{5,13},{6,14},{7,15},{8,0},{9,1},... | collective-permute-start | bytes 196616 | tf_op jit(solution)/shard_map/ppermute | solution.py:397
  (24 other events, 183.0 us)

commit v8 on v4

--- a/solution.py
+++ b/solution.py
@@ -19,19 +19,21 @@
 
 CHUNKS = (2, 2)
 STEP_HEADS = (4, 2)
-PIECE = 32
+PIECES = (32, 16)
+TURNED = (True, False)
 
 
 def attention_kernel(
     owner_ref, tokens_ref, place_ref,
     q_ref, g_ref, leaf_k_ref, leaf_v_ref, leaf_ref, mask_ref, *rest,
     prompts, per_prefix, block_len, planes, ranks, chained, steps, step_heads,
+    piece_rows, turned,
 ):
     sources = rest[:2 * ranks]
     rest = rest[2 * ranks + 2 * chained:]
     out_ref, dq_ref, dleaf_ref = rest[:3]
     totals = rest[3:3 + 2 * ranks]
-    (kv, kcat, vcat, kcat_t, vcat_t, bias, q_pick, g_pick, q2, g2, scores, dprob, probs_b, dscore,
+    (kv, kcat, vcat, kcat_t, vcat_t, bias, q_pick, g_pick, q_pick_t, g_pick_t, q2, g2, scores, dprob, probs_b, dscore,
      dk_sum, dv_sum, sems) = rest[3 + 2 * ranks:]
     step = pl.program_id(0)
     per_group = GQ // step_heads
@@ -96,6 +98,8 @@
         pick = (in_first == left).astype(jnp.float32)
         q_pick[...] = pick.astype(jnp.bfloat16)
         g_pick[...] = (pick * mask_col).astype(jnp.bfloat16)
+        q_pick_t[...] = q_pick[...].T
+        g_pick_t[...] = g_pick[...].T
         for n in range(step_heads):
             bias[:, n * count:(n + 1) * count] = allowed_bias
         for ref in totals:
@@ -148,21 +152,30 @@
             parts.append(jnp.concatenate([part, part], axis=1) * chosen[...])
         return jnp.concatenate(parts, axis=0)
 
+    def times(cat, new, source, chosen_t):
+        if not turned:
+            return dot(cat[...], new, ((1,), (1,)))
+        parts = []
+        for n in range(step_heads):
+            part = source[:, n * HEAD_SIZE:(n + 1) * HEAD_SIZE].T
+            parts.append(jnp.concatenate([part, part], axis=0) * chosen_t[...])
+        return dot(cat[...], jnp.concatenate(parts, axis=1), ((1,), (0,)))
+
     def fold(value, op):
-        value = value.reshape(PIECE // 8, 8, columns)
+        value = value.reshape(piece_rows // 8, 8, columns)
         total = value[0]
-        for n in range(1, PIECE // 8):
+        for n in range(1, piece_rows // 8):
             total = op(total, value[n])
         return total
 
     def score(new_q):
-        product = dot(kcat[...], new_q, ((1,), (1,)))
+        product = times(kcat, new_q, q_ref, q_pick_t)
         top = None
-        for at in range(0, keys, PIECE):
-            piece = product[at:at + PIECE]
+        for at in range(0, keys, piece_rows):
+            piece = product[at:at + piece_rows]
             if at >= span:
-                piece = piece + bias[at - span:at - span + PIECE, :]
-            scores[at:at + PIECE, :] = piece
+                piece = piece + bias[at - span:at - span + piece_rows, :]
+            scores[at:at + piece_rows, :] = piece
             piece = fold(piece, jnp.maximum)
             top = piece if top is None else jnp.maximum(top, piece)
         return jnp.max(top, axis=0, keepdims=True)
@@ -170,20 +183,20 @@
     def sums(top):
         total = jnp.zeros((8, columns), jnp.float32)
         delta = jnp.zeros((8, columns), jnp.float32)
-        for at in range(0, keys, PIECE):
-            weight = jnp.exp2((scores[at:at + PIECE, :] - top) * (SCALE * LOG2E))
+        for at in range(0, keys, piece_rows):
+            weight = jnp.exp2((scores[at:at + piece_rows, :] - top) * (SCALE * LOG2E))
             total = total + fold(weight, jnp.add)
-            delta = delta + fold(weight * dprob[at:at + PIECE, :], jnp.add)
+            delta = delta + fold(weight * dprob[at:at + piece_rows, :], jnp.add)
         total = jnp.sum(total, axis=0, keepdims=True)
         return total, jnp.sum(delta, axis=0, keepdims=True) / total
 
     def finish(top, total, delta):
         shift = jnp.log2(total)
-        for at in range(0, keys, PIECE):
-            power = (scores[at:at + PIECE, :] - top) * (SCALE * LOG2E)
+        for at in range(0, keys, piece_rows):
+            power = (scores[at:at + piece_rows, :] - top) * (SCALE * LOG2E)
             probs = jnp.exp2(power - shift)
-            probs_b[at:at + PIECE, :] = probs.astype(jnp.bfloat16)
-            dscore[at:at + PIECE, :] = (probs * (dprob[at:at + PIECE, :] - delta)).astype(jnp.bfloat16)
+            probs_b[at:at + piece_rows, :] = probs.astype(jnp.bfloat16)
+            dscore[at:at + piece_rows, :] = (probs * (dprob[at:at + piece_rows, :] - delta)).astype(jnp.bfloat16)
 
     def work(later):
         new_q = pick(q_ref, q_pick)
@@ -191,7 +204,7 @@
         top = score(new_q)
         if later:
             later_rows()
-        dprob[...] = dot(vcat[...], new_g, ((1,), (1,)))
+        dprob[...] = times(vcat, new_g, g_ref, g_pick_t)
         total, delta = sums(top)
         if later:
             later_columns()
@@ -284,6 +297,7 @@
         functools.partial(
             attention_kernel, prompts=prompts, per_prefix=per_prefix, block_len=block_len,
             planes=planes, ranks=ranks, chained=chained, steps=steps, step_heads=step_heads,
+            piece_rows=PIECES[chunk], turned=TURNED[chunk],
         ),
         grid_spec=pltpu.PrefetchScalarGridSpec(
             num_scalar_prefetch=3,
@@ -301,6 +315,8 @@
                 pltpu.VMEM((count, step_heads * count), f32),
                 pltpu.VMEM((count, 2 * HEAD_SIZE), bf16),
                 pltpu.VMEM((count, 2 * HEAD_SIZE), bf16),
+                pltpu.VMEM((2 * HEAD_SIZE, count), bf16),
+                pltpu.VMEM((2 * HEAD_SIZE, count), bf16),
                 pltpu.VMEM((step_heads * count, 2 * HEAD_SIZE), bf16),
                 pltpu.VMEM((step_heads * count, 2 * HEAD_SIZE), bf16),
                 pltpu.VMEM((keys, step_heads * count), f32),
@@ -368,10 +384,11 @@
         total = add(totals[0], send(totals[1], 0, 0, 1))
         return add(total, send(away, 0, 1, 0)) if ranks == 2 else total
 
-    def reduce_planes(total):
+    def reduce_planes(total, *begun):
         mine = total[0]
         for k in range(1, planes):
-            mine = add(mine, send(total[k].astype(jnp.bfloat16), k, 0, 0))
+            away = tie(total[k].astype(jnp.bfloat16), *begun)
+            mine = add(mine, send(away, k, 0, 0))
         return mine.astype(jnp.bfloat16)
 
     chunks = len(CHUNKS)
@@ -396,7 +413,10 @@
         d_leaf.append(leaf_part)
         away = add(totals[2], send(totals[3], 0, 0, 1)).astype(jnp.bfloat16) if ranks == 2 else None
         parts.append((totals, away))
-    d_prefix = [reduce_planes(reduce_ranks(*part)) for part in parts]
+    begun = [parts[-1][1]] if ranks == 2 else []
+    d_prefix = [reduce_planes(reduce_ranks(*part), *begun) for part in parts[:-1]]
+    d_prefix.append(reduce_planes(reduce_ranks(*parts[-1])))
+    d_leaf = [tie(part, d_leaf[-1]) for part in d_leaf[:-1]] + d_leaf[-1:]
 
     def join(parts):
         halves = [jnp.split(p, 2, axis=1) for p in parts]

time: 117 us -> 117 us (level)
  waiting for transfers between devices: 35.5 us -> 32.2 us
  starting transfers between devices: 28.5 us -> 30.2 us
    ppermute x24, waiting for transfers between devices: 35.5 us -> 32.2 us  [send(): return lax.ppermute(array, 'dp', pairs)]
    ppermute x24, starting transfers between devices: 28.5 us -> 30.2 us  [send(): return lax.ppermute(array, 'dp', pairs)]
  transfers between devices with their start and end apart: 24 -> 24, of which waited for: 12 -> 12; matrix products, arithmetic and copies ran while one was open for 3% -> 3% of each run, Pallas kernels for 38% -> 39%
where the time goes in v8:
time: 117 us; the launch traced here: 116 us
  Pallas kernels  44.8 us (38%)
  waiting for transfers between devices  32.2 us (28%)
  starting transfers between devices  30.2 us (26%)
  local copies, waits for them, and re-layouts  4.08 us (3%)
  other arithmetic  3.61 us (3%)
    pallas_call x2, Pallas kernels, attention(): pl.pallas_call(functools.partial(attention_kernel, prompts=prompts, per_p...  44.8 us
    ppermute x24, waiting for transfers between devices, send(): return lax.ppermute(array, 'dp', pairs)  32.2 us
    ppermute x24, starting transfers between devices, send(): return lax.ppermute(array, 'dp', pairs)  30.2 us
  transfers between devices with their start and end apart: 24, of which 12 were waited for; matrix products, arithmetic and copies ran while one was open for 3% of the time, Pallas kernels for 39%

profile of v8, /device:TPU:0, one launch (start us, length us, event | category | flops | bytes accessed | tf_op | source)
XLA Modules:
  0.0 115.8 jit_solution(9343364515533306604)
XLA Ops:
  1.6 3.1 %collective-permute-start.4 = (bf16[128,512]{1,0:T(8,128)(2,1)S(1)}, bf16[128,512]{1,0:T(8,128)(2,1)S(1)}, u32[]{:S(2)}, u32[]{:S(2)}) collective-permute-start(bf16[128,512]{1,0:T(8,128)(2,1)S(1)} %pad_maximum_fusion.5), channel_id=1, source_target_pairs={{0,4},{1,5},{2,6},{3,7},{4,8},{5,9},{6,10},{7,11},{8,12},{9,13},{1... | collective-permute-start | bytes 393224 | tf_op jit(solution)/shard_map/ppermute | solution.py:365
  4.7 2.6 %collective-permute-start.5 = (bf16[128,512]{1,0:T(8,128)(2,1)S(1)}, bf16[128,512]{1,0:T(8,128)(2,1)S(1)}, u32[]{:S(2)}, u32[]{:S(2)}) collective-permute-start(bf16[128,512]{1,0:T(8,128)(2,1)S(1)} %pad_maximum_fusion.5), channel_id=1, source_target_pairs={{0,8},{1,9},{2,10},{3,11},{4,12},{5,13},{6,14},{7,15},{8,0},{9,1},... | collective-permute-start | bytes 393224 | tf_op jit(solution)/shard_map/ppermute | solution.py:365
  7.3 1.3 %collective-permute-start.6 = (bf16[128,512]{1,0:T(8,128)(2,1)S(1)}, bf16[128,512]{1,0:T(8,128)(2,1)S(1)}, u32[]{:S(2)}, u32[]{:S(2)}) collective-permute-start(bf16[128,512]{1,0:T(8,128)(2,1)S(1)} %pad_maximum_fusion.5), channel_id=1, source_target_pairs={{0,12},{1,13},{2,14},{3,15},{4,0},{5,1},{6,2},{7,3},{8,4},{9,5},{1... | collective-permute-start | bytes 393224 | tf_op jit(solution)/shard_map/ppermute | solution.py:365
  8.6 2.5 %collective-permute-done.4 = bf16[128,512]{1,0:T(8,128)(2,1)S(1)} collective-permute-done((bf16[128,512]{1,0:T(8,128)(2,1)S(1)}, bf16[128,512]{1,0:T(8,128)(2,1)S(1)}, u32[]{:S(2)}, u32[]{:S(2)}) %collective-permute-start.4) | collective-permute-done | bytes 131104 | tf_op jit(solution)/shard_map/ppermute | solution.py:365
  11.1 4.8 %collective-permute-done.5 = bf16[128,512]{1,0:T(8,128)(2,1)S(1)} collective-permute-done((bf16[128,512]{1,0:T(8,128)(2,1)S(1)}, bf16[128,512]{1,0:T(8,128)(2,1)S(1)}, u32[]{:S(2)}, u32[]{:S(2)}) %collective-permute-start.5) | collective-permute-done | bytes 131104 | tf_op jit(solution)/shard_map/ppermute | solution.py:365
  16.0 1.6 %collective-permute-start.8 = (bf16[512,512]{1,0:T(8,128)(2,1)S(1)}, bf16[512,512]{1,0:T(8,128)(2,1)S(1)}, u32[]{:S(2)}, u32[]{:S(2)}) collective-permute-start(bf16[512,512]{1,0:T(8,128)(2,1)S(1)} %pad_maximum_fusion.1.rest_0_), channel_id=1, source_target_pairs={{0,2},{1,3},{2,0},{3,1},{4,6},{5,7},{6,4},{7,5},{8,10},{9,11},{10,... | collective-permute-start | bytes 1572872 | tf_op jit(solution)/shard_map/ppermute | solution.py:365
  17.6 3.3 %collective-permute-start = (bf16[128,512]{1,0:T(8,128)(2,1)S(1)}, bf16[128,512]{1,0:T(8,128)(2,1)S(1)}, u32[]{:S(2)}, u32[]{:S(2)}) collective-permute-start(bf16[128,512]{1,0:T(8,128)(2,1)S(1)} %pad_maximum_fusion.4), channel_id=1, source_target_pairs={{0,4},{1,5},{2,6},{3,7},{4,8},{5,9},{6,10},{7,11},{8,12},{9,13},{1... | collective-permute-start | bytes 393224 | tf_op jit(solution)/shard_map/ppermute | solution.py:365
  20.9 1.6 %collective-permute-start.1 = (bf16[128,512]{1,0:T(8,128)(2,1)S(1)}, bf16[128,512]{1,0:T(8,128)(2,1)S(1)}, u32[]{:S(2)}, u32[]{:S(2)}) collective-permute-start(bf16[128,512]{1,0:T(8,128)(2,1)S(1)} %pad_maximum_fusion.4), channel_id=1, source_target_pairs={{0,8},{1,9},{2,10},{3,11},{4,12},{5,13},{6,14},{7,15},{8,0},{9,1},... | collective-permute-start | bytes 393224 | tf_op jit(solution)/shard_map/ppermute | solution.py:365
  23.3 2.9 %collective-permute-done = bf16[128,512]{1,0:T(8,128)(2,1)S(1)} collective-permute-done((bf16[128,512]{1,0:T(8,128)(2,1)S(1)}, bf16[128,512]{1,0:T(8,128)(2,1)S(1)}, u32[]{:S(2)}, u32[]{:S(2)}) %collective-permute-start) | collective-permute-done | bytes 131104 | tf_op jit(solution)/shard_map/ppermute | solution.py:365
  26.3 4.3 %collective-permute-done.1 = bf16[128,512]{1,0:T(8,128)(2,1)S(1)} collective-permute-done((bf16[128,512]{1,0:T(8,128)(2,1)S(1)}, bf16[128,512]{1,0:T(8,128)(2,1)S(1)}, u32[]{:S(2)}, u32[]{:S(2)}) %collective-permute-start.1) | collective-permute-done | bytes 131104 | tf_op jit(solution)/shard_map/ppermute | solution.py:365
  34.2 22.2 %shard_map.111 = (bf16[256,4096]{1,0:T(8,128)(2,1)}, bf16[256,4096]{1,0:T(8,128)(2,1)}, bf16[256,512]{1,0:T(8,128)(2,1)}, bf16[4,128,512]{2,1,0:T(8,128)(2,1)}, ...) custom-call(s32[16]{0:T(128)} %owner_ref.3, s32[4]{0:T(128)} %tokens_ref.3, ...), custom_call_target="tpu_custom_call" | custom-call | flops 9663676416 | bytes 8388608 | tf_op jit(solution)/shard_map/pallas_call | solution.py:296
  57.1 1.5 %collective-permute-done.10 = bf16[4,128,512]{2,1,0:T(8,128)(2,1)S(1)} collective-permute-done((bf16[4,128,512]{2,1,0:T(8,128)(2,1)}, bf16[4,128,512]{2,1,0:T(8,128)(2,1)S(1)}, u32[]{:S(2)}, u32[]{:S(2)}) %collective-permute-start.10) | collective-permute-done | bytes 524320 | tf_op jit(solution)/shard_map/ppermute | solution.py:365
  58.6 1.2 %add_convert_fusion.1 = bf16[4,128,512]{2,1,0:T(8,128)(2,1)S(1)} fusion(bf16[4,128,512]{2,1,0:T(8,128)(2,1)S(1)} %collective-permute-done.10, bf16[4,128,512]{2,1,0:T(8,128)(2,1)} %get-tuple-element.28), kind=kLoop, calls=%fused_computation.3 | loop fusion | flops 1048576 | bytes 1572864 | tf_op jit(solution)/shard_map/convert_element_type | solution.py:414
  61.1 22.7 %shard_map.112 = (bf16[256,4096]{1,0:T(8,128)(2,1)}, bf16[256,4096]{1,0:T(8,128)(2,1)}, bf16[256,512]{1,0:T(8,128)(2,1)}, bf16[4,128,512]{2,1,0:T(8,128)(2,1)}, ...) custom-call(s32[16]{0:T(128)} %owner_ref.3, ...), custom_call_target="tpu_custom_call", output_to_operand_aliasing={{0}: (13, {}), {1}: (14, {})} | custom-call | flops 9663676416 | bytes 8388608 | tf_op jit(solution)/shard_map/pallas_call | solution.py:296
  86.6 1.6 %collective-permute-start.20 = (bf16[4,128,512]{2,1,0:T(8,128)(2,1)S(1)}, bf16[4,128,512]{2,1,0:T(8,128)(2,1)S(1)}, u32[]{:S(2)}, u32[]{:S(2)}) collective-permute-start(bf16[4,128,512]{2,1,0:T(8,128)(2,1)S(1)} %add_convert_fusion), channel_id=1, source_target_pairs={{0,2},{1,3},{2,0},{3,1},{4,6},{5,7},{6,4},{7,5},{8,10},{9,11},{10,... | collective-permute-start | bytes 1572872 | tf_op jit(solution)/shard_map/ppermute | solution.py:365
  88.1 3.3 %collective-permute-start.16 = (bf16[128,512]{1,0:T(8,128)(2,1)S(1)}, bf16[128,512]{1,0:T(8,128)(2,1)S(1)}, u32[]{:S(2)}, u32[]{:S(2)}) collective-permute-start(bf16[128,512]{1,0:T(8,128)(2,1)S(1)} %get-tuple-element.43), channel_id=1, source_target_pairs={{0,4},{1,5},{2,6},{3,7},{4,8},{5,9},{6,10},{7,11},{8,12},{9,13},{1... | collective-permute-start | bytes 393224 | tf_op jit(solution)/shard_map/ppermute | solution.py:365
  91.4 1.7 %collective-permute-start.17 = (bf16[128,512]{1,0:T(8,128)(2,1)S(1)}, bf16[128,512]{1,0:T(8,128)(2,1)S(1)}, u32[]{:S(2)}, u32[]{:S(2)}) collective-permute-start(bf16[128,512]{1,0:T(8,128)(2,1)S(1)} %get-tuple-element.44), channel_id=1, source_target_pairs={{0,8},{1,9},{2,10},{3,11},{4,12},{5,13},{6,14},{7,15},{8,0},{9,1},... | collective-permute-start | bytes 393224 | tf_op jit(solution)/shard_map/ppermute | solution.py:365
  94.7 2.3 %collective-permute-done.16 = bf16[128,512]{1,0:T(8,128)(2,1)S(1)} collective-permute-done((bf16[128,512]{1,0:T(8,128)(2,1)S(1)}, bf16[128,512]{1,0:T(8,128)(2,1)S(1)}, u32[]{:S(2)}, u32[]{:S(2)}) %collective-permute-start.16) | collective-permute-done | bytes 131104 | tf_op jit(solution)/shard_map/ppermute | solution.py:365
  97.0 4.7 %collective-permute-done.17 = bf16[128,512]{1,0:T(8,128)(2,1)S(1)} collective-permute-done((bf16[128,512]{1,0:T(8,128)(2,1)S(1)}, bf16[128,512]{1,0:T(8,128)(2,1)S(1)}, u32[]{:S(2)}, u32[]{:S(2)}) %collective-permute-start.17) | collective-permute-done | bytes 131104 | tf_op jit(solution)/shard_map/ppermute | solution.py:365
  102.1 3.3 %collective-permute-start.21 = (bf16[128,512]{1,0:T(8,128)(2,1)S(1)}, bf16[128,512]{1,0:T(8,128)(2,1)S(1)}, u32[]{:S(2)}, u32[]{:S(2)}) collective-permute-start(bf16[128,512]{1,0:T(8,128)(2,1)S(1)} %get-tuple-element.55), channel_id=1, source_target_pairs={{0,4},{1,5},{2,6},{3,7},{4,8},{5,9},{6,10},{7,11},{8,12},{9,13},{1... | collective-permute-start | bytes 393224 | tf_op jit(solution)/shard_map/ppermute | solution.py:365
  105.5 1.2 %collective-permute-start.22 = (bf16[128,512]{1,0:T(8,128)(2,1)S(1)}, bf16[128,512]{1,0:T(8,128)(2,1)S(1)}, u32[]{:S(2)}, u32[]{:S(2)}) collective-permute-start(bf16[128,512]{1,0:T(8,128)(2,1)S(1)} %get-tuple-element.57), channel_id=1, source_target_pairs={{0,8},{1,9},{2,10},{3,11},{4,12},{5,13},{6,14},{7,15},{8,0},{9,1},... | collective-permute-start | bytes 393224 | tf_op jit(solution)/shard_map/ppermute | solution.py:365
  106.7 1.2 %collective-permute-start.23 = (bf16[128,512]{1,0:T(8,128)(2,1)S(1)}, bf16[128,512]{1,0:T(8,128)(2,1)S(1)}, u32[]{:S(2)}, u32[]{:S(2)}) collective-permute-start(bf16[128,512]{1,0:T(8,128)(2,1)S(1)} %get-tuple-element.56), channel_id=1, source_target_pairs={{0,12},{1,13},{2,14},{3,15},{4,0},{5,1},{6,2},{7,3},{8,4},{9,5},{1... | collective-permute-start | bytes 393224 | tf_op jit(solution)/shard_map/ppermute | solution.py:365
  107.9 2.3 %collective-permute-done.21 = bf16[128,512]{1,0:T(8,128)(2,1)S(1)} collective-permute-done((bf16[128,512]{1,0:T(8,128)(2,1)S(1)}, bf16[128,512]{1,0:T(8,128)(2,1)S(1)}, u32[]{:S(2)}, u32[]{:S(2)}) %collective-permute-start.21) | collective-permute-done | bytes 131104 | tf_op jit(solution)/shard_map/ppermute | solution.py:365
  110.2 4.8 %collective-permute-done.22 = bf16[128,512]{1,0:T(8,128)(2,1)S(1)} collective-permute-done((bf16[128,512]{1,0:T(8,128)(2,1)S(1)}, bf16[128,512]{1,0:T(8,128)(2,1)S(1)}, u32[]{:S(2)}, u32[]{:S(2)}) %collective-permute-start.22) | collective-permute-done | bytes 131104 | tf_op jit(solution)/shard_map/ppermute | solution.py:365
  (69 shorter events, 12.8 us)
Async XLA Ops:
  1.6 9.5 %collective-permute-start.4 = (bf16[128,512]{1,0:T(8,128)(2,1)S(1)}, bf16[128,512]{1,0:T(8,128)(2,1)S(1)}, u32[]{:S(2)}, u32[]{:S(2)}) collective-permute-start(bf16[128,512]{1,0:T(8,128)(2,1)S(1)} %pad_maximum_fusion.5), channel_id=1, source_target_pairs={{0,4},{1,5},{2,6},{3,7},{4,8},{5,9},{6,10},{7,11},{8,12},{9,13},{1... | collective-permute-start | bytes 393224 | tf_op jit(solution)/shard_map/ppermute | solution.py:365
  4.7 11.2 %collective-permute-start.5 = (bf16[128,512]{1,0:T(8,128)(2,1)S(1)}, bf16[128,512]{1,0:T(8,128)(2,1)S(1)}, u32[]{:S(2)}, u32[]{:S(2)}) collective-permute-start(bf16[128,512]{1,0:T(8,128)(2,1)S(1)} %pad_maximum_fusion.5), channel_id=1, source_target_pairs={{0,8},{1,9},{2,10},{3,11},{4,12},{5,13},{6,14},{7,15},{8,0},{9,1},... | collective-permute-start | bytes 393224 | tf_op jit(solution)/shard_map/ppermute | solution.py:365
  7.3 8.6 %collective-permute-start.6 = (bf16[128,512]{1,0:T(8,128)(2,1)S(1)}, bf16[128,512]{1,0:T(8,128)(2,1)S(1)}, u32[]{:S(2)}, u32[]{:S(2)}) collective-permute-start(bf16[128,512]{1,0:T(8,128)(2,1)S(1)} %pad_maximum_fusion.5), channel_id=1, source_target_pairs={{0,12},{1,13},{2,14},{3,15},{4,0},{5,1},{6,2},{7,3},{8,4},{9,5},{1... | collective-permute-start | bytes 393224 | tf_op jit(solution)/shard_map/ppermute | solution.py:365
  16.0 14.8 %collective-permute-start.8 = (bf16[512,512]{1,0:T(8,128)(2,1)S(1)}, bf16[512,512]{1,0:T(8,128)(2,1)S(1)}, u32[]{:S(2)}, u32[]{:S(2)}) collective-permute-start(bf16[512,512]{1,0:T(8,128)(2,1)S(1)} %pad_maximum_fusion.1.rest_0_), channel_id=1, source_target_pairs={{0,2},{1,3},{2,0},{3,1},{4,6},{5,7},{6,4},{7,5},{8,10},{9,11},{10,... | collective-permute-start | bytes 1572872 | tf_op jit(solution)/shard_map/ppermute | solution.py:365
  17.6 8.7 %collective-permute-start = (bf16[128,512]{1,0:T(8,128)(2,1)S(1)}, bf16[128,512]{1,0:T(8,128)(2,1)S(1)}, u32[]{:S(2)}, u32[]{:S(2)}) collective-permute-start(bf16[128,512]{1,0:T(8,128)(2,1)S(1)} %pad_maximum_fusion.4), channel_id=1, source_target_pairs={{0,4},{1,5},{2,6},{3,7},{4,8},{5,9},{6,10},{7,11},{8,12},{9,13},{1... | collective-permute-start | bytes 393224 | tf_op jit(solution)/shard_map/ppermute | solution.py:365
  20.9 9.7 %collective-permute-start.1 = (bf16[128,512]{1,0:T(8,128)(2,1)S(1)}, bf16[128,512]{1,0:T(8,128)(2,1)S(1)}, u32[]{:S(2)}, u32[]{:S(2)}) collective-permute-start(bf16[128,512]{1,0:T(8,128)(2,1)S(1)} %pad_maximum_fusion.4), channel_id=1, source_target_pairs={{0,8},{1,9},{2,10},{3,11},{4,12},{5,13},{6,14},{7,15},{8,0},{9,1},... | collective-permute-start | bytes 393224 | tf_op jit(solution)/shard_map/ppermute | solution.py:365
  22.5 8.1 %collective-permute-start.2 = (bf16[128,512]{1,0:T(8,128)(2,1)S(1)}, bf16[128,512]{1,0:T(8,128)(2,1)S(1)}, u32[]{:S(2)}, u32[]{:S(2)}) collective-permute-start(bf16[128,512]{1,0:T(8,128)(2,1)S(1)} %pad_maximum_fusion.4), channel_id=1, source_target_pairs={{0,12},{1,13},{2,14},{3,15},{4,0},{5,1},{6,2},{7,3},{8,4},{9,5},{1... | collective-permute-start | bytes 393224 | tf_op jit(solution)/shard_map/ppermute | solution.py:365
  23.3 9.3 %collective-permute-start.7 = (bf16[512,512]{1,0:T(8,128)(2,1)S(1)}, bf16[512,512]{1,0:T(8,128)(2,1)S(1)}, u32[]{:S(2)}, u32[]{:S(2)}) collective-permute-start(bf16[512,512]{1,0:T(8,128)(2,1)S(1)} %pad_maximum_fusion.1.rest_0_), channel_id=1, source_target_pairs={{0,1},{1,0},{2,3},{3,2},{4,5},{5,4},{6,7},{7,6},{8,9},{9,8},{10,11... | collective-permute-start | bytes 1572872 | tf_op jit(solution)/shard_map/ppermute | solution.py:365
  30.7 2.0 %collective-permute-start.3 = (bf16[512,512]{1,0:T(8,128)(2,1)S(1)}, bf16[512,512]{1,0:T(8,128)(2,1)S(1)}, u32[]{:S(2)}, u32[]{:S(2)}) collective-permute-start(bf16[512,512]{1,0:T(8,128)(2,1)S(1)} %pad_maximum_fusion.rest_0_), channel_id=1, source_target_pairs={{0,1},{1,0},{2,3},{3,2},{4,5},{5,4},{6,7},{7,6},{8,9},{9,8},{10,11... | collective-permute-start | bytes 1572872 | tf_op jit(solution)/shard_map/ppermute | solution.py:365
  30.8 2.6 %collective-permute-start.9 = (bf16[512,512]{1,0:T(8,128)(2,1)S(1)}, bf16[512,512]{1,0:T(8,128)(2,1)S(1)}, u32[]{:S(2)}, u32[]{:S(2)}) collective-permute-start(bf16[512,512]{1,0:T(8,128)(2,1)S(1)} %collective-permute-done.8.rest_2_), channel_id=1, source_target_pairs={{0,1},{1,0},{2,3},{3,2},{4,5},{5,4},{6,7},{7,6},{8,9},{9,8},{10,11... | collective-permute-start | bytes 1572872 | tf_op jit(solution)/shard_map/ppermute | solution.py:365
  31.3 25.3 %collective-permute-start.11 = (bf16[512,512]{1,0:T(8,128)(2,1)S(1)}, bf16[512,512]{1,0:T(8,128)(2,1)S(1)}, u32[]{:S(2)}, u32[]{:S(2)}) collective-permute-start(bf16[512,512]{1,0:T(8,128)(2,1)S(1)} %pad_maximum_fusion.rest_0_), channel_id=1, source_target_pairs={{0,2},{1,3},{2,0},{3,1},{4,6},{5,7},{6,4},{7,5},{8,10},{9,11},{10,... | collective-permute-start | bytes 1572872 | tf_op jit(solution)/shard_map/ppermute | solution.py:365
  56.4 2.2 %collective-permute-start.10 = (bf16[4,128,512]{2,1,0:T(8,128)(2,1)}, bf16[4,128,512]{2,1,0:T(8,128)(2,1)S(1)}, u32[]{:S(2)}, u32[]{:S(2)}) collective-permute-start(bf16[4,128,512]{2,1,0:T(8,128)(2,1)} %get-tuple-element.29), channel_id=1, source_target_pairs={{0,1},{1,0},{2,3},{3,2},{4,5},{5,4},{6,7},{7,6},{8,9},{9,8},{10,11... | collective-permute-start | bytes 1572872 | tf_op jit(solution)/shard_map/ppermute | solution.py:365
  56.6 3.7 %collective-permute-start.12 = (bf16[512,512]{1,0:T(8,128)(2,1)S(1)}, bf16[512,512]{1,0:T(8,128)(2,1)S(1)}, u32[]{:S(2)}, u32[]{:S(2)}) collective-permute-start(bf16[512,512]{1,0:T(8,128)(2,1)S(1)} %collective-permute-done.11.rest_2_), channel_id=1, source_target_pairs={{0,1},{1,0},{2,3},{3,2},{4,5},{5,4},{6,7},{7,6},{8,9},{9,8},{10,11... | collective-permute-start | bytes 1572872 | tf_op jit(solution)/shard_map/ppermute | solution.py:365
  57.0 28.4 %collective-permute-start.13 = (bf16[4,128,512]{2,1,0:T(8,128)(2,1)}, bf16[4,128,512]{2,1,0:T(8,128)(2,1)S(1)}, u32[]{:S(2)}, u32[]{:S(2)}) collective-permute-start(bf16[4,128,512]{2,1,0:T(8,128)(2,1)} %get-tuple-element.40), channel_id=1, source_target_pairs={{0,1},{1,0},{2,3},{3,2},{4,5},{5,4},{6,7},{7,6},{8,9},{9,8},{10,11... | collective-permute-start | bytes 1572872 | tf_op jit(solution)/shard_map/ppermute | solution.py:365
  59.8 25.6 %collective-permute-start.14 = (bf16[4,128,512]{2,1,0:T(8,128)(2,1)S(1)}, bf16[4,128,512]{2,1,0:T(8,128)(2,1)S(1)}, u32[]{:S(2)}, u32[]{:S(2)}) collective-permute-start(bf16[4,128,512]{2,1,0:T(8,128)(2,1)S(1)} %add_convert_fusion.1), channel_id=1, source_target_pairs={{0,2},{1,3},{2,0},{3,1},{4,6},{5,7},{6,4},{7,5},{8,10},{9,11},{10,... | collective-permute-start | bytes 1572872 | tf_op jit(solution)/shard_map/ppermute | solution.py:365
  83.8 2.2 %collective-permute-start.15 = (bf16[4,128,512]{2,1,0:T(8,128)(2,1)}, bf16[4,128,512]{2,1,0:T(8,128)(2,1)S(1)}, u32[]{:S(2)}, u32[]{:S(2)}) collective-permute-start(bf16[4,128,512]{2,1,0:T(8,128)(2,1)} %get-tuple-element.42), channel_id=1, source_target_pairs={{0,1},{1,0},{2,3},{3,2},{4,5},{5,4},{6,7},{7,6},{8,9},{9,8},{10,11... | collective-permute-start | bytes 1572872 | tf_op jit(solution)/shard_map/ppermute | solution.py:365
  83.9 17.9 %collective-permute-start.19 = (bf16[4,128,512]{2,1,0:T(8,128)(2,1)}, bf16[4,128,512]{2,1,0:T(8,128)(2,1)S(1)}, u32[]{:S(2)}, u32[]{:S(2)}) collective-permute-start(bf16[4,128,512]{2,1,0:T(8,128)(2,1)} %get-tuple-element.47), channel_id=1, source_target_pairs={{0,1},{1,0},{2,3},{3,2},{4,5},{5,4},{6,7},{7,6},{8,9},{9,8},{10,11... | collective-permute-start | bytes 1572872 | tf_op jit(solution)/shard_map/ppermute | solution.py:365
  86.6 15.3 %collective-permute-start.20 = (bf16[4,128,512]{2,1,0:T(8,128)(2,1)S(1)}, bf16[4,128,512]{2,1,0:T(8,128)(2,1)S(1)}, u32[]{:S(2)}, u32[]{:S(2)}) collective-permute-start(bf16[4,128,512]{2,1,0:T(8,128)(2,1)S(1)} %add_convert_fusion), channel_id=1, source_target_pairs={{0,2},{1,3},{2,0},{3,1},{4,6},{5,7},{6,4},{7,5},{8,10},{9,11},{10,... | collective-permute-start | bytes 1572872 | tf_op jit(solution)/shard_map/ppermute | solution.py:365
  88.1 8.9 %collective-permute-start.16 = (bf16[128,512]{1,0:T(8,128)(2,1)S(1)}, bf16[128,512]{1,0:T(8,128)(2,1)S(1)}, u32[]{:S(2)}, u32[]{:S(2)}) collective-permute-start(bf16[128,512]{1,0:T(8,128)(2,1)S(1)} %get-tuple-element.43), channel_id=1, source_target_pairs={{0,4},{1,5},{2,6},{3,7},{4,8},{5,9},{6,10},{7,11},{8,12},{9,13},{1... | collective-permute-start | bytes 393224 | tf_op jit(solution)/shard_map/ppermute | solution.py:365
  91.4 10.3 %collective-permute-start.17 = (bf16[128,512]{1,0:T(8,128)(2,1)S(1)}, bf16[128,512]{1,0:T(8,128)(2,1)S(1)}, u32[]{:S(2)}, u32[]{:S(2)}) collective-permute-start(bf16[128,512]{1,0:T(8,128)(2,1)S(1)} %get-tuple-element.44), channel_id=1, source_target_pairs={{0,8},{1,9},{2,10},{3,11},{4,12},{5,13},{6,14},{7,15},{8,0},{9,1},... | collective-permute-start | bytes 393224 | tf_op jit(solution)/shard_map/ppermute | solution.py:365
  93.1 8.6 %collective-permute-start.18 = (bf16[128,512]{1,0:T(8,128)(2,1)S(1)}, bf16[128,512]{1,0:T(8,128)(2,1)S(1)}, u32[]{:S(2)}, u32[]{:S(2)}) collective-permute-start(bf16[128,512]{1,0:T(8,128)(2,1)S(1)} %get-tuple-element.45), channel_id=1, source_target_pairs={{0,12},{1,13},{2,14},{3,15},{4,0},{5,1},{6,2},{7,3},{8,4},{9,5},{1... | collective-permute-start | bytes 393224 | tf_op jit(solution)/shard_map/ppermute | solution.py:365
  102.1 8.1 %collective-permute-start.21 = (bf16[128,512]{1,0:T(8,128)(2,1)S(1)}, bf16[128,512]{1,0:T(8,128)(2,1)S(1)}, u32[]{:S(2)}, u32[]{:S(2)}) collective-permute-start(bf16[128,512]{1,0:T(8,128)(2,1)S(1)} %get-tuple-element.55), channel_id=1, source_target_pairs={{0,4},{1,5},{2,6},{3,7},{4,8},{5,9},{6,10},{7,11},{8,12},{9,13},{1... | collective-permute-start | bytes 393224 | tf_op jit(solution)/shard_map/ppermute | solution.py:365
  105.5 9.6 %collective-permute-start.22 = (bf16[128,512]{1,0:T(8,128)(2,1)S(1)}, bf16[128,512]{1,0:T(8,128)(2,1)S(1)}, u32[]{:S(2)}, u32[]{:S(2)}) collective-permute-start(bf16[128,512]{1,0:T(8,128)(2,1)S(1)} %get-tuple-element.57), channel_id=1, source_target_pairs={{0,8},{1,9},{2,10},{3,11},{4,12},{5,13},{6,14},{7,15},{8,0},{9,1},... | collective-permute-start | bytes 393224 | tf_op jit(solution)/shard_map/ppermute | solution.py:365
  106.7 8.4 %collective-permute-start.23 = (bf16[128,512]{1,0:T(8,128)(2,1)S(1)}, bf16[128,512]{1,0:T(8,128)(2,1)S(1)}, u32[]{:S(2)}, u32[]{:S(2)}) collective-permute-start(bf16[128,512]{1,0:T(8,128)(2,1)S(1)} %get-tuple-element.56), channel_id=1, source_target_pairs={{0,12},{1,13},{2,14},{3,15},{4,0},{5,1},{6,2},{7,3},{8,4},{9,5},{1... | collective-permute-start | bytes 393224 | tf_op jit(solution)/shard_map/ppermute | solution.py:365
  (12 other events, 125.5 us)

commit v9 on v8

--- a/solution.py
+++ b/solution.py
@@ -17,10 +17,10 @@
 def dot(a, b, contract):
     return lax.dot_general(a, b, (contract, ((), ())), preferred_element_type=jnp.float32)
 
-CHUNKS = (2, 2)
-STEP_HEADS = (4, 2)
-PIECES = (32, 16)
-TURNED = (True, False)
+CHUNKS = (1, 3)
+STEP_HEADS = (2, 4)
+PIECES = (32, 32)
+TURNED = (False, False)
 
 
 def attention_kernel(
@@ -375,35 +375,53 @@
         mine = jnp.concatenate(
             [prefix_key_value[:, low:high], prefix_key_value[:, middle + low:middle + high]], axis=1
         )
-        return jnp.concatenate([mine] + [send(mine, k, 0, 0) for k in range(1, planes)], axis=0)
+        return [mine] + [send(mine, k, 0, 0) for k in range(1, planes)]
 
     def add(own, received):
         return own.astype(f32) + received.astype(f32)
 
-    def reduce_ranks(totals, away):
-        total = add(totals[0], send(totals[1], 0, 0, 1))
-        return add(total, send(away, 0, 1, 0)) if ranks == 2 else total
-
-    def reduce_planes(total, *begun):
-        mine = total[0]
+    def reduce_cores(totals):
+        away = add(totals[2], send(totals[3], 0, 0, 1)).astype(jnp.bfloat16) if ranks == 2 else None
+        return away, add(totals[0], send(totals[1], 0, 0, 1))
+
+    def reduce_ranks(away, keep, in_pieces, *last):
+        if ranks == 1:
+            sums = [keep[k] for k in range(planes)]
+        elif in_pieces:
+            sums, before = [None] * planes, []
+            for k in sorted(range(planes), key=lambda k: -min(k, planes - k)):
+                mine = tie(away[k], *before) if k == 0 else away[k]
+                sums[k] = add(keep[k], tie(send(mine, 0, 1, 0), *before))
+                before = [sums[k]]
+        else:
+            total = add(keep, tie(send(away, 0, 1, 0), *last))
+            sums = [total[k] for k in range(planes)]
+        return sums[:1] + [part.astype(jnp.bfloat16) for part in sums[1:]]
+
+    def reduce_planes(sums, *last):
+        mine = sums[0]
         for k in range(1, planes):
-            away = tie(total[k].astype(jnp.bfloat16), *begun)
-            mine = add(mine, send(away, k, 0, 0))
+            mine = add(mine, tie(send(sums[k], k, 0, 0), *last))
         return mine.astype(jnp.bfloat16)
 
     chunks = len(CHUNKS)
-    near = [by_planes(chunk) for chunk in range(chunks)]
-    near_far = [send(n, 0, 0, 1) for n in near]
-    other = [send(n, 0, 1, 0) for n in near] if ranks == 2 else []
-    d_leaf, d_prefix, earlier = [], [], ()
-    parts = []
+    pieces = [by_planes(chunk) for chunk in range(chunks)]
+    d_leaf, parts, earlier = [], [], ()
     for chunk in range(chunks):
-        first = [place] + near[chunk + 1:chunk + 2] + near_far[chunk + 1:chunk + 2]
-        if chunk and ranks == 2:
-            first.append(parts[-1][1])
-        sources = [near[chunk], near_far[chunk]]
+        first = [place]
+        own, rest = pieces[chunk][0], pieces[chunk][1:]
+        if chunk:
+            if ranks == 2:
+                first.append(parts[-1][0])
+            rest = [tie(piece, d_leaf[-1]) for piece in rest]
+        rest = jnp.concatenate(rest, axis=0)
+        near = jnp.concatenate([own, rest], axis=0)
+        sources = [near, send(near, 0, 0, 1)]
         if ranks == 2:
-            row = tie(other[chunk], d_leaf[-1] if chunk else near[1])
+            if chunk:
+                row = jnp.concatenate([send(own, 0, 1, 0), send(rest, 0, 1, 0)], axis=0)
+            else:
+                row = tie(send(near, 0, 1, 0), pieces[1][1])
             sources += [row, send(row, 0, 0, 1)]
         attended, d_query, leaf_part, *totals = attention(
             chunk, block_owner, subtree_tokens, tie(*first), query, d_out, leaf_key_value,
@@ -411,11 +429,13 @@
         )
         earlier = (attended, d_query)
         d_leaf.append(leaf_part)
-        away = add(totals[2], send(totals[3], 0, 0, 1)).astype(jnp.bfloat16) if ranks == 2 else None
-        parts.append((totals, away))
-    begun = [parts[-1][1]] if ranks == 2 else []
-    d_prefix = [reduce_planes(reduce_ranks(*part), *begun) for part in parts[:-1]]
-    d_prefix.append(reduce_planes(reduce_ranks(*parts[-1])))
+        parts.append(reduce_cores(totals))
+    last = reduce_ranks(*parts[-1], True)
+    d_prefix = [
+        reduce_planes(reduce_ranks(*part, False, d_leaf[-1]), last[planes // 2])
+        for part in parts[:-1]
+    ]
+    d_prefix.append(reduce_planes(last))
     d_leaf = [tie(part, d_leaf[-1]) for part in d_leaf[:-1]] + d_leaf[-1:]
 
     def join(parts):

time: 117 us -> 133 us (1.14)
  waiting for transfers between devices: 32.2 us -> 55.1 us
  starting transfers between devices: 30.2 us -> 25.8 us
    ppermute x24 -> x28, waiting for transfers between devices: 32.2 us -> 55.1 us  [send(): return lax.ppermute(array, 'dp', pairs)]
    ppermute x24 -> x28, starting transfers between devices: 30.2 us -> 25.8 us  [send(): return lax.ppermute(array, 'dp', pairs)]
  transfers between devices with their start and end apart: 24 -> 28, of which waited for: 12 -> 10; matrix products, arithmetic and copies ran while one was open for 3% -> 2% of each run, Pallas kernels for 39% -> 33%
where the time goes in v9:
time: 133 us; the launch traced here: 132 us
  waiting for transfers between devices  55.1 us (41%)
  Pallas kernels  44.2 us (33%)
  starting transfers between devices  25.8 us (19%)
  local copies, waits for them, and re-layouts  3.83 us (3%)
  other arithmetic  2.51 us (2%)
    ppermute x28, waiting for transfers between devices, send(): return lax.ppermute(array, 'dp', pairs)  55.1 us
    pallas_call x2, Pallas kernels, attention(): pl.pallas_call(functools.partial(attention_kernel, prompts=prompts, per_p...  44.2 us
    ppermute x28, starting transfers between devices, send(): return lax.ppermute(array, 'dp', pairs)  25.8 us
  transfers between devices with their start and end apart: 28, of which 10 were waited for; matrix products, arithmetic and copies ran while one was open for 2% of the time, Pallas kernels for 33%

profile of v9, /device:TPU:0, one launch (start us, length us, event | category | flops | bytes accessed | tf_op | source)
XLA Modules:
  0.0 132.5 jit_solution(15955336694713285258)
XLA Ops:
  1.4 5.1 %collective-permute-start.2 = (bf16[128,256]{1,0:T(8,128)(2,1)S(1)}, bf16[128,256]{1,0:T(8,128)(2,1)S(1)}, u32[]{:S(2)}, u32[]{:S(2)}) collective-permute-start(bf16[128,256]{1,0:T(8,128)(2,1)S(1)} %pad_maximum_fusion.6), channel_id=1, source_target_pairs={{0,12},{1,13},{2,14},{3,15},{4,0},{5,1},{6,2},{7,3},{8,4},{9,5},{1... | collective-permute-start | bytes 196616 | tf_op jit(solution)/shard_map/ppermute | solution.py:365
  6.5 1.0 collective-permute-start
  7.5 1.0 fusion.14
  9.0 4.0 %collective-permute-done.1 = bf16[128,256]{1,0:T(8,128)(2,1)S(1)} collective-permute-done((bf16[128,256]{1,0:T(8,128)(2,1)S(1)}, bf16[128,256]{1,0:T(8,128)(2,1)S(1)}, u32[]{:S(2)}, u32[]{:S(2)}) %collective-permute-start.1) | collective-permute-done | bytes 65568 | tf_op jit(solution)/shard_map/ppermute | solution.py:365
  13.0 1.6 %collective-permute-start.4 = (bf16[512,256]{1,0:T(8,128)(2,1)S(1)}, bf16[512,256]{1,0:T(8,128)(2,1)S(1)}, u32[]{:S(2)}, u32[]{:S(2)}) collective-permute-start(bf16[512,256]{1,0:T(8,128)(2,1)S(1)} %pad_maximum_fusion.3.rest_0_), channel_id=1, source_target_pairs={{0,2},{1,3},{2,0},{3,1},{4,6},{5,7},{6,4},{7,5},{8,10},{9,11},{10,... | collective-permute-start | bytes 786440 | tf_op jit(solution)/shard_map/ppermute | solution.py:365
  14.9 8.0 %collective-permute-done.5 = bf16[128,768]{1,0:T(8,128)(2,1)S(1)} collective-permute-done((bf16[128,768]{1,0:T(8,128)(2,1)S(1)}, bf16[128,768]{1,0:T(8,128)(2,1)S(1)}, u32[]{:S(2)}, u32[]{:S(2)}) %collective-permute-start.5) | collective-permute-done | bytes 196640 | tf_op jit(solution)/shard_map/ppermute | solution.py:365
  23.0 1.4 %collective-permute-done.6.rest_3_ = bf16[512,256]{1,0:T(8,128)(2,1)S(1)} collective-permute-done((bf16[512,256]{1,0:T(8,128)(2,1)S(1)}, bf16[512,256]{1,0:T(8,128)(2,1)S(1)}, u32[]{:S(2)}, u32[]{:S(2)}) %collective-permute-start.6) | collective-permute-done | bytes 262176 | tf_op jit(solution)/shard_map/ppermute | solution.py:365
  25.1 13.2 %shard_map.111 = (bf16[256,4096]{1,0:T(8,128)(2,1)}, bf16[256,4096]{1,0:T(8,128)(2,1)}, bf16[256,256]{1,0:T(8,128)(2,1)}, bf16[4,128,256]{2,1,0:T(8,128)(2,1)}, ...) custom-call(s32[16]{0:T(128)} %owner_ref.3, s32[4]{0:T(128)} %tokens_ref.3, ...), custom_call_target="tpu_custom_call" | custom-call | flops 4831838208 | bytes 4194304 | tf_op jit(solution)/shard_map/pallas_call | solution.py:296
  39.0 1.5 %collective-permute-start.11 = (bf16[128,768]{1,0:T(8,128)(2,1)S(1)}, bf16[128,768]{1,0:T(8,128)(2,1)S(1)}, u32[]{:S(2)}, u32[]{:S(2)}) collective-permute-start(bf16[128,768]{1,0:T(8,128)(2,1)S(1)} %pad_maximum_fusion.5), channel_id=1, source_target_pairs={{0,2},{1,3},{2,0},{3,1},{4,6},{5,7},{6,4},{7,5},{8,10},{9,11},{10,... | collective-permute-start | bytes 589832 | tf_op jit(solution)/shard_map/ppermute | solution.py:365
  40.5 17.6 %collective-permute-done.11 = bf16[128,768]{1,0:T(8,128)(2,1)S(1)} collective-permute-done((bf16[128,768]{1,0:T(8,128)(2,1)S(1)}, bf16[128,768]{1,0:T(8,128)(2,1)S(1)}, u32[]{:S(2)}, u32[]{:S(2)}) %collective-permute-start.11) | collective-permute-done | bytes 196640 | tf_op jit(solution)/shard_map/ppermute | solution.py:365
  59.3 2.6 %collective-permute-done.7 = bf16[4,128,256]{2,1,0:T(8,128)(2,1)S(1)} collective-permute-done((bf16[4,128,256]{2,1,0:T(8,128)(2,1)S(1)}, bf16[4,128,256]{2,1,0:T(8,128)(2,1)S(1)}, u32[]{:S(2)}, u32[]{:S(2)}) %collective-permute-start.7) | collective-permute-done | bytes 262176 | tf_op jit(solution)/shard_map/ppermute | solution.py:365
  63.8 31.0 %shard_map.112 = (bf16[256,4096]{1,0:T(8,128)(2,1)}, bf16[256,4096]{1,0:T(8,128)(2,1)}, bf16[256,768]{1,0:T(8,128)(2,1)}, bf16[4,128,768]{2,1,0:T(8,128)(2,1)}, ...) custom-call(s32[16]{0:T(128)} %owner_ref.3, ...), custom_call_target="tpu_custom_call", output_to_operand_aliasing={{0}: (13, {}), {1}: (14, {})} | custom-call | flops 14495514624 | bytes 12582912 | tf_op jit(solution)/shard_map/pallas_call | solution.py:296
  95.1 1.2 collective-permute-start.16
  96.3 2.7 %collective-permute-start.21 = (bf16[128,256]{1,0:T(8,128)(2,1)S(1)}, bf16[128,256]{1,0:T(8,128)(2,1)S(1)}, u32[]{:S(2)}, u32[]{:S(2)}) collective-permute-start(bf16[128,256]{1,0:T(8,128)(2,1)S(1)} %get-tuple-element.69), channel_id=1, source_target_pairs={{0,12},{1,13},{2,14},{3,15},{4,0},{5,1},{6,2},{7,3},{8,4},{9,5},{1... | collective-permute-start | bytes 196616 | tf_op jit(solution)/shard_map/ppermute | solution.py:365
  99.0 0.9 pad_maximum_fusion.2
  100.2 1.6 %collective-permute-start.23 = (bf16[128,768]{1,0:T(8,128)(2,1)S(1)}, bf16[128,768]{1,0:T(8,128)(2,1)S(1)}, u32[]{:S(2)}, u32[]{:S(2)}) collective-permute-start(bf16[128,768]{1,0:T(8,128)(2,1)S(1)} %get-tuple-element.63), channel_id=1, source_target_pairs={{0,2},{1,3},{2,0},{3,1},{4,6},{5,7},{6,4},{7,5},{8,10},{9,11},{10,... | collective-permute-start | bytes 589832 | tf_op jit(solution)/shard_map/ppermute | solution.py:365
  101.8 1.0 collective-permute-start.19
  102.9 8.8 %collective-permute-done.19 = bf16[128,768]{1,0:T(8,128)(2,1)S(1)} collective-permute-done((bf16[128,768]{1,0:T(8,128)(2,1)S(1)}, bf16[128,768]{1,0:T(8,128)(2,1)S(1)}, u32[]{:S(2)}, u32[]{:S(2)}) %collective-permute-start.19) | collective-permute-done | bytes 196640 | tf_op jit(solution)/shard_map/ppermute | solution.py:365
  111.7 1.5 %collective-permute-start.22 = (bf16[128,768]{1,0:T(8,128)(2,1)S(1)}, bf16[128,768]{1,0:T(8,128)(2,1)S(1)}, u32[]{:S(2)}, u32[]{:S(2)}) collective-permute-start(bf16[128,768]{1,0:T(8,128)(2,1)S(1)} %get-tuple-element.64), channel_id=1, source_target_pairs={{0,2},{1,3},{2,0},{3,1},{4,6},{5,7},{6,4},{7,5},{8,10},{9,11},{10,... | collective-permute-start | bytes 589832 | tf_op jit(solution)/shard_map/ppermute | solution.py:365
  113.3 3.0 %collective-permute-start.26 = (bf16[128,768]{1,0:T(8,128)(2,1)S(1)}, bf16[128,768]{1,0:T(8,128)(2,1)S(1)}, u32[]{:S(2)}, u32[]{:S(2)}) collective-permute-start(bf16[128,768]{1,0:T(8,128)(2,1)S(1)} %fusion.7), channel_id=1, source_target_pairs={{0,8},{1,9},{2,10},{3,11},{4,12},{5,13},{6,14},{7,15},{8,0},{9,1},... | collective-permute-start | bytes 589832 | tf_op jit(solution)/shard_map/ppermute | solution.py:365
  116.4 1.8 %collective-permute-done.22 = bf16[128,768]{1,0:T(8,128)(2,1)S(1)} collective-permute-done((bf16[128,768]{1,0:T(8,128)(2,1)S(1)}, bf16[128,768]{1,0:T(8,128)(2,1)S(1)}, u32[]{:S(2)}, u32[]{:S(2)}) %collective-permute-start.22) | collective-permute-done | bytes 196640 | tf_op jit(solution)/shard_map/ppermute | solution.py:365
  118.3 2.1 %collective-permute-start.27 = (bf16[128,768]{1,0:T(8,128)(2,1)S(1)}, bf16[128,768]{1,0:T(8,128)(2,1)S(1)}, u32[]{:S(2)}, u32[]{:S(2)}) collective-permute-start(bf16[128,768]{1,0:T(8,128)(2,1)S(1)} %fusion.1), channel_id=1, source_target_pairs={{0,12},{1,13},{2,14},{3,15},{4,0},{5,1},{6,2},{7,3},{8,4},{9,5},{1... | collective-permute-start | bytes 589832 | tf_op jit(solution)/shard_map/ppermute | solution.py:365
  121.1 4.9 %collective-permute-done.24 = bf16[128,768]{1,0:T(8,128)(2,1)S(1)} collective-permute-done((bf16[128,768]{1,0:T(8,128)(2,1)S(1)}, bf16[128,768]{1,0:T(8,128)(2,1)S(1)}, u32[]{:S(2)}, u32[]{:S(2)}) %collective-permute-start.24) | collective-permute-done | bytes 196640 | tf_op jit(solution)/shard_map/ppermute | solution.py:365
  126.0 5.6 %collective-permute-done.27 = bf16[128,768]{1,0:T(8,128)(2,1)S(1)} collective-permute-done((bf16[128,768]{1,0:T(8,128)(2,1)S(1)}, bf16[128,768]{1,0:T(8,128)(2,1)S(1)}, u32[]{:S(2)}, u32[]{:S(2)}) %collective-permute-start.27) | collective-permute-done | bytes 196640 | tf_op jit(solution)/shard_map/ppermute | solution.py:365
  (94 shorter events, 8.6 us)
Async XLA Ops:
  1.4 7.6 %collective-permute-start.2 = (bf16[128,256]{1,0:T(8,128)(2,1)S(1)}, bf16[128,256]{1,0:T(8,128)(2,1)S(1)}, u32[]{:S(2)}, u32[]{:S(2)}) collective-permute-start(bf16[128,256]{1,0:T(8,128)(2,1)S(1)} %pad_maximum_fusion.6), channel_id=1, source_target_pairs={{0,12},{1,13},{2,14},{3,15},{4,0},{5,1},{6,2},{7,3},{8,4},{9,5},{1... | collective-permute-start | bytes 196616 | tf_op jit(solution)/shard_map/ppermute | solution.py:365
  6.5 6.5 %collective-permute-start.1 = (bf16[128,256]{1,0:T(8,128)(2,1)S(1)}, bf16[128,256]{1,0:T(8,128)(2,1)S(1)}, u32[]{:S(2)}, u32[]{:S(2)}) collective-permute-start(bf16[128,256]{1,0:T(8,128)(2,1)S(1)} %pad_maximum_fusion.6), channel_id=1, source_target_pairs={{0,8},{1,9},{2,10},{3,11},{4,12},{5,13},{6,14},{7,15},{8,0},{9,1},... | collective-permute-start | bytes 196616 | tf_op jit(solution)/shard_map/ppermute | solution.py:365
  6.5 6.5 %collective-permute-start = (bf16[128,256]{1,0:T(8,128)(2,1)S(1)}, bf16[128,256]{1,0:T(8,128)(2,1)S(1)}, u32[]{:S(2)}, u32[]{:S(2)}) collective-permute-start(bf16[128,256]{1,0:T(8,128)(2,1)S(1)} %pad_maximum_fusion.6), channel_id=1, source_target_pairs={{0,4},{1,5},{2,6},{3,7},{4,8},{5,9},{6,10},{7,11},{8,12},{9,13},{1... | collective-permute-start | bytes 196616 | tf_op jit(solution)/shard_map/ppermute | solution.py:365
  13.0 9.8 %collective-permute-start.4 = (bf16[512,256]{1,0:T(8,128)(2,1)S(1)}, bf16[512,256]{1,0:T(8,128)(2,1)S(1)}, u32[]{:S(2)}, u32[]{:S(2)}) collective-permute-start(bf16[512,256]{1,0:T(8,128)(2,1)S(1)} %pad_maximum_fusion.3.rest_0_), channel_id=1, source_target_pairs={{0,2},{1,3},{2,0},{3,1},{4,6},{5,7},{6,4},{7,5},{8,10},{9,11},{10,... | collective-permute-start | bytes 786440 | tf_op jit(solution)/shard_map/ppermute | solution.py:365
  14.6 8.2 %collective-permute-start.5 = (bf16[128,768]{1,0:T(8,128)(2,1)S(1)}, bf16[128,768]{1,0:T(8,128)(2,1)S(1)}, u32[]{:S(2)}, u32[]{:S(2)}) collective-permute-start(bf16[128,768]{1,0:T(8,128)(2,1)S(1)} %pad_maximum_fusion.5), channel_id=1, source_target_pairs={{0,4},{1,5},{2,6},{3,7},{4,8},{5,9},{6,10},{7,11},{8,12},{9,13},{1... | collective-permute-start | bytes 589832 | tf_op jit(solution)/shard_map/ppermute | solution.py:365
  14.9 8.1 %collective-permute-start.3 = (bf16[512,256]{1,0:T(8,128)(2,1)S(1)}, bf16[512,256]{1,0:T(8,128)(2,1)S(1)}, u32[]{:S(2)}, u32[]{:S(2)}) collective-permute-start(bf16[512,256]{1,0:T(8,128)(2,1)S(1)} %pad_maximum_fusion.3.rest_0_), channel_id=1, source_target_pairs={{0,1},{1,0},{2,3},{3,2},{4,5},{5,4},{6,7},{7,6},{8,9},{9,8},{10,11... | collective-permute-start | bytes 786440 | tf_op jit(solution)/shard_map/ppermute | solution.py:365
  22.9 15.4 %collective-permute-start.9 = (bf16[128,768]{1,0:T(8,128)(2,1)S(1)}, bf16[128,768]{1,0:T(8,128)(2,1)S(1)}, u32[]{:S(2)}, u32[]{:S(2)}) collective-permute-start(bf16[128,768]{1,0:T(8,128)(2,1)S(1)} %pad_maximum_fusion.5), channel_id=1, source_target_pairs={{0,12},{1,13},{2,14},{3,15},{4,0},{5,1},{6,2},{7,3},{8,4},{9,5},{1... | collective-permute-start | bytes 589832 | tf_op jit(solution)/shard_map/ppermute | solution.py:365
  22.9 15.4 %collective-permute-start.8 = (bf16[128,768]{1,0:T(8,128)(2,1)S(1)}, bf16[128,768]{1,0:T(8,128)(2,1)S(1)}, u32[]{:S(2)}, u32[]{:S(2)}) collective-permute-start(bf16[128,768]{1,0:T(8,128)(2,1)S(1)} %pad_maximum_fusion.5), channel_id=1, source_target_pairs={{0,8},{1,9},{2,10},{3,11},{4,12},{5,13},{6,14},{7,15},{8,0},{9,1},... | collective-permute-start | bytes 589832 | tf_op jit(solution)/shard_map/ppermute | solution.py:365
  38.4 19.8 %collective-permute-start.12 = (bf16[384,768]{1,0:T(8,128)(2,1)S(1)}, bf16[384,768]{1,0:T(8,128)(2,1)S(1)}, u32[]{:S(2)}, u32[]{:S(2)}) collective-permute-start(bf16[384,768]{1,0:T(8,128)(2,1)S(1)} %pad_maximum_fusion.1), channel_id=1, source_target_pairs={{0,2},{1,3},{2,0},{3,1},{4,6},{5,7},{6,4},{7,5},{8,10},{9,11},{10,... | collective-permute-start | bytes 1769480 | tf_op jit(solution)/shard_map/ppermute | solution.py:365
  39.0 19.1 %collective-permute-start.11 = (bf16[128,768]{1,0:T(8,128)(2,1)S(1)}, bf16[128,768]{1,0:T(8,128)(2,1)S(1)}, u32[]{:S(2)}, u32[]{:S(2)}) collective-permute-start(bf16[128,768]{1,0:T(8,128)(2,1)S(1)} %pad_maximum_fusion.5), channel_id=1, source_target_pairs={{0,2},{1,3},{2,0},{3,1},{4,6},{5,7},{6,4},{7,5},{8,10},{9,11},{10,... | collective-permute-start | bytes 589832 | tf_op jit(solution)/shard_map/ppermute | solution.py:365
  58.1 4.5 %collective-permute-start.10 = (bf16[512,768]{1,0:T(8,128)(2,1)S(1)}, bf16[512,768]{1,0:T(8,128)(2,1)S(1)}, u32[]{:S(2)}, u32[]{:S(2)}) collective-permute-start(bf16[512,768]{1,0:T(8,128)(2,1)S(1)} %pad_maximum_fusion.rest_0_), channel_id=1, source_target_pairs={{0,1},{1,0},{2,3},{3,2},{4,5},{5,4},{6,7},{7,6},{8,9},{9,8},{10,11... | collective-permute-start | bytes 2359304 | tf_op jit(solution)/shard_map/ppermute | solution.py:365
  58.9 36.0 %collective-permute-start.14 = (bf16[4,128,256]{2,1,0:T(8,128)(2,1)S(1)}, bf16[4,128,256]{2,1,0:T(8,128)(2,1)S(1)}, u32[]{:S(2)}, u32[]{:S(2)}) collective-permute-start(bf16[4,128,256]{2,1,0:T(8,128)(2,1)S(1)} %copy-done.12), channel_id=1, source_target_pairs={{0,1},{1,0},{2,3},{3,2},{4,5},{5,4},{6,7},{7,6},{8,9},{9,8},{10,11... | collective-permute-start | bytes 786440 | tf_op jit(solution)/shard_map/ppermute | solution.py:365
  62.0 32.8 %collective-permute-start.15 = (bf16[4,128,256]{2,1,0:T(8,128)(2,1)S(1)}, bf16[4,128,256]{2,1,0:T(8,128)(2,1)S(1)}, u32[]{:S(2)}, u32[]{:S(2)}) collective-permute-start(bf16[4,128,256]{2,1,0:T(8,128)(2,1)S(1)} %add_convert_fusion.1), channel_id=1, source_target_pairs={{0,2},{1,3},{2,0},{3,1},{4,6},{5,7},{6,4},{7,5},{8,10},{9,11},{10,... | collective-permute-start | bytes 786440 | tf_op jit(solution)/shard_map/ppermute | solution.py:365
  94.8 5.1 %collective-permute-start.18 = (bf16[4,128,768]{2,1,0:T(8,128)(2,1)}, bf16[4,128,768]{2,1,0:T(8,128)(2,1)S(1)}, u32[]{:S(2)}, u32[]{:S(2)}) collective-permute-start(bf16[4,128,768]{2,1,0:T(8,128)(2,1)} %get-tuple-element.52), channel_id=1, source_target_pairs={{0,1},{1,0},{2,3},{3,2},{4,5},{5,4},{6,7},{7,6},{8,9},{9,8},{10,11... | collective-permute-start | bytes 2359304 | tf_op jit(solution)/shard_map/ppermute | solution.py:365
  95.1 21.3 %collective-permute-start.16 = (bf16[128,256]{1,0:T(8,128)(2,1)S(1)}, bf16[128,256]{1,0:T(8,128)(2,1)S(1)}, u32[]{:S(2)}, u32[]{:S(2)}) collective-permute-start(bf16[128,256]{1,0:T(8,128)(2,1)S(1)} %get-tuple-element.68), channel_id=1, source_target_pairs={{0,4},{1,5},{2,6},{3,7},{4,8},{5,9},{6,10},{7,11},{8,12},{9,13},{1... | collective-permute-start | bytes 196616 | tf_op jit(solution)/shard_map/ppermute | solution.py:365
  96.3 17.0 %collective-permute-start.21 = (bf16[128,256]{1,0:T(8,128)(2,1)S(1)}, bf16[128,256]{1,0:T(8,128)(2,1)S(1)}, u32[]{:S(2)}, u32[]{:S(2)}) collective-permute-start(bf16[128,256]{1,0:T(8,128)(2,1)S(1)} %get-tuple-element.69), channel_id=1, source_target_pairs={{0,12},{1,13},{2,14},{3,15},{4,0},{5,1},{6,2},{7,3},{8,4},{9,5},{1... | collective-permute-start | bytes 196616 | tf_op jit(solution)/shard_map/ppermute | solution.py:365
  98.9 17.4 %collective-permute-start.20 = (bf16[128,256]{1,0:T(8,128)(2,1)S(1)}, bf16[128,256]{1,0:T(8,128)(2,1)S(1)}, u32[]{:S(2)}, u32[]{:S(2)}) collective-permute-start(bf16[128,256]{1,0:T(8,128)(2,1)S(1)} %get-tuple-element.70), channel_id=1, source_target_pairs={{0,8},{1,9},{2,10},{3,11},{4,12},{5,13},{6,14},{7,15},{8,0},{9,1},... | collective-permute-start | bytes 196616 | tf_op jit(solution)/shard_map/ppermute | solution.py:365
  100.2 16.2 %collective-permute-start.23 = (bf16[128,768]{1,0:T(8,128)(2,1)S(1)}, bf16[128,768]{1,0:T(8,128)(2,1)S(1)}, u32[]{:S(2)}, u32[]{:S(2)}) collective-permute-start(bf16[128,768]{1,0:T(8,128)(2,1)S(1)} %get-tuple-element.63), channel_id=1, source_target_pairs={{0,2},{1,3},{2,0},{3,1},{4,6},{5,7},{6,4},{7,5},{8,10},{9,11},{10,... | collective-permute-start | bytes 589832 | tf_op jit(solution)/shard_map/ppermute | solution.py:365
  101.8 10.0 %collective-permute-start.19 = (bf16[128,768]{1,0:T(8,128)(2,1)S(1)}, bf16[128,768]{1,0:T(8,128)(2,1)S(1)}, u32[]{:S(2)}, u32[]{:S(2)}) collective-permute-start(bf16[128,768]{1,0:T(8,128)(2,1)S(1)} %get-tuple-element.65), channel_id=1, source_target_pairs={{0,2},{1,3},{2,0},{3,1},{4,6},{5,7},{6,4},{7,5},{8,10},{9,11},{10,... | collective-permute-start | bytes 589832 | tf_op jit(solution)/shard_map/ppermute | solution.py:365
  111.7 6.5 %collective-permute-start.22 = (bf16[128,768]{1,0:T(8,128)(2,1)S(1)}, bf16[128,768]{1,0:T(8,128)(2,1)S(1)}, u32[]{:S(2)}, u32[]{:S(2)}) collective-permute-start(bf16[128,768]{1,0:T(8,128)(2,1)S(1)} %get-tuple-element.64), channel_id=1, source_target_pairs={{0,2},{1,3},{2,0},{3,1},{4,6},{5,7},{6,4},{7,5},{8,10},{9,11},{10,... | collective-permute-start | bytes 589832 | tf_op jit(solution)/shard_map/ppermute | solution.py:365
  113.3 18.3 %collective-permute-start.26 = (bf16[128,768]{1,0:T(8,128)(2,1)S(1)}, bf16[128,768]{1,0:T(8,128)(2,1)S(1)}, u32[]{:S(2)}, u32[]{:S(2)}) collective-permute-start(bf16[128,768]{1,0:T(8,128)(2,1)S(1)} %fusion.7), channel_id=1, source_target_pairs={{0,8},{1,9},{2,10},{3,11},{4,12},{5,13},{6,14},{7,15},{8,0},{9,1},... | collective-permute-start | bytes 589832 | tf_op jit(solution)/shard_map/ppermute | solution.py:365
  116.4 15.2 %collective-permute-start.25 = (bf16[128,768]{1,0:T(8,128)(2,1)S(1)}, bf16[128,768]{1,0:T(8,128)(2,1)S(1)}, u32[]{:S(2)}, u32[]{:S(2)}) collective-permute-start(bf16[128,768]{1,0:T(8,128)(2,1)S(1)} %fusion), channel_id=1, source_target_pairs={{0,4},{1,5},{2,6},{3,7},{4,8},{5,9},{6,10},{7,11},{8,12},{9,13},{1... | collective-permute-start | bytes 589832 | tf_op jit(solution)/shard_map/ppermute | solution.py:365
  118.3 13.3 %collective-permute-start.27 = (bf16[128,768]{1,0:T(8,128)(2,1)S(1)}, bf16[128,768]{1,0:T(8,128)(2,1)S(1)}, u32[]{:S(2)}, u32[]{:S(2)}) collective-permute-start(bf16[128,768]{1,0:T(8,128)(2,1)S(1)} %fusion.1), channel_id=1, source_target_pairs={{0,12},{1,13},{2,14},{3,15},{4,0},{5,1},{6,2},{7,3},{8,4},{9,5},{1... | collective-permute-start | bytes 589832 | tf_op jit(solution)/shard_map/ppermute | solution.py:365
  120.4 5.7 %collective-permute-start.24 = (bf16[128,768]{1,0:T(8,128)(2,1)S(1)}, bf16[128,768]{1,0:T(8,128)(2,1)S(1)}, u32[]{:S(2)}, u32[]{:S(2)}) collective-permute-start(bf16[128,768]{1,0:T(8,128)(2,1)S(1)} %get-tuple-element.58), channel_id=1, source_target_pairs={{0,2},{1,3},{2,0},{3,1},{4,6},{5,7},{6,4},{7,5},{8,10},{9,11},{10,... | collective-permute-start | bytes 589832 | tf_op jit(solution)/shard_map/ppermute | solution.py:365
  (21 other events, 153.9 us)

commit v10 on v8

--- a/solution.py
+++ b/solution.py
@@ -18,22 +18,22 @@
     return lax.dot_general(a, b, (contract, ((), ())), preferred_element_type=jnp.float32)
 
 CHUNKS = (2, 2)
-STEP_HEADS = (4, 2)
-PIECES = (32, 16)
-TURNED = (True, False)
+STEP_HEADS = (4, 4)
+PIECES = (32, 32)
+BY_TOKENS = ((True, True), (True, False))
 
 
 def attention_kernel(
     owner_ref, tokens_ref, place_ref,
     q_ref, g_ref, leaf_k_ref, leaf_v_ref, leaf_ref, mask_ref, *rest,
     prompts, per_prefix, block_len, planes, ranks, chained, steps, step_heads,
-    piece_rows, turned,
+    piece_rows, by_tokens,
 ):
     sources = rest[:2 * ranks]
     rest = rest[2 * ranks + 2 * chained:]
     out_ref, dq_ref, dleaf_ref = rest[:3]
     totals = rest[3:3 + 2 * ranks]
-    (kv, kcat, vcat, kcat_t, vcat_t, bias, q_pick, g_pick, q_pick_t, g_pick_t, q2, g2, scores, dprob, probs_b, dscore,
+    (kv, kcat, vcat, klast, vlast, bias, q_pick, g_pick, q2, g2, scores, dprob, probs_b, dscore,
      dk_sum, dv_sum, sems) = rest[3 + 2 * ranks:]
     step = pl.program_id(0)
     per_group = GQ // step_heads
@@ -98,8 +98,6 @@
         pick = (in_first == left).astype(jnp.float32)
         q_pick[...] = pick.astype(jnp.bfloat16)
         g_pick[...] = (pick * mask_col).astype(jnp.bfloat16)
-        q_pick_t[...] = q_pick[...].T
-        g_pick_t[...] = g_pick[...].T
         for n in range(step_heads):
             bias[:, n * count:(n + 1) * count] = allowed_bias
         for ref in totals:
@@ -131,18 +129,25 @@
         dv_sum[...] += dot(probs_b[...], g2[...], ((1,), (0,)))
 
     def later_columns():
-        token_at = lax.rem(lax.broadcasted_iota(jnp.int32, (HEAD_SIZE, columns), 1), count)
-        first_side = token_at < border
-        for source, cat_t, factor, target in (
-            (probs_b, vcat_t, 1.0, out_ref), (dscore, kcat_t, SCALE, dq_ref)
+        for source, cat, factor, target, rows in (
+            (probs_b, vlast, 1.0, out_ref, by_tokens[0]),
+            (dscore, klast, SCALE, dq_ref, by_tokens[1]),
         ):
-            both = dot(cat_t[...], source[...], ((1,), (0,)))
-            mine = jnp.where(first_side, both[:HEAD_SIZE], both[HEAD_SIZE:])
+            if rows:
+                both = dot(source[...], cat[...], ((0,), (0,)))
+                token_at = lax.rem(lax.broadcasted_iota(jnp.int32, (columns, HEAD_SIZE), 0), count)
+                mine = jnp.where(token_at < border, both[:, :HEAD_SIZE], both[:, HEAD_SIZE:])
+            else:
+                both = dot(cat[...], source[...], ((1,), (0,)))
+                token_at = lax.rem(lax.broadcasted_iota(jnp.int32, (HEAD_SIZE, columns), 1), count)
+                mine = jnp.where(token_at < border, both[:HEAD_SIZE], both[HEAD_SIZE:])
             if factor != 1.0:
                 mine = mine * factor
             for n in range(step_heads):
                 lanes = slice(n * HEAD_SIZE, (n + 1) * HEAD_SIZE)
-                target[:, lanes] = mine[:, n * count:(n + 1) * count].T.astype(jnp.bfloat16)
+                span_n = slice(n * count, (n + 1) * count)
+                part = mine[span_n] if rows else mine[:, span_n].T
+                target[:, lanes] = part.astype(jnp.bfloat16)
 
 
     def pick(source, chosen):
@@ -152,15 +157,6 @@
             parts.append(jnp.concatenate([part, part], axis=1) * chosen[...])
         return jnp.concatenate(parts, axis=0)
 
-    def times(cat, new, source, chosen_t):
-        if not turned:
-            return dot(cat[...], new, ((1,), (1,)))
-        parts = []
-        for n in range(step_heads):
-            part = source[:, n * HEAD_SIZE:(n + 1) * HEAD_SIZE].T
-            parts.append(jnp.concatenate([part, part], axis=0) * chosen_t[...])
-        return dot(cat[...], jnp.concatenate(parts, axis=1), ((1,), (0,)))
-
     def fold(value, op):
         value = value.reshape(piece_rows // 8, 8, columns)
         total = value[0]
@@ -169,7 +165,7 @@
         return total
 
     def score(new_q):
-        product = times(kcat, new_q, q_ref, q_pick_t)
+        product = dot(kcat[...], new_q, ((1,), (1,)))
         top = None
         for at in range(0, keys, piece_rows):
             piece = product[at:at + piece_rows]
@@ -204,7 +200,7 @@
         top = score(new_q)
         if later:
             later_rows()
-        dprob[...] = times(vcat, new_g, g_ref, g_pick_t)
+        dprob[...] = dot(vcat[...], new_g, ((1,), (1,)))
         total, delta = sums(top)
         if later:
             later_columns()
@@ -249,8 +245,8 @@
 
     @pl.when(new_group & (step < steps))
     def _():
-        kcat_t[...] = kcat[...].T
-        vcat_t[...] = vcat[...].T
+        vlast[...] = vcat[...] if by_tokens[0] else vcat[...].T
+        klast[...] = kcat[...] if by_tokens[1] else kcat[...].T
 
 
 def attention(
@@ -292,12 +288,15 @@
         return pl.BlockSpec(shape, lambda h, *_: (0,) * len(shape))
 
     sum_shape = (planes, block_len, width)
+    last_shape = {
+        True: pltpu.VMEM((keys, 2 * HEAD_SIZE), bf16), False: pltpu.VMEM((2 * HEAD_SIZE, keys), bf16)
+    }
     chained = len(earlier) > 0
     return pl.pallas_call(
         functools.partial(
             attention_kernel, prompts=prompts, per_prefix=per_prefix, block_len=block_len,
             planes=planes, ranks=ranks, chained=chained, steps=steps, step_heads=step_heads,
-            piece_rows=PIECES[chunk], turned=TURNED[chunk],
+            piece_rows=PIECES[chunk], by_tokens=BY_TOKENS[chunk],
         ),
         grid_spec=pltpu.PrefetchScalarGridSpec(
             num_scalar_prefetch=3,
@@ -310,13 +309,11 @@
                 pltpu.VMEM((2 * span, width), bf16),
                 pltpu.VMEM((keys, 2 * HEAD_SIZE), bf16),
                 pltpu.VMEM((keys, 2 * HEAD_SIZE), bf16),
-                pltpu.VMEM((2 * HEAD_SIZE, keys), bf16),
-                pltpu.VMEM((2 * HEAD_SIZE, keys), bf16),
+                last_shape[BY_TOKENS[chunk][1]],
+                last_shape[BY_TOKENS[chunk][0]],
                 pltpu.VMEM((count, step_heads * count), f32),
                 pltpu.VMEM((count, 2 * HEAD_SIZE), bf16),
                 pltpu.VMEM((count, 2 * HEAD_SIZE), bf16),
-                pltpu.VMEM((2 * HEAD_SIZE, count), bf16),
-                pltpu.VMEM((2 * HEAD_SIZE, count), bf16),
                 pltpu.VMEM((step_heads * count, 2 * HEAD_SIZE), bf16),
                 pltpu.VMEM((step_heads * count, 2 * HEAD_SIZE), bf16),
                 pltpu.VMEM((keys, step_heads * count), f32),

time: 117 us -> 117 us (level)
  no operation moved by 1% of the time
where the time goes in v10:
time: 117 us; the launch traced here: 116 us
  Pallas kernels  45.1 us (39%)
  waiting for transfers between devices  32.2 us (28%)
  starting transfers between devices  30.2 us (26%)
  local copies, waits for them, and re-layouts  4.08 us (3%)
  other arithmetic  3.61 us (3%)
    pallas_call x2, Pallas kernels, attention(): pl.pallas_call(functools.partial(attention_kernel, prompts=prompts, per_p...  45.1 us
    ppermute x24, waiting for transfers between devices, send(): return lax.ppermute(array, 'dp', pairs)  32.2 us
    ppermute x24, starting transfers between devices, send(): return lax.ppermute(array, 'dp', pairs)  30.2 us
  transfers between devices with their start and end apart: 24, of which 12 were waited for; matrix products, arithmetic and copies ran while one was open for 3% of the time, Pallas kernels for 39%

profile of v10, /device:TPU:0, one launch (start us, length us, event | category | flops | bytes accessed | tf_op | source)
XLA Modules:
  0.0 116.2 jit_solution(5080054957778684821)
XLA Ops:
  1.6 3.1 %collective-permute-start.4 = (bf16[128,512]{1,0:T(8,128)(2,1)S(1)}, bf16[128,512]{1,0:T(8,128)(2,1)S(1)}, u32[]{:S(2)}, u32[]{:S(2)}) collective-permute-start(bf16[128,512]{1,0:T(8,128)(2,1)S(1)} %pad_maximum_fusion.5), channel_id=1, source_target_pairs={{0,4},{1,5},{2,6},{3,7},{4,8},{5,9},{6,10},{7,11},{8,12},{9,13},{1... | collective-permute-start | bytes 393224 | tf_op jit(solution)/shard_map/ppermute | solution.py:362
  4.7 2.6 %collective-permute-start.5 = (bf16[128,512]{1,0:T(8,128)(2,1)S(1)}, bf16[128,512]{1,0:T(8,128)(2,1)S(1)}, u32[]{:S(2)}, u32[]{:S(2)}) collective-permute-start(bf16[128,512]{1,0:T(8,128)(2,1)S(1)} %pad_maximum_fusion.5), channel_id=1, source_target_pairs={{0,8},{1,9},{2,10},{3,11},{4,12},{5,13},{6,14},{7,15},{8,0},{9,1},... | collective-permute-start | bytes 393224 | tf_op jit(solution)/shard_map/ppermute | solution.py:362
  7.3 1.3 %collective-permute-start.6 = (bf16[128,512]{1,0:T(8,128)(2,1)S(1)}, bf16[128,512]{1,0:T(8,128)(2,1)S(1)}, u32[]{:S(2)}, u32[]{:S(2)}) collective-permute-start(bf16[128,512]{1,0:T(8,128)(2,1)S(1)} %pad_maximum_fusion.5), channel_id=1, source_target_pairs={{0,12},{1,13},{2,14},{3,15},{4,0},{5,1},{6,2},{7,3},{8,4},{9,5},{1... | collective-permute-start | bytes 393224 | tf_op jit(solution)/shard_map/ppermute | solution.py:362
  8.6 2.5 %collective-permute-done.4 = bf16[128,512]{1,0:T(8,128)(2,1)S(1)} collective-permute-done((bf16[128,512]{1,0:T(8,128)(2,1)S(1)}, bf16[128,512]{1,0:T(8,128)(2,1)S(1)}, u32[]{:S(2)}, u32[]{:S(2)}) %collective-permute-start.4) | collective-permute-done | bytes 131104 | tf_op jit(solution)/shard_map/ppermute | solution.py:362
  11.1 4.8 %collective-permute-done.5 = bf16[128,512]{1,0:T(8,128)(2,1)S(1)} collective-permute-done((bf16[128,512]{1,0:T(8,128)(2,1)S(1)}, bf16[128,512]{1,0:T(8,128)(2,1)S(1)}, u32[]{:S(2)}, u32[]{:S(2)}) %collective-permute-start.5) | collective-permute-done | bytes 131104 | tf_op jit(solution)/shard_map/ppermute | solution.py:362
  16.0 1.6 %collective-permute-start.8 = (bf16[512,512]{1,0:T(8,128)(2,1)S(1)}, bf16[512,512]{1,0:T(8,128)(2,1)S(1)}, u32[]{:S(2)}, u32[]{:S(2)}) collective-permute-start(bf16[512,512]{1,0:T(8,128)(2,1)S(1)} %pad_maximum_fusion.1.rest_0_), channel_id=1, source_target_pairs={{0,2},{1,3},{2,0},{3,1},{4,6},{5,7},{6,4},{7,5},{8,10},{9,11},{10,... | collective-permute-start | bytes 1572872 | tf_op jit(solution)/shard_map/ppermute | solution.py:362
  17.6 3.3 %collective-permute-start = (bf16[128,512]{1,0:T(8,128)(2,1)S(1)}, bf16[128,512]{1,0:T(8,128)(2,1)S(1)}, u32[]{:S(2)}, u32[]{:S(2)}) collective-permute-start(bf16[128,512]{1,0:T(8,128)(2,1)S(1)} %pad_maximum_fusion.4), channel_id=1, source_target_pairs={{0,4},{1,5},{2,6},{3,7},{4,8},{5,9},{6,10},{7,11},{8,12},{9,13},{1... | collective-permute-start | bytes 393224 | tf_op jit(solution)/shard_map/ppermute | solution.py:362
  20.9 1.6 %collective-permute-start.1 = (bf16[128,512]{1,0:T(8,128)(2,1)S(1)}, bf16[128,512]{1,0:T(8,128)(2,1)S(1)}, u32[]{:S(2)}, u32[]{:S(2)}) collective-permute-start(bf16[128,512]{1,0:T(8,128)(2,1)S(1)} %pad_maximum_fusion.4), channel_id=1, source_target_pairs={{0,8},{1,9},{2,10},{3,11},{4,12},{5,13},{6,14},{7,15},{8,0},{9,1},... | collective-permute-start | bytes 393224 | tf_op jit(solution)/shard_map/ppermute | solution.py:362
  23.3 2.9 %collective-permute-done = bf16[128,512]{1,0:T(8,128)(2,1)S(1)} collective-permute-done((bf16[128,512]{1,0:T(8,128)(2,1)S(1)}, bf16[128,512]{1,0:T(8,128)(2,1)S(1)}, u32[]{:S(2)}, u32[]{:S(2)}) %collective-permute-start) | collective-permute-done | bytes 131104 | tf_op jit(solution)/shard_map/ppermute | solution.py:362
  26.3 4.3 %collective-permute-done.1 = bf16[128,512]{1,0:T(8,128)(2,1)S(1)} collective-permute-done((bf16[128,512]{1,0:T(8,128)(2,1)S(1)}, bf16[128,512]{1,0:T(8,128)(2,1)S(1)}, u32[]{:S(2)}, u32[]{:S(2)}) %collective-permute-start.1) | collective-permute-done | bytes 131104 | tf_op jit(solution)/shard_map/ppermute | solution.py:362
  34.2 22.8 %shard_map.111 = (bf16[256,4096]{1,0:T(8,128)(2,1)}, bf16[256,4096]{1,0:T(8,128)(2,1)}, bf16[256,512]{1,0:T(8,128)(2,1)}, bf16[4,128,512]{2,1,0:T(8,128)(2,1)}, ...) custom-call(s32[16]{0:T(128)} %owner_ref.3, s32[4]{0:T(128)} %tokens_ref.3, ...), custom_call_target="tpu_custom_call" | custom-call | flops 9663676416 | bytes 8388608 | tf_op jit(solution)/shard_map/pallas_call | solution.py:295
  57.8 1.5 %collective-permute-done.10 = bf16[4,128,512]{2,1,0:T(8,128)(2,1)S(1)} collective-permute-done((bf16[4,128,512]{2,1,0:T(8,128)(2,1)}, bf16[4,128,512]{2,1,0:T(8,128)(2,1)S(1)}, u32[]{:S(2)}, u32[]{:S(2)}) %collective-permute-start.10) | collective-permute-done | bytes 524320 | tf_op jit(solution)/shard_map/ppermute | solution.py:362
  59.2 1.2 %add_convert_fusion.1 = bf16[4,128,512]{2,1,0:T(8,128)(2,1)S(1)} fusion(bf16[4,128,512]{2,1,0:T(8,128)(2,1)S(1)} %collective-permute-done.10, bf16[4,128,512]{2,1,0:T(8,128)(2,1)} %get-tuple-element.28), kind=kLoop, calls=%fused_computation.3 | loop fusion | flops 1048576 | bytes 1572864 | tf_op jit(solution)/shard_map/convert_element_type | solution.py:411
  61.8 22.3 %shard_map.112 = (bf16[256,4096]{1,0:T(8,128)(2,1)}, bf16[256,4096]{1,0:T(8,128)(2,1)}, bf16[256,512]{1,0:T(8,128)(2,1)}, bf16[4,128,512]{2,1,0:T(8,128)(2,1)}, ...) custom-call(s32[16]{0:T(128)} %owner_ref.3, ...), custom_call_target="tpu_custom_call", output_to_operand_aliasing={{0}: (13, {}), {1}: (14, {})} | custom-call | flops 9663676416 | bytes 8388608 | tf_op jit(solution)/shard_map/pallas_call | solution.py:295
  86.8 1.6 %collective-permute-start.20 = (bf16[4,128,512]{2,1,0:T(8,128)(2,1)S(1)}, bf16[4,128,512]{2,1,0:T(8,128)(2,1)S(1)}, u32[]{:S(2)}, u32[]{:S(2)}) collective-permute-start(bf16[4,128,512]{2,1,0:T(8,128)(2,1)S(1)} %add_convert_fusion), channel_id=1, source_target_pairs={{0,2},{1,3},{2,0},{3,1},{4,6},{5,7},{6,4},{7,5},{8,10},{9,11},{10,... | collective-permute-start | bytes 1572872 | tf_op jit(solution)/shard_map/ppermute | solution.py:362
  88.5 3.2 %collective-permute-start.16 = (bf16[128,512]{1,0:T(8,128)(2,1)S(1)}, bf16[128,512]{1,0:T(8,128)(2,1)S(1)}, u32[]{:S(2)}, u32[]{:S(2)}) collective-permute-start(bf16[128,512]{1,0:T(8,128)(2,1)S(1)} %get-tuple-element.43), channel_id=1, source_target_pairs={{0,4},{1,5},{2,6},{3,7},{4,8},{5,9},{6,10},{7,11},{8,12},{9,13},{1... | collective-permute-start | bytes 393224 | tf_op jit(solution)/shard_map/ppermute | solution.py:362
  91.7 1.8 %collective-permute-start.17 = (bf16[128,512]{1,0:T(8,128)(2,1)S(1)}, bf16[128,512]{1,0:T(8,128)(2,1)S(1)}, u32[]{:S(2)}, u32[]{:S(2)}) collective-permute-start(bf16[128,512]{1,0:T(8,128)(2,1)S(1)} %get-tuple-element.44), channel_id=1, source_target_pairs={{0,8},{1,9},{2,10},{3,11},{4,12},{5,13},{6,14},{7,15},{8,0},{9,1},... | collective-permute-start | bytes 393224 | tf_op jit(solution)/shard_map/ppermute | solution.py:362
  94.9 2.4 %collective-permute-done.16 = bf16[128,512]{1,0:T(8,128)(2,1)S(1)} collective-permute-done((bf16[128,512]{1,0:T(8,128)(2,1)S(1)}, bf16[128,512]{1,0:T(8,128)(2,1)S(1)}, u32[]{:S(2)}, u32[]{:S(2)}) %collective-permute-start.16) | collective-permute-done | bytes 131104 | tf_op jit(solution)/shard_map/ppermute | solution.py:362
  97.3 4.7 %collective-permute-done.17 = bf16[128,512]{1,0:T(8,128)(2,1)S(1)} collective-permute-done((bf16[128,512]{1,0:T(8,128)(2,1)S(1)}, bf16[128,512]{1,0:T(8,128)(2,1)S(1)}, u32[]{:S(2)}, u32[]{:S(2)}) %collective-permute-start.17) | collective-permute-done | bytes 131104 | tf_op jit(solution)/shard_map/ppermute | solution.py:362
  102.5 3.3 %collective-permute-start.21 = (bf16[128,512]{1,0:T(8,128)(2,1)S(1)}, bf16[128,512]{1,0:T(8,128)(2,1)S(1)}, u32[]{:S(2)}, u32[]{:S(2)}) collective-permute-start(bf16[128,512]{1,0:T(8,128)(2,1)S(1)} %get-tuple-element.55), channel_id=1, source_target_pairs={{0,4},{1,5},{2,6},{3,7},{4,8},{5,9},{6,10},{7,11},{8,12},{9,13},{1... | collective-permute-start | bytes 393224 | tf_op jit(solution)/shard_map/ppermute | solution.py:362
  105.8 1.2 %collective-permute-start.22 = (bf16[128,512]{1,0:T(8,128)(2,1)S(1)}, bf16[128,512]{1,0:T(8,128)(2,1)S(1)}, u32[]{:S(2)}, u32[]{:S(2)}) collective-permute-start(bf16[128,512]{1,0:T(8,128)(2,1)S(1)} %get-tuple-element.57), channel_id=1, source_target_pairs={{0,8},{1,9},{2,10},{3,11},{4,12},{5,13},{6,14},{7,15},{8,0},{9,1},... | collective-permute-start | bytes 393224 | tf_op jit(solution)/shard_map/ppermute | solution.py:362
  107.0 1.3 %collective-permute-start.23 = (bf16[128,512]{1,0:T(8,128)(2,1)S(1)}, bf16[128,512]{1,0:T(8,128)(2,1)S(1)}, u32[]{:S(2)}, u32[]{:S(2)}) collective-permute-start(bf16[128,512]{1,0:T(8,128)(2,1)S(1)} %get-tuple-element.56), channel_id=1, source_target_pairs={{0,12},{1,13},{2,14},{3,15},{4,0},{5,1},{6,2},{7,3},{8,4},{9,5},{1... | collective-permute-start | bytes 393224 | tf_op jit(solution)/shard_map/ppermute | solution.py:362
  108.2 2.3 %collective-permute-done.21 = bf16[128,512]{1,0:T(8,128)(2,1)S(1)} collective-permute-done((bf16[128,512]{1,0:T(8,128)(2,1)S(1)}, bf16[128,512]{1,0:T(8,128)(2,1)S(1)}, u32[]{:S(2)}, u32[]{:S(2)}) %collective-permute-start.21) | collective-permute-done | bytes 131104 | tf_op jit(solution)/shard_map/ppermute | solution.py:362
  110.6 4.8 %collective-permute-done.22 = bf16[128,512]{1,0:T(8,128)(2,1)S(1)} collective-permute-done((bf16[128,512]{1,0:T(8,128)(2,1)S(1)}, bf16[128,512]{1,0:T(8,128)(2,1)S(1)}, u32[]{:S(2)}, u32[]{:S(2)}) %collective-permute-start.22) | collective-permute-done | bytes 131104 | tf_op jit(solution)/shard_map/ppermute | solution.py:362
  (69 shorter events, 12.7 us)
Async XLA Ops:
  1.6 9.5 %collective-permute-start.4 = (bf16[128,512]{1,0:T(8,128)(2,1)S(1)}, bf16[128,512]{1,0:T(8,128)(2,1)S(1)}, u32[]{:S(2)}, u32[]{:S(2)}) collective-permute-start(bf16[128,512]{1,0:T(8,128)(2,1)S(1)} %pad_maximum_fusion.5), channel_id=1, source_target_pairs={{0,4},{1,5},{2,6},{3,7},{4,8},{5,9},{6,10},{7,11},{8,12},{9,13},{1... | collective-permute-start | bytes 393224 | tf_op jit(solution)/shard_map/ppermute | solution.py:362
  4.7 11.2 %collective-permute-start.5 = (bf16[128,512]{1,0:T(8,128)(2,1)S(1)}, bf16[128,512]{1,0:T(8,128)(2,1)S(1)}, u32[]{:S(2)}, u32[]{:S(2)}) collective-permute-start(bf16[128,512]{1,0:T(8,128)(2,1)S(1)} %pad_maximum_fusion.5), channel_id=1, source_target_pairs={{0,8},{1,9},{2,10},{3,11},{4,12},{5,13},{6,14},{7,15},{8,0},{9,1},... | collective-permute-start | bytes 393224 | tf_op jit(solution)/shard_map/ppermute | solution.py:362
  7.3 8.6 %collective-permute-start.6 = (bf16[128,512]{1,0:T(8,128)(2,1)S(1)}, bf16[128,512]{1,0:T(8,128)(2,1)S(1)}, u32[]{:S(2)}, u32[]{:S(2)}) collective-permute-start(bf16[128,512]{1,0:T(8,128)(2,1)S(1)} %pad_maximum_fusion.5), channel_id=1, source_target_pairs={{0,12},{1,13},{2,14},{3,15},{4,0},{5,1},{6,2},{7,3},{8,4},{9,5},{1... | collective-permute-start | bytes 393224 | tf_op jit(solution)/shard_map/ppermute | solution.py:362
  16.0 14.8 %collective-permute-start.8 = (bf16[512,512]{1,0:T(8,128)(2,1)S(1)}, bf16[512,512]{1,0:T(8,128)(2,1)S(1)}, u32[]{:S(2)}, u32[]{:S(2)}) collective-permute-start(bf16[512,512]{1,0:T(8,128)(2,1)S(1)} %pad_maximum_fusion.1.rest_0_), channel_id=1, source_target_pairs={{0,2},{1,3},{2,0},{3,1},{4,6},{5,7},{6,4},{7,5},{8,10},{9,11},{10,... | collective-permute-start | bytes 1572872 | tf_op jit(solution)/shard_map/ppermute | solution.py:362
  17.6 8.7 %collective-permute-start = (bf16[128,512]{1,0:T(8,128)(2,1)S(1)}, bf16[128,512]{1,0:T(8,128)(2,1)S(1)}, u32[]{:S(2)}, u32[]{:S(2)}) collective-permute-start(bf16[128,512]{1,0:T(8,128)(2,1)S(1)} %pad_maximum_fusion.4), channel_id=1, source_target_pairs={{0,4},{1,5},{2,6},{3,7},{4,8},{5,9},{6,10},{7,11},{8,12},{9,13},{1... | collective-permute-start | bytes 393224 | tf_op jit(solution)/shard_map/ppermute | solution.py:362
  20.9 9.7 %collective-permute-start.1 = (bf16[128,512]{1,0:T(8,128)(2,1)S(1)}, bf16[128,512]{1,0:T(8,128)(2,1)S(1)}, u32[]{:S(2)}, u32[]{:S(2)}) collective-permute-start(bf16[128,512]{1,0:T(8,128)(2,1)S(1)} %pad_maximum_fusion.4), channel_id=1, source_target_pairs={{0,8},{1,9},{2,10},{3,11},{4,12},{5,13},{6,14},{7,15},{8,0},{9,1},... | collective-permute-start | bytes 393224 | tf_op jit(solution)/shard_map/ppermute | solution.py:362
  22.5 8.1 %collective-permute-start.2 = (bf16[128,512]{1,0:T(8,128)(2,1)S(1)}, bf16[128,512]{1,0:T(8,128)(2,1)S(1)}, u32[]{:S(2)}, u32[]{:S(2)}) collective-permute-start(bf16[128,512]{1,0:T(8,128)(2,1)S(1)} %pad_maximum_fusion.4), channel_id=1, source_target_pairs={{0,12},{1,13},{2,14},{3,15},{4,0},{5,1},{6,2},{7,3},{8,4},{9,5},{1... | collective-permute-start | bytes 393224 | tf_op jit(solution)/shard_map/ppermute | solution.py:362
  23.3 9.3 %collective-permute-start.7 = (bf16[512,512]{1,0:T(8,128)(2,1)S(1)}, bf16[512,512]{1,0:T(8,128)(2,1)S(1)}, u32[]{:S(2)}, u32[]{:S(2)}) collective-permute-start(bf16[512,512]{1,0:T(8,128)(2,1)S(1)} %pad_maximum_fusion.1.rest_0_), channel_id=1, source_target_pairs={{0,1},{1,0},{2,3},{3,2},{4,5},{5,4},{6,7},{7,6},{8,9},{9,8},{10,11... | collective-permute-start | bytes 1572872 | tf_op jit(solution)/shard_map/ppermute | solution.py:362
  30.7 2.0 %collective-permute-start.3 = (bf16[512,512]{1,0:T(8,128)(2,1)S(1)}, bf16[512,512]{1,0:T(8,128)(2,1)S(1)}, u32[]{:S(2)}, u32[]{:S(2)}) collective-permute-start(bf16[512,512]{1,0:T(8,128)(2,1)S(1)} %pad_maximum_fusion.rest_0_), channel_id=1, source_target_pairs={{0,1},{1,0},{2,3},{3,2},{4,5},{5,4},{6,7},{7,6},{8,9},{9,8},{10,11... | collective-permute-start | bytes 1572872 | tf_op jit(solution)/shard_map/ppermute | solution.py:362
  30.8 2.6 %collective-permute-start.9 = (bf16[512,512]{1,0:T(8,128)(2,1)S(1)}, bf16[512,512]{1,0:T(8,128)(2,1)S(1)}, u32[]{:S(2)}, u32[]{:S(2)}) collective-permute-start(bf16[512,512]{1,0:T(8,128)(2,1)S(1)} %collective-permute-done.8.rest_2_), channel_id=1, source_target_pairs={{0,1},{1,0},{2,3},{3,2},{4,5},{5,4},{6,7},{7,6},{8,9},{9,8},{10,11... | collective-permute-start | bytes 1572872 | tf_op jit(solution)/shard_map/ppermute | solution.py:362
  31.3 26.0 %collective-permute-start.11 = (bf16[512,512]{1,0:T(8,128)(2,1)S(1)}, bf16[512,512]{1,0:T(8,128)(2,1)S(1)}, u32[]{:S(2)}, u32[]{:S(2)}) collective-permute-start(bf16[512,512]{1,0:T(8,128)(2,1)S(1)} %pad_maximum_fusion.rest_0_), channel_id=1, source_target_pairs={{0,2},{1,3},{2,0},{3,1},{4,6},{5,7},{6,4},{7,5},{8,10},{9,11},{10,... | collective-permute-start | bytes 1572872 | tf_op jit(solution)/shard_map/ppermute | solution.py:362
  57.1 2.2 %collective-permute-start.10 = (bf16[4,128,512]{2,1,0:T(8,128)(2,1)}, bf16[4,128,512]{2,1,0:T(8,128)(2,1)S(1)}, u32[]{:S(2)}, u32[]{:S(2)}) collective-permute-start(bf16[4,128,512]{2,1,0:T(8,128)(2,1)} %get-tuple-element.29), channel_id=1, source_target_pairs={{0,1},{1,0},{2,3},{3,2},{4,5},{5,4},{6,7},{7,6},{8,9},{9,8},{10,11... | collective-permute-start | bytes 1572872 | tf_op jit(solution)/shard_map/ppermute | solution.py:362
  57.2 3.7 %collective-permute-start.12 = (bf16[512,512]{1,0:T(8,128)(2,1)S(1)}, bf16[512,512]{1,0:T(8,128)(2,1)S(1)}, u32[]{:S(2)}, u32[]{:S(2)}) collective-permute-start(bf16[512,512]{1,0:T(8,128)(2,1)S(1)} %collective-permute-done.11.rest_2_), channel_id=1, source_target_pairs={{0,1},{1,0},{2,3},{3,2},{4,5},{5,4},{6,7},{7,6},{8,9},{9,8},{10,11... | collective-permute-start | bytes 1572872 | tf_op jit(solution)/shard_map/ppermute | solution.py:362
  57.6 28.0 %collective-permute-start.13 = (bf16[4,128,512]{2,1,0:T(8,128)(2,1)}, bf16[4,128,512]{2,1,0:T(8,128)(2,1)S(1)}, u32[]{:S(2)}, u32[]{:S(2)}) collective-permute-start(bf16[4,128,512]{2,1,0:T(8,128)(2,1)} %get-tuple-element.40), channel_id=1, source_target_pairs={{0,1},{1,0},{2,3},{3,2},{4,5},{5,4},{6,7},{7,6},{8,9},{9,8},{10,11... | collective-permute-start | bytes 1572872 | tf_op jit(solution)/shard_map/ppermute | solution.py:362
  60.4 25.3 %collective-permute-start.14 = (bf16[4,128,512]{2,1,0:T(8,128)(2,1)S(1)}, bf16[4,128,512]{2,1,0:T(8,128)(2,1)S(1)}, u32[]{:S(2)}, u32[]{:S(2)}) collective-permute-start(bf16[4,128,512]{2,1,0:T(8,128)(2,1)S(1)} %add_convert_fusion.1), channel_id=1, source_target_pairs={{0,2},{1,3},{2,0},{3,1},{4,6},{5,7},{6,4},{7,5},{8,10},{9,11},{10,... | collective-permute-start | bytes 1572872 | tf_op jit(solution)/shard_map/ppermute | solution.py:362
  84.1 2.2 %collective-permute-start.15 = (bf16[4,128,512]{2,1,0:T(8,128)(2,1)}, bf16[4,128,512]{2,1,0:T(8,128)(2,1)S(1)}, u32[]{:S(2)}, u32[]{:S(2)}) collective-permute-start(bf16[4,128,512]{2,1,0:T(8,128)(2,1)} %get-tuple-element.42), channel_id=1, source_target_pairs={{0,1},{1,0},{2,3},{3,2},{4,5},{5,4},{6,7},{7,6},{8,9},{9,8},{10,11... | collective-permute-start | bytes 1572872 | tf_op jit(solution)/shard_map/ppermute | solution.py:362
  84.2 18.0 %collective-permute-start.19 = (bf16[4,128,512]{2,1,0:T(8,128)(2,1)}, bf16[4,128,512]{2,1,0:T(8,128)(2,1)S(1)}, u32[]{:S(2)}, u32[]{:S(2)}) collective-permute-start(bf16[4,128,512]{2,1,0:T(8,128)(2,1)} %get-tuple-element.47), channel_id=1, source_target_pairs={{0,1},{1,0},{2,3},{3,2},{4,5},{5,4},{6,7},{7,6},{8,9},{9,8},{10,11... | collective-permute-start | bytes 1572872 | tf_op jit(solution)/shard_map/ppermute | solution.py:362
  86.8 15.3 %collective-permute-start.20 = (bf16[4,128,512]{2,1,0:T(8,128)(2,1)S(1)}, bf16[4,128,512]{2,1,0:T(8,128)(2,1)S(1)}, u32[]{:S(2)}, u32[]{:S(2)}) collective-permute-start(bf16[4,128,512]{2,1,0:T(8,128)(2,1)S(1)} %add_convert_fusion), channel_id=1, source_target_pairs={{0,2},{1,3},{2,0},{3,1},{4,6},{5,7},{6,4},{7,5},{8,10},{9,11},{10,... | collective-permute-start | bytes 1572872 | tf_op jit(solution)/shard_map/ppermute | solution.py:362
  88.5 8.9 %collective-permute-start.16 = (bf16[128,512]{1,0:T(8,128)(2,1)S(1)}, bf16[128,512]{1,0:T(8,128)(2,1)S(1)}, u32[]{:S(2)}, u32[]{:S(2)}) collective-permute-start(bf16[128,512]{1,0:T(8,128)(2,1)S(1)} %get-tuple-element.43), channel_id=1, source_target_pairs={{0,4},{1,5},{2,6},{3,7},{4,8},{5,9},{6,10},{7,11},{8,12},{9,13},{1... | collective-permute-start | bytes 393224 | tf_op jit(solution)/shard_map/ppermute | solution.py:362
  91.7 10.4 %collective-permute-start.17 = (bf16[128,512]{1,0:T(8,128)(2,1)S(1)}, bf16[128,512]{1,0:T(8,128)(2,1)S(1)}, u32[]{:S(2)}, u32[]{:S(2)}) collective-permute-start(bf16[128,512]{1,0:T(8,128)(2,1)S(1)} %get-tuple-element.44), channel_id=1, source_target_pairs={{0,8},{1,9},{2,10},{3,11},{4,12},{5,13},{6,14},{7,15},{8,0},{9,1},... | collective-permute-start | bytes 393224 | tf_op jit(solution)/shard_map/ppermute | solution.py:362
  93.5 8.6 %collective-permute-start.18 = (bf16[128,512]{1,0:T(8,128)(2,1)S(1)}, bf16[128,512]{1,0:T(8,128)(2,1)S(1)}, u32[]{:S(2)}, u32[]{:S(2)}) collective-permute-start(bf16[128,512]{1,0:T(8,128)(2,1)S(1)} %get-tuple-element.45), channel_id=1, source_target_pairs={{0,12},{1,13},{2,14},{3,15},{4,0},{5,1},{6,2},{7,3},{8,4},{9,5},{1... | collective-permute-start | bytes 393224 | tf_op jit(solution)/shard_map/ppermute | solution.py:362
  102.5 8.1 %collective-permute-start.21 = (bf16[128,512]{1,0:T(8,128)(2,1)S(1)}, bf16[128,512]{1,0:T(8,128)(2,1)S(1)}, u32[]{:S(2)}, u32[]{:S(2)}) collective-permute-start(bf16[128,512]{1,0:T(8,128)(2,1)S(1)} %get-tuple-element.55), channel_id=1, source_target_pairs={{0,4},{1,5},{2,6},{3,7},{4,8},{5,9},{6,10},{7,11},{8,12},{9,13},{1... | collective-permute-start | bytes 393224 | tf_op jit(solution)/shard_map/ppermute | solution.py:362
  105.8 9.6 %collective-permute-start.22 = (bf16[128,512]{1,0:T(8,128)(2,1)S(1)}, bf16[128,512]{1,0:T(8,128)(2,1)S(1)}, u32[]{:S(2)}, u32[]{:S(2)}) collective-permute-start(bf16[128,512]{1,0:T(8,128)(2,1)S(1)} %get-tuple-element.57), channel_id=1, source_target_pairs={{0,8},{1,9},{2,10},{3,11},{4,12},{5,13},{6,14},{7,15},{8,0},{9,1},... | collective-permute-start | bytes 393224 | tf_op jit(solution)/shard_map/ppermute | solution.py:362
  107.0 8.4 %collective-permute-start.23 = (bf16[128,512]{1,0:T(8,128)(2,1)S(1)}, bf16[128,512]{1,0:T(8,128)(2,1)S(1)}, u32[]{:S(2)}, u32[]{:S(2)}) collective-permute-start(bf16[128,512]{1,0:T(8,128)(2,1)S(1)} %get-tuple-element.56), channel_id=1, source_target_pairs={{0,12},{1,13},{2,14},{3,15},{4,0},{5,1},{6,2},{7,3},{8,4},{9,5},{1... | collective-permute-start | bytes 393224 | tf_op jit(solution)/shard_map/ppermute | solution.py:362
  (12 other events, 126.5 us)

commit v11 on v4

--- a/solution.py
+++ b/solution.py
@@ -18,7 +18,7 @@
     return lax.dot_general(a, b, (contract, ((), ())), preferred_element_type=jnp.float32)
 
 CHUNKS = (2, 2)
-STEP_HEADS = (4, 2)
+STEP_HEADS = (4, 4)
 PIECE = 32
 
 
@@ -31,7 +31,7 @@
     rest = rest[2 * ranks + 2 * chained:]
     out_ref, dq_ref, dleaf_ref = rest[:3]
     totals = rest[3:3 + 2 * ranks]
-    (kv, kcat, vcat, kcat_t, vcat_t, bias, q_pick, g_pick, q2, g2, scores, dprob, probs_b, dscore,
+    (kv, held, kcat, vcat, kcat_t, vcat_t, bias, q_pick, g_pick, q2, g2, scores, dprob, probs_b, dscore,
      dk_sum, dv_sum, sems) = rest[3 + 2 * ranks:]
     step = pl.program_id(0)
     per_group = GQ // step_heads
@@ -58,10 +58,10 @@
     def block_place(side, j):
         prefix = pair_first if side == 0 else pair_last
         owner = owner_ref[prefix * per_prefix + j]
-        same_core = lax.rem(owner, 2) == lax.rem(place, 2)
-        row = lax.rem(owner // 2 + place // 2, ranks)
-        ahead = lax.rem(owner // (2 * ranks) + planes - place // (2 * ranks), planes)
-        return same_core, row, ahead
+        core = lax.rem(owner + place, 2)
+        row = lax.rem(lax.div(owner, 2) + lax.div(place, 2), ranks)
+        ahead = lax.rem(lax.div(owner, 2 * ranks) + planes - lax.div(place, 2 * ranks), planes)
+        return core + 2 * row, ahead
 
     def key_columns(group):
         return pl.ds(pl.multiple_of(group * HEAD_SIZE, HEAD_SIZE), HEAD_SIZE)
@@ -71,18 +71,12 @@
 
     @pl.when(step == 0)
     def _():
-        for side in range(2):
-            for j in range(per_prefix):
-                n = side * per_prefix + j
-                same_core, row, ahead = block_place(side, j)
-                slot = lax.rem(planes - ahead, planes)
-                rows = pl.ds(pl.multiple_of(slot * block_len, block_len), block_len)
-                target = kv.at[pl.ds(n * block_len, block_len), :]
-                for at, source in enumerate(sources):
-                    @pl.when((same_core == (at % 2 == 0)) & (row == at // 2))
-                    def _():
-                        pltpu.make_async_copy(source.at[rows, :], target, sems.at[n]).start()
-
+        copies = [
+            pltpu.make_async_copy(source, kv.at[at], sems.at[at])
+            for at, source in enumerate(sources)
+        ]
+        for copy in copies:
+            copy.start()
         leaf_row = jnp.broadcast_to(leaf_ref[...], (count, count))
         leaf_col = leaf_row.T
         key_at = lax.broadcasted_iota(jnp.int32, (count, count), 0)
@@ -98,15 +92,10 @@
         g_pick[...] = (pick * mask_col).astype(jnp.bfloat16)
         for n in range(step_heads):
             bias[:, n * count:(n + 1) * count] = allowed_bias
-        for ref in totals:
+        for ref in (held, dk_sum, dv_sum):
             ref[...] = jnp.zeros_like(ref)
-        dk_sum[...] = jnp.zeros_like(dk_sum)
-        dv_sum[...] = jnp.zeros_like(dv_sum)
-        for n in range(2 * per_prefix):
-            target = kv.at[pl.ds(n * block_len, block_len), :]
-            pltpu.make_async_copy(
-                sources[0].at[pl.ds(0, block_len), :], target, sems.at[n]
-            ).wait()
+        for copy in copies:
+            copy.wait()
 
     new_group = lax.rem(step, per_group) == 0
 
@@ -118,7 +107,11 @@
         ):
             for side in range(2):
                 lanes = slice(side * HEAD_SIZE, (side + 1) * HEAD_SIZE)
-                cat[0:span, lanes] = kv[side * span:(side + 1) * span, cols]
+                for j in range(per_prefix):
+                    holder, ahead = block_place(side, j)
+                    at = lax.rem(planes - ahead, planes) * block_len
+                    rows = pl.ds(pl.multiple_of(at, block_len), block_len)
+                    cat[j * block_len:(j + 1) * block_len, lanes] = kv[holder, rows, cols]
                 cat[span:, lanes] = leaf[...]
 
 
@@ -225,11 +218,8 @@
                 for j in range(per_prefix):
                     value = total_ref[j * block_len:(j + 1) * block_len, lanes] * factor
                     value = value.astype(jnp.bfloat16)
-                    same_core, row, ahead = block_place(side, j)
-                    for at, ref in enumerate(totals):
-                        @pl.when((same_core == (at % 2 == 0)) & (row == at // 2))
-                        def _():
-                            ref[ahead, :, cols] += value
+                    holder, ahead = block_place(side, j)
+                    held[holder, ahead, :, cols] += value
 
         dk_sum[...] = jnp.zeros_like(dk_sum)
         dv_sum[...] = jnp.zeros_like(dv_sum)
@@ -238,6 +228,17 @@
     def _():
         kcat_t[...] = kcat[...].T
         vcat_t[...] = vcat[...].T
+
+    @pl.when(step == steps)
+    def _():
+        copies = [
+            pltpu.make_async_copy(held.at[at], total, sems.at[at])
+            for at, total in enumerate(totals)
+        ]
+        for copy in copies:
+            copy.start()
+        for copy in copies:
+            copy.wait()
 
 
 def attention(
@@ -291,9 +292,10 @@
             in_specs=[
                 ahead, ahead, leaf_k, leaf_v, full(leaf.shape), full(mask.shape),
             ] + [anywhere] * (2 * ranks + len(earlier)),
-            out_specs=[behind, behind, full((count, width))] + [full(sum_shape)] * (2 * ranks),
+            out_specs=[behind, behind, full((count, width))] + [anywhere] * (2 * ranks),
             scratch_shapes=[
-                pltpu.VMEM((2 * span, width), bf16),
+                pltpu.VMEM((2 * ranks, planes * block_len, width), bf16),
+                pltpu.VMEM((2 * ranks, *sum_shape), bf16),
                 pltpu.VMEM((keys, 2 * HEAD_SIZE), bf16),
                 pltpu.VMEM((keys, 2 * HEAD_SIZE), bf16),
                 pltpu.VMEM((2 * HEAD_SIZE, keys), bf16),
@@ -309,7 +311,7 @@
                 pltpu.VMEM((keys, step_heads * count), bf16),
                 pltpu.VMEM((keys, 2 * HEAD_SIZE), f32),
                 pltpu.VMEM((keys, 2 * HEAD_SIZE), f32),
-                pltpu.SemaphoreType.DMA((2 * per_prefix,)),
+                pltpu.SemaphoreType.DMA((2 * ranks,)),
             ],
         ),
         out_shape=[
@@ -368,10 +370,11 @@
         total = add(totals[0], send(totals[1], 0, 0, 1))
         return add(total, send(away, 0, 1, 0)) if ranks == 2 else total
 
-    def reduce_planes(total):
+    def reduce_planes(total, *begun):
         mine = total[0]
         for k in range(1, planes):
-            mine = add(mine, send(total[k].astype(jnp.bfloat16), k, 0, 0))
+            away = tie(total[k].astype(jnp.bfloat16), *begun)
+            mine = add(mine, send(away, k, 0, 0))
         return mine.astype(jnp.bfloat16)
 
     chunks = len(CHUNKS)
@@ -396,7 +399,10 @@
         d_leaf.append(leaf_part)
         away = add(totals[2], send(totals[3], 0, 0, 1)).astype(jnp.bfloat16) if ranks == 2 else None
         parts.append((totals, away))
-    d_prefix = [reduce_planes(reduce_ranks(*part)) for part in parts]
+    begun = [parts[-1][1]] if ranks == 2 else []
+    d_prefix = [reduce_planes(reduce_ranks(*part), *begun) for part in parts[:-1]]
+    d_prefix.append(reduce_planes(reduce_ranks(*parts[-1])))
+    d_leaf = [tie(part, d_leaf[-1]) for part in d_leaf[:-1]] + d_leaf[-1:]
 
     def join(parts):
         halves = [jnp.split(p, 2, axis=1) for p in parts]

time: 117 us -> 117 us (level)
  waiting for transfers between devices: 35.5 us -> 32.2 us
  starting transfers between devices: 28.5 us -> 30.3 us
    ppermute x24, waiting for transfers between devices: 35.5 us -> 32.2 us  [send(): return lax.ppermute(array, 'dp', pairs)]
    ppermute x24, starting transfers between devices: 28.5 us -> 30.3 us  [send(): return lax.ppermute(array, 'dp', pairs)]
  transfers between devices with their start and end apart: 24 -> 24, of which waited for: 12 -> 12; matrix products, arithmetic and copies ran while one was open for 3% -> 3% of each run, Pallas kernels for 38% -> 39%
where the time goes in v11:
time: 117 us; the launch traced here: 116 us
  Pallas kernels  44.9 us (38%)
  waiting for transfers between devices  32.2 us (28%)
  starting transfers between devices  30.3 us (26%)
  local copies, waits for them, and re-layouts  4.08 us (3%)
  other arithmetic  3.61 us (3%)
    pallas_call x2, Pallas kernels, attention(): pl.pallas_call(functools.partial(attention_kernel, prompts=prompts, per_p...  44.9 us
    ppermute x24, waiting for transfers between devices, send(): return lax.ppermute(array, 'dp', pairs)  32.2 us
    ppermute x24, starting transfers between devices, send(): return lax.ppermute(array, 'dp', pairs)  30.3 us
  transfers between devices with their start and end apart: 24, of which 12 were waited for; matrix products, arithmetic and copies ran while one was open for 3% of the time, Pallas kernels for 39%

profile of v11, /device:TPU:0, one launch (start us, length us, event | category | flops | bytes accessed | tf_op | source)
XLA Modules:
  0.0 116.0 jit_solution(3703830351350194332)
XLA Ops:
  1.6 3.1 %collective-permute-start.4 = (bf16[128,512]{1,0:T(8,128)(2,1)S(1)}, bf16[128,512]{1,0:T(8,128)(2,1)S(1)}, u32[]{:S(2)}, u32[]{:S(2)}) collective-permute-start(bf16[128,512]{1,0:T(8,128)(2,1)S(1)} %pad_maximum_fusion.5), channel_id=1, source_target_pairs={{0,4},{1,5},{2,6},{3,7},{4,8},{5,9},{6,10},{7,11},{8,12},{9,13},{1... | collective-permute-start | bytes 393224 | tf_op jit(solution)/shard_map/ppermute | solution.py:351
  4.7 2.6 %collective-permute-start.5 = (bf16[128,512]{1,0:T(8,128)(2,1)S(1)}, bf16[128,512]{1,0:T(8,128)(2,1)S(1)}, u32[]{:S(2)}, u32[]{:S(2)}) collective-permute-start(bf16[128,512]{1,0:T(8,128)(2,1)S(1)} %pad_maximum_fusion.5), channel_id=1, source_target_pairs={{0,8},{1,9},{2,10},{3,11},{4,12},{5,13},{6,14},{7,15},{8,0},{9,1},... | collective-permute-start | bytes 393224 | tf_op jit(solution)/shard_map/ppermute | solution.py:351
  7.3 1.3 %collective-permute-start.6 = (bf16[128,512]{1,0:T(8,128)(2,1)S(1)}, bf16[128,512]{1,0:T(8,128)(2,1)S(1)}, u32[]{:S(2)}, u32[]{:S(2)}) collective-permute-start(bf16[128,512]{1,0:T(8,128)(2,1)S(1)} %pad_maximum_fusion.5), channel_id=1, source_target_pairs={{0,12},{1,13},{2,14},{3,15},{4,0},{5,1},{6,2},{7,3},{8,4},{9,5},{1... | collective-permute-start | bytes 393224 | tf_op jit(solution)/shard_map/ppermute | solution.py:351
  8.6 2.5 %collective-permute-done.4 = bf16[128,512]{1,0:T(8,128)(2,1)S(1)} collective-permute-done((bf16[128,512]{1,0:T(8,128)(2,1)S(1)}, bf16[128,512]{1,0:T(8,128)(2,1)S(1)}, u32[]{:S(2)}, u32[]{:S(2)}) %collective-permute-start.4) | collective-permute-done | bytes 131104 | tf_op jit(solution)/shard_map/ppermute | solution.py:351
  11.1 4.8 %collective-permute-done.5 = bf16[128,512]{1,0:T(8,128)(2,1)S(1)} collective-permute-done((bf16[128,512]{1,0:T(8,128)(2,1)S(1)}, bf16[128,512]{1,0:T(8,128)(2,1)S(1)}, u32[]{:S(2)}, u32[]{:S(2)}) %collective-permute-start.5) | collective-permute-done | bytes 131104 | tf_op jit(solution)/shard_map/ppermute | solution.py:351
  16.0 1.6 %collective-permute-start.8 = (bf16[512,512]{1,0:T(8,128)(2,1)S(1)}, bf16[512,512]{1,0:T(8,128)(2,1)S(1)}, u32[]{:S(2)}, u32[]{:S(2)}) collective-permute-start(bf16[512,512]{1,0:T(8,128)(2,1)S(1)} %pad_maximum_fusion.1.rest_0_), channel_id=1, source_target_pairs={{0,2},{1,3},{2,0},{3,1},{4,6},{5,7},{6,4},{7,5},{8,10},{9,11},{10,... | collective-permute-start | bytes 1572872 | tf_op jit(solution)/shard_map/ppermute | solution.py:351
  17.6 3.3 %collective-permute-start = (bf16[128,512]{1,0:T(8,128)(2,1)S(1)}, bf16[128,512]{1,0:T(8,128)(2,1)S(1)}, u32[]{:S(2)}, u32[]{:S(2)}) collective-permute-start(bf16[128,512]{1,0:T(8,128)(2,1)S(1)} %pad_maximum_fusion.4), channel_id=1, source_target_pairs={{0,4},{1,5},{2,6},{3,7},{4,8},{5,9},{6,10},{7,11},{8,12},{9,13},{1... | collective-permute-start | bytes 393224 | tf_op jit(solution)/shard_map/ppermute | solution.py:351
  20.9 1.6 %collective-permute-start.1 = (bf16[128,512]{1,0:T(8,128)(2,1)S(1)}, bf16[128,512]{1,0:T(8,128)(2,1)S(1)}, u32[]{:S(2)}, u32[]{:S(2)}) collective-permute-start(bf16[128,512]{1,0:T(8,128)(2,1)S(1)} %pad_maximum_fusion.4), channel_id=1, source_target_pairs={{0,8},{1,9},{2,10},{3,11},{4,12},{5,13},{6,14},{7,15},{8,0},{9,1},... | collective-permute-start | bytes 393224 | tf_op jit(solution)/shard_map/ppermute | solution.py:351
  23.3 2.9 %collective-permute-done = bf16[128,512]{1,0:T(8,128)(2,1)S(1)} collective-permute-done((bf16[128,512]{1,0:T(8,128)(2,1)S(1)}, bf16[128,512]{1,0:T(8,128)(2,1)S(1)}, u32[]{:S(2)}, u32[]{:S(2)}) %collective-permute-start) | collective-permute-done | bytes 131104 | tf_op jit(solution)/shard_map/ppermute | solution.py:351
  26.3 4.3 %collective-permute-done.1 = bf16[128,512]{1,0:T(8,128)(2,1)S(1)} collective-permute-done((bf16[128,512]{1,0:T(8,128)(2,1)S(1)}, bf16[128,512]{1,0:T(8,128)(2,1)S(1)}, u32[]{:S(2)}, u32[]{:S(2)}) %collective-permute-start.1) | collective-permute-done | bytes 131104 | tf_op jit(solution)/shard_map/ppermute | solution.py:351
  34.2 22.3 %shard_map.111 = (bf16[256,4096]{1,0:T(8,128)(2,1)}, bf16[256,4096]{1,0:T(8,128)(2,1)}, bf16[256,512]{1,0:T(8,128)(2,1)}, bf16[4,128,512]{2,1,0:T(8,128)(2,1)}, ...) custom-call(s32[16]{0:T(128)} %owner_ref.3, s32[4]{0:T(128)} %tokens_ref.3, ...), custom_call_target="tpu_custom_call" | custom-call | flops 9663676416 | bytes 8388608 | tf_op jit(solution)/shard_map/pallas_call | solution.py:284
  57.2 1.4 %collective-permute-done.10 = bf16[4,128,512]{2,1,0:T(8,128)(2,1)S(1)} collective-permute-done((bf16[4,128,512]{2,1,0:T(8,128)(2,1)}, bf16[4,128,512]{2,1,0:T(8,128)(2,1)S(1)}, u32[]{:S(2)}, u32[]{:S(2)}) %collective-permute-start.10) | collective-permute-done | bytes 524320 | tf_op jit(solution)/shard_map/ppermute | solution.py:351
  58.7 1.2 %add_convert_fusion.1 = bf16[4,128,512]{2,1,0:T(8,128)(2,1)S(1)} fusion(bf16[4,128,512]{2,1,0:T(8,128)(2,1)S(1)} %collective-permute-done.10, bf16[4,128,512]{2,1,0:T(8,128)(2,1)} %get-tuple-element.28), kind=kLoop, calls=%fused_computation.3 | loop fusion | flops 1048576 | bytes 1572864 | tf_op jit(solution)/shard_map/convert_element_type | solution.py:400
  61.2 22.6 %shard_map.112 = (bf16[256,4096]{1,0:T(8,128)(2,1)}, bf16[256,4096]{1,0:T(8,128)(2,1)}, bf16[256,512]{1,0:T(8,128)(2,1)}, bf16[4,128,512]{2,1,0:T(8,128)(2,1)}, ...) custom-call(s32[16]{0:T(128)} %owner_ref.3, ...), custom_call_target="tpu_custom_call", output_to_operand_aliasing={{0}: (13, {}), {1}: (14, {})} | custom-call | flops 9663676416 | bytes 8388608 | tf_op jit(solution)/shard_map/pallas_call | solution.py:284
  86.6 1.6 %collective-permute-start.20 = (bf16[4,128,512]{2,1,0:T(8,128)(2,1)S(1)}, bf16[4,128,512]{2,1,0:T(8,128)(2,1)S(1)}, u32[]{:S(2)}, u32[]{:S(2)}) collective-permute-start(bf16[4,128,512]{2,1,0:T(8,128)(2,1)S(1)} %add_convert_fusion), channel_id=1, source_target_pairs={{0,2},{1,3},{2,0},{3,1},{4,6},{5,7},{6,4},{7,5},{8,10},{9,11},{10,... | collective-permute-start | bytes 1572872 | tf_op jit(solution)/shard_map/ppermute | solution.py:351
  88.2 3.3 %collective-permute-start.16 = (bf16[128,512]{1,0:T(8,128)(2,1)S(1)}, bf16[128,512]{1,0:T(8,128)(2,1)S(1)}, u32[]{:S(2)}, u32[]{:S(2)}) collective-permute-start(bf16[128,512]{1,0:T(8,128)(2,1)S(1)} %get-tuple-element.43), channel_id=1, source_target_pairs={{0,4},{1,5},{2,6},{3,7},{4,8},{5,9},{6,10},{7,11},{8,12},{9,13},{1... | collective-permute-start | bytes 393224 | tf_op jit(solution)/shard_map/ppermute | solution.py:351
  91.5 1.8 %collective-permute-start.17 = (bf16[128,512]{1,0:T(8,128)(2,1)S(1)}, bf16[128,512]{1,0:T(8,128)(2,1)S(1)}, u32[]{:S(2)}, u32[]{:S(2)}) collective-permute-start(bf16[128,512]{1,0:T(8,128)(2,1)S(1)} %get-tuple-element.44), channel_id=1, source_target_pairs={{0,8},{1,9},{2,10},{3,11},{4,12},{5,13},{6,14},{7,15},{8,0},{9,1},... | collective-permute-start | bytes 393224 | tf_op jit(solution)/shard_map/ppermute | solution.py:351
  94.8 2.4 %collective-permute-done.16 = bf16[128,512]{1,0:T(8,128)(2,1)S(1)} collective-permute-done((bf16[128,512]{1,0:T(8,128)(2,1)S(1)}, bf16[128,512]{1,0:T(8,128)(2,1)S(1)}, u32[]{:S(2)}, u32[]{:S(2)}) %collective-permute-start.16) | collective-permute-done | bytes 131104 | tf_op jit(solution)/shard_map/ppermute | solution.py:351
  97.1 4.7 %collective-permute-done.17 = bf16[128,512]{1,0:T(8,128)(2,1)S(1)} collective-permute-done((bf16[128,512]{1,0:T(8,128)(2,1)S(1)}, bf16[128,512]{1,0:T(8,128)(2,1)S(1)}, u32[]{:S(2)}, u32[]{:S(2)}) %collective-permute-start.17) | collective-permute-done | bytes 131104 | tf_op jit(solution)/shard_map/ppermute | solution.py:351
  102.3 3.3 %collective-permute-start.21 = (bf16[128,512]{1,0:T(8,128)(2,1)S(1)}, bf16[128,512]{1,0:T(8,128)(2,1)S(1)}, u32[]{:S(2)}, u32[]{:S(2)}) collective-permute-start(bf16[128,512]{1,0:T(8,128)(2,1)S(1)} %get-tuple-element.55), channel_id=1, source_target_pairs={{0,4},{1,5},{2,6},{3,7},{4,8},{5,9},{6,10},{7,11},{8,12},{9,13},{1... | collective-permute-start | bytes 393224 | tf_op jit(solution)/shard_map/ppermute | solution.py:351
  105.6 1.2 collective-permute-start.22
  106.8 1.3 %collective-permute-start.23 = (bf16[128,512]{1,0:T(8,128)(2,1)S(1)}, bf16[128,512]{1,0:T(8,128)(2,1)S(1)}, u32[]{:S(2)}, u32[]{:S(2)}) collective-permute-start(bf16[128,512]{1,0:T(8,128)(2,1)S(1)} %get-tuple-element.56), channel_id=1, source_target_pairs={{0,12},{1,13},{2,14},{3,15},{4,0},{5,1},{6,2},{7,3},{8,4},{9,5},{1... | collective-permute-start | bytes 393224 | tf_op jit(solution)/shard_map/ppermute | solution.py:351
  108.1 2.3 %collective-permute-done.21 = bf16[128,512]{1,0:T(8,128)(2,1)S(1)} collective-permute-done((bf16[128,512]{1,0:T(8,128)(2,1)S(1)}, bf16[128,512]{1,0:T(8,128)(2,1)S(1)}, u32[]{:S(2)}, u32[]{:S(2)}) %collective-permute-start.21) | collective-permute-done | bytes 131104 | tf_op jit(solution)/shard_map/ppermute | solution.py:351
  110.4 4.8 %collective-permute-done.22 = bf16[128,512]{1,0:T(8,128)(2,1)S(1)} collective-permute-done((bf16[128,512]{1,0:T(8,128)(2,1)S(1)}, bf16[128,512]{1,0:T(8,128)(2,1)S(1)}, u32[]{:S(2)}, u32[]{:S(2)}) %collective-permute-start.22) | collective-permute-done | bytes 131104 | tf_op jit(solution)/shard_map/ppermute | solution.py:351
  (69 shorter events, 12.8 us)
Async XLA Ops:
  1.6 9.5 %collective-permute-start.4 = (bf16[128,512]{1,0:T(8,128)(2,1)S(1)}, bf16[128,512]{1,0:T(8,128)(2,1)S(1)}, u32[]{:S(2)}, u32[]{:S(2)}) collective-permute-start(bf16[128,512]{1,0:T(8,128)(2,1)S(1)} %pad_maximum_fusion.5), channel_id=1, source_target_pairs={{0,4},{1,5},{2,6},{3,7},{4,8},{5,9},{6,10},{7,11},{8,12},{9,13},{1... | collective-permute-start | bytes 393224 | tf_op jit(solution)/shard_map/ppermute | solution.py:351
  4.7 11.2 %collective-permute-start.5 = (bf16[128,512]{1,0:T(8,128)(2,1)S(1)}, bf16[128,512]{1,0:T(8,128)(2,1)S(1)}, u32[]{:S(2)}, u32[]{:S(2)}) collective-permute-start(bf16[128,512]{1,0:T(8,128)(2,1)S(1)} %pad_maximum_fusion.5), channel_id=1, source_target_pairs={{0,8},{1,9},{2,10},{3,11},{4,12},{5,13},{6,14},{7,15},{8,0},{9,1},... | collective-permute-start | bytes 393224 | tf_op jit(solution)/shard_map/ppermute | solution.py:351
  7.3 8.6 %collective-permute-start.6 = (bf16[128,512]{1,0:T(8,128)(2,1)S(1)}, bf16[128,512]{1,0:T(8,128)(2,1)S(1)}, u32[]{:S(2)}, u32[]{:S(2)}) collective-permute-start(bf16[128,512]{1,0:T(8,128)(2,1)S(1)} %pad_maximum_fusion.5), channel_id=1, source_target_pairs={{0,12},{1,13},{2,14},{3,15},{4,0},{5,1},{6,2},{7,3},{8,4},{9,5},{1... | collective-permute-start | bytes 393224 | tf_op jit(solution)/shard_map/ppermute | solution.py:351
  16.0 14.8 %collective-permute-start.8 = (bf16[512,512]{1,0:T(8,128)(2,1)S(1)}, bf16[512,512]{1,0:T(8,128)(2,1)S(1)}, u32[]{:S(2)}, u32[]{:S(2)}) collective-permute-start(bf16[512,512]{1,0:T(8,128)(2,1)S(1)} %pad_maximum_fusion.1.rest_0_), channel_id=1, source_target_pairs={{0,2},{1,3},{2,0},{3,1},{4,6},{5,7},{6,4},{7,5},{8,10},{9,11},{10,... | collective-permute-start | bytes 1572872 | tf_op jit(solution)/shard_map/ppermute | solution.py:351
  17.6 8.7 %collective-permute-start = (bf16[128,512]{1,0:T(8,128)(2,1)S(1)}, bf16[128,512]{1,0:T(8,128)(2,1)S(1)}, u32[]{:S(2)}, u32[]{:S(2)}) collective-permute-start(bf16[128,512]{1,0:T(8,128)(2,1)S(1)} %pad_maximum_fusion.4), channel_id=1, source_target_pairs={{0,4},{1,5},{2,6},{3,7},{4,8},{5,9},{6,10},{7,11},{8,12},{9,13},{1... | collective-permute-start | bytes 393224 | tf_op jit(solution)/shard_map/ppermute | solution.py:351
  20.9 9.7 %collective-permute-start.1 = (bf16[128,512]{1,0:T(8,128)(2,1)S(1)}, bf16[128,512]{1,0:T(8,128)(2,1)S(1)}, u32[]{:S(2)}, u32[]{:S(2)}) collective-permute-start(bf16[128,512]{1,0:T(8,128)(2,1)S(1)} %pad_maximum_fusion.4), channel_id=1, source_target_pairs={{0,8},{1,9},{2,10},{3,11},{4,12},{5,13},{6,14},{7,15},{8,0},{9,1},... | collective-permute-start | bytes 393224 | tf_op jit(solution)/shard_map/ppermute | solution.py:351
  22.5 8.1 %collective-permute-start.2 = (bf16[128,512]{1,0:T(8,128)(2,1)S(1)}, bf16[128,512]{1,0:T(8,128)(2,1)S(1)}, u32[]{:S(2)}, u32[]{:S(2)}) collective-permute-start(bf16[128,512]{1,0:T(8,128)(2,1)S(1)} %pad_maximum_fusion.4), channel_id=1, source_target_pairs={{0,12},{1,13},{2,14},{3,15},{4,0},{5,1},{6,2},{7,3},{8,4},{9,5},{1... | collective-permute-start | bytes 393224 | tf_op jit(solution)/shard_map/ppermute | solution.py:351
  23.3 9.3 %collective-permute-start.7 = (bf16[512,512]{1,0:T(8,128)(2,1)S(1)}, bf16[512,512]{1,0:T(8,128)(2,1)S(1)}, u32[]{:S(2)}, u32[]{:S(2)}) collective-permute-start(bf16[512,512]{1,0:T(8,128)(2,1)S(1)} %pad_maximum_fusion.1.rest_0_), channel_id=1, source_target_pairs={{0,1},{1,0},{2,3},{3,2},{4,5},{5,4},{6,7},{7,6},{8,9},{9,8},{10,11... | collective-permute-start | bytes 1572872 | tf_op jit(solution)/shard_map/ppermute | solution.py:351
  30.7 2.0 %collective-permute-start.3 = (bf16[512,512]{1,0:T(8,128)(2,1)S(1)}, bf16[512,512]{1,0:T(8,128)(2,1)S(1)}, u32[]{:S(2)}, u32[]{:S(2)}) collective-permute-start(bf16[512,512]{1,0:T(8,128)(2,1)S(1)} %pad_maximum_fusion.rest_0_), channel_id=1, source_target_pairs={{0,1},{1,0},{2,3},{3,2},{4,5},{5,4},{6,7},{7,6},{8,9},{9,8},{10,11... | collective-permute-start | bytes 1572872 | tf_op jit(solution)/shard_map/ppermute | solution.py:351
  30.8 2.6 %collective-permute-start.9 = (bf16[512,512]{1,0:T(8,128)(2,1)S(1)}, bf16[512,512]{1,0:T(8,128)(2,1)S(1)}, u32[]{:S(2)}, u32[]{:S(2)}) collective-permute-start(bf16[512,512]{1,0:T(8,128)(2,1)S(1)} %collective-permute-done.8.rest_2_), channel_id=1, source_target_pairs={{0,1},{1,0},{2,3},{3,2},{4,5},{5,4},{6,7},{7,6},{8,9},{9,8},{10,11... | collective-permute-start | bytes 1572872 | tf_op jit(solution)/shard_map/ppermute | solution.py:351
  31.3 25.5 %collective-permute-start.11 = (bf16[512,512]{1,0:T(8,128)(2,1)S(1)}, bf16[512,512]{1,0:T(8,128)(2,1)S(1)}, u32[]{:S(2)}, u32[]{:S(2)}) collective-permute-start(bf16[512,512]{1,0:T(8,128)(2,1)S(1)} %pad_maximum_fusion.rest_0_), channel_id=1, source_target_pairs={{0,2},{1,3},{2,0},{3,1},{4,6},{5,7},{6,4},{7,5},{8,10},{9,11},{10,... | collective-permute-start | bytes 1572872 | tf_op jit(solution)/shard_map/ppermute | solution.py:351
  56.5 2.2 %collective-permute-start.10 = (bf16[4,128,512]{2,1,0:T(8,128)(2,1)}, bf16[4,128,512]{2,1,0:T(8,128)(2,1)S(1)}, u32[]{:S(2)}, u32[]{:S(2)}) collective-permute-start(bf16[4,128,512]{2,1,0:T(8,128)(2,1)} %get-tuple-element.29), channel_id=1, source_target_pairs={{0,1},{1,0},{2,3},{3,2},{4,5},{5,4},{6,7},{7,6},{8,9},{9,8},{10,11... | collective-permute-start | bytes 1572872 | tf_op jit(solution)/shard_map/ppermute | solution.py:351
  56.7 3.7 %collective-permute-start.12 = (bf16[512,512]{1,0:T(8,128)(2,1)S(1)}, bf16[512,512]{1,0:T(8,128)(2,1)S(1)}, u32[]{:S(2)}, u32[]{:S(2)}) collective-permute-start(bf16[512,512]{1,0:T(8,128)(2,1)S(1)} %collective-permute-done.11.rest_2_), channel_id=1, source_target_pairs={{0,1},{1,0},{2,3},{3,2},{4,5},{5,4},{6,7},{7,6},{8,9},{9,8},{10,11... | collective-permute-start | bytes 1572872 | tf_op jit(solution)/shard_map/ppermute | solution.py:351
  57.1 28.4 %collective-permute-start.13 = (bf16[4,128,512]{2,1,0:T(8,128)(2,1)}, bf16[4,128,512]{2,1,0:T(8,128)(2,1)S(1)}, u32[]{:S(2)}, u32[]{:S(2)}) collective-permute-start(bf16[4,128,512]{2,1,0:T(8,128)(2,1)} %get-tuple-element.40), channel_id=1, source_target_pairs={{0,1},{1,0},{2,3},{3,2},{4,5},{5,4},{6,7},{7,6},{8,9},{9,8},{10,11... | collective-permute-start | bytes 1572872 | tf_op jit(solution)/shard_map/ppermute | solution.py:351
  59.9 25.6 %collective-permute-start.14 = (bf16[4,128,512]{2,1,0:T(8,128)(2,1)S(1)}, bf16[4,128,512]{2,1,0:T(8,128)(2,1)S(1)}, u32[]{:S(2)}, u32[]{:S(2)}) collective-permute-start(bf16[4,128,512]{2,1,0:T(8,128)(2,1)S(1)} %add_convert_fusion.1), channel_id=1, source_target_pairs={{0,2},{1,3},{2,0},{3,1},{4,6},{5,7},{6,4},{7,5},{8,10},{9,11},{10,... | collective-permute-start | bytes 1572872 | tf_op jit(solution)/shard_map/ppermute | solution.py:351
  83.9 2.2 %collective-permute-start.15 = (bf16[4,128,512]{2,1,0:T(8,128)(2,1)}, bf16[4,128,512]{2,1,0:T(8,128)(2,1)S(1)}, u32[]{:S(2)}, u32[]{:S(2)}) collective-permute-start(bf16[4,128,512]{2,1,0:T(8,128)(2,1)} %get-tuple-element.42), channel_id=1, source_target_pairs={{0,1},{1,0},{2,3},{3,2},{4,5},{5,4},{6,7},{7,6},{8,9},{9,8},{10,11... | collective-permute-start | bytes 1572872 | tf_op jit(solution)/shard_map/ppermute | solution.py:351
  84.0 18.0 %collective-permute-start.19 = (bf16[4,128,512]{2,1,0:T(8,128)(2,1)}, bf16[4,128,512]{2,1,0:T(8,128)(2,1)S(1)}, u32[]{:S(2)}, u32[]{:S(2)}) collective-permute-start(bf16[4,128,512]{2,1,0:T(8,128)(2,1)} %get-tuple-element.47), channel_id=1, source_target_pairs={{0,1},{1,0},{2,3},{3,2},{4,5},{5,4},{6,7},{7,6},{8,9},{9,8},{10,11... | collective-permute-start | bytes 1572872 | tf_op jit(solution)/shard_map/ppermute | solution.py:351
  86.6 15.3 %collective-permute-start.20 = (bf16[4,128,512]{2,1,0:T(8,128)(2,1)S(1)}, bf16[4,128,512]{2,1,0:T(8,128)(2,1)S(1)}, u32[]{:S(2)}, u32[]{:S(2)}) collective-permute-start(bf16[4,128,512]{2,1,0:T(8,128)(2,1)S(1)} %add_convert_fusion), channel_id=1, source_target_pairs={{0,2},{1,3},{2,0},{3,1},{4,6},{5,7},{6,4},{7,5},{8,10},{9,11},{10,... | collective-permute-start | bytes 1572872 | tf_op jit(solution)/shard_map/ppermute | solution.py:351
  88.2 8.9 %collective-permute-start.16 = (bf16[128,512]{1,0:T(8,128)(2,1)S(1)}, bf16[128,512]{1,0:T(8,128)(2,1)S(1)}, u32[]{:S(2)}, u32[]{:S(2)}) collective-permute-start(bf16[128,512]{1,0:T(8,128)(2,1)S(1)} %get-tuple-element.43), channel_id=1, source_target_pairs={{0,4},{1,5},{2,6},{3,7},{4,8},{5,9},{6,10},{7,11},{8,12},{9,13},{1... | collective-permute-start | bytes 393224 | tf_op jit(solution)/shard_map/ppermute | solution.py:351
  91.5 10.4 %collective-permute-start.17 = (bf16[128,512]{1,0:T(8,128)(2,1)S(1)}, bf16[128,512]{1,0:T(8,128)(2,1)S(1)}, u32[]{:S(2)}, u32[]{:S(2)}) collective-permute-start(bf16[128,512]{1,0:T(8,128)(2,1)S(1)} %get-tuple-element.44), channel_id=1, source_target_pairs={{0,8},{1,9},{2,10},{3,11},{4,12},{5,13},{6,14},{7,15},{8,0},{9,1},... | collective-permute-start | bytes 393224 | tf_op jit(solution)/shard_map/ppermute | solution.py:351
  93.3 8.6 %collective-permute-start.18 = (bf16[128,512]{1,0:T(8,128)(2,1)S(1)}, bf16[128,512]{1,0:T(8,128)(2,1)S(1)}, u32[]{:S(2)}, u32[]{:S(2)}) collective-permute-start(bf16[128,512]{1,0:T(8,128)(2,1)S(1)} %get-tuple-element.45), channel_id=1, source_target_pairs={{0,12},{1,13},{2,14},{3,15},{4,0},{5,1},{6,2},{7,3},{8,4},{9,5},{1... | collective-permute-start | bytes 393224 | tf_op jit(solution)/shard_map/ppermute | solution.py:351
  102.3 8.1 %collective-permute-start.21 = (bf16[128,512]{1,0:T(8,128)(2,1)S(1)}, bf16[128,512]{1,0:T(8,128)(2,1)S(1)}, u32[]{:S(2)}, u32[]{:S(2)}) collective-permute-start(bf16[128,512]{1,0:T(8,128)(2,1)S(1)} %get-tuple-element.55), channel_id=1, source_target_pairs={{0,4},{1,5},{2,6},{3,7},{4,8},{5,9},{6,10},{7,11},{8,12},{9,13},{1... | collective-permute-start | bytes 393224 | tf_op jit(solution)/shard_map/ppermute | solution.py:351
  105.6 9.6 %collective-permute-start.22 = (bf16[128,512]{1,0:T(8,128)(2,1)S(1)}, bf16[128,512]{1,0:T(8,128)(2,1)S(1)}, u32[]{:S(2)}, u32[]{:S(2)}) collective-permute-start(bf16[128,512]{1,0:T(8,128)(2,1)S(1)} %get-tuple-element.57), channel_id=1, source_target_pairs={{0,8},{1,9},{2,10},{3,11},{4,12},{5,13},{6,14},{7,15},{8,0},{9,1},... | collective-permute-start | bytes 393224 | tf_op jit(solution)/shard_map/ppermute | solution.py:351
  106.8 8.4 %collective-permute-start.23 = (bf16[128,512]{1,0:T(8,128)(2,1)S(1)}, bf16[128,512]{1,0:T(8,128)(2,1)S(1)}, u32[]{:S(2)}, u32[]{:S(2)}) collective-permute-start(bf16[128,512]{1,0:T(8,128)(2,1)S(1)} %get-tuple-element.56), channel_id=1, source_target_pairs={{0,12},{1,13},{2,14},{3,15},{4,0},{5,1},{6,2},{7,3},{8,4},{9,5},{1... | collective-permute-start | bytes 393224 | tf_op jit(solution)/shard_map/ppermute | solution.py:351
  (12 other events, 125.7 us)

commit v12 on v11

--- a/solution.py
+++ b/solution.py
@@ -26,9 +26,11 @@
     owner_ref, tokens_ref, place_ref,
     q_ref, g_ref, leaf_k_ref, leaf_v_ref, leaf_ref, mask_ref, *rest,
     prompts, per_prefix, block_len, planes, ranks, chained, steps, step_heads,
+    first_column,
 ):
-    sources = rest[:2 * ranks]
-    rest = rest[2 * ranks + 2 * chained:]
+    blocks = 2 * ranks * planes
+    sources = rest[:blocks]
+    rest = rest[blocks + 2 * chained:]
     out_ref, dq_ref, dleaf_ref = rest[:3]
     totals = rest[3:3 + 2 * ranks]
     (kv, held, kcat, vcat, kcat_t, vcat_t, bias, q_pick, g_pick, q2, g2, scores, dprob, probs_b, dscore,
@@ -39,7 +41,7 @@
     columns = step_heads * count
     span = per_prefix * block_len
     keys = span + count
-    half = sources[0].shape[1] // 2
+    half = kv.shape[2] // 2
 
     place = place_ref[0]
     first = place * count
@@ -71,10 +73,15 @@
 
     @pl.when(step == 0)
     def _():
-        copies = [
-            pltpu.make_async_copy(source, kv.at[at], sems.at[at])
-            for at, source in enumerate(sources)
-        ]
+        copies = []
+        for at, source in enumerate(sources):
+            rows = pl.ds(at % planes * block_len, block_len)
+            for side in range(2):
+                columns_in = pl.ds(first_column + side * (source.shape[1] // 2), half)
+                columns_to = pl.ds(side * half, half)
+                copies.append(pltpu.make_async_copy(
+                    source.at[:, columns_in], kv.at[at // planes, rows, columns_to], sems.at[at, side]
+                ))
         for copy in copies:
             copy.start()
         leaf_row = jnp.broadcast_to(leaf_ref[...], (count, count))
@@ -232,7 +239,7 @@
     @pl.when(step == steps)
     def _():
         copies = [
-            pltpu.make_async_copy(held.at[at], total, sems.at[at])
+            pltpu.make_async_copy(held.at[at], total, sems.at[at, 0])
             for at, total in enumerate(totals)
         ]
         for copy in copies:
@@ -245,13 +252,13 @@
     chunk, owner, tokens, place, q, g, leaf_kv, leaf, mask, sources, earlier, planes, ranks
 ):
     count = q.shape[0]
-    block_len = sources[0].shape[0] // planes
+    block_len = sources[0].shape[0]
     prompts = tokens.shape[0]
     per_prefix = owner.shape[0] // prompts
     span = per_prefix * block_len
     keys = span + count
-    width = sources[0].shape[1]
     groups = CHUNKS[chunk]
+    width = 2 * groups * HEAD_SIZE
     step_heads = STEP_HEADS[chunk]
     skipped = sum(CHUNKS[:chunk])
     heads = groups * GQ
@@ -285,13 +292,14 @@
         functools.partial(
             attention_kernel, prompts=prompts, per_prefix=per_prefix, block_len=block_len,
             planes=planes, ranks=ranks, chained=chained, steps=steps, step_heads=step_heads,
+            first_column=skipped * HEAD_SIZE,
         ),
         grid_spec=pltpu.PrefetchScalarGridSpec(
             num_scalar_prefetch=3,
             grid=(steps + 1,),
             in_specs=[
                 ahead, ahead, leaf_k, leaf_v, full(leaf.shape), full(mask.shape),
-            ] + [anywhere] * (2 * ranks + len(earlier)),
+            ] + [anywhere] * (len(sources) + len(earlier)),
             out_specs=[behind, behind, full((count, width))] + [anywhere] * (2 * ranks),
             scratch_shapes=[
                 pltpu.VMEM((2 * ranks, planes * block_len, width), bf16),
@@ -311,7 +319,7 @@
                 pltpu.VMEM((keys, step_heads * count), bf16),
                 pltpu.VMEM((keys, 2 * HEAD_SIZE), f32),
                 pltpu.VMEM((keys, 2 * HEAD_SIZE), f32),
-                pltpu.SemaphoreType.DMA((2 * ranks,)),
+                pltpu.SemaphoreType.DMA((2 * ranks * planes, 2)),
             ],
         ),
         out_shape=[
@@ -319,7 +327,7 @@
             jax.ShapeDtypeStruct(q.shape, bf16),
             jax.ShapeDtypeStruct((count, width), bf16),
         ] + [jax.ShapeDtypeStruct(sum_shape, bf16)] * (2 * ranks),
-        input_output_aliases={9 + 2 * ranks: 0, 10 + 2 * ranks: 1} if chained else {},
+        input_output_aliases={9 + len(sources): 0, 10 + len(sources): 1} if chained else {},
         compiler_params=pltpu.CompilerParams(
             vmem_limit_bytes=54 * 2**20, dimension_semantics=("arbitrary",)
         ),
@@ -350,18 +358,8 @@
         ]
         return lax.ppermute(array, "dp", pairs)
 
-    middle = KEY_VALUE_HEADS * HEAD_SIZE
-
     def tie(value, *others):
         return lax.optimization_barrier((value, *others))[0]
-
-    def by_planes(chunk):
-        low = sum(CHUNKS[:chunk]) * HEAD_SIZE
-        high = low + CHUNKS[chunk] * HEAD_SIZE
-        mine = jnp.concatenate(
-            [prefix_key_value[:, low:high], prefix_key_value[:, middle + low:middle + high]], axis=1
-        )
-        return jnp.concatenate([mine] + [send(mine, k, 0, 0) for k in range(1, planes)], axis=0)
 
     def add(own, received):
         return own.astype(f32) + received.astype(f32)
@@ -378,19 +376,19 @@
         return mine.astype(jnp.bfloat16)
 
     chunks = len(CHUNKS)
-    near = [by_planes(chunk) for chunk in range(chunks)]
-    near_far = [send(n, 0, 0, 1) for n in near]
-    other = [send(n, 0, 1, 0) for n in near] if ranks == 2 else []
-    d_leaf, d_prefix, earlier = [], [], ()
-    parts = []
+    near, rows = [], []
+    for plane in range(planes):
+        near.append(send(tie(near[-1], *rows[-2:-1]), 1, 0, 0) if plane else prefix_key_value)
+        if ranks == 2:
+            rows.append(send(near[-1], 0, 1, 0))
+    sources = []
+    for held in (near, rows):
+        sources += held + [send(piece, 0, 0, 1) for piece in held]
+    d_leaf, parts, earlier = [], [], ()
     for chunk in range(chunks):
-        first = [place] + near[chunk + 1:chunk + 2] + near_far[chunk + 1:chunk + 2]
+        first = [place]
         if chunk and ranks == 2:
             first.append(parts[-1][1])
-        sources = [near[chunk], near_far[chunk]]
-        if ranks == 2:
-            row = tie(other[chunk], d_leaf[-1] if chunk else near[1])
-            sources += [row, send(row, 0, 0, 1)]
         attended, d_query, leaf_part, *totals = attention(
             chunk, block_owner, subtree_tokens, tie(*first), query, d_out, leaf_key_value,
             leaf_id, mask, sources, earlier, planes, ranks,

time: 117 us -> 120 us (1.026)
  waiting for transfers between devices: 32.2 us -> 42.4 us
  starting transfers between devices: 30.3 us -> 25.2 us
  local copies, waits for them, and re-layouts: 4.08 us -> 1.56 us
    ppermute x24 -> x27, waiting for transfers between devices: 32.2 us -> 42.4 us  [send(): return lax.ppermute(array, 'dp', pairs)]
    ppermute x24 -> x27, starting transfers between devices: 30.3 us -> 25.2 us  [send(): return lax.ppermute(array, 'dp', pairs)]
    unnamed x24 -> x34, local copies, waits for them, and re-layouts: 2.04 us -> 0.48 us
  transfers between devices with their start and end apart: 24 -> 27, of which waited for: 12 -> 12; matrix products, arithmetic and copies ran while one was open for 3% -> 3% of each run, Pallas kernels for 39% -> 19%
where the time goes in v12:
time: 120 us; the launch traced here: 119 us
  Pallas kernels  45.3 us (38%)
  waiting for transfers between devices  42.4 us (35%)
  starting transfers between devices  25.2 us (21%)
  other arithmetic  3.52 us (3%)
  local copies, waits for them, and re-layouts  1.56 us (1%)
    pallas_call x2, Pallas kernels, attention(): pl.pallas_call(functools.partial(attention_kernel, prompts=prompts, per_p...  45.3 us
    ppermute x27, waiting for transfers between devices, send(): return lax.ppermute(array, 'dp', pairs)  42.4 us
    ppermute x27, starting transfers between devices, send(): return lax.ppermute(array, 'dp', pairs)  25.2 us
  transfers between devices with their start and end apart: 27, of which 12 were waited for; matrix products, arithmetic and copies ran while one was open for 3% of the time, Pallas kernels for 19%

profile of v12, /device:TPU:0, one launch (start us, length us, event | category | flops | bytes accessed | tf_op | source)
XLA Modules:
  0.0 119.0 jit_solution(13496809268003804772)
XLA Ops:
  0.6 3.1 %collective-permute-start = (bf16[128,1024]{1,0:T(8,128)(2,1)}, bf16[128,1024]{1,0:T(8,128)(2,1)S(1)}, u32[]{:S(2)}, u32[]{:S(2)}) collective-permute-start(bf16[128,1024]{1,0:T(8,128)(2,1)} %rest_0_.3), channel_id=1, source_target_pairs={{0,4},{1,5},{2,6},{3,7},{4,8},{5,9},{6,10},{7,11},{8,12},{9,13},{1... | collective-permute-start | bytes 786440 | tf_op jit(solution)/shard_map/ppermute | solution.py:359
  3.7 1.5 %collective-permute-start.1 = (bf16[128,1024]{1,0:T(8,128)(2,1)}, bf16[128,1024]{1,0:T(8,128)(2,1)S(1)}, u32[]{:S(2)}, u32[]{:S(2)}) collective-permute-start(bf16[128,1024]{1,0:T(8,128)(2,1)} %rest_0_.3), channel_id=1, source_target_pairs={{0,2},{1,3},{2,0},{3,1},{4,6},{5,7},{6,4},{7,5},{8,10},{9,11},{10,... | collective-permute-start | bytes 786440 | tf_op jit(solution)/shard_map/ppermute | solution.py:359
  5.2 7.0 %collective-permute-done.rest_1_ = bf16[128,1024]{1,0:T(8,128)(2,1)S(1)} collective-permute-done((bf16[128,1024]{1,0:T(8,128)(2,1)}, bf16[128,1024]{1,0:T(8,128)(2,1)S(1)}, u32[]{:S(2)}, u32[]{:S(2)}) %collective-permute-start) | collective-permute-done | bytes 262176 | tf_op jit(solution)/shard_map/ppermute | solution.py:359
  12.3 1.0 collective-permute-start.2
  13.3 1.5 %collective-permute-start.3 = (bf16[128,1024]{1,0:T(8,128)(2,1)S(1)}, bf16[128,1024]{1,0:T(8,128)(2,1)S(1)}, u32[]{:S(2)}, u32[]{:S(2)}) collective-permute-start(bf16[128,1024]{1,0:T(8,128)(2,1)S(1)} %collective-permute-done.rest_1_), channel_id=1, source_target_pairs={{0,2},{1,3},{2,0},{3,1},{4,6},{5,7},{6,4},{7,5},{8,10},{9,11},{10,... | collective-permute-start | bytes 786440 | tf_op jit(solution)/shard_map/ppermute | solution.py:359
  14.8 6.8 %collective-permute-done.2.rest_2_ = bf16[128,1024]{1,0:T(8,128)(2,1)S(1)} collective-permute-done((bf16[128,1024]{1,0:T(8,128)(2,1)S(1)}, bf16[128,1024]{1,0:T(8,128)(2,1)S(1)}, u32[]{:S(2)}, u32[]{:S(2)}) %collective-permute-start.2) | collective-permute-done | bytes 262176 | tf_op jit(solution)/shard_map/ppermute | solution.py:359
  22.3 1.3 %collective-permute-start.9 = (bf16[128,1024]{1,0:T(8,128)(2,1)S(1)}, bf16[128,1024]{1,0:T(8,128)(2,1)S(1)}, u32[]{:S(2)}, u32[]{:S(2)}) collective-permute-start(bf16[128,1024]{1,0:T(8,128)(2,1)S(1)} %collective-permute-done.2.rest_2_), channel_id=1, source_target_pairs={{0,2},{1,3},{2,0},{3,1},{4,6},{5,7},{6,4},{7,5},{8,10},{9,11},{10,... | collective-permute-start | bytes 786440 | tf_op jit(solution)/shard_map/ppermute | solution.py:359
  23.6 6.4 %collective-permute-done.4.rest_3_ = bf16[128,1024]{1,0:T(8,128)(2,1)S(1)} collective-permute-done((bf16[128,1024]{1,0:T(8,128)(2,1)S(1)}, bf16[128,1024]{1,0:T(8,128)(2,1)S(1)}, u32[]{:S(2)}, u32[]{:S(2)}) %collective-permute-start.4) | collective-permute-done | bytes 262176 | tf_op jit(solution)/shard_map/ppermute | solution.py:359
  30.0 1.1 collective-permute-start.10
  32.1 4.4 %collective-permute-done.10.rest_11_ = bf16[128,1024]{1,0:T(8,128)(2,1)S(1)} collective-permute-done((bf16[128,1024]{1,0:T(8,128)(2,1)S(1)}, bf16[128,1024]{1,0:T(8,128)(2,1)S(1)}, u32[]{:S(2)}, u32[]{:S(2)}) %collective-permute-start.10) | collective-permute-done | bytes 262176 | tf_op jit(solution)/shard_map/ppermute | solution.py:359
  36.7 1.6 %collective-permute-done.14.rest_15_ = bf16[128,1024]{1,0:T(8,128)(2,1)} collective-permute-done((bf16[128,1024]{1,0:T(8,128)(2,1)S(1)}, bf16[128,1024]{1,0:T(8,128)(2,1)}, u32[]{:S(2)}, u32[]{:S(2)}) %collective-permute-start.14) | collective-permute-done | bytes 262176 | tf_op jit(solution)/shard_map/ppermute | solution.py:359
  38.4 22.5 %shard_map.111 = (bf16[256,4096]{1,0:T(8,128)(2,1)}, bf16[256,4096]{1,0:T(8,128)(2,1)}, bf16[256,512]{1,0:T(8,128)(2,1)}, bf16[4,128,512]{2,1,0:T(8,128)(2,1)}, ...) custom-call(s32[16]{0:T(128)} %owner_ref.3, s32[4]{0:T(128)} %tokens_ref.3, ...), custom_call_target="tpu_custom_call" | custom-call | flops 9663676416 | bytes 8388608 | tf_op jit(solution)/shard_map/pallas_call | solution.py:291
  61.5 1.6 %collective-permute-done.15 = bf16[4,128,512]{2,1,0:T(8,128)(2,1)S(1)} collective-permute-done((bf16[4,128,512]{2,1,0:T(8,128)(2,1)}, bf16[4,128,512]{2,1,0:T(8,128)(2,1)S(1)}, u32[]{:S(2)}, u32[]{:S(2)}) %collective-permute-start.15) | collective-permute-done | bytes 524320 | tf_op jit(solution)/shard_map/ppermute | solution.py:359
  63.1 1.2 add_convert_fusion.1
  64.3 1.4 %collective-permute-start.17 = (bf16[4,128,512]{2,1,0:T(8,128)(2,1)S(1)}, bf16[4,128,512]{2,1,0:T(8,128)(2,1)S(1)}, u32[]{:S(2)}, u32[]{:S(2)}) collective-permute-start(bf16[4,128,512]{2,1,0:T(8,128)(2,1)S(1)} %add_convert_fusion.1), channel_id=1, source_target_pairs={{0,2},{1,3},{2,0},{3,1},{4,6},{5,7},{6,4},{7,5},{8,10},{9,11},{10,... | collective-permute-start | bytes 1572872 | tf_op jit(solution)/shard_map/ppermute | solution.py:359
  65.6 22.8 %shard_map.112 = (bf16[256,4096]{1,0:T(8,128)(2,1)}, bf16[256,4096]{1,0:T(8,128)(2,1)}, bf16[256,512]{1,0:T(8,128)(2,1)}, bf16[4,128,512]{2,1,0:T(8,128)(2,1)}, ...) custom-call(s32[16]{0:T(128)} %owner_ref.3, ...), custom_call_target="tpu_custom_call", output_to_operand_aliasing={{0}: (25, {}), {1}: (26, {})} | custom-call | flops 9663676416 | bytes 8388608 | tf_op jit(solution)/shard_map/pallas_call | solution.py:291
  92.3 3.9 %collective-permute-start.20 = (bf16[128,512]{1,0:T(8,128)(2,1)S(1)}, bf16[128,512]{1,0:T(8,128)(2,1)S(1)}, u32[]{:S(2)}, u32[]{:S(2)}) collective-permute-start(bf16[128,512]{1,0:T(8,128)(2,1)S(1)} %get-tuple-element.42), channel_id=1, source_target_pairs={{0,8},{1,9},{2,10},{3,11},{4,12},{5,13},{6,14},{7,15},{8,0},{9,1},... | collective-permute-start | bytes 393224 | tf_op jit(solution)/shard_map/ppermute | solution.py:359
  98.0 2.3 %collective-permute-done.19 = bf16[128,512]{1,0:T(8,128)(2,1)S(1)} collective-permute-done((bf16[128,512]{1,0:T(8,128)(2,1)S(1)}, bf16[128,512]{1,0:T(8,128)(2,1)S(1)}, u32[]{:S(2)}, u32[]{:S(2)}) %collective-permute-start.19) | collective-permute-done | bytes 131104 | tf_op jit(solution)/shard_map/ppermute | solution.py:359
  100.2 4.6 %collective-permute-done.20 = bf16[128,512]{1,0:T(8,128)(2,1)S(1)} collective-permute-done((bf16[128,512]{1,0:T(8,128)(2,1)S(1)}, bf16[128,512]{1,0:T(8,128)(2,1)S(1)}, u32[]{:S(2)}, u32[]{:S(2)}) %collective-permute-start.20) | collective-permute-done | bytes 131104 | tf_op jit(solution)/shard_map/ppermute | solution.py:359
  105.4 3.1 %collective-permute-start.24 = (bf16[128,512]{1,0:T(8,128)(2,1)S(1)}, bf16[128,512]{1,0:T(8,128)(2,1)S(1)}, u32[]{:S(2)}, u32[]{:S(2)}) collective-permute-start(bf16[128,512]{1,0:T(8,128)(2,1)S(1)} %get-tuple-element.53), channel_id=1, source_target_pairs={{0,4},{1,5},{2,6},{3,7},{4,8},{5,9},{6,10},{7,11},{8,12},{9,13},{1... | collective-permute-start | bytes 393224 | tf_op jit(solution)/shard_map/ppermute | solution.py:359
  108.6 1.2 %collective-permute-start.25 = (bf16[128,512]{1,0:T(8,128)(2,1)S(1)}, bf16[128,512]{1,0:T(8,128)(2,1)S(1)}, u32[]{:S(2)}, u32[]{:S(2)}) collective-permute-start(bf16[128,512]{1,0:T(8,128)(2,1)S(1)} %get-tuple-element.55), channel_id=1, source_target_pairs={{0,8},{1,9},{2,10},{3,11},{4,12},{5,13},{6,14},{7,15},{8,0},{9,1},... | collective-permute-start | bytes 393224 | tf_op jit(solution)/shard_map/ppermute | solution.py:359
  109.8 1.2 %collective-permute-start.26 = (bf16[128,512]{1,0:T(8,128)(2,1)S(1)}, bf16[128,512]{1,0:T(8,128)(2,1)S(1)}, u32[]{:S(2)}, u32[]{:S(2)}) collective-permute-start(bf16[128,512]{1,0:T(8,128)(2,1)S(1)} %get-tuple-element.54), channel_id=1, source_target_pairs={{0,12},{1,13},{2,14},{3,15},{4,0},{5,1},{6,2},{7,3},{8,4},{9,5},{1... | collective-permute-start | bytes 393224 | tf_op jit(solution)/shard_map/ppermute | solution.py:359
  111.0 2.4 %collective-permute-done.24 = bf16[128,512]{1,0:T(8,128)(2,1)S(1)} collective-permute-done((bf16[128,512]{1,0:T(8,128)(2,1)S(1)}, bf16[128,512]{1,0:T(8,128)(2,1)S(1)}, u32[]{:S(2)}, u32[]{:S(2)}) %collective-permute-start.24) | collective-permute-done | bytes 131104 | tf_op jit(solution)/shard_map/ppermute | solution.py:359
  113.4 4.8 %collective-permute-done.25 = bf16[128,512]{1,0:T(8,128)(2,1)S(1)} collective-permute-done((bf16[128,512]{1,0:T(8,128)(2,1)S(1)}, bf16[128,512]{1,0:T(8,128)(2,1)S(1)}, u32[]{:S(2)}, u32[]{:S(2)}) %collective-permute-start.25) | collective-permute-done | bytes 131104 | tf_op jit(solution)/shard_map/ppermute | solution.py:359
  (80 shorter events, 9.3 us)
Async XLA Ops:
  0.6 11.6 %collective-permute-start = (bf16[128,1024]{1,0:T(8,128)(2,1)}, bf16[128,1024]{1,0:T(8,128)(2,1)S(1)}, u32[]{:S(2)}, u32[]{:S(2)}) collective-permute-start(bf16[128,1024]{1,0:T(8,128)(2,1)} %rest_0_.3), channel_id=1, source_target_pairs={{0,4},{1,5},{2,6},{3,7},{4,8},{5,9},{6,10},{7,11},{8,12},{9,13},{1... | collective-permute-start | bytes 786440 | tf_op jit(solution)/shard_map/ppermute | solution.py:359
  3.7 8.5 %collective-permute-start.1 = (bf16[128,1024]{1,0:T(8,128)(2,1)}, bf16[128,1024]{1,0:T(8,128)(2,1)S(1)}, u32[]{:S(2)}, u32[]{:S(2)}) collective-permute-start(bf16[128,1024]{1,0:T(8,128)(2,1)} %rest_0_.3), channel_id=1, source_target_pairs={{0,2},{1,3},{2,0},{3,1},{4,6},{5,7},{6,4},{7,5},{8,10},{9,11},{10,... | collective-permute-start | bytes 786440 | tf_op jit(solution)/shard_map/ppermute | solution.py:359
  12.3 9.3 %collective-permute-start.2 = (bf16[128,1024]{1,0:T(8,128)(2,1)S(1)}, bf16[128,1024]{1,0:T(8,128)(2,1)S(1)}, u32[]{:S(2)}, u32[]{:S(2)}) collective-permute-start(bf16[128,1024]{1,0:T(8,128)(2,1)S(1)} %collective-permute-done.rest_1_), channel_id=1, source_target_pairs={{0,4},{1,5},{2,6},{3,7},{4,8},{5,9},{6,10},{7,11},{8,12},{9,13},{1... | collective-permute-start | bytes 786440 | tf_op jit(solution)/shard_map/ppermute | solution.py:359
  13.3 8.3 %collective-permute-start.3 = (bf16[128,1024]{1,0:T(8,128)(2,1)S(1)}, bf16[128,1024]{1,0:T(8,128)(2,1)S(1)}, u32[]{:S(2)}, u32[]{:S(2)}) collective-permute-start(bf16[128,1024]{1,0:T(8,128)(2,1)S(1)} %collective-permute-done.rest_1_), channel_id=1, source_target_pairs={{0,2},{1,3},{2,0},{3,1},{4,6},{5,7},{6,4},{7,5},{8,10},{9,11},{10,... | collective-permute-start | bytes 786440 | tf_op jit(solution)/shard_map/ppermute | solution.py:359
  21.6 8.4 %collective-permute-start.4 = (bf16[128,1024]{1,0:T(8,128)(2,1)S(1)}, bf16[128,1024]{1,0:T(8,128)(2,1)S(1)}, u32[]{:S(2)}, u32[]{:S(2)}) collective-permute-start(bf16[128,1024]{1,0:T(8,128)(2,1)S(1)} %collective-permute-done.2.rest_2_), channel_id=1, source_target_pairs={{0,4},{1,5},{2,6},{3,7},{4,8},{5,9},{6,10},{7,11},{8,12},{9,13},{1... | collective-permute-start | bytes 786440 | tf_op jit(solution)/shard_map/ppermute | solution.py:359
  21.7 9.4 %collective-permute-start.5 = (bf16[128,1024]{1,0:T(8,128)(2,1)}, bf16[128,1024]{1,0:T(8,128)(2,1)S(1)}, u32[]{:S(2)}, u32[]{:S(2)}) collective-permute-start(bf16[128,1024]{1,0:T(8,128)(2,1)} %rest_0_.3), channel_id=1, source_target_pairs={{0,1},{1,0},{2,3},{3,2},{4,5},{5,4},{6,7},{7,6},{8,9},{9,8},{10,11... | collective-permute-start | bytes 786440 | tf_op jit(solution)/shard_map/ppermute | solution.py:359
  21.7 9.4 %collective-permute-start.6 = (bf16[128,1024]{1,0:T(8,128)(2,1)S(1)}, bf16[128,1024]{1,0:T(8,128)(2,1)S(1)}, u32[]{:S(2)}, u32[]{:S(2)}) collective-permute-start(bf16[128,1024]{1,0:T(8,128)(2,1)S(1)} %collective-permute-done.rest_1_), channel_id=1, source_target_pairs={{0,1},{1,0},{2,3},{3,2},{4,5},{5,4},{6,7},{7,6},{8,9},{9,8},{10,11... | collective-permute-start | bytes 786440 | tf_op jit(solution)/shard_map/ppermute | solution.py:359
  22.2 9.4 %collective-permute-start.11 = (bf16[128,1024]{1,0:T(8,128)(2,1)S(1)}, bf16[128,1024]{1,0:T(8,128)(2,1)S(1)}, u32[]{:S(2)}, u32[]{:S(2)}) collective-permute-start(bf16[128,1024]{1,0:T(8,128)(2,1)S(1)} %collective-permute-done.1.rest_8_), channel_id=1, source_target_pairs={{0,1},{1,0},{2,3},{3,2},{4,5},{5,4},{6,7},{7,6},{8,9},{9,8},{10,11... | collective-permute-start | bytes 786440 | tf_op jit(solution)/shard_map/ppermute | solution.py:359
  22.3 9.4 %collective-permute-start.9 = (bf16[128,1024]{1,0:T(8,128)(2,1)S(1)}, bf16[128,1024]{1,0:T(8,128)(2,1)S(1)}, u32[]{:S(2)}, u32[]{:S(2)}) collective-permute-start(bf16[128,1024]{1,0:T(8,128)(2,1)S(1)} %collective-permute-done.2.rest_2_), channel_id=1, source_target_pairs={{0,2},{1,3},{2,0},{3,1},{4,6},{5,7},{6,4},{7,5},{8,10},{9,11},{10,... | collective-permute-start | bytes 786440 | tf_op jit(solution)/shard_map/ppermute | solution.py:359
  30.0 6.6 %collective-permute-start.10 = (bf16[128,1024]{1,0:T(8,128)(2,1)S(1)}, bf16[128,1024]{1,0:T(8,128)(2,1)S(1)}, u32[]{:S(2)}, u32[]{:S(2)}) collective-permute-start(bf16[128,1024]{1,0:T(8,128)(2,1)S(1)} %collective-permute-done.4.rest_3_), channel_id=1, source_target_pairs={{0,2},{1,3},{2,0},{3,1},{4,6},{5,7},{6,4},{7,5},{8,10},{9,11},{10,... | collective-permute-start | bytes 786440 | tf_op jit(solution)/shard_map/ppermute | solution.py:359
  31.1 5.5 %collective-permute-start.7 = (bf16[128,1024]{1,0:T(8,128)(2,1)S(1)}, bf16[128,1024]{1,0:T(8,128)(2,1)S(1)}, u32[]{:S(2)}, u32[]{:S(2)}) collective-permute-start(bf16[128,1024]{1,0:T(8,128)(2,1)S(1)} %collective-permute-done.2.rest_2_), channel_id=1, source_target_pairs={{0,1},{1,0},{2,3},{3,2},{4,5},{5,4},{6,7},{7,6},{8,9},{9,8},{10,11... | collective-permute-start | bytes 786440 | tf_op jit(solution)/shard_map/ppermute | solution.py:359
  31.1 5.5 %collective-permute-start.12 = (bf16[128,1024]{1,0:T(8,128)(2,1)S(1)}, bf16[128,1024]{1,0:T(8,128)(2,1)S(1)}, u32[]{:S(2)}, u32[]{:S(2)}) collective-permute-start(bf16[128,1024]{1,0:T(8,128)(2,1)S(1)} %collective-permute-done.3.rest_9_), channel_id=1, source_target_pairs={{0,1},{1,0},{2,3},{3,2},{4,5},{5,4},{6,7},{7,6},{8,9},{9,8},{10,11... | collective-permute-start | bytes 786440 | tf_op jit(solution)/shard_map/ppermute | solution.py:359
  31.6 5.0 %collective-permute-start.8 = (bf16[128,1024]{1,0:T(8,128)(2,1)S(1)}, bf16[128,1024]{1,0:T(8,128)(2,1)S(1)}, u32[]{:S(2)}, u32[]{:S(2)}) collective-permute-start(bf16[128,1024]{1,0:T(8,128)(2,1)S(1)} %collective-permute-done.4.rest_3_), channel_id=1, source_target_pairs={{0,1},{1,0},{2,3},{3,2},{4,5},{5,4},{6,7},{7,6},{8,9},{9,8},{10,11... | collective-permute-start | bytes 786440 | tf_op jit(solution)/shard_map/ppermute | solution.py:359
  31.7 4.9 %collective-permute-start.13 = (bf16[128,1024]{1,0:T(8,128)(2,1)S(1)}, bf16[128,1024]{1,0:T(8,128)(2,1)}, u32[]{:S(2)}, u32[]{:S(2)}) collective-permute-start(bf16[128,1024]{1,0:T(8,128)(2,1)S(1)} %collective-permute-done.9.rest_10_), channel_id=1, source_target_pairs={{0,1},{1,0},{2,3},{3,2},{4,5},{5,4},{6,7},{7,6},{8,9},{9,8},{10,11... | collective-permute-start | bytes 786440 | tf_op jit(solution)/shard_map/ppermute | solution.py:359
  61.1 28.9 %collective-permute-start.16 = (bf16[4,128,512]{2,1,0:T(8,128)(2,1)}, bf16[4,128,512]{2,1,0:T(8,128)(2,1)S(1)}, u32[]{:S(2)}, u32[]{:S(2)}) collective-permute-start(bf16[4,128,512]{2,1,0:T(8,128)(2,1)} %get-tuple-element.38), channel_id=1, source_target_pairs={{0,1},{1,0},{2,3},{3,2},{4,5},{5,4},{6,7},{7,6},{8,9},{9,8},{10,11... | collective-permute-start | bytes 1572872 | tf_op jit(solution)/shard_map/ppermute | solution.py:359
  64.3 25.7 %collective-permute-start.17 = (bf16[4,128,512]{2,1,0:T(8,128)(2,1)S(1)}, bf16[4,128,512]{2,1,0:T(8,128)(2,1)S(1)}, u32[]{:S(2)}, u32[]{:S(2)}) collective-permute-start(bf16[4,128,512]{2,1,0:T(8,128)(2,1)S(1)} %add_convert_fusion.1), channel_id=1, source_target_pairs={{0,2},{1,3},{2,0},{3,1},{4,6},{5,7},{6,4},{7,5},{8,10},{9,11},{10,... | collective-permute-start | bytes 1572872 | tf_op jit(solution)/shard_map/ppermute | solution.py:359
  88.5 16.4 %collective-permute-start.22 = (bf16[4,128,512]{2,1,0:T(8,128)(2,1)}, bf16[4,128,512]{2,1,0:T(8,128)(2,1)S(1)}, u32[]{:S(2)}, u32[]{:S(2)}) collective-permute-start(bf16[4,128,512]{2,1,0:T(8,128)(2,1)} %get-tuple-element.45), channel_id=1, source_target_pairs={{0,1},{1,0},{2,3},{3,2},{4,5},{5,4},{6,7},{7,6},{8,9},{9,8},{10,11... | collective-permute-start | bytes 1572872 | tf_op jit(solution)/shard_map/ppermute | solution.py:359
  91.2 14.0 %collective-permute-start.23 = (bf16[4,128,512]{2,1,0:T(8,128)(2,1)S(1)}, bf16[4,128,512]{2,1,0:T(8,128)(2,1)S(1)}, u32[]{:S(2)}, u32[]{:S(2)}) collective-permute-start(bf16[4,128,512]{2,1,0:T(8,128)(2,1)S(1)} %add_convert_fusion), channel_id=1, source_target_pairs={{0,2},{1,3},{2,0},{3,1},{4,6},{5,7},{6,4},{7,5},{8,10},{9,11},{10,... | collective-permute-start | bytes 1572872 | tf_op jit(solution)/shard_map/ppermute | solution.py:359
  92.0 8.3 %collective-permute-start.19 = (bf16[128,512]{1,0:T(8,128)(2,1)S(1)}, bf16[128,512]{1,0:T(8,128)(2,1)S(1)}, u32[]{:S(2)}, u32[]{:S(2)}) collective-permute-start(bf16[128,512]{1,0:T(8,128)(2,1)S(1)} %get-tuple-element.41), channel_id=1, source_target_pairs={{0,4},{1,5},{2,6},{3,7},{4,8},{5,9},{6,10},{7,11},{8,12},{9,13},{1... | collective-permute-start | bytes 393224 | tf_op jit(solution)/shard_map/ppermute | solution.py:359
  92.3 12.5 %collective-permute-start.20 = (bf16[128,512]{1,0:T(8,128)(2,1)S(1)}, bf16[128,512]{1,0:T(8,128)(2,1)S(1)}, u32[]{:S(2)}, u32[]{:S(2)}) collective-permute-start(bf16[128,512]{1,0:T(8,128)(2,1)S(1)} %get-tuple-element.42), channel_id=1, source_target_pairs={{0,8},{1,9},{2,10},{3,11},{4,12},{5,13},{6,14},{7,15},{8,0},{9,1},... | collective-permute-start | bytes 393224 | tf_op jit(solution)/shard_map/ppermute | solution.py:359
  96.3 8.6 %collective-permute-start.21 = (bf16[128,512]{1,0:T(8,128)(2,1)S(1)}, bf16[128,512]{1,0:T(8,128)(2,1)S(1)}, u32[]{:S(2)}, u32[]{:S(2)}) collective-permute-start(bf16[128,512]{1,0:T(8,128)(2,1)S(1)} %get-tuple-element.43), channel_id=1, source_target_pairs={{0,12},{1,13},{2,14},{3,15},{4,0},{5,1},{6,2},{7,3},{8,4},{9,5},{1... | collective-permute-start | bytes 393224 | tf_op jit(solution)/shard_map/ppermute | solution.py:359
  105.4 8.0 %collective-permute-start.24 = (bf16[128,512]{1,0:T(8,128)(2,1)S(1)}, bf16[128,512]{1,0:T(8,128)(2,1)S(1)}, u32[]{:S(2)}, u32[]{:S(2)}) collective-permute-start(bf16[128,512]{1,0:T(8,128)(2,1)S(1)} %get-tuple-element.53), channel_id=1, source_target_pairs={{0,4},{1,5},{2,6},{3,7},{4,8},{5,9},{6,10},{7,11},{8,12},{9,13},{1... | collective-permute-start | bytes 393224 | tf_op jit(solution)/shard_map/ppermute | solution.py:359
  108.6 9.6 %collective-permute-start.25 = (bf16[128,512]{1,0:T(8,128)(2,1)S(1)}, bf16[128,512]{1,0:T(8,128)(2,1)S(1)}, u32[]{:S(2)}, u32[]{:S(2)}) collective-permute-start(bf16[128,512]{1,0:T(8,128)(2,1)S(1)} %get-tuple-element.55), channel_id=1, source_target_pairs={{0,8},{1,9},{2,10},{3,11},{4,12},{5,13},{6,14},{7,15},{8,0},{9,1},... | collective-permute-start | bytes 393224 | tf_op jit(solution)/shard_map/ppermute | solution.py:359
  109.8 8.4 %collective-permute-start.26 = (bf16[128,512]{1,0:T(8,128)(2,1)S(1)}, bf16[128,512]{1,0:T(8,128)(2,1)S(1)}, u32[]{:S(2)}, u32[]{:S(2)}) collective-permute-start(bf16[128,512]{1,0:T(8,128)(2,1)S(1)} %get-tuple-element.54), channel_id=1, source_target_pairs={{0,12},{1,13},{2,14},{3,15},{4,0},{5,1},{6,2},{7,3},{8,4},{9,5},{1... | collective-permute-start | bytes 393224 | tf_op jit(solution)/shard_map/ppermute | solution.py:359
  (20 other events, 181.6 us)

commit v13 on v12

--- a/solution.py
+++ b/solution.py
@@ -380,7 +380,7 @@
     for plane in range(planes):
         near.append(send(tie(near[-1], *rows[-2:-1]), 1, 0, 0) if plane else prefix_key_value)
         if ranks == 2:
-            rows.append(send(near[-1], 0, 1, 0))
+            rows.append(send(tie(near[-1], *rows[-1:]), 0, 1, 0))
     sources = []
     for held in (near, rows):
         sources += held + [send(piece, 0, 0, 1) for piece in held]

time: 120 us -> 119 us (level)
  starting transfers between devices: 25.2 us -> 23.1 us
  waiting for transfers between devices: 42.4 us -> 43.7 us
    ppermute x27, starting transfers between devices: 25.2 us -> 23.1 us  [send(): return lax.ppermute(array, 'dp', pairs)]
    ppermute x27, waiting for transfers between devices: 42.4 us -> 43.7 us  [send(): return lax.ppermute(array, 'dp', pairs)]
where the time goes in v13:
time: 119 us; the launch traced here: 118 us
  Pallas kernels  45.3 us (38%)
  waiting for transfers between devices  43.7 us (37%)
  starting transfers between devices  23.1 us (19%)
  other arithmetic  3.52 us (3%)
  local copies, waits for them, and re-layouts  1.56 us (1%)
    pallas_call x2, Pallas kernels, attention(): pl.pallas_call(functools.partial(attention_kernel, prompts=prompts, per_p...  45.3 us
    ppermute x27, waiting for transfers between devices, send(): return lax.ppermute(array, 'dp', pairs)  43.7 us
    ppermute x27, starting transfers between devices, send(): return lax.ppermute(array, 'dp', pairs)  23.1 us
  transfers between devices with their start and end apart: 27, of which 12 were waited for; matrix products, arithmetic and copies ran while one was open for 3% of the time, Pallas kernels for 19%

profile of v13, /device:TPU:0, one launch (start us, length us, event | category | flops | bytes accessed | tf_op | source)
XLA Modules:
  0.0 118.1 jit_solution(13309937886007733170)
XLA Ops:
  0.6 3.1 %collective-permute-start = (bf16[128,1024]{1,0:T(8,128)(2,1)}, bf16[128,1024]{1,0:T(8,128)(2,1)S(1)}, u32[]{:S(2)}, u32[]{:S(2)}) collective-permute-start(bf16[128,1024]{1,0:T(8,128)(2,1)} %rest_0_.3), channel_id=1, source_target_pairs={{0,4},{1,5},{2,6},{3,7},{4,8},{5,9},{6,10},{7,11},{8,12},{9,13},{1... | collective-permute-start | bytes 786440 | tf_op jit(solution)/shard_map/ppermute | solution.py:359
  3.7 1.5 %collective-permute-start.1 = (bf16[128,1024]{1,0:T(8,128)(2,1)}, bf16[128,1024]{1,0:T(8,128)(2,1)S(1)}, u32[]{:S(2)}, u32[]{:S(2)}) collective-permute-start(bf16[128,1024]{1,0:T(8,128)(2,1)} %rest_0_.3), channel_id=1, source_target_pairs={{0,2},{1,3},{2,0},{3,1},{4,6},{5,7},{6,4},{7,5},{8,10},{9,11},{10,... | collective-permute-start | bytes 786440 | tf_op jit(solution)/shard_map/ppermute | solution.py:359
  5.2 7.0 %collective-permute-done.rest_1_ = bf16[128,1024]{1,0:T(8,128)(2,1)S(1)} collective-permute-done((bf16[128,1024]{1,0:T(8,128)(2,1)}, bf16[128,1024]{1,0:T(8,128)(2,1)S(1)}, u32[]{:S(2)}, u32[]{:S(2)}) %collective-permute-start) | collective-permute-done | bytes 262176 | tf_op jit(solution)/shard_map/ppermute | solution.py:359
  13.3 1.5 %collective-permute-start.3 = (bf16[128,1024]{1,0:T(8,128)(2,1)S(1)}, bf16[128,1024]{1,0:T(8,128)(2,1)S(1)}, u32[]{:S(2)}, u32[]{:S(2)}) collective-permute-start(bf16[128,1024]{1,0:T(8,128)(2,1)S(1)} %collective-permute-done.rest_1_), channel_id=1, source_target_pairs={{0,2},{1,3},{2,0},{3,1},{4,6},{5,7},{6,4},{7,5},{8,10},{9,11},{10,... | collective-permute-start | bytes 786440 | tf_op jit(solution)/shard_map/ppermute | solution.py:359
  14.8 6.8 %collective-permute-done.2.rest_2_ = bf16[128,1024]{1,0:T(8,128)(2,1)S(1)} collective-permute-done((bf16[128,1024]{1,0:T(8,128)(2,1)S(1)}, bf16[128,1024]{1,0:T(8,128)(2,1)S(1)}, u32[]{:S(2)}, u32[]{:S(2)}) %collective-permute-start.2) | collective-permute-done | bytes 262176 | tf_op jit(solution)/shard_map/ppermute | solution.py:359
  21.7 1.3 %collective-permute-start.9 = (bf16[128,1024]{1,0:T(8,128)(2,1)S(1)}, bf16[128,1024]{1,0:T(8,128)(2,1)S(1)}, u32[]{:S(2)}, u32[]{:S(2)}) collective-permute-start(bf16[128,1024]{1,0:T(8,128)(2,1)S(1)} %collective-permute-done.2.rest_2_), channel_id=1, source_target_pairs={{0,2},{1,3},{2,0},{3,1},{4,6},{5,7},{6,4},{7,5},{8,10},{9,11},{10,... | collective-permute-start | bytes 786440 | tf_op jit(solution)/shard_map/ppermute | solution.py:359
  23.5 6.5 %collective-permute-done.4.rest_3_ = bf16[128,1024]{1,0:T(8,128)(2,1)S(1)} collective-permute-done((bf16[128,1024]{1,0:T(8,128)(2,1)S(1)}, bf16[128,1024]{1,0:T(8,128)(2,1)S(1)}, u32[]{:S(2)}, u32[]{:S(2)}) %collective-permute-start.4) | collective-permute-done | bytes 262176 | tf_op jit(solution)/shard_map/ppermute | solution.py:359
  30.0 1.1 collective-permute-start.10
  32.2 4.3 %collective-permute-done.10.rest_11_ = bf16[128,1024]{1,0:T(8,128)(2,1)S(1)} collective-permute-done((bf16[128,1024]{1,0:T(8,128)(2,1)S(1)}, bf16[128,1024]{1,0:T(8,128)(2,1)S(1)}, u32[]{:S(2)}, u32[]{:S(2)}) %collective-permute-start.10) | collective-permute-done | bytes 262176 | tf_op jit(solution)/shard_map/ppermute | solution.py:359
  36.5 1.6 %collective-permute-done.14.rest_15_ = bf16[128,1024]{1,0:T(8,128)(2,1)} collective-permute-done((bf16[128,1024]{1,0:T(8,128)(2,1)S(1)}, bf16[128,1024]{1,0:T(8,128)(2,1)}, u32[]{:S(2)}, u32[]{:S(2)}) %collective-permute-start.14) | collective-permute-done | bytes 262176 | tf_op jit(solution)/shard_map/ppermute | solution.py:359
  38.2 22.5 %shard_map.111 = (bf16[256,4096]{1,0:T(8,128)(2,1)}, bf16[256,4096]{1,0:T(8,128)(2,1)}, bf16[256,512]{1,0:T(8,128)(2,1)}, bf16[4,128,512]{2,1,0:T(8,128)(2,1)}, ...) custom-call(s32[16]{0:T(128)} %owner_ref.3, s32[4]{0:T(128)} %tokens_ref.3, ...), custom_call_target="tpu_custom_call" | custom-call | flops 9663676416 | bytes 8388608 | tf_op jit(solution)/shard_map/pallas_call | solution.py:291
  61.4 1.6 %collective-permute-done.15 = bf16[4,128,512]{2,1,0:T(8,128)(2,1)S(1)} collective-permute-done((bf16[4,128,512]{2,1,0:T(8,128)(2,1)}, bf16[4,128,512]{2,1,0:T(8,128)(2,1)S(1)}, u32[]{:S(2)}, u32[]{:S(2)}) %collective-permute-start.15) | collective-permute-done | bytes 524320 | tf_op jit(solution)/shard_map/ppermute | solution.py:359
  63.0 1.2 add_convert_fusion.1
  64.1 1.1 collective-permute-start.17
  65.3 22.8 %shard_map.112 = (bf16[256,4096]{1,0:T(8,128)(2,1)}, bf16[256,4096]{1,0:T(8,128)(2,1)}, bf16[256,512]{1,0:T(8,128)(2,1)}, bf16[4,128,512]{2,1,0:T(8,128)(2,1)}, ...) custom-call(s32[16]{0:T(128)} %owner_ref.3, ...), custom_call_target="tpu_custom_call", output_to_operand_aliasing={{0}: (25, {}), {1}: (26, {})} | custom-call | flops 9663676416 | bytes 8388608 | tf_op jit(solution)/shard_map/pallas_call | solution.py:291
  90.8 1.0 collective-permute-start.23
  91.8 2.5 %collective-permute-start.20 = (bf16[128,512]{1,0:T(8,128)(2,1)S(1)}, bf16[128,512]{1,0:T(8,128)(2,1)S(1)}, u32[]{:S(2)}, u32[]{:S(2)}) collective-permute-start(bf16[128,512]{1,0:T(8,128)(2,1)S(1)} %get-tuple-element.44), channel_id=1, source_target_pairs={{0,8},{1,9},{2,10},{3,11},{4,12},{5,13},{6,14},{7,15},{8,0},{9,1},... | collective-permute-start | bytes 393224 | tf_op jit(solution)/shard_map/ppermute | solution.py:359
  94.3 1.4 %collective-permute-start.21 = (bf16[128,512]{1,0:T(8,128)(2,1)S(1)}, bf16[128,512]{1,0:T(8,128)(2,1)S(1)}, u32[]{:S(2)}, u32[]{:S(2)}) collective-permute-start(bf16[128,512]{1,0:T(8,128)(2,1)S(1)} %get-tuple-element.45), channel_id=1, source_target_pairs={{0,12},{1,13},{2,14},{3,15},{4,0},{5,1},{6,2},{7,3},{8,4},{9,5},{1... | collective-permute-start | bytes 393224 | tf_op jit(solution)/shard_map/ppermute | solution.py:359
  96.5 3.5 %collective-permute-done.19 = bf16[128,512]{1,0:T(8,128)(2,1)S(1)} collective-permute-done((bf16[128,512]{1,0:T(8,128)(2,1)S(1)}, bf16[128,512]{1,0:T(8,128)(2,1)S(1)}, u32[]{:S(2)}, u32[]{:S(2)}) %collective-permute-start.19) | collective-permute-done | bytes 131104 | tf_op jit(solution)/shard_map/ppermute | solution.py:359
  100.1 4.5 %collective-permute-done.20 = bf16[128,512]{1,0:T(8,128)(2,1)S(1)} collective-permute-done((bf16[128,512]{1,0:T(8,128)(2,1)S(1)}, bf16[128,512]{1,0:T(8,128)(2,1)S(1)}, u32[]{:S(2)}, u32[]{:S(2)}) %collective-permute-start.20) | collective-permute-done | bytes 131104 | tf_op jit(solution)/shard_map/ppermute | solution.py:359
  105.1 2.3 %collective-permute-start.24 = (bf16[128,512]{1,0:T(8,128)(2,1)S(1)}, bf16[128,512]{1,0:T(8,128)(2,1)S(1)}, u32[]{:S(2)}, u32[]{:S(2)}) collective-permute-start(bf16[128,512]{1,0:T(8,128)(2,1)S(1)} %get-tuple-element.55), channel_id=1, source_target_pairs={{0,4},{1,5},{2,6},{3,7},{4,8},{5,9},{6,10},{7,11},{8,12},{9,13},{1... | collective-permute-start | bytes 393224 | tf_op jit(solution)/shard_map/ppermute | solution.py:359
  108.0 1.8 %collective-permute-start.26 = (bf16[128,512]{1,0:T(8,128)(2,1)S(1)}, bf16[128,512]{1,0:T(8,128)(2,1)S(1)}, u32[]{:S(2)}, u32[]{:S(2)}) collective-permute-start(bf16[128,512]{1,0:T(8,128)(2,1)S(1)} %get-tuple-element.56), channel_id=1, source_target_pairs={{0,12},{1,13},{2,14},{3,15},{4,0},{5,1},{6,2},{7,3},{8,4},{9,5},{1... | collective-permute-start | bytes 393224 | tf_op jit(solution)/shard_map/ppermute | solution.py:359
  109.8 3.6 %collective-permute-done.24 = bf16[128,512]{1,0:T(8,128)(2,1)S(1)} collective-permute-done((bf16[128,512]{1,0:T(8,128)(2,1)S(1)}, bf16[128,512]{1,0:T(8,128)(2,1)S(1)}, u32[]{:S(2)}, u32[]{:S(2)}) %collective-permute-start.24) | collective-permute-done | bytes 131104 | tf_op jit(solution)/shard_map/ppermute | solution.py:359
  113.4 3.8 %collective-permute-done.25 = bf16[128,512]{1,0:T(8,128)(2,1)S(1)} collective-permute-done((bf16[128,512]{1,0:T(8,128)(2,1)S(1)}, bf16[128,512]{1,0:T(8,128)(2,1)S(1)}, u32[]{:S(2)}, u32[]{:S(2)}) %collective-permute-start.25) | collective-permute-done | bytes 131104 | tf_op jit(solution)/shard_map/ppermute | solution.py:359
  (80 shorter events, 8.8 us)
Async XLA Ops:
  0.6 11.6 %collective-permute-start = (bf16[128,1024]{1,0:T(8,128)(2,1)}, bf16[128,1024]{1,0:T(8,128)(2,1)S(1)}, u32[]{:S(2)}, u32[]{:S(2)}) collective-permute-start(bf16[128,1024]{1,0:T(8,128)(2,1)} %rest_0_.3), channel_id=1, source_target_pairs={{0,4},{1,5},{2,6},{3,7},{4,8},{5,9},{6,10},{7,11},{8,12},{9,13},{1... | collective-permute-start | bytes 786440 | tf_op jit(solution)/shard_map/ppermute | solution.py:359
  3.7 8.5 %collective-permute-start.1 = (bf16[128,1024]{1,0:T(8,128)(2,1)}, bf16[128,1024]{1,0:T(8,128)(2,1)S(1)}, u32[]{:S(2)}, u32[]{:S(2)}) collective-permute-start(bf16[128,1024]{1,0:T(8,128)(2,1)} %rest_0_.3), channel_id=1, source_target_pairs={{0,2},{1,3},{2,0},{3,1},{4,6},{5,7},{6,4},{7,5},{8,10},{9,11},{10,... | collective-permute-start | bytes 786440 | tf_op jit(solution)/shard_map/ppermute | solution.py:359
  12.3 9.3 %collective-permute-start.2 = (bf16[128,1024]{1,0:T(8,128)(2,1)S(1)}, bf16[128,1024]{1,0:T(8,128)(2,1)S(1)}, u32[]{:S(2)}, u32[]{:S(2)}) collective-permute-start(bf16[128,1024]{1,0:T(8,128)(2,1)S(1)} %collective-permute-done.rest_1_), channel_id=1, source_target_pairs={{0,4},{1,5},{2,6},{3,7},{4,8},{5,9},{6,10},{7,11},{8,12},{9,13},{1... | collective-permute-start | bytes 786440 | tf_op jit(solution)/shard_map/ppermute | solution.py:359
  13.3 8.3 %collective-permute-start.3 = (bf16[128,1024]{1,0:T(8,128)(2,1)S(1)}, bf16[128,1024]{1,0:T(8,128)(2,1)S(1)}, u32[]{:S(2)}, u32[]{:S(2)}) collective-permute-start(bf16[128,1024]{1,0:T(8,128)(2,1)S(1)} %collective-permute-done.rest_1_), channel_id=1, source_target_pairs={{0,2},{1,3},{2,0},{3,1},{4,6},{5,7},{6,4},{7,5},{8,10},{9,11},{10,... | collective-permute-start | bytes 786440 | tf_op jit(solution)/shard_map/ppermute | solution.py:359
  21.6 8.4 %collective-permute-start.4 = (bf16[128,1024]{1,0:T(8,128)(2,1)S(1)}, bf16[128,1024]{1,0:T(8,128)(2,1)S(1)}, u32[]{:S(2)}, u32[]{:S(2)}) collective-permute-start(bf16[128,1024]{1,0:T(8,128)(2,1)S(1)} %collective-permute-done.2.rest_2_), channel_id=1, source_target_pairs={{0,4},{1,5},{2,6},{3,7},{4,8},{5,9},{6,10},{7,11},{8,12},{9,13},{1... | collective-permute-start | bytes 786440 | tf_op jit(solution)/shard_map/ppermute | solution.py:359
  21.7 8.4 %collective-permute-start.9 = (bf16[128,1024]{1,0:T(8,128)(2,1)S(1)}, bf16[128,1024]{1,0:T(8,128)(2,1)S(1)}, u32[]{:S(2)}, u32[]{:S(2)}) collective-permute-start(bf16[128,1024]{1,0:T(8,128)(2,1)S(1)} %collective-permute-done.2.rest_2_), channel_id=1, source_target_pairs={{0,2},{1,3},{2,0},{3,1},{4,6},{5,7},{6,4},{7,5},{8,10},{9,11},{10,... | collective-permute-start | bytes 786440 | tf_op jit(solution)/shard_map/ppermute | solution.py:359
  23.0 8.2 %collective-permute-start.5 = (bf16[128,1024]{1,0:T(8,128)(2,1)}, bf16[128,1024]{1,0:T(8,128)(2,1)S(1)}, u32[]{:S(2)}, u32[]{:S(2)}) collective-permute-start(bf16[128,1024]{1,0:T(8,128)(2,1)} %rest_0_.3), channel_id=1, source_target_pairs={{0,1},{1,0},{2,3},{3,2},{4,5},{5,4},{6,7},{7,6},{8,9},{9,8},{10,11... | collective-permute-start | bytes 786440 | tf_op jit(solution)/shard_map/ppermute | solution.py:359
  23.0 8.7 %collective-permute-start.11 = (bf16[128,1024]{1,0:T(8,128)(2,1)S(1)}, bf16[128,1024]{1,0:T(8,128)(2,1)S(1)}, u32[]{:S(2)}, u32[]{:S(2)}) collective-permute-start(bf16[128,1024]{1,0:T(8,128)(2,1)S(1)} %collective-permute-done.1.rest_8_), channel_id=1, source_target_pairs={{0,1},{1,0},{2,3},{3,2},{4,5},{5,4},{6,7},{7,6},{8,9},{9,8},{10,11... | collective-permute-start | bytes 786440 | tf_op jit(solution)/shard_map/ppermute | solution.py:359
  23.5 8.3 %collective-permute-start.6 = (bf16[128,1024]{1,0:T(8,128)(2,1)S(1)}, bf16[128,1024]{1,0:T(8,128)(2,1)S(1)}, u32[]{:S(2)}, u32[]{:S(2)}) collective-permute-start(bf16[128,1024]{1,0:T(8,128)(2,1)S(1)} %collective-permute-done.rest_1_), channel_id=1, source_target_pairs={{0,1},{1,0},{2,3},{3,2},{4,5},{5,4},{6,7},{7,6},{8,9},{9,8},{10,11... | collective-permute-start | bytes 786440 | tf_op jit(solution)/shard_map/ppermute | solution.py:359
  30.0 6.4 %collective-permute-start.10 = (bf16[128,1024]{1,0:T(8,128)(2,1)S(1)}, bf16[128,1024]{1,0:T(8,128)(2,1)S(1)}, u32[]{:S(2)}, u32[]{:S(2)}) collective-permute-start(bf16[128,1024]{1,0:T(8,128)(2,1)S(1)} %collective-permute-done.4.rest_3_), channel_id=1, source_target_pairs={{0,2},{1,3},{2,0},{3,1},{4,6},{5,7},{6,4},{7,5},{8,10},{9,11},{10,... | collective-permute-start | bytes 786440 | tf_op jit(solution)/shard_map/ppermute | solution.py:359
  31.2 5.3 %collective-permute-start.12 = (bf16[128,1024]{1,0:T(8,128)(2,1)S(1)}, bf16[128,1024]{1,0:T(8,128)(2,1)S(1)}, u32[]{:S(2)}, u32[]{:S(2)}) collective-permute-start(bf16[128,1024]{1,0:T(8,128)(2,1)S(1)} %collective-permute-done.3.rest_9_), channel_id=1, source_target_pairs={{0,1},{1,0},{2,3},{3,2},{4,5},{5,4},{6,7},{7,6},{8,9},{9,8},{10,11... | collective-permute-start | bytes 786440 | tf_op jit(solution)/shard_map/ppermute | solution.py:359
  31.2 5.3 %collective-permute-start.7 = (bf16[128,1024]{1,0:T(8,128)(2,1)S(1)}, bf16[128,1024]{1,0:T(8,128)(2,1)S(1)}, u32[]{:S(2)}, u32[]{:S(2)}) collective-permute-start(bf16[128,1024]{1,0:T(8,128)(2,1)S(1)} %collective-permute-done.2.rest_2_), channel_id=1, source_target_pairs={{0,1},{1,0},{2,3},{3,2},{4,5},{5,4},{6,7},{7,6},{8,9},{9,8},{10,11... | collective-permute-start | bytes 786440 | tf_op jit(solution)/shard_map/ppermute | solution.py:359
  31.7 4.8 %collective-permute-start.13 = (bf16[128,1024]{1,0:T(8,128)(2,1)S(1)}, bf16[128,1024]{1,0:T(8,128)(2,1)S(1)}, u32[]{:S(2)}, u32[]{:S(2)}) collective-permute-start(bf16[128,1024]{1,0:T(8,128)(2,1)S(1)} %collective-permute-done.9.rest_10_), channel_id=1, source_target_pairs={{0,1},{1,0},{2,3},{3,2},{4,5},{5,4},{6,7},{7,6},{8,9},{9,8},{10,11... | collective-permute-start | bytes 786440 | tf_op jit(solution)/shard_map/ppermute | solution.py:359
  31.8 4.7 %collective-permute-start.8 = (bf16[128,1024]{1,0:T(8,128)(2,1)S(1)}, bf16[128,1024]{1,0:T(8,128)(2,1)}, u32[]{:S(2)}, u32[]{:S(2)}) collective-permute-start(bf16[128,1024]{1,0:T(8,128)(2,1)S(1)} %collective-permute-done.4.rest_3_), channel_id=1, source_target_pairs={{0,1},{1,0},{2,3},{3,2},{4,5},{5,4},{6,7},{7,6},{8,9},{9,8},{10,11... | collective-permute-start | bytes 786440 | tf_op jit(solution)/shard_map/ppermute | solution.py:359
  61.0 28.7 %collective-permute-start.16 = (bf16[4,128,512]{2,1,0:T(8,128)(2,1)}, bf16[4,128,512]{2,1,0:T(8,128)(2,1)S(1)}, u32[]{:S(2)}, u32[]{:S(2)}) collective-permute-start(bf16[4,128,512]{2,1,0:T(8,128)(2,1)} %get-tuple-element.40), channel_id=1, source_target_pairs={{0,1},{1,0},{2,3},{3,2},{4,5},{5,4},{6,7},{7,6},{8,9},{9,8},{10,11... | collective-permute-start | bytes 1572872 | tf_op jit(solution)/shard_map/ppermute | solution.py:359
  64.1 25.5 %collective-permute-start.17 = (bf16[4,128,512]{2,1,0:T(8,128)(2,1)S(1)}, bf16[4,128,512]{2,1,0:T(8,128)(2,1)S(1)}, u32[]{:S(2)}, u32[]{:S(2)}) collective-permute-start(bf16[4,128,512]{2,1,0:T(8,128)(2,1)S(1)} %add_convert_fusion.1), channel_id=1, source_target_pairs={{0,2},{1,3},{2,0},{3,1},{4,6},{5,7},{6,4},{7,5},{8,10},{9,11},{10,... | collective-permute-start | bytes 1572872 | tf_op jit(solution)/shard_map/ppermute | solution.py:359
  88.1 16.5 %collective-permute-start.22 = (bf16[4,128,512]{2,1,0:T(8,128)(2,1)}, bf16[4,128,512]{2,1,0:T(8,128)(2,1)S(1)}, u32[]{:S(2)}, u32[]{:S(2)}) collective-permute-start(bf16[4,128,512]{2,1,0:T(8,128)(2,1)} %get-tuple-element.47), channel_id=1, source_target_pairs={{0,1},{1,0},{2,3},{3,2},{4,5},{5,4},{6,7},{7,6},{8,9},{9,8},{10,11... | collective-permute-start | bytes 1572872 | tf_op jit(solution)/shard_map/ppermute | solution.py:359
  90.8 14.0 %collective-permute-start.23 = (bf16[4,128,512]{2,1,0:T(8,128)(2,1)S(1)}, bf16[4,128,512]{2,1,0:T(8,128)(2,1)S(1)}, u32[]{:S(2)}, u32[]{:S(2)}) collective-permute-start(bf16[4,128,512]{2,1,0:T(8,128)(2,1)S(1)} %add_convert_fusion), channel_id=1, source_target_pairs={{0,2},{1,3},{2,0},{3,1},{4,6},{5,7},{6,4},{7,5},{8,10},{9,11},{10,... | collective-permute-start | bytes 1572872 | tf_op jit(solution)/shard_map/ppermute | solution.py:359
  91.8 8.2 %collective-permute-start.19 = (bf16[128,512]{1,0:T(8,128)(2,1)S(1)}, bf16[128,512]{1,0:T(8,128)(2,1)S(1)}, u32[]{:S(2)}, u32[]{:S(2)}) collective-permute-start(bf16[128,512]{1,0:T(8,128)(2,1)S(1)} %get-tuple-element.43), channel_id=1, source_target_pairs={{0,4},{1,5},{2,6},{3,7},{4,8},{5,9},{6,10},{7,11},{8,12},{9,13},{1... | collective-permute-start | bytes 393224 | tf_op jit(solution)/shard_map/ppermute | solution.py:359
  91.8 12.7 %collective-permute-start.20 = (bf16[128,512]{1,0:T(8,128)(2,1)S(1)}, bf16[128,512]{1,0:T(8,128)(2,1)S(1)}, u32[]{:S(2)}, u32[]{:S(2)}) collective-permute-start(bf16[128,512]{1,0:T(8,128)(2,1)S(1)} %get-tuple-element.44), channel_id=1, source_target_pairs={{0,8},{1,9},{2,10},{3,11},{4,12},{5,13},{6,14},{7,15},{8,0},{9,1},... | collective-permute-start | bytes 393224 | tf_op jit(solution)/shard_map/ppermute | solution.py:359
  94.3 10.3 %collective-permute-start.21 = (bf16[128,512]{1,0:T(8,128)(2,1)S(1)}, bf16[128,512]{1,0:T(8,128)(2,1)S(1)}, u32[]{:S(2)}, u32[]{:S(2)}) collective-permute-start(bf16[128,512]{1,0:T(8,128)(2,1)S(1)} %get-tuple-element.45), channel_id=1, source_target_pairs={{0,12},{1,13},{2,14},{3,15},{4,0},{5,1},{6,2},{7,3},{8,4},{9,5},{1... | collective-permute-start | bytes 393224 | tf_op jit(solution)/shard_map/ppermute | solution.py:359
  105.1 8.4 %collective-permute-start.24 = (bf16[128,512]{1,0:T(8,128)(2,1)S(1)}, bf16[128,512]{1,0:T(8,128)(2,1)S(1)}, u32[]{:S(2)}, u32[]{:S(2)}) collective-permute-start(bf16[128,512]{1,0:T(8,128)(2,1)S(1)} %get-tuple-element.55), channel_id=1, source_target_pairs={{0,4},{1,5},{2,6},{3,7},{4,8},{5,9},{6,10},{7,11},{8,12},{9,13},{1... | collective-permute-start | bytes 393224 | tf_op jit(solution)/shard_map/ppermute | solution.py:359
  107.4 9.9 %collective-permute-start.25 = (bf16[128,512]{1,0:T(8,128)(2,1)S(1)}, bf16[128,512]{1,0:T(8,128)(2,1)S(1)}, u32[]{:S(2)}, u32[]{:S(2)}) collective-permute-start(bf16[128,512]{1,0:T(8,128)(2,1)S(1)} %get-tuple-element.57), channel_id=1, source_target_pairs={{0,8},{1,9},{2,10},{3,11},{4,12},{5,13},{6,14},{7,15},{8,0},{9,1},... | collective-permute-start | bytes 393224 | tf_op jit(solution)/shard_map/ppermute | solution.py:359
  108.0 9.2 %collective-permute-start.26 = (bf16[128,512]{1,0:T(8,128)(2,1)S(1)}, bf16[128,512]{1,0:T(8,128)(2,1)S(1)}, u32[]{:S(2)}, u32[]{:S(2)}) collective-permute-start(bf16[128,512]{1,0:T(8,128)(2,1)S(1)} %get-tuple-element.56), channel_id=1, source_target_pairs={{0,12},{1,13},{2,14},{3,15},{4,0},{5,1},{6,2},{7,3},{8,4},{9,5},{1... | collective-permute-start | bytes 393224 | tf_op jit(solution)/shard_map/ppermute | solution.py:359
  (20 other events, 180.2 us)

commit v14 on v11

--- a/solution.py
+++ b/solution.py
@@ -366,16 +366,34 @@
     def add(own, received):
         return own.astype(f32) + received.astype(f32)
 
-    def reduce_ranks(totals, away):
+    def reduce_planes(totals, away):
         total = add(totals[0], send(totals[1], 0, 0, 1))
-        return add(total, send(away, 0, 1, 0)) if ranks == 2 else total
-
-    def reduce_planes(total, *begun):
+        total = add(total, send(away, 0, 1, 0)) if ranks == 2 else total
         mine = total[0]
         for k in range(1, planes):
-            away = tie(total[k].astype(jnp.bfloat16), *begun)
-            mine = add(mine, send(away, k, 0, 0))
+            mine = add(mine, send(total[k].astype(jnp.bfloat16), k, 0, 0))
         return mine.astype(jnp.bfloat16)
+
+
+    def reduce_ranks(totals, away, in_pieces):
+        total = add(totals[0], send(totals[1], 0, 0, 1))
+        if not in_pieces:
+            total = add(total, send(away, 0, 1, 0))
+            return total[1::2].astype(jnp.bfloat16), total[0::2]
+        odd = add(total[1::2], send(away[1::2], 0, 1, 0)).astype(jnp.bfloat16)
+        return odd, add(total[0::2], tie(send(away[0::2], 0, 1, 0), odd))
+
+    def reduce_halves(odd, even, first, second):
+        pairs = [
+            (index(p, r, c), index(p ^ 1, r, c))
+            for p in range(planes) for r in range(ranks) for c in range(2)
+        ]
+        received = tie(lax.ppermute(odd, "dp", pairs), *first).astype(f32)
+        is_odd = lax.bitwise_and(place[0], jnp.int32(2 * ranks)) != 0
+        mine = even[0] + jnp.where(is_odd, received[0], received[1])
+        rest = even[1] + jnp.where(is_odd, received[1], received[0])
+        received = tie(send(rest.astype(jnp.bfloat16), 2, 0, 0), *second)
+        return add(mine, received).astype(jnp.bfloat16)
 
     chunks = len(CHUNKS)
     near = [by_planes(chunk) for chunk in range(chunks)]
@@ -399,10 +417,14 @@
         d_leaf.append(leaf_part)
         away = add(totals[2], send(totals[3], 0, 0, 1)).astype(jnp.bfloat16) if ranks == 2 else None
         parts.append((totals, away))
-    begun = [parts[-1][1]] if ranks == 2 else []
-    d_prefix = [reduce_planes(reduce_ranks(*part), *begun) for part in parts[:-1]]
-    d_prefix.append(reduce_planes(reduce_ranks(*parts[-1])))
-    d_leaf = [tie(part, d_leaf[-1]) for part in d_leaf[:-1]] + d_leaf[-1:]
+    if planes == 4 and ranks == 2:
+        away = parts[-1][1]
+        odd, even = reduce_ranks(*parts[-1], True)
+        d_prefix = [reduce_halves(*reduce_ranks(*part, False), [away], [odd]) for part in parts[:-1]]
+        d_prefix.append(reduce_halves(odd, even, [], []))
+        d_leaf = [tie(part, odd) for part in d_leaf]
+    else:
+        d_prefix = [reduce_planes(*part) for part in parts]
 
     def join(parts):
         halves = [jnp.split(p, 2, axis=1) for p in parts]

time: 117 us -> 115 us (0.983)
  starting transfers between devices: 30.3 us -> 28.5 us
  waiting for transfers between devices: 32.2 us -> 34 us
  local copies, waits for them, and re-layouts: 4.08 us -> 2.74 us
    ppermute x24 -> x21, starting transfers between devices: 30.3 us -> 23.9 us  [send(): return lax.ppermute(array, 'dp', pairs)]
    ppermute x0 -> x2, starting transfers between devices: none -> 4.54 us  [reduce_halves(): received = tie(lax.ppermute(odd, 'dp', pairs), *first).astype(f32)]
    ppermute x24 -> x21, waiting for transfers between devices: 32.2 us -> 33.3 us  [send(): return lax.ppermute(array, 'dp', pairs)]
  transfers between devices with their start and end apart: 24 -> 23, of which waited for: 12 -> 12; matrix products, arithmetic and copies ran while one was open for 3% -> 3% of each run, Pallas kernels for 39% -> 39%
where the time goes in v14:
time: 115 us
  Pallas kernels  44.9 us (39%)
  waiting for transfers between devices  34 us (30%)
  starting transfers between devices  28.5 us (25%)
  other arithmetic  3.95 us (3%)
  local copies, waits for them, and re-layouts  2.74 us (2%)
    pallas_call x2, Pallas kernels, attention(): pl.pallas_call(functools.partial(attention_kernel, prompts=prompts, per_p...  44.9 us
    ppermute x21, waiting for transfers between devices, send(): return lax.ppermute(array, 'dp', pairs)  33.3 us
    ppermute x21, starting transfers between devices, send(): return lax.ppermute(array, 'dp', pairs)  23.9 us
    ppermute x2, starting transfers between devices, reduce_halves(): received = tie(lax.ppermute(odd, 'dp', pairs), *first).astype(f32)  4.54 us
  transfers between devices with their start and end apart: 23, of which 12 were waited for; matrix products, arithmetic and copies ran while one was open for 3% of the time, Pallas kernels for 39%

profile of v14, /device:TPU:0, one launch (start us, length us, event | category | flops | bytes accessed | tf_op | source)
XLA Modules:
  0.0 115.0 jit_solution(15148602561816332358)
XLA Ops:
  0.6 1.0 fusion.14
  1.6 3.1 %collective-permute-start.4 = (bf16[128,512]{1,0:T(8,128)(2,1)S(1)}, bf16[128,512]{1,0:T(8,128)(2,1)S(1)}, u32[]{:S(2)}, u32[]{:S(2)}) collective-permute-start(bf16[128,512]{1,0:T(8,128)(2,1)S(1)} %pad_maximum_fusion.5), channel_id=1, source_target_pairs={{0,4},{1,5},{2,6},{3,7},{4,8},{5,9},{6,10},{7,11},{8,12},{9,13},{1... | collective-permute-start | bytes 393224 | tf_op jit(solution)/shard_map/ppermute | solution.py:351
  4.7 2.6 %collective-permute-start.5 = (bf16[128,512]{1,0:T(8,128)(2,1)S(1)}, bf16[128,512]{1,0:T(8,128)(2,1)S(1)}, u32[]{:S(2)}, u32[]{:S(2)}) collective-permute-start(bf16[128,512]{1,0:T(8,128)(2,1)S(1)} %pad_maximum_fusion.5), channel_id=1, source_target_pairs={{0,8},{1,9},{2,10},{3,11},{4,12},{5,13},{6,14},{7,15},{8,0},{9,1},... | collective-permute-start | bytes 393224 | tf_op jit(solution)/shard_map/ppermute | solution.py:351
  7.3 1.3 %collective-permute-start.6 = (bf16[128,512]{1,0:T(8,128)(2,1)S(1)}, bf16[128,512]{1,0:T(8,128)(2,1)S(1)}, u32[]{:S(2)}, u32[]{:S(2)}) collective-permute-start(bf16[128,512]{1,0:T(8,128)(2,1)S(1)} %pad_maximum_fusion.5), channel_id=1, source_target_pairs={{0,12},{1,13},{2,14},{3,15},{4,0},{5,1},{6,2},{7,3},{8,4},{9,5},{1... | collective-permute-start | bytes 393224 | tf_op jit(solution)/shard_map/ppermute | solution.py:351
  8.6 2.5 %collective-permute-done.4 = bf16[128,512]{1,0:T(8,128)(2,1)S(1)} collective-permute-done((bf16[128,512]{1,0:T(8,128)(2,1)S(1)}, bf16[128,512]{1,0:T(8,128)(2,1)S(1)}, u32[]{:S(2)}, u32[]{:S(2)}) %collective-permute-start.4) | collective-permute-done | bytes 131104 | tf_op jit(solution)/shard_map/ppermute | solution.py:351
  11.1 4.8 %collective-permute-done.5 = bf16[128,512]{1,0:T(8,128)(2,1)S(1)} collective-permute-done((bf16[128,512]{1,0:T(8,128)(2,1)S(1)}, bf16[128,512]{1,0:T(8,128)(2,1)S(1)}, u32[]{:S(2)}, u32[]{:S(2)}) %collective-permute-start.5) | collective-permute-done | bytes 131104 | tf_op jit(solution)/shard_map/ppermute | solution.py:351
  16.0 1.6 %collective-permute-start.8 = (bf16[512,512]{1,0:T(8,128)(2,1)S(1)}, bf16[512,512]{1,0:T(8,128)(2,1)S(1)}, u32[]{:S(2)}, u32[]{:S(2)}) collective-permute-start(bf16[512,512]{1,0:T(8,128)(2,1)S(1)} %pad_maximum_fusion.1.rest_0_), channel_id=1, source_target_pairs={{0,2},{1,3},{2,0},{3,1},{4,6},{5,7},{6,4},{7,5},{8,10},{9,11},{10,... | collective-permute-start | bytes 1572872 | tf_op jit(solution)/shard_map/ppermute | solution.py:351
  17.6 3.3 %collective-permute-start = (bf16[128,512]{1,0:T(8,128)(2,1)S(1)}, bf16[128,512]{1,0:T(8,128)(2,1)S(1)}, u32[]{:S(2)}, u32[]{:S(2)}) collective-permute-start(bf16[128,512]{1,0:T(8,128)(2,1)S(1)} %pad_maximum_fusion.4), channel_id=1, source_target_pairs={{0,4},{1,5},{2,6},{3,7},{4,8},{5,9},{6,10},{7,11},{8,12},{9,13},{1... | collective-permute-start | bytes 393224 | tf_op jit(solution)/shard_map/ppermute | solution.py:351
  20.9 1.6 %collective-permute-start.1 = (bf16[128,512]{1,0:T(8,128)(2,1)S(1)}, bf16[128,512]{1,0:T(8,128)(2,1)S(1)}, u32[]{:S(2)}, u32[]{:S(2)}) collective-permute-start(bf16[128,512]{1,0:T(8,128)(2,1)S(1)} %pad_maximum_fusion.4), channel_id=1, source_target_pairs={{0,8},{1,9},{2,10},{3,11},{4,12},{5,13},{6,14},{7,15},{8,0},{9,1},... | collective-permute-start | bytes 393224 | tf_op jit(solution)/shard_map/ppermute | solution.py:351
  23.3 2.9 %collective-permute-done = bf16[128,512]{1,0:T(8,128)(2,1)S(1)} collective-permute-done((bf16[128,512]{1,0:T(8,128)(2,1)S(1)}, bf16[128,512]{1,0:T(8,128)(2,1)S(1)}, u32[]{:S(2)}, u32[]{:S(2)}) %collective-permute-start) | collective-permute-done | bytes 131104 | tf_op jit(solution)/shard_map/ppermute | solution.py:351
  26.3 4.3 %collective-permute-done.1 = bf16[128,512]{1,0:T(8,128)(2,1)S(1)} collective-permute-done((bf16[128,512]{1,0:T(8,128)(2,1)S(1)}, bf16[128,512]{1,0:T(8,128)(2,1)S(1)}, u32[]{:S(2)}, u32[]{:S(2)}) %collective-permute-start.1) | collective-permute-done | bytes 131104 | tf_op jit(solution)/shard_map/ppermute | solution.py:351
  34.2 22.3 %shard_map.111 = (bf16[256,4096]{1,0:T(8,128)(2,1)}, bf16[256,4096]{1,0:T(8,128)(2,1)}, bf16[256,512]{1,0:T(8,128)(2,1)}, bf16[4,128,512]{2,1,0:T(8,128)(2,1)}, ...) custom-call(s32[16]{0:T(128)} %owner_ref.3, s32[4]{0:T(128)} %tokens_ref.3, ...), custom_call_target="tpu_custom_call" | custom-call | flops 9663676416 | bytes 8388608 | tf_op jit(solution)/shard_map/pallas_call | solution.py:284
  57.2 1.5 %collective-permute-done.10 = bf16[4,128,512]{2,1,0:T(8,128)(2,1)S(1)} collective-permute-done((bf16[4,128,512]{2,1,0:T(8,128)(2,1)}, bf16[4,128,512]{2,1,0:T(8,128)(2,1)S(1)}, u32[]{:S(2)}, u32[]{:S(2)}) %collective-permute-start.10) | collective-permute-done | bytes 524320 | tf_op jit(solution)/shard_map/ppermute | solution.py:351
  58.7 1.2 %add_convert_fusion.1 = bf16[4,128,512]{2,1,0:T(8,128)(2,1)S(1)} fusion(bf16[4,128,512]{2,1,0:T(8,128)(2,1)S(1)} %collective-permute-done.10, bf16[4,128,512]{2,1,0:T(8,128)(2,1)} %get-tuple-element.29), kind=kLoop, calls=%fused_computation.3 | loop fusion | flops 1048576 | bytes 1572864 | tf_op jit(solution)/shard_map/convert_element_type | solution.py:418
  61.3 22.6 %shard_map.112 = (bf16[256,4096]{1,0:T(8,128)(2,1)}, bf16[256,4096]{1,0:T(8,128)(2,1)}, bf16[256,512]{1,0:T(8,128)(2,1)}, bf16[4,128,512]{2,1,0:T(8,128)(2,1)}, ...) custom-call(s32[16]{0:T(128)} %owner_ref.3, ...), custom_call_target="tpu_custom_call", output_to_operand_aliasing={{0}: (13, {}), {1}: (14, {})} | custom-call | flops 9663676416 | bytes 8388608 | tf_op jit(solution)/shard_map/pallas_call | solution.py:284
  84.8 3.4 %collective-permute-start.18 = (bf16[2,128,512]{2,1,0:T(8,128)(2,1)S(1)}, bf16[2,128,512]{2,1,0:T(8,128)(2,1)S(1)}, u32[]{:S(2)}, u32[]{:S(2)}) collective-permute-start(bf16[2,128,512]{2,1,0:T(8,128)(2,1)S(1)} %slice.67), channel_id=1, source_target_pairs={{0,4},{1,5},{2,6},{3,7},{4,0},{5,1},{6,2},{7,3},{8,12},{9,13},{10,... | collective-permute-start | bytes 786440 | tf_op jit(solution)/shard_map/ppermute | solution.py:391
  88.4 1.6 %collective-permute-start.15 = (bf16[2,128,512]{2,1,0:T(8,128)(2,1)S(1)}, bf16[2,128,512]{2,1,0:T(8,128)(2,1)S(1)}, u32[]{:S(2)}, u32[]{:S(2)}) collective-permute-start(bf16[2,128,512]{2,1,0:T(8,128)(2,1)S(1)} %get-tuple-element.53), channel_id=1, source_target_pairs={{0,2},{1,3},{2,0},{3,1},{4,6},{5,7},{6,4},{7,5},{8,10},{9,11},{10,... | collective-permute-start | bytes 786440 | tf_op jit(solution)/shard_map/ppermute | solution.py:351
  90.6 7.0 %collective-permute-done.15 = bf16[2,128,512]{2,1,0:T(8,128)(2,1)S(1)} collective-permute-done((bf16[2,128,512]{2,1,0:T(8,128)(2,1)S(1)}, bf16[2,128,512]{2,1,0:T(8,128)(2,1)S(1)}, u32[]{:S(2)}, u32[]{:S(2)}) %collective-permute-start.15) | collective-permute-done | bytes 262176 | tf_op jit(solution)/shard_map/ppermute | solution.py:351
  97.7 1.2 %collective-permute-start.21 = (bf16[2,128,512]{2,1,0:T(8,128)(2,1)S(1)}, bf16[2,128,512]{2,1,0:T(8,128)(2,1)S(1)}, u32[]{:S(2)}, u32[]{:S(2)}) collective-permute-start(bf16[2,128,512]{2,1,0:T(8,128)(2,1)S(1)} %add_convert_fusion.2), channel_id=1, source_target_pairs={{0,4},{1,5},{2,6},{3,7},{4,0},{5,1},{6,2},{7,3},{8,12},{9,13},{10,... | collective-permute-start | bytes 786440 | tf_op jit(solution)/shard_map/ppermute | solution.py:391
  99.0 1.8 %collective-permute-start.19 = (bf16[128,512]{1,0:T(8,128)(2,1)S(1)}, bf16[128,512]{1,0:T(8,128)(2,1)S(1)}, u32[]{:S(2)}, u32[]{:S(2)}) collective-permute-start(bf16[128,512]{1,0:T(8,128)(2,1)S(1)} %fusion.8), channel_id=1, source_target_pairs={{0,8},{1,9},{2,10},{3,11},{4,12},{5,13},{6,14},{7,15},{8,0},{9,1},... | collective-permute-start | bytes 393224 | tf_op jit(solution)/shard_map/ppermute | solution.py:351
  100.8 1.2 %collective-permute-done.20 = bf16[2,128,512]{2,1,0:T(8,128)(2,1)S(1)} collective-permute-done((bf16[2,128,512]{2,1,0:T(8,128)(2,1)S(1)}, bf16[2,128,512]{2,1,0:T(8,128)(2,1)S(1)}, u32[]{:S(2)}, u32[]{:S(2)}) %collective-permute-start.20) | collective-permute-done | bytes 262176 | tf_op jit(solution)/shard_map/ppermute | solution.py:351
  103.1 2.9 %collective-permute-done.19 = bf16[128,512]{1,0:T(8,128)(2,1)S(1)} collective-permute-done((bf16[128,512]{1,0:T(8,128)(2,1)S(1)}, bf16[128,512]{1,0:T(8,128)(2,1)S(1)}, u32[]{:S(2)}, u32[]{:S(2)}) %collective-permute-start.19) | collective-permute-done | bytes 131104 | tf_op jit(solution)/shard_map/ppermute | solution.py:351
  106.8 2.8 %collective-permute-start.22 = (bf16[128,512]{1,0:T(8,128)(2,1)S(1)}, bf16[128,512]{1,0:T(8,128)(2,1)S(1)}, u32[]{:S(2)}, u32[]{:S(2)}) collective-permute-start(bf16[128,512]{1,0:T(8,128)(2,1)S(1)} %fusion.9), channel_id=1, source_target_pairs={{0,8},{1,9},{2,10},{3,11},{4,12},{5,13},{6,14},{7,15},{8,0},{9,1},... | collective-permute-start | bytes 393224 | tf_op jit(solution)/shard_map/ppermute | solution.py:351
  109.6 4.5 %collective-permute-done.22 = bf16[128,512]{1,0:T(8,128)(2,1)S(1)} collective-permute-done((bf16[128,512]{1,0:T(8,128)(2,1)S(1)}, bf16[128,512]{1,0:T(8,128)(2,1)S(1)}, u32[]{:S(2)}, u32[]{:S(2)}) %collective-permute-start.22) | collective-permute-done | bytes 131104 | tf_op jit(solution)/shard_map/ppermute | solution.py:351
  (75 shorter events, 11.0 us)
Async XLA Ops:
  1.6 9.5 %collective-permute-start.4 = (bf16[128,512]{1,0:T(8,128)(2,1)S(1)}, bf16[128,512]{1,0:T(8,128)(2,1)S(1)}, u32[]{:S(2)}, u32[]{:S(2)}) collective-permute-start(bf16[128,512]{1,0:T(8,128)(2,1)S(1)} %pad_maximum_fusion.5), channel_id=1, source_target_pairs={{0,4},{1,5},{2,6},{3,7},{4,8},{5,9},{6,10},{7,11},{8,12},{9,13},{1... | collective-permute-start | bytes 393224 | tf_op jit(solution)/shard_map/ppermute | solution.py:351
  4.7 11.2 %collective-permute-start.5 = (bf16[128,512]{1,0:T(8,128)(2,1)S(1)}, bf16[128,512]{1,0:T(8,128)(2,1)S(1)}, u32[]{:S(2)}, u32[]{:S(2)}) collective-permute-start(bf16[128,512]{1,0:T(8,128)(2,1)S(1)} %pad_maximum_fusion.5), channel_id=1, source_target_pairs={{0,8},{1,9},{2,10},{3,11},{4,12},{5,13},{6,14},{7,15},{8,0},{9,1},... | collective-permute-start | bytes 393224 | tf_op jit(solution)/shard_map/ppermute | solution.py:351
  7.3 8.6 %collective-permute-start.6 = (bf16[128,512]{1,0:T(8,128)(2,1)S(1)}, bf16[128,512]{1,0:T(8,128)(2,1)S(1)}, u32[]{:S(2)}, u32[]{:S(2)}) collective-permute-start(bf16[128,512]{1,0:T(8,128)(2,1)S(1)} %pad_maximum_fusion.5), channel_id=1, source_target_pairs={{0,12},{1,13},{2,14},{3,15},{4,0},{5,1},{6,2},{7,3},{8,4},{9,5},{1... | collective-permute-start | bytes 393224 | tf_op jit(solution)/shard_map/ppermute | solution.py:351
  16.0 14.8 %collective-permute-start.8 = (bf16[512,512]{1,0:T(8,128)(2,1)S(1)}, bf16[512,512]{1,0:T(8,128)(2,1)S(1)}, u32[]{:S(2)}, u32[]{:S(2)}) collective-permute-start(bf16[512,512]{1,0:T(8,128)(2,1)S(1)} %pad_maximum_fusion.1.rest_0_), channel_id=1, source_target_pairs={{0,2},{1,3},{2,0},{3,1},{4,6},{5,7},{6,4},{7,5},{8,10},{9,11},{10,... | collective-permute-start | bytes 1572872 | tf_op jit(solution)/shard_map/ppermute | solution.py:351
  17.6 8.7 %collective-permute-start = (bf16[128,512]{1,0:T(8,128)(2,1)S(1)}, bf16[128,512]{1,0:T(8,128)(2,1)S(1)}, u32[]{:S(2)}, u32[]{:S(2)}) collective-permute-start(bf16[128,512]{1,0:T(8,128)(2,1)S(1)} %pad_maximum_fusion.4), channel_id=1, source_target_pairs={{0,4},{1,5},{2,6},{3,7},{4,8},{5,9},{6,10},{7,11},{8,12},{9,13},{1... | collective-permute-start | bytes 393224 | tf_op jit(solution)/shard_map/ppermute | solution.py:351
  20.9 9.7 %collective-permute-start.1 = (bf16[128,512]{1,0:T(8,128)(2,1)S(1)}, bf16[128,512]{1,0:T(8,128)(2,1)S(1)}, u32[]{:S(2)}, u32[]{:S(2)}) collective-permute-start(bf16[128,512]{1,0:T(8,128)(2,1)S(1)} %pad_maximum_fusion.4), channel_id=1, source_target_pairs={{0,8},{1,9},{2,10},{3,11},{4,12},{5,13},{6,14},{7,15},{8,0},{9,1},... | collective-permute-start | bytes 393224 | tf_op jit(solution)/shard_map/ppermute | solution.py:351
  22.5 8.1 %collective-permute-start.2 = (bf16[128,512]{1,0:T(8,128)(2,1)S(1)}, bf16[128,512]{1,0:T(8,128)(2,1)S(1)}, u32[]{:S(2)}, u32[]{:S(2)}) collective-permute-start(bf16[128,512]{1,0:T(8,128)(2,1)S(1)} %pad_maximum_fusion.4), channel_id=1, source_target_pairs={{0,12},{1,13},{2,14},{3,15},{4,0},{5,1},{6,2},{7,3},{8,4},{9,5},{1... | collective-permute-start | bytes 393224 | tf_op jit(solution)/shard_map/ppermute | solution.py:351
  23.3 9.3 %collective-permute-start.7 = (bf16[512,512]{1,0:T(8,128)(2,1)S(1)}, bf16[512,512]{1,0:T(8,128)(2,1)S(1)}, u32[]{:S(2)}, u32[]{:S(2)}) collective-permute-start(bf16[512,512]{1,0:T(8,128)(2,1)S(1)} %pad_maximum_fusion.1.rest_0_), channel_id=1, source_target_pairs={{0,1},{1,0},{2,3},{3,2},{4,5},{5,4},{6,7},{7,6},{8,9},{9,8},{10,11... | collective-permute-start | bytes 1572872 | tf_op jit(solution)/shard_map/ppermute | solution.py:351
  30.7 25.8 %copy-start.1 = (bf16[512,512]{1,0:T(8,128)(2,1)}, bf16[512,512]{1,0:T(8,128)(2,1)S(1)}, u32[]{:S(2)}) copy-start(bf16[512,512]{1,0:T(8,128)(2,1)S(1)} %pad_maximum_fusion.rest_0_) | copy-start | bytes 1572868
  30.7 2.0 %collective-permute-start.3 = (bf16[512,512]{1,0:T(8,128)(2,1)S(1)}, bf16[512,512]{1,0:T(8,128)(2,1)S(1)}, u32[]{:S(2)}, u32[]{:S(2)}) collective-permute-start(bf16[512,512]{1,0:T(8,128)(2,1)S(1)} %pad_maximum_fusion.rest_0_), channel_id=1, source_target_pairs={{0,1},{1,0},{2,3},{3,2},{4,5},{5,4},{6,7},{7,6},{8,9},{9,8},{10,11... | collective-permute-start | bytes 1572872 | tf_op jit(solution)/shard_map/ppermute | solution.py:351
  30.8 2.6 %collective-permute-start.9 = (bf16[512,512]{1,0:T(8,128)(2,1)S(1)}, bf16[512,512]{1,0:T(8,128)(2,1)S(1)}, u32[]{:S(2)}, u32[]{:S(2)}) collective-permute-start(bf16[512,512]{1,0:T(8,128)(2,1)S(1)} %collective-permute-done.8.rest_2_), channel_id=1, source_target_pairs={{0,1},{1,0},{2,3},{3,2},{4,5},{5,4},{6,7},{7,6},{8,9},{9,8},{10,11... | collective-permute-start | bytes 1572872 | tf_op jit(solution)/shard_map/ppermute | solution.py:351
  31.3 25.5 %collective-permute-start.11 = (bf16[512,512]{1,0:T(8,128)(2,1)S(1)}, bf16[512,512]{1,0:T(8,128)(2,1)S(1)}, u32[]{:S(2)}, u32[]{:S(2)}) collective-permute-start(bf16[512,512]{1,0:T(8,128)(2,1)S(1)} %pad_maximum_fusion.rest_0_), channel_id=1, source_target_pairs={{0,2},{1,3},{2,0},{3,1},{4,6},{5,7},{6,4},{7,5},{8,10},{9,11},{10,... | collective-permute-start | bytes 1572872 | tf_op jit(solution)/shard_map/ppermute | solution.py:351
  56.5 2.2 %collective-permute-start.10 = (bf16[4,128,512]{2,1,0:T(8,128)(2,1)}, bf16[4,128,512]{2,1,0:T(8,128)(2,1)S(1)}, u32[]{:S(2)}, u32[]{:S(2)}) collective-permute-start(bf16[4,128,512]{2,1,0:T(8,128)(2,1)} %get-tuple-element.30), channel_id=1, source_target_pairs={{0,1},{1,0},{2,3},{3,2},{4,5},{5,4},{6,7},{7,6},{8,9},{9,8},{10,11... | collective-permute-start | bytes 1572872 | tf_op jit(solution)/shard_map/ppermute | solution.py:351
  56.7 3.7 %collective-permute-start.12 = (bf16[512,512]{1,0:T(8,128)(2,1)S(1)}, bf16[512,512]{1,0:T(8,128)(2,1)S(1)}, u32[]{:S(2)}, u32[]{:S(2)}) collective-permute-start(bf16[512,512]{1,0:T(8,128)(2,1)S(1)} %collective-permute-done.11.rest_2_), channel_id=1, source_target_pairs={{0,1},{1,0},{2,3},{3,2},{4,5},{5,4},{6,7},{7,6},{8,9},{9,8},{10,11... | collective-permute-start | bytes 1572872 | tf_op jit(solution)/shard_map/ppermute | solution.py:351
  57.1 27.3 %collective-permute-start.16 = (bf16[4,128,512]{2,1,0:T(8,128)(2,1)}, bf16[4,128,512]{2,1,0:T(8,128)(2,1)S(1)}, u32[]{:S(2)}, u32[]{:S(2)}) collective-permute-start(bf16[4,128,512]{2,1,0:T(8,128)(2,1)} %get-tuple-element.46), channel_id=1, source_target_pairs={{0,1},{1,0},{2,3},{3,2},{4,5},{5,4},{6,7},{7,6},{8,9},{9,8},{10,11... | collective-permute-start | bytes 1572872 | tf_op jit(solution)/shard_map/ppermute | solution.py:351
  59.9 24.6 %collective-permute-start.17 = (bf16[4,128,512]{2,1,0:T(8,128)(2,1)S(1)}, bf16[4,128,512]{2,1,0:T(8,128)(2,1)S(1)}, u32[]{:S(2)}, u32[]{:S(2)}) collective-permute-start(bf16[4,128,512]{2,1,0:T(8,128)(2,1)S(1)} %add_convert_fusion.1), channel_id=1, source_target_pairs={{0,2},{1,3},{2,0},{3,1},{4,6},{5,7},{6,4},{7,5},{8,10},{9,11},{10,... | collective-permute-start | bytes 1572872 | tf_op jit(solution)/shard_map/ppermute | solution.py:351
  83.9 4.3 %collective-permute-start.14 = (bf16[4,128,512]{2,1,0:T(8,128)(2,1)}, bf16[4,128,512]{2,1,0:T(8,128)(2,1)S(1)}, u32[]{:S(2)}, u32[]{:S(2)}) collective-permute-start(bf16[4,128,512]{2,1,0:T(8,128)(2,1)} %get-tuple-element.41), channel_id=1, source_target_pairs={{0,1},{1,0},{2,3},{3,2},{4,5},{5,4},{6,7},{7,6},{8,9},{9,8},{10,11... | collective-permute-start | bytes 1572872 | tf_op jit(solution)/shard_map/ppermute | solution.py:351
  84.0 6.5 %collective-permute-start.13 = (bf16[4,128,512]{2,1,0:T(8,128)(2,1)}, bf16[4,128,512]{2,1,0:T(8,128)(2,1)S(1)}, u32[]{:S(2)}, u32[]{:S(2)}) collective-permute-start(bf16[4,128,512]{2,1,0:T(8,128)(2,1)} %get-tuple-element.39), channel_id=1, source_target_pairs={{0,1},{1,0},{2,3},{3,2},{4,5},{5,4},{6,7},{7,6},{8,9},{9,8},{10,11... | collective-permute-start | bytes 1572872 | tf_op jit(solution)/shard_map/ppermute | solution.py:351
  84.8 14.1 %collective-permute-start.18 = (bf16[2,128,512]{2,1,0:T(8,128)(2,1)S(1)}, bf16[2,128,512]{2,1,0:T(8,128)(2,1)S(1)}, u32[]{:S(2)}, u32[]{:S(2)}) collective-permute-start(bf16[2,128,512]{2,1,0:T(8,128)(2,1)S(1)} %slice.67), channel_id=1, source_target_pairs={{0,4},{1,5},{2,6},{3,7},{4,0},{5,1},{6,2},{7,3},{8,12},{9,13},{10,... | collective-permute-start | bytes 786440 | tf_op jit(solution)/shard_map/ppermute | solution.py:391
  88.4 9.3 %collective-permute-start.15 = (bf16[2,128,512]{2,1,0:T(8,128)(2,1)S(1)}, bf16[2,128,512]{2,1,0:T(8,128)(2,1)S(1)}, u32[]{:S(2)}, u32[]{:S(2)}) collective-permute-start(bf16[2,128,512]{2,1,0:T(8,128)(2,1)S(1)} %get-tuple-element.53), channel_id=1, source_target_pairs={{0,2},{1,3},{2,0},{3,1},{4,6},{5,7},{6,4},{7,5},{8,10},{9,11},{10,... | collective-permute-start | bytes 786440 | tf_op jit(solution)/shard_map/ppermute | solution.py:351
  90.0 12.1 %collective-permute-start.20 = (bf16[2,128,512]{2,1,0:T(8,128)(2,1)S(1)}, bf16[2,128,512]{2,1,0:T(8,128)(2,1)S(1)}, u32[]{:S(2)}, u32[]{:S(2)}) collective-permute-start(bf16[2,128,512]{2,1,0:T(8,128)(2,1)S(1)} %get-tuple-element.52), channel_id=1, source_target_pairs={{0,2},{1,3},{2,0},{3,1},{4,6},{5,7},{6,4},{7,5},{8,10},{9,11},{10,... | collective-permute-start | bytes 786440 | tf_op jit(solution)/shard_map/ppermute | solution.py:351
  97.7 9.0 %collective-permute-start.21 = (bf16[2,128,512]{2,1,0:T(8,128)(2,1)S(1)}, bf16[2,128,512]{2,1,0:T(8,128)(2,1)S(1)}, u32[]{:S(2)}, u32[]{:S(2)}) collective-permute-start(bf16[2,128,512]{2,1,0:T(8,128)(2,1)S(1)} %add_convert_fusion.2), channel_id=1, source_target_pairs={{0,4},{1,5},{2,6},{3,7},{4,0},{5,1},{6,2},{7,3},{8,12},{9,13},{10,... | collective-permute-start | bytes 786440 | tf_op jit(solution)/shard_map/ppermute | solution.py:391
  99.0 6.9 %collective-permute-start.19 = (bf16[128,512]{1,0:T(8,128)(2,1)S(1)}, bf16[128,512]{1,0:T(8,128)(2,1)S(1)}, u32[]{:S(2)}, u32[]{:S(2)}) collective-permute-start(bf16[128,512]{1,0:T(8,128)(2,1)S(1)} %fusion.8), channel_id=1, source_target_pairs={{0,8},{1,9},{2,10},{3,11},{4,12},{5,13},{6,14},{7,15},{8,0},{9,1},... | collective-permute-start | bytes 393224 | tf_op jit(solution)/shard_map/ppermute | solution.py:351
  106.8 7.3 %collective-permute-start.22 = (bf16[128,512]{1,0:T(8,128)(2,1)S(1)}, bf16[128,512]{1,0:T(8,128)(2,1)S(1)}, u32[]{:S(2)}, u32[]{:S(2)}) collective-permute-start(bf16[128,512]{1,0:T(8,128)(2,1)S(1)} %fusion.9), channel_id=1, source_target_pairs={{0,8},{1,9},{2,10},{3,11},{4,12},{5,13},{6,14},{7,15},{8,0},{9,1},... | collective-permute-start | bytes 393224 | tf_op jit(solution)/shard_map/ppermute | solution.py:351
  (12 other events, 105.8 us)

commit v15 on v14

--- a/solution.py
+++ b/solution.py
@@ -62,6 +62,15 @@
         row = lax.rem(lax.div(owner, 2) + lax.div(place, 2), ranks)
         ahead = lax.rem(lax.div(owner, 2 * ranks) + planes - lax.div(place, 2 * ranks), planes)
         return core + 2 * row, ahead
+
+    def block_slot(ahead):
+        back = lax.rem(planes - ahead, planes)
+        if not (planes == 4 and ranks == 2):
+            return back
+        is_odd = lax.bitwise_and(place, jnp.int32(2 * ranks)) != 0
+        last = jnp.where(is_odd, 3, 1)
+        near = 2 + (back == last).astype(jnp.int32)
+        return jnp.where(lax.rem(back, 2) == 0, lax.div(back, 2), near)
 
     def key_columns(group):
         return pl.ds(pl.multiple_of(group * HEAD_SIZE, HEAD_SIZE), HEAD_SIZE)
@@ -109,7 +118,7 @@
                 lanes = slice(side * HEAD_SIZE, (side + 1) * HEAD_SIZE)
                 for j in range(per_prefix):
                     holder, ahead = block_place(side, j)
-                    at = lax.rem(planes - ahead, planes) * block_len
+                    at = block_slot(ahead) * block_len
                     rows = pl.ds(pl.multiple_of(at, block_len), block_len)
                     cat[j * block_len:(j + 1) * block_len, lanes] = kv[holder, rows, cols]
                 cat[span:, lanes] = leaf[...]
@@ -350,6 +359,10 @@
         ]
         return lax.ppermute(array, "dp", pairs)
 
+    neighbours = [
+        (index(p, r, c), index(p ^ 1, r, c))
+        for p in range(planes) for r in range(ranks) for c in range(2)
+    ]
     middle = KEY_VALUE_HEADS * HEAD_SIZE
 
     def tie(value, *others):
@@ -361,6 +374,9 @@
         mine = jnp.concatenate(
             [prefix_key_value[:, low:high], prefix_key_value[:, middle + low:middle + high]], axis=1
         )
+        if planes == 4 and ranks == 2:
+            both = jnp.concatenate([mine, send(mine, 2, 0, 0)], axis=0)
+            return jnp.concatenate([both, lax.ppermute(both, "dp", neighbours)], axis=0)
         return jnp.concatenate([mine] + [send(mine, k, 0, 0) for k in range(1, planes)], axis=0)
 
     def add(own, received):
@@ -384,11 +400,7 @@
         return odd, add(total[0::2], tie(send(away[0::2], 0, 1, 0), odd))
 
     def reduce_halves(odd, even, first, second):
-        pairs = [
-            (index(p, r, c), index(p ^ 1, r, c))
-            for p in range(planes) for r in range(ranks) for c in range(2)
-        ]
-        received = tie(lax.ppermute(odd, "dp", pairs), *first).astype(f32)
+        received = tie(lax.ppermute(odd, "dp", neighbours), *first).astype(f32)
         is_odd = lax.bitwise_and(place[0], jnp.int32(2 * ranks)) != 0
         mine = even[0] + jnp.where(is_odd, received[0], received[1])
         rest = even[1] + jnp.where(is_odd, received[1], received[0])

time: 115 us -> 118 us (1.026)
  waiting for transfers between devices: 34 us -> 39.3 us
  starting transfers between devices: 28.5 us -> 25.9 us
    ppermute x2 -> x4, waiting for transfers between devices: 0.65 us -> 12.1 us  [the longest x2 12.1 us: by_planes(): return jnp.concatenate([both, lax.ppermute(both, 'dp', neighbours)], axis=0)]
    ppermute x21 -> x17, waiting for transfers between devices: 33.3 us -> 27.2 us  [send(): return lax.ppermute(array, 'dp', pairs)]
    ppermute x21 -> x17, starting transfers between devices: 23.9 us -> 22.3 us  [send(): return lax.ppermute(array, 'dp', pairs)]
    ppermute x2 -> x4, starting transfers between devices: 4.54 us -> 3.6 us  [the longest x2 2.56 us: by_planes(): return jnp.concatenate([both, lax.ppermute(both, 'dp', neighbours)], axis=0)]
  transfers between devices with their start and end apart: 23 -> 21, of which waited for: 12 -> 10; matrix products, arithmetic and copies ran while one was open for 3% -> 3% of each run, Pallas kernels for 39% -> 38%
where the time goes in v15:
time: 118 us
  Pallas kernels  45.1 us (38%)
  waiting for transfers between devices  39.3 us (33%)
  starting transfers between devices  25.9 us (22%)
  other arithmetic  3.98 us (3%)
  local copies, waits for them, and re-layouts  2.74 us (2%)
    pallas_call x2, Pallas kernels, attention(): pl.pallas_call(functools.partial(attention_kernel, prompts=prompts, per_p...  45.1 us
    ppermute x17, waiting for transfers between devices, send(): return lax.ppermute(array, 'dp', pairs)  27.2 us
    ppermute x17, starting transfers between devices, send(): return lax.ppermute(array, 'dp', pairs)  22.3 us
    ppermute x2, waiting for transfers between devices, by_planes(): return jnp.concatenate([both, lax.ppermute(both, 'dp', neighbours)], axis=0)  12.1 us
    ppermute x2, starting transfers between devices, by_planes(): return jnp.concatenate([both, lax.ppermute(both, 'dp', neighbours)], axis=0)  2.56 us
  transfers between devices with their start and end apart: 21, of which 10 were waited for; matrix products, arithmetic and copies ran while one was open for 3% of the time, Pallas kernels for 38%

profile of v15, /device:TPU:0, one launch (start us, length us, event | category | flops | bytes accessed | tf_op | source)
XLA Modules:
  0.0 118.0 jit_solution(14567728868119950829)
XLA Ops:
  0.6 1.0 fusion.14
  1.6 4.1 %collective-permute-start.3 = (bf16[128,512]{1,0:T(8,128)(2,1)S(1)}, bf16[128,512]{1,0:T(8,128)(2,1)S(1)}, u32[]{:S(2)}, u32[]{:S(2)}) collective-permute-start(bf16[128,512]{1,0:T(8,128)(2,1)S(1)} %pad_maximum_fusion.7), channel_id=1, source_target_pairs={{0,8},{1,9},{2,10},{3,11},{4,12},{5,13},{6,14},{7,15},{8,0},{9,1},... | collective-permute-start | bytes 393224 | tf_op jit(solution)/shard_map/ppermute | solution.py:360
  5.7 6.3 %collective-permute-done.3 = bf16[128,512]{1,0:T(8,128)(2,1)S(1)} collective-permute-done((bf16[128,512]{1,0:T(8,128)(2,1)S(1)}, bf16[128,512]{1,0:T(8,128)(2,1)S(1)}, u32[]{:S(2)}, u32[]{:S(2)}) %collective-permute-start.3) | collective-permute-done | bytes 131104 | tf_op jit(solution)/shard_map/ppermute | solution.py:360
  12.8 3.4 %collective-permute-start = (bf16[128,512]{1,0:T(8,128)(2,1)S(1)}, bf16[128,512]{1,0:T(8,128)(2,1)S(1)}, u32[]{:S(2)}, u32[]{:S(2)}) collective-permute-start(bf16[128,512]{1,0:T(8,128)(2,1)S(1)} %pad_maximum_fusion.6), channel_id=1, source_target_pairs={{0,8},{1,9},{2,10},{3,11},{4,12},{5,13},{6,14},{7,15},{8,0},{9,1},... | collective-permute-start | bytes 393224 | tf_op jit(solution)/shard_map/ppermute | solution.py:360
  16.3 6.1 %collective-permute-done.4 = bf16[256,512]{1,0:T(8,128)(2,1)S(1)} collective-permute-done((bf16[256,512]{1,0:T(8,128)(2,1)S(1)}, bf16[256,512]{1,0:T(8,128)(2,1)S(1)}, u32[]{:S(2)}, u32[]{:S(2)}) %collective-permute-start.4) | collective-permute-done | bytes 262176 | tf_op jit(solution)/shard_map/ppermute | solution.py:379
  22.5 1.3 %collective-permute-start.6 = (bf16[512,512]{1,0:T(8,128)(2,1)S(1)}, bf16[512,512]{1,0:T(8,128)(2,1)S(1)}, u32[]{:S(2)}, u32[]{:S(2)}) collective-permute-start(bf16[512,512]{1,0:T(8,128)(2,1)S(1)} %pad_maximum_fusion.1.rest_0_), channel_id=1, source_target_pairs={{0,2},{1,3},{2,0},{3,1},{4,6},{5,7},{6,4},{7,5},{8,10},{9,11},{10,... | collective-permute-start | bytes 1572872 | tf_op jit(solution)/shard_map/ppermute | solution.py:360
  23.8 1.8 %collective-permute-start.1 = (bf16[256,512]{1,0:T(8,128)(2,1)S(1)}, bf16[256,512]{1,0:T(8,128)(2,1)S(1)}, u32[]{:S(2)}, u32[]{:S(2)}) collective-permute-start(bf16[256,512]{1,0:T(8,128)(2,1)S(1)} %pad_maximum_fusion.3), channel_id=1, source_target_pairs={{0,4},{1,5},{2,6},{3,7},{4,0},{5,1},{6,2},{7,3},{8,12},{9,13},{10,... | collective-permute-start | bytes 786440 | tf_op jit(solution)/shard_map/ppermute | solution.py:379
  25.6 6.0 %collective-permute-done.1 = bf16[256,512]{1,0:T(8,128)(2,1)S(1)} collective-permute-done((bf16[256,512]{1,0:T(8,128)(2,1)S(1)}, bf16[256,512]{1,0:T(8,128)(2,1)S(1)}, u32[]{:S(2)}, u32[]{:S(2)}) %collective-permute-start.1) | collective-permute-done | bytes 262176 | tf_op jit(solution)/shard_map/ppermute | solution.py:379
  31.7 3.0 %collective-permute-done.6.rest_2_ = bf16[512,512]{1,0:T(8,128)(2,1)S(1)} collective-permute-done((bf16[512,512]{1,0:T(8,128)(2,1)S(1)}, bf16[512,512]{1,0:T(8,128)(2,1)S(1)}, u32[]{:S(2)}, u32[]{:S(2)}) %collective-permute-start.6) | collective-permute-done | bytes 524320 | tf_op jit(solution)/shard_map/ppermute | solution.py:360
  34.7 1.0 collective-permute-start.9
  37.4 22.4 %shard_map.111 = (bf16[256,4096]{1,0:T(8,128)(2,1)}, bf16[256,4096]{1,0:T(8,128)(2,1)}, bf16[256,512]{1,0:T(8,128)(2,1)}, bf16[4,128,512]{2,1,0:T(8,128)(2,1)}, ...) custom-call(s32[16]{0:T(128)} %owner_ref.3, s32[4]{0:T(128)} %tokens_ref.3, ...), custom_call_target="tpu_custom_call" | custom-call | flops 9663676416 | bytes 8388608 | tf_op jit(solution)/shard_map/pallas_call | solution.py:293
  60.5 1.5 %collective-permute-done.8 = bf16[4,128,512]{2,1,0:T(8,128)(2,1)S(1)} collective-permute-done((bf16[4,128,512]{2,1,0:T(8,128)(2,1)}, bf16[4,128,512]{2,1,0:T(8,128)(2,1)S(1)}, u32[]{:S(2)}, u32[]{:S(2)}) %collective-permute-start.8) | collective-permute-done | bytes 524320 | tf_op jit(solution)/shard_map/ppermute | solution.py:360
  62.0 1.2 add_convert_fusion.1
  63.2 1.0 collective-permute-start.15
  65.0 22.7 %shard_map.112 = (bf16[256,4096]{1,0:T(8,128)(2,1)}, bf16[256,4096]{1,0:T(8,128)(2,1)}, bf16[256,512]{1,0:T(8,128)(2,1)}, bf16[4,128,512]{2,1,0:T(8,128)(2,1)}, ...) custom-call(s32[16]{0:T(128)} %owner_ref.3, ...), custom_call_target="tpu_custom_call", output_to_operand_aliasing={{0}: (13, {}), {1}: (14, {})} | custom-call | flops 9663676416 | bytes 8388608 | tf_op jit(solution)/shard_map/pallas_call | solution.py:293
  88.8 1.2 collective-permute-done.12
  90.2 1.1 collective-permute-start.13
  91.3 1.0 collective-permute-start.18
  92.4 6.9 %collective-permute-done.13 = bf16[2,128,512]{2,1,0:T(8,128)(2,1)S(1)} collective-permute-done((bf16[2,128,512]{2,1,0:T(8,128)(2,1)S(1)}, bf16[2,128,512]{2,1,0:T(8,128)(2,1)S(1)}, u32[]{:S(2)}, u32[]{:S(2)}) %collective-permute-start.13) | collective-permute-done | bytes 262176 | tf_op jit(solution)/shard_map/ppermute | solution.py:360
  99.5 1.0 collective-permute-start.19
  100.6 5.4 %collective-permute-start.17 = (bf16[128,512]{1,0:T(8,128)(2,1)S(1)}, bf16[128,512]{1,0:T(8,128)(2,1)S(1)}, u32[]{:S(2)}, u32[]{:S(2)}) collective-permute-start(bf16[128,512]{1,0:T(8,128)(2,1)S(1)} %fusion.8), channel_id=1, source_target_pairs={{0,8},{1,9},{2,10},{3,11},{4,12},{5,13},{6,14},{7,15},{8,0},{9,1},... | collective-permute-start | bytes 393224 | tf_op jit(solution)/shard_map/ppermute | solution.py:360
  106.9 3.2 %collective-permute-done.17 = bf16[128,512]{1,0:T(8,128)(2,1)S(1)} collective-permute-done((bf16[128,512]{1,0:T(8,128)(2,1)S(1)}, bf16[128,512]{1,0:T(8,128)(2,1)S(1)}, u32[]{:S(2)}, u32[]{:S(2)}) %collective-permute-start.17) | collective-permute-done | bytes 131104 | tf_op jit(solution)/shard_map/ppermute | solution.py:360
  110.3 2.6 %collective-permute-start.20 = (bf16[128,512]{1,0:T(8,128)(2,1)S(1)}, bf16[128,512]{1,0:T(8,128)(2,1)S(1)}, u32[]{:S(2)}, u32[]{:S(2)}) collective-permute-start(bf16[128,512]{1,0:T(8,128)(2,1)S(1)} %fusion.9), channel_id=1, source_target_pairs={{0,8},{1,9},{2,10},{3,11},{4,12},{5,13},{6,14},{7,15},{8,0},{9,1},... | collective-permute-start | bytes 393224 | tf_op jit(solution)/shard_map/ppermute | solution.py:360
  113.0 4.2 %collective-permute-done.20 = bf16[128,512]{1,0:T(8,128)(2,1)S(1)} collective-permute-done((bf16[128,512]{1,0:T(8,128)(2,1)S(1)}, bf16[128,512]{1,0:T(8,128)(2,1)S(1)}, u32[]{:S(2)}, u32[]{:S(2)}) %collective-permute-start.20) | collective-permute-done | bytes 131104 | tf_op jit(solution)/shard_map/ppermute | solution.py:360
  (73 shorter events, 7.7 us)
Async XLA Ops:
  1.6 10.4 %collective-permute-start.3 = (bf16[128,512]{1,0:T(8,128)(2,1)S(1)}, bf16[128,512]{1,0:T(8,128)(2,1)S(1)}, u32[]{:S(2)}, u32[]{:S(2)}) collective-permute-start(bf16[128,512]{1,0:T(8,128)(2,1)S(1)} %pad_maximum_fusion.7), channel_id=1, source_target_pairs={{0,8},{1,9},{2,10},{3,11},{4,12},{5,13},{6,14},{7,15},{8,0},{9,1},... | collective-permute-start | bytes 393224 | tf_op jit(solution)/shard_map/ppermute | solution.py:360
  12.0 10.4 %collective-permute-start.4 = (bf16[256,512]{1,0:T(8,128)(2,1)S(1)}, bf16[256,512]{1,0:T(8,128)(2,1)S(1)}, u32[]{:S(2)}, u32[]{:S(2)}) collective-permute-start(bf16[256,512]{1,0:T(8,128)(2,1)S(1)} %pad_maximum_fusion.4), channel_id=1, source_target_pairs={{0,4},{1,5},{2,6},{3,7},{4,0},{5,1},{6,2},{7,3},{8,12},{9,13},{10,... | collective-permute-start | bytes 786440 | tf_op jit(solution)/shard_map/ppermute | solution.py:379
  12.8 11.0 %collective-permute-start = (bf16[128,512]{1,0:T(8,128)(2,1)S(1)}, bf16[128,512]{1,0:T(8,128)(2,1)S(1)}, u32[]{:S(2)}, u32[]{:S(2)}) collective-permute-start(bf16[128,512]{1,0:T(8,128)(2,1)S(1)} %pad_maximum_fusion.6), channel_id=1, source_target_pairs={{0,8},{1,9},{2,10},{3,11},{4,12},{5,13},{6,14},{7,15},{8,0},{9,1},... | collective-permute-start | bytes 393224 | tf_op jit(solution)/shard_map/ppermute | solution.py:360
  22.5 12.3 %collective-permute-start.6 = (bf16[512,512]{1,0:T(8,128)(2,1)S(1)}, bf16[512,512]{1,0:T(8,128)(2,1)S(1)}, u32[]{:S(2)}, u32[]{:S(2)}) collective-permute-start(bf16[512,512]{1,0:T(8,128)(2,1)S(1)} %pad_maximum_fusion.1.rest_0_), channel_id=1, source_target_pairs={{0,2},{1,3},{2,0},{3,1},{4,6},{5,7},{6,4},{7,5},{8,10},{9,11},{10,... | collective-permute-start | bytes 1572872 | tf_op jit(solution)/shard_map/ppermute | solution.py:360
  23.8 7.7 %collective-permute-start.1 = (bf16[256,512]{1,0:T(8,128)(2,1)S(1)}, bf16[256,512]{1,0:T(8,128)(2,1)S(1)}, u32[]{:S(2)}, u32[]{:S(2)}) collective-permute-start(bf16[256,512]{1,0:T(8,128)(2,1)S(1)} %pad_maximum_fusion.3), channel_id=1, source_target_pairs={{0,4},{1,5},{2,6},{3,7},{4,0},{5,1},{6,2},{7,3},{8,12},{9,13},{10,... | collective-permute-start | bytes 786440 | tf_op jit(solution)/shard_map/ppermute | solution.py:379
  25.6 10.1 %collective-permute-start.5 = (bf16[512,512]{1,0:T(8,128)(2,1)S(1)}, bf16[512,512]{1,0:T(8,128)(2,1)S(1)}, u32[]{:S(2)}, u32[]{:S(2)}) collective-permute-start(bf16[512,512]{1,0:T(8,128)(2,1)S(1)} %pad_maximum_fusion.1.rest_0_), channel_id=1, source_target_pairs={{0,1},{1,0},{2,3},{3,2},{4,5},{5,4},{6,7},{7,6},{8,9},{9,8},{10,11... | collective-permute-start | bytes 1572872 | tf_op jit(solution)/shard_map/ppermute | solution.py:360
  31.6 28.2 %copy-start.1 = (bf16[512,512]{1,0:T(8,128)(2,1)}, bf16[512,512]{1,0:T(8,128)(2,1)S(1)}, u32[]{:S(2)}) copy-start(bf16[512,512]{1,0:T(8,128)(2,1)S(1)} %pad_maximum_fusion.rest_0_) | copy-start | bytes 1572868
  31.6 4.1 %collective-permute-start.2 = (bf16[512,512]{1,0:T(8,128)(2,1)S(1)}, bf16[512,512]{1,0:T(8,128)(2,1)S(1)}, u32[]{:S(2)}, u32[]{:S(2)}) collective-permute-start(bf16[512,512]{1,0:T(8,128)(2,1)S(1)} %pad_maximum_fusion.rest_0_), channel_id=1, source_target_pairs={{0,1},{1,0},{2,3},{3,2},{4,5},{5,4},{6,7},{7,6},{8,9},{9,8},{10,11... | collective-permute-start | bytes 1572872 | tf_op jit(solution)/shard_map/ppermute | solution.py:360
  34.7 1.9 %collective-permute-start.7 = (bf16[512,512]{1,0:T(8,128)(2,1)S(1)}, bf16[512,512]{1,0:T(8,128)(2,1)S(1)}, u32[]{:S(2)}, u32[]{:S(2)}) collective-permute-start(bf16[512,512]{1,0:T(8,128)(2,1)S(1)} %collective-permute-done.6.rest_2_), channel_id=1, source_target_pairs={{0,1},{1,0},{2,3},{3,2},{4,5},{5,4},{6,7},{7,6},{8,9},{9,8},{10,11... | collective-permute-start | bytes 1572872 | tf_op jit(solution)/shard_map/ppermute | solution.py:360
  34.7 25.3 %collective-permute-start.9 = (bf16[512,512]{1,0:T(8,128)(2,1)S(1)}, bf16[512,512]{1,0:T(8,128)(2,1)S(1)}, u32[]{:S(2)}, u32[]{:S(2)}) collective-permute-start(bf16[512,512]{1,0:T(8,128)(2,1)S(1)} %pad_maximum_fusion.rest_0_), channel_id=1, source_target_pairs={{0,2},{1,3},{2,0},{3,1},{4,6},{5,7},{6,4},{7,5},{8,10},{9,11},{10,... | collective-permute-start | bytes 1572872 | tf_op jit(solution)/shard_map/ppermute | solution.py:360
  35.7 24.1 %copy-start.7 = (bf16[512,512]{1,0:T(8,128)(2,1)}, bf16[512,512]{1,0:T(8,128)(2,1)S(1)}, u32[]{:S(2)}) copy-start(bf16[512,512]{1,0:T(8,128)(2,1)S(1)} %collective-permute-done.2.rest_1_) | copy-start | bytes 1572868
  59.8 2.2 %collective-permute-start.8 = (bf16[4,128,512]{2,1,0:T(8,128)(2,1)}, bf16[4,128,512]{2,1,0:T(8,128)(2,1)S(1)}, u32[]{:S(2)}, u32[]{:S(2)}) collective-permute-start(bf16[4,128,512]{2,1,0:T(8,128)(2,1)} %get-tuple-element.30), channel_id=1, source_target_pairs={{0,1},{1,0},{2,3},{3,2},{4,5},{5,4},{6,7},{7,6},{8,9},{9,8},{10,11... | collective-permute-start | bytes 1572872 | tf_op jit(solution)/shard_map/ppermute | solution.py:360
  60.0 4.2 %collective-permute-start.10 = (bf16[512,512]{1,0:T(8,128)(2,1)S(1)}, bf16[512,512]{1,0:T(8,128)(2,1)S(1)}, u32[]{:S(2)}, u32[]{:S(2)}) collective-permute-start(bf16[512,512]{1,0:T(8,128)(2,1)S(1)} %collective-permute-done.9.rest_2_), channel_id=1, source_target_pairs={{0,1},{1,0},{2,3},{3,2},{4,5},{5,4},{6,7},{7,6},{8,9},{9,8},{10,11... | collective-permute-start | bytes 1572872 | tf_op jit(solution)/shard_map/ppermute | solution.py:360
  60.4 28.0 %collective-permute-start.14 = (bf16[4,128,512]{2,1,0:T(8,128)(2,1)}, bf16[4,128,512]{2,1,0:T(8,128)(2,1)S(1)}, u32[]{:S(2)}, u32[]{:S(2)}) collective-permute-start(bf16[4,128,512]{2,1,0:T(8,128)(2,1)} %get-tuple-element.46), channel_id=1, source_target_pairs={{0,1},{1,0},{2,3},{3,2},{4,5},{5,4},{6,7},{7,6},{8,9},{9,8},{10,11... | collective-permute-start | bytes 1572872 | tf_op jit(solution)/shard_map/ppermute | solution.py:360
  63.2 25.2 %collective-permute-start.15 = (bf16[4,128,512]{2,1,0:T(8,128)(2,1)S(1)}, bf16[4,128,512]{2,1,0:T(8,128)(2,1)S(1)}, u32[]{:S(2)}, u32[]{:S(2)}) collective-permute-start(bf16[4,128,512]{2,1,0:T(8,128)(2,1)S(1)} %add_convert_fusion.1), channel_id=1, source_target_pairs={{0,2},{1,3},{2,0},{3,1},{4,6},{5,7},{6,4},{7,5},{8,10},{9,11},{10,... | collective-permute-start | bytes 1572872 | tf_op jit(solution)/shard_map/ppermute | solution.py:360
  65.0 23.3 %copy-start.3 = (bf16[4,128,512]{2,1,0:T(8,128)(2,1)S(1)}, bf16[4,128,512]{2,1,0:T(8,128)(2,1)}, u32[]{:S(2)}) copy-start(bf16[4,128,512]{2,1,0:T(8,128)(2,1)} %get-tuple-element.45) | copy-start | bytes 1572868
  87.8 2.2 %collective-permute-start.12 = (bf16[4,128,512]{2,1,0:T(8,128)(2,1)}, bf16[4,128,512]{2,1,0:T(8,128)(2,1)S(1)}, u32[]{:S(2)}, u32[]{:S(2)}) collective-permute-start(bf16[4,128,512]{2,1,0:T(8,128)(2,1)} %get-tuple-element.41), channel_id=1, source_target_pairs={{0,1},{1,0},{2,3},{3,2},{4,5},{5,4},{6,7},{7,6},{8,9},{9,8},{10,11... | collective-permute-start | bytes 1572872 | tf_op jit(solution)/shard_map/ppermute | solution.py:360
  87.9 4.4 %collective-permute-start.11 = (bf16[4,128,512]{2,1,0:T(8,128)(2,1)}, bf16[4,128,512]{2,1,0:T(8,128)(2,1)S(1)}, u32[]{:S(2)}, u32[]{:S(2)}) collective-permute-start(bf16[4,128,512]{2,1,0:T(8,128)(2,1)} %get-tuple-element.39), channel_id=1, source_target_pairs={{0,1},{1,0},{2,3},{3,2},{4,5},{5,4},{6,7},{7,6},{8,9},{9,8},{10,11... | collective-permute-start | bytes 1572872 | tf_op jit(solution)/shard_map/ppermute | solution.py:360
  88.7 11.7 %collective-permute-start.16 = (bf16[2,128,512]{2,1,0:T(8,128)(2,1)S(1)}, bf16[2,128,512]{2,1,0:T(8,128)(2,1)S(1)}, u32[]{:S(2)}, u32[]{:S(2)}) collective-permute-start(bf16[2,128,512]{2,1,0:T(8,128)(2,1)S(1)} %slice.67), channel_id=1, source_target_pairs={{0,4},{1,5},{2,6},{3,7},{4,0},{5,1},{6,2},{7,3},{8,12},{9,13},{10,... | collective-permute-start | bytes 786440 | tf_op jit(solution)/shard_map/ppermute | solution.py:403
  90.2 9.2 %collective-permute-start.13 = (bf16[2,128,512]{2,1,0:T(8,128)(2,1)S(1)}, bf16[2,128,512]{2,1,0:T(8,128)(2,1)S(1)}, u32[]{:S(2)}, u32[]{:S(2)}) collective-permute-start(bf16[2,128,512]{2,1,0:T(8,128)(2,1)S(1)} %get-tuple-element.53), channel_id=1, source_target_pairs={{0,2},{1,3},{2,0},{3,1},{4,6},{5,7},{6,4},{7,5},{8,10},{9,11},{10,... | collective-permute-start | bytes 786440 | tf_op jit(solution)/shard_map/ppermute | solution.py:360
  91.3 14.7 %collective-permute-start.18 = (bf16[2,128,512]{2,1,0:T(8,128)(2,1)S(1)}, bf16[2,128,512]{2,1,0:T(8,128)(2,1)S(1)}, u32[]{:S(2)}, u32[]{:S(2)}) collective-permute-start(bf16[2,128,512]{2,1,0:T(8,128)(2,1)S(1)} %get-tuple-element.52), channel_id=1, source_target_pairs={{0,2},{1,3},{2,0},{3,1},{4,6},{5,7},{6,4},{7,5},{8,10},{9,11},{10,... | collective-permute-start | bytes 786440 | tf_op jit(solution)/shard_map/ppermute | solution.py:360
  99.5 10.8 %collective-permute-start.19 = (bf16[2,128,512]{2,1,0:T(8,128)(2,1)S(1)}, bf16[2,128,512]{2,1,0:T(8,128)(2,1)S(1)}, u32[]{:S(2)}, u32[]{:S(2)}) collective-permute-start(bf16[2,128,512]{2,1,0:T(8,128)(2,1)S(1)} %add_convert_fusion.2), channel_id=1, source_target_pairs={{0,4},{1,5},{2,6},{3,7},{4,0},{5,1},{6,2},{7,3},{8,12},{9,13},{10,... | collective-permute-start | bytes 786440 | tf_op jit(solution)/shard_map/ppermute | solution.py:403
  100.6 9.6 %collective-permute-start.17 = (bf16[128,512]{1,0:T(8,128)(2,1)S(1)}, bf16[128,512]{1,0:T(8,128)(2,1)S(1)}, u32[]{:S(2)}, u32[]{:S(2)}) collective-permute-start(bf16[128,512]{1,0:T(8,128)(2,1)S(1)} %fusion.8), channel_id=1, source_target_pairs={{0,8},{1,9},{2,10},{3,11},{4,12},{5,13},{6,14},{7,15},{8,0},{9,1},... | collective-permute-start | bytes 393224 | tf_op jit(solution)/shard_map/ppermute | solution.py:360
  110.3 6.8 %collective-permute-start.20 = (bf16[128,512]{1,0:T(8,128)(2,1)S(1)}, bf16[128,512]{1,0:T(8,128)(2,1)S(1)}, u32[]{:S(2)}, u32[]{:S(2)}) collective-permute-start(bf16[128,512]{1,0:T(8,128)(2,1)S(1)} %fusion.9), channel_id=1, source_target_pairs={{0,8},{1,9},{2,10},{3,11},{4,12},{5,13},{6,14},{7,15},{8,0},{9,1},... | collective-permute-start | bytes 393224 | tf_op jit(solution)/shard_map/ppermute | solution.py:360
  (10 other events, 55.3 us)

commit v16 on v13

--- a/solution.py
+++ b/solution.py
@@ -364,16 +364,34 @@
     def add(own, received):
         return own.astype(f32) + received.astype(f32)
 
-    def reduce_ranks(totals, away):
+    def reduce_planes(totals, away):
         total = add(totals[0], send(totals[1], 0, 0, 1))
-        return add(total, send(away, 0, 1, 0)) if ranks == 2 else total
-
-    def reduce_planes(total, *begun):
+        total = add(total, send(away, 0, 1, 0)) if ranks == 2 else total
         mine = total[0]
         for k in range(1, planes):
-            away = tie(total[k].astype(jnp.bfloat16), *begun)
-            mine = add(mine, send(away, k, 0, 0))
+            mine = add(mine, send(total[k].astype(jnp.bfloat16), k, 0, 0))
         return mine.astype(jnp.bfloat16)
+
+
+    def reduce_ranks(totals, away, in_pieces):
+        total = add(totals[0], send(totals[1], 0, 0, 1))
+        if not in_pieces:
+            total = add(total, send(away, 0, 1, 0))
+            return total[1::2].astype(jnp.bfloat16), total[0::2]
+        odd = add(total[1::2], send(away[1::2], 0, 1, 0)).astype(jnp.bfloat16)
+        return odd, add(total[0::2], tie(send(away[0::2], 0, 1, 0), odd))
+
+    def reduce_halves(odd, even, first, second):
+        pairs = [
+            (index(p, r, c), index(p ^ 1, r, c))
+            for p in range(planes) for r in range(ranks) for c in range(2)
+        ]
+        received = tie(lax.ppermute(odd, "dp", pairs), *first).astype(f32)
+        is_odd = lax.bitwise_and(place[0], jnp.int32(2 * ranks)) != 0
+        mine = even[0] + jnp.where(is_odd, received[0], received[1])
+        rest = even[1] + jnp.where(is_odd, received[1], received[0])
+        received = tie(send(rest.astype(jnp.bfloat16), 2, 0, 0), *second)
+        return add(mine, received).astype(jnp.bfloat16)
 
     chunks = len(CHUNKS)
     near, rows = [], []
@@ -397,10 +415,13 @@
         d_leaf.append(leaf_part)
         away = add(totals[2], send(totals[3], 0, 0, 1)).astype(jnp.bfloat16) if ranks == 2 else None
         parts.append((totals, away))
-    begun = [parts[-1][1]] if ranks == 2 else []
-    d_prefix = [reduce_planes(reduce_ranks(*part), *begun) for part in parts[:-1]]
-    d_prefix.append(reduce_planes(reduce_ranks(*parts[-1])))
-    d_leaf = [tie(part, d_leaf[-1]) for part in d_leaf[:-1]] + d_leaf[-1:]
+    if planes == 4 and ranks == 2:
+        odd, even = reduce_ranks(*parts[-1], True)
+        d_prefix = [reduce_halves(*reduce_ranks(*part, False), [odd], [odd]) for part in parts[:-1]]
+        d_prefix.append(reduce_halves(odd, even, [], []))
+        d_leaf = [tie(part, odd) for part in d_leaf]
+    else:
+        d_prefix = [reduce_planes(*part) for part in parts]
 
     def join(parts):
         halves = [jnp.split(p, 2, axis=1) for p in parts]

time: 119 us -> 118 us (level)
  waiting for transfers between devices: 43.7 us -> 47.6 us
  starting transfers between devices: 23.1 us -> 20.1 us
  local copies, waits for them, and re-layouts: 1.56 us -> 0.22 us
    ppermute x27 -> x24, starting transfers between devices: 23.1 us -> 19.1 us  [send(): return lax.ppermute(array, 'dp', pairs)]
    ppermute x27 -> x24, waiting for transfers between devices: 43.7 us -> 45.9 us  [send(): return lax.ppermute(array, 'dp', pairs)]
    ppermute x0 -> x2, waiting for transfers between devices: none -> 1.65 us  [reduce_halves(): received = tie(lax.ppermute(odd, 'dp', pairs), *first).astype(f32)]
  transfers between devices with their start and end apart: 27 -> 26, of which waited for: 12 -> 12; matrix products, arithmetic and copies ran while one was open for 3% -> 3% of each run, Pallas kernels for 19% -> 19%
where the time goes in v16:
time: 118 us
  waiting for transfers between devices  47.6 us (40%)
  Pallas kernels  45.3 us (38%)
  starting transfers between devices  20.1 us (17%)
  other arithmetic  3.84 us (3%)
    ppermute x24, waiting for transfers between devices, send(): return lax.ppermute(array, 'dp', pairs)  45.9 us
    pallas_call x2, Pallas kernels, attention(): pl.pallas_call(functools.partial(attention_kernel, prompts=prompts, per_p...  45.3 us
    ppermute x24, starting transfers between devices, send(): return lax.ppermute(array, 'dp', pairs)  19.1 us
  transfers between devices with their start and end apart: 26, of which 12 were waited for; matrix products, arithmetic and copies ran while one was open for 3% of the time, Pallas kernels for 19%

profile of v16, /device:TPU:0, one launch (start us, length us, event | category | flops | bytes accessed | tf_op | source)
XLA Modules:
  0.0 118.0 jit_solution(4705654261867812331)
XLA Ops:
  0.6 3.1 %collective-permute-start = (bf16[128,1024]{1,0:T(8,128)(2,1)}, bf16[128,1024]{1,0:T(8,128)(2,1)S(1)}, u32[]{:S(2)}, u32[]{:S(2)}) collective-permute-start(bf16[128,1024]{1,0:T(8,128)(2,1)} %rest_0_.3), channel_id=1, source_target_pairs={{0,4},{1,5},{2,6},{3,7},{4,8},{5,9},{6,10},{7,11},{8,12},{9,13},{1... | collective-permute-start | bytes 786440 | tf_op jit(solution)/shard_map/ppermute | solution.py:359
  3.7 1.5 %collective-permute-start.1 = (bf16[128,1024]{1,0:T(8,128)(2,1)}, bf16[128,1024]{1,0:T(8,128)(2,1)S(1)}, u32[]{:S(2)}, u32[]{:S(2)}) collective-permute-start(bf16[128,1024]{1,0:T(8,128)(2,1)} %rest_0_.3), channel_id=1, source_target_pairs={{0,2},{1,3},{2,0},{3,1},{4,6},{5,7},{6,4},{7,5},{8,10},{9,11},{10,... | collective-permute-start | bytes 786440 | tf_op jit(solution)/shard_map/ppermute | solution.py:359
  5.2 7.0 %collective-permute-done.rest_1_ = bf16[128,1024]{1,0:T(8,128)(2,1)S(1)} collective-permute-done((bf16[128,1024]{1,0:T(8,128)(2,1)}, bf16[128,1024]{1,0:T(8,128)(2,1)S(1)}, u32[]{:S(2)}, u32[]{:S(2)}) %collective-permute-start) | collective-permute-done | bytes 262176 | tf_op jit(solution)/shard_map/ppermute | solution.py:359
  13.3 1.5 %collective-permute-start.3 = (bf16[128,1024]{1,0:T(8,128)(2,1)S(1)}, bf16[128,1024]{1,0:T(8,128)(2,1)S(1)}, u32[]{:S(2)}, u32[]{:S(2)}) collective-permute-start(bf16[128,1024]{1,0:T(8,128)(2,1)S(1)} %collective-permute-done.rest_1_), channel_id=1, source_target_pairs={{0,2},{1,3},{2,0},{3,1},{4,6},{5,7},{6,4},{7,5},{8,10},{9,11},{10,... | collective-permute-start | bytes 786440 | tf_op jit(solution)/shard_map/ppermute | solution.py:359
  14.8 6.8 %collective-permute-done.2.rest_2_ = bf16[128,1024]{1,0:T(8,128)(2,1)S(1)} collective-permute-done((bf16[128,1024]{1,0:T(8,128)(2,1)S(1)}, bf16[128,1024]{1,0:T(8,128)(2,1)S(1)}, u32[]{:S(2)}, u32[]{:S(2)}) %collective-permute-start.2) | collective-permute-done | bytes 262176 | tf_op jit(solution)/shard_map/ppermute | solution.py:359
  21.7 1.3 %collective-permute-start.9 = (bf16[128,1024]{1,0:T(8,128)(2,1)S(1)}, bf16[128,1024]{1,0:T(8,128)(2,1)S(1)}, u32[]{:S(2)}, u32[]{:S(2)}) collective-permute-start(bf16[128,1024]{1,0:T(8,128)(2,1)S(1)} %collective-permute-done.2.rest_2_), channel_id=1, source_target_pairs={{0,2},{1,3},{2,0},{3,1},{4,6},{5,7},{6,4},{7,5},{8,10},{9,11},{10,... | collective-permute-start | bytes 786440 | tf_op jit(solution)/shard_map/ppermute | solution.py:359
  23.5 6.5 %collective-permute-done.4.rest_3_ = bf16[128,1024]{1,0:T(8,128)(2,1)S(1)} collective-permute-done((bf16[128,1024]{1,0:T(8,128)(2,1)S(1)}, bf16[128,1024]{1,0:T(8,128)(2,1)S(1)}, u32[]{:S(2)}, u32[]{:S(2)}) %collective-permute-start.4) | collective-permute-done | bytes 262176 | tf_op jit(solution)/shard_map/ppermute | solution.py:359
  30.0 1.1 collective-permute-start.10
  32.2 4.3 %collective-permute-done.10.rest_11_ = bf16[128,1024]{1,0:T(8,128)(2,1)S(1)} collective-permute-done((bf16[128,1024]{1,0:T(8,128)(2,1)S(1)}, bf16[128,1024]{1,0:T(8,128)(2,1)S(1)}, u32[]{:S(2)}, u32[]{:S(2)}) %collective-permute-start.10) | collective-permute-done | bytes 262176 | tf_op jit(solution)/shard_map/ppermute | solution.py:359
  36.5 1.6 %collective-permute-done.14.rest_15_ = bf16[128,1024]{1,0:T(8,128)(2,1)} collective-permute-done((bf16[128,1024]{1,0:T(8,128)(2,1)S(1)}, bf16[128,1024]{1,0:T(8,128)(2,1)}, u32[]{:S(2)}, u32[]{:S(2)}) %collective-permute-start.14) | collective-permute-done | bytes 262176 | tf_op jit(solution)/shard_map/ppermute | solution.py:359
  38.2 22.6 %shard_map.111 = (bf16[256,4096]{1,0:T(8,128)(2,1)}, bf16[256,4096]{1,0:T(8,128)(2,1)}, bf16[256,512]{1,0:T(8,128)(2,1)}, bf16[4,128,512]{2,1,0:T(8,128)(2,1)}, ...) custom-call(s32[16]{0:T(128)} %owner_ref.3, s32[4]{0:T(128)} %tokens_ref.3, ...), custom_call_target="tpu_custom_call" | custom-call | flops 9663676416 | bytes 8388608 | tf_op jit(solution)/shard_map/pallas_call | solution.py:291
  61.4 1.6 %collective-permute-done.15 = bf16[4,128,512]{2,1,0:T(8,128)(2,1)S(1)} collective-permute-done((bf16[4,128,512]{2,1,0:T(8,128)(2,1)}, bf16[4,128,512]{2,1,0:T(8,128)(2,1)S(1)}, u32[]{:S(2)}, u32[]{:S(2)}) %collective-permute-start.15) | collective-permute-done | bytes 524320 | tf_op jit(solution)/shard_map/ppermute | solution.py:359
  63.0 1.2 add_convert_fusion.1
  64.2 1.1 collective-permute-start.20
  65.3 22.8 %shard_map.112 = (bf16[256,4096]{1,0:T(8,128)(2,1)}, bf16[256,4096]{1,0:T(8,128)(2,1)}, bf16[256,512]{1,0:T(8,128)(2,1)}, bf16[4,128,512]{2,1,0:T(8,128)(2,1)}, ...) custom-call(s32[16]{0:T(128)} %owner_ref.3, ...), custom_call_target="tpu_custom_call", output_to_operand_aliasing={{0}: (25, {}), {1}: (26, {})} | custom-call | flops 9663676416 | bytes 8388608 | tf_op jit(solution)/shard_map/pallas_call | solution.py:291
  89.1 1.2 %collective-permute-done.17 = bf16[4,128,512]{2,1,0:T(8,128)(2,1)S(1)} collective-permute-done((bf16[4,128,512]{2,1,0:T(8,128)(2,1)}, bf16[4,128,512]{2,1,0:T(8,128)(2,1)S(1)}, u32[]{:S(2)}, u32[]{:S(2)}) %collective-permute-start.17) | collective-permute-done | bytes 524320 | tf_op jit(solution)/shard_map/ppermute | solution.py:359
  91.5 1.1 collective-permute-start.23
  92.9 6.8 %collective-permute-done.18 = bf16[2,128,512]{2,1,0:T(8,128)(2,1)S(1)} collective-permute-done((bf16[2,128,512]{2,1,0:T(8,128)(2,1)S(1)}, bf16[2,128,512]{2,1,0:T(8,128)(2,1)S(1)}, u32[]{:S(2)}, u32[]{:S(2)}) %collective-permute-start.18) | collective-permute-done | bytes 262176 | tf_op jit(solution)/shard_map/ppermute | solution.py:359
  100.8 2.2 %collective-permute-start.22 = (bf16[128,512]{1,0:T(8,128)(2,1)S(1)}, bf16[128,512]{1,0:T(8,128)(2,1)S(1)}, u32[]{:S(2)}, u32[]{:S(2)}) collective-permute-start(bf16[128,512]{1,0:T(8,128)(2,1)S(1)} %fusion.8), channel_id=1, source_target_pairs={{0,8},{1,9},{2,10},{3,11},{4,12},{5,13},{6,14},{7,15},{8,0},{9,1},... | collective-permute-start | bytes 393224 | tf_op jit(solution)/shard_map/ppermute | solution.py:359
  103.0 1.6 %collective-permute-done.23 = bf16[2,128,512]{2,1,0:T(8,128)(2,1)S(1)} collective-permute-done((bf16[2,128,512]{2,1,0:T(8,128)(2,1)S(1)}, bf16[2,128,512]{2,1,0:T(8,128)(2,1)S(1)}, u32[]{:S(2)}, u32[]{:S(2)}) %collective-permute-start.23) | collective-permute-done | bytes 262176 | tf_op jit(solution)/shard_map/ppermute | solution.py:359
  105.5 2.1 %collective-permute-done.22 = bf16[128,512]{1,0:T(8,128)(2,1)S(1)} collective-permute-done((bf16[128,512]{1,0:T(8,128)(2,1)S(1)}, bf16[128,512]{1,0:T(8,128)(2,1)S(1)}, u32[]{:S(2)}, u32[]{:S(2)}) %collective-permute-start.22) | collective-permute-done | bytes 131104 | tf_op jit(solution)/shard_map/ppermute | solution.py:359
  107.7 1.6 %collective-permute-done.24 = bf16[2,128,512]{2,1,0:T(8,128)(2,1)S(1)} collective-permute-done((bf16[2,128,512]{2,1,0:T(8,128)(2,1)S(1)}, bf16[2,128,512]{2,1,0:T(8,128)(2,1)S(1)}, u32[]{:S(2)}, u32[]{:S(2)}) %collective-permute-start.24) | collective-permute-done | bytes 262176 | tf_op jit(solution)/shard_map/ppermute | solution.py:389
  109.5 1.4 %collective-permute-start.25 = (bf16[128,512]{1,0:T(8,128)(2,1)S(1)}, bf16[128,512]{1,0:T(8,128)(2,1)S(1)}, u32[]{:S(2)}, u32[]{:S(2)}) collective-permute-start(bf16[128,512]{1,0:T(8,128)(2,1)S(1)} %fusion.9), channel_id=1, source_target_pairs={{0,8},{1,9},{2,10},{3,11},{4,12},{5,13},{6,14},{7,15},{8,0},{9,1},... | collective-permute-start | bytes 393224 | tf_op jit(solution)/shard_map/ppermute | solution.py:359
  110.8 6.4 %collective-permute-done.25 = bf16[128,512]{1,0:T(8,128)(2,1)S(1)} collective-permute-done((bf16[128,512]{1,0:T(8,128)(2,1)S(1)}, bf16[128,512]{1,0:T(8,128)(2,1)S(1)}, u32[]{:S(2)}, u32[]{:S(2)}) %collective-permute-start.25) | collective-permute-done | bytes 131104 | tf_op jit(solution)/shard_map/ppermute | solution.py:359
  (86 shorter events, 8.6 us)
Async XLA Ops:
  0.6 11.6 %collective-permute-start = (bf16[128,1024]{1,0:T(8,128)(2,1)}, bf16[128,1024]{1,0:T(8,128)(2,1)S(1)}, u32[]{:S(2)}, u32[]{:S(2)}) collective-permute-start(bf16[128,1024]{1,0:T(8,128)(2,1)} %rest_0_.3), channel_id=1, source_target_pairs={{0,4},{1,5},{2,6},{3,7},{4,8},{5,9},{6,10},{7,11},{8,12},{9,13},{1... | collective-permute-start | bytes 786440 | tf_op jit(solution)/shard_map/ppermute | solution.py:359
  3.7 8.5 %collective-permute-start.1 = (bf16[128,1024]{1,0:T(8,128)(2,1)}, bf16[128,1024]{1,0:T(8,128)(2,1)S(1)}, u32[]{:S(2)}, u32[]{:S(2)}) collective-permute-start(bf16[128,1024]{1,0:T(8,128)(2,1)} %rest_0_.3), channel_id=1, source_target_pairs={{0,2},{1,3},{2,0},{3,1},{4,6},{5,7},{6,4},{7,5},{8,10},{9,11},{10,... | collective-permute-start | bytes 786440 | tf_op jit(solution)/shard_map/ppermute | solution.py:359
  12.3 9.3 %collective-permute-start.2 = (bf16[128,1024]{1,0:T(8,128)(2,1)S(1)}, bf16[128,1024]{1,0:T(8,128)(2,1)S(1)}, u32[]{:S(2)}, u32[]{:S(2)}) collective-permute-start(bf16[128,1024]{1,0:T(8,128)(2,1)S(1)} %collective-permute-done.rest_1_), channel_id=1, source_target_pairs={{0,4},{1,5},{2,6},{3,7},{4,8},{5,9},{6,10},{7,11},{8,12},{9,13},{1... | collective-permute-start | bytes 786440 | tf_op jit(solution)/shard_map/ppermute | solution.py:359
  13.3 8.3 %collective-permute-start.3 = (bf16[128,1024]{1,0:T(8,128)(2,1)S(1)}, bf16[128,1024]{1,0:T(8,128)(2,1)S(1)}, u32[]{:S(2)}, u32[]{:S(2)}) collective-permute-start(bf16[128,1024]{1,0:T(8,128)(2,1)S(1)} %collective-permute-done.rest_1_), channel_id=1, source_target_pairs={{0,2},{1,3},{2,0},{3,1},{4,6},{5,7},{6,4},{7,5},{8,10},{9,11},{10,... | collective-permute-start | bytes 786440 | tf_op jit(solution)/shard_map/ppermute | solution.py:359
  21.6 8.4 %collective-permute-start.4 = (bf16[128,1024]{1,0:T(8,128)(2,1)S(1)}, bf16[128,1024]{1,0:T(8,128)(2,1)S(1)}, u32[]{:S(2)}, u32[]{:S(2)}) collective-permute-start(bf16[128,1024]{1,0:T(8,128)(2,1)S(1)} %collective-permute-done.2.rest_2_), channel_id=1, source_target_pairs={{0,4},{1,5},{2,6},{3,7},{4,8},{5,9},{6,10},{7,11},{8,12},{9,13},{1... | collective-permute-start | bytes 786440 | tf_op jit(solution)/shard_map/ppermute | solution.py:359
  21.7 8.4 %collective-permute-start.9 = (bf16[128,1024]{1,0:T(8,128)(2,1)S(1)}, bf16[128,1024]{1,0:T(8,128)(2,1)S(1)}, u32[]{:S(2)}, u32[]{:S(2)}) collective-permute-start(bf16[128,1024]{1,0:T(8,128)(2,1)S(1)} %collective-permute-done.2.rest_2_), channel_id=1, source_target_pairs={{0,2},{1,3},{2,0},{3,1},{4,6},{5,7},{6,4},{7,5},{8,10},{9,11},{10,... | collective-permute-start | bytes 786440 | tf_op jit(solution)/shard_map/ppermute | solution.py:359
  23.0 8.2 %collective-permute-start.5 = (bf16[128,1024]{1,0:T(8,128)(2,1)}, bf16[128,1024]{1,0:T(8,128)(2,1)S(1)}, u32[]{:S(2)}, u32[]{:S(2)}) collective-permute-start(bf16[128,1024]{1,0:T(8,128)(2,1)} %rest_0_.3), channel_id=1, source_target_pairs={{0,1},{1,0},{2,3},{3,2},{4,5},{5,4},{6,7},{7,6},{8,9},{9,8},{10,11... | collective-permute-start | bytes 786440 | tf_op jit(solution)/shard_map/ppermute | solution.py:359
  23.0 8.7 %collective-permute-start.11 = (bf16[128,1024]{1,0:T(8,128)(2,1)S(1)}, bf16[128,1024]{1,0:T(8,128)(2,1)S(1)}, u32[]{:S(2)}, u32[]{:S(2)}) collective-permute-start(bf16[128,1024]{1,0:T(8,128)(2,1)S(1)} %collective-permute-done.1.rest_8_), channel_id=1, source_target_pairs={{0,1},{1,0},{2,3},{3,2},{4,5},{5,4},{6,7},{7,6},{8,9},{9,8},{10,11... | collective-permute-start | bytes 786440 | tf_op jit(solution)/shard_map/ppermute | solution.py:359
  23.5 8.3 %collective-permute-start.6 = (bf16[128,1024]{1,0:T(8,128)(2,1)S(1)}, bf16[128,1024]{1,0:T(8,128)(2,1)S(1)}, u32[]{:S(2)}, u32[]{:S(2)}) collective-permute-start(bf16[128,1024]{1,0:T(8,128)(2,1)S(1)} %collective-permute-done.rest_1_), channel_id=1, source_target_pairs={{0,1},{1,0},{2,3},{3,2},{4,5},{5,4},{6,7},{7,6},{8,9},{9,8},{10,11... | collective-permute-start | bytes 786440 | tf_op jit(solution)/shard_map/ppermute | solution.py:359
  30.0 6.4 %collective-permute-start.10 = (bf16[128,1024]{1,0:T(8,128)(2,1)S(1)}, bf16[128,1024]{1,0:T(8,128)(2,1)S(1)}, u32[]{:S(2)}, u32[]{:S(2)}) collective-permute-start(bf16[128,1024]{1,0:T(8,128)(2,1)S(1)} %collective-permute-done.4.rest_3_), channel_id=1, source_target_pairs={{0,2},{1,3},{2,0},{3,1},{4,6},{5,7},{6,4},{7,5},{8,10},{9,11},{10,... | collective-permute-start | bytes 786440 | tf_op jit(solution)/shard_map/ppermute | solution.py:359
  31.2 5.3 %collective-permute-start.12 = (bf16[128,1024]{1,0:T(8,128)(2,1)S(1)}, bf16[128,1024]{1,0:T(8,128)(2,1)S(1)}, u32[]{:S(2)}, u32[]{:S(2)}) collective-permute-start(bf16[128,1024]{1,0:T(8,128)(2,1)S(1)} %collective-permute-done.3.rest_9_), channel_id=1, source_target_pairs={{0,1},{1,0},{2,3},{3,2},{4,5},{5,4},{6,7},{7,6},{8,9},{9,8},{10,11... | collective-permute-start | bytes 786440 | tf_op jit(solution)/shard_map/ppermute | solution.py:359
  31.2 5.3 %collective-permute-start.7 = (bf16[128,1024]{1,0:T(8,128)(2,1)S(1)}, bf16[128,1024]{1,0:T(8,128)(2,1)S(1)}, u32[]{:S(2)}, u32[]{:S(2)}) collective-permute-start(bf16[128,1024]{1,0:T(8,128)(2,1)S(1)} %collective-permute-done.2.rest_2_), channel_id=1, source_target_pairs={{0,1},{1,0},{2,3},{3,2},{4,5},{5,4},{6,7},{7,6},{8,9},{9,8},{10,11... | collective-permute-start | bytes 786440 | tf_op jit(solution)/shard_map/ppermute | solution.py:359
  31.7 4.8 %collective-permute-start.13 = (bf16[128,1024]{1,0:T(8,128)(2,1)S(1)}, bf16[128,1024]{1,0:T(8,128)(2,1)S(1)}, u32[]{:S(2)}, u32[]{:S(2)}) collective-permute-start(bf16[128,1024]{1,0:T(8,128)(2,1)S(1)} %collective-permute-done.9.rest_10_), channel_id=1, source_target_pairs={{0,1},{1,0},{2,3},{3,2},{4,5},{5,4},{6,7},{7,6},{8,9},{9,8},{10,11... | collective-permute-start | bytes 786440 | tf_op jit(solution)/shard_map/ppermute | solution.py:359
  31.8 4.7 %collective-permute-start.8 = (bf16[128,1024]{1,0:T(8,128)(2,1)S(1)}, bf16[128,1024]{1,0:T(8,128)(2,1)}, u32[]{:S(2)}, u32[]{:S(2)}) collective-permute-start(bf16[128,1024]{1,0:T(8,128)(2,1)S(1)} %collective-permute-done.4.rest_3_), channel_id=1, source_target_pairs={{0,1},{1,0},{2,3},{3,2},{4,5},{5,4},{6,7},{7,6},{8,9},{9,8},{10,11... | collective-permute-start | bytes 786440 | tf_op jit(solution)/shard_map/ppermute | solution.py:359
  60.8 2.2 %collective-permute-start.15 = (bf16[4,128,512]{2,1,0:T(8,128)(2,1)}, bf16[4,128,512]{2,1,0:T(8,128)(2,1)S(1)}, u32[]{:S(2)}, u32[]{:S(2)}) collective-permute-start(bf16[4,128,512]{2,1,0:T(8,128)(2,1)} %get-tuple-element.31), channel_id=1, source_target_pairs={{0,1},{1,0},{2,3},{3,2},{4,5},{5,4},{6,7},{7,6},{8,9},{9,8},{10,11... | collective-permute-start | bytes 1572872 | tf_op jit(solution)/shard_map/ppermute | solution.py:359
  61.0 27.7 %collective-permute-start.19 = (bf16[4,128,512]{2,1,0:T(8,128)(2,1)}, bf16[4,128,512]{2,1,0:T(8,128)(2,1)S(1)}, u32[]{:S(2)}, u32[]{:S(2)}) collective-permute-start(bf16[4,128,512]{2,1,0:T(8,128)(2,1)} %get-tuple-element.46), channel_id=1, source_target_pairs={{0,1},{1,0},{2,3},{3,2},{4,5},{5,4},{6,7},{7,6},{8,9},{9,8},{10,11... | collective-permute-start | bytes 1572872 | tf_op jit(solution)/shard_map/ppermute | solution.py:359
  64.2 24.5 %collective-permute-start.20 = (bf16[4,128,512]{2,1,0:T(8,128)(2,1)S(1)}, bf16[4,128,512]{2,1,0:T(8,128)(2,1)S(1)}, u32[]{:S(2)}, u32[]{:S(2)}) collective-permute-start(bf16[4,128,512]{2,1,0:T(8,128)(2,1)S(1)} %add_convert_fusion.1), channel_id=1, source_target_pairs={{0,2},{1,3},{2,0},{3,1},{4,6},{5,7},{6,4},{7,5},{8,10},{9,11},{10,... | collective-permute-start | bytes 1572872 | tf_op jit(solution)/shard_map/ppermute | solution.py:359
  88.2 4.5 %collective-permute-start.16 = (bf16[4,128,512]{2,1,0:T(8,128)(2,1)}, bf16[4,128,512]{2,1,0:T(8,128)(2,1)S(1)}, u32[]{:S(2)}, u32[]{:S(2)}) collective-permute-start(bf16[4,128,512]{2,1,0:T(8,128)(2,1)} %get-tuple-element.39), channel_id=1, source_target_pairs={{0,1},{1,0},{2,3},{3,2},{4,5},{5,4},{6,7},{7,6},{8,9},{9,8},{10,11... | collective-permute-start | bytes 1572872 | tf_op jit(solution)/shard_map/ppermute | solution.py:359
  89.0 11.7 %collective-permute-start.21 = (bf16[2,128,512]{2,1,0:T(8,128)(2,1)S(1)}, bf16[2,128,512]{2,1,0:T(8,128)(2,1)S(1)}, u32[]{:S(2)}, u32[]{:S(2)}) collective-permute-start(bf16[2,128,512]{2,1,0:T(8,128)(2,1)S(1)} %slice.51), channel_id=1, source_target_pairs={{0,4},{1,5},{2,6},{3,7},{4,0},{5,1},{6,2},{7,3},{8,12},{9,13},{10,... | collective-permute-start | bytes 786440 | tf_op jit(solution)/shard_map/ppermute | solution.py:389
  90.5 9.2 %collective-permute-start.18 = (bf16[2,128,512]{2,1,0:T(8,128)(2,1)S(1)}, bf16[2,128,512]{2,1,0:T(8,128)(2,1)S(1)}, u32[]{:S(2)}, u32[]{:S(2)}) collective-permute-start(bf16[2,128,512]{2,1,0:T(8,128)(2,1)S(1)} %get-tuple-element.53), channel_id=1, source_target_pairs={{0,2},{1,3},{2,0},{3,1},{4,6},{5,7},{6,4},{7,5},{8,10},{9,11},{10,... | collective-permute-start | bytes 786440 | tf_op jit(solution)/shard_map/ppermute | solution.py:359
  91.5 13.0 %collective-permute-start.23 = (bf16[2,128,512]{2,1,0:T(8,128)(2,1)S(1)}, bf16[2,128,512]{2,1,0:T(8,128)(2,1)S(1)}, u32[]{:S(2)}, u32[]{:S(2)}) collective-permute-start(bf16[2,128,512]{2,1,0:T(8,128)(2,1)S(1)} %get-tuple-element.52), channel_id=1, source_target_pairs={{0,2},{1,3},{2,0},{3,1},{4,6},{5,7},{6,4},{7,5},{8,10},{9,11},{10,... | collective-permute-start | bytes 786440 | tf_op jit(solution)/shard_map/ppermute | solution.py:359
  99.8 9.6 %collective-permute-start.24 = (bf16[2,128,512]{2,1,0:T(8,128)(2,1)S(1)}, bf16[2,128,512]{2,1,0:T(8,128)(2,1)S(1)}, u32[]{:S(2)}, u32[]{:S(2)}) collective-permute-start(bf16[2,128,512]{2,1,0:T(8,128)(2,1)S(1)} %add_convert_fusion.2), channel_id=1, source_target_pairs={{0,4},{1,5},{2,6},{3,7},{4,0},{5,1},{6,2},{7,3},{8,12},{9,13},{10,... | collective-permute-start | bytes 786440 | tf_op jit(solution)/shard_map/ppermute | solution.py:389
  100.8 6.8 %collective-permute-start.22 = (bf16[128,512]{1,0:T(8,128)(2,1)S(1)}, bf16[128,512]{1,0:T(8,128)(2,1)S(1)}, u32[]{:S(2)}, u32[]{:S(2)}) collective-permute-start(bf16[128,512]{1,0:T(8,128)(2,1)S(1)} %fusion.8), channel_id=1, source_target_pairs={{0,8},{1,9},{2,10},{3,11},{4,12},{5,13},{6,14},{7,15},{8,0},{9,1},... | collective-permute-start | bytes 393224 | tf_op jit(solution)/shard_map/ppermute | solution.py:359
  109.5 7.7 %collective-permute-start.25 = (bf16[128,512]{1,0:T(8,128)(2,1)S(1)}, bf16[128,512]{1,0:T(8,128)(2,1)S(1)}, u32[]{:S(2)}, u32[]{:S(2)}) collective-permute-start(bf16[128,512]{1,0:T(8,128)(2,1)S(1)} %fusion.9), channel_id=1, source_target_pairs={{0,8},{1,9},{2,10},{3,11},{4,12},{5,13},{6,14},{7,15},{8,0},{9,1},... | collective-permute-start | bytes 393224 | tf_op jit(solution)/shard_map/ppermute | solution.py:359
  (20 other events, 184.6 us)
